TPU v7x, 32 devices: a whole 2x2x4 slice. The times are simulated.
32 devices in a mesh: groups: 2 (over y), seq: 4 (over z), head: 2 (over x), batch: 2 (over core).
Axes of the slice: x: 2, y: 2, z: 4, core: 2. Of those that a mesh axis runs over, the one named last changes fastest.
Arguments:
- x_values: bfloat16 [4, 1024, 8192], P(('groups', 'batch'), 'seq', 'head'), parts along dimension 0, may hold values from -6 to 6
- z_gate: bfloat16 [4, 1024, 8192], P(('groups', 'batch'), 'seq', 'head'), parts along dimension 0, may hold values from -6 to 6
- write_basis: bfloat16 [4, 1024, 1024], P(('groups', 'batch'), 'seq', 'head'), parts along dimension 0, may hold values from -6 to 6
- read_basis: bfloat16 [4, 1024, 1024], P(('groups', 'batch'), 'seq', 'head'), parts along dimension 0, may hold values from -0.5 to 0.5
- step_size: float32 [4, 1024, 128], P(('groups', 'batch'), 'seq', 'head'), parts along dimension 0, may hold values from 0.5 to 2
- log_decay: float32 [4, 1024, 128], P(('groups', 'batch'), 'seq', 'head'), parts along dimension 0, may hold values from -0.8 to 0
- cached_states: bfloat16 [4, 4, 128, 64, 128], P(('groups', 'batch'), None, 'head', 'seq'), parts along dimension 0, may hold values from -96 to 96
- session_slots: int32 [4, 4], P(('groups', 'batch')), parts along dimension 0, may hold values from 0 to 3, each once within a row
- conv_lengths: int32 [4, 4], P(('groups', 'batch')), parts along dimension 0, may hold values from 1 to 4, 8 in all within a row
- norm_gain: float32 [8192], P('head'), may hold values from 0.1 to 1.9
- out_weight: bfloat16 [8192, 4096], P('head', 'seq'), may hold values from -0.0625 to 0.0625
Outputs:
- layer_out: bfloat16 [4, 1024, 4096], P(('groups', 'batch'), 'seq', 'head'), parts along dimension 0
There are 2 independent parts, one for each index of `groups`. A program takes and returns all parts, laid end to end along the dimension named above; an argument that names none is the same for every part. Nothing has to cross between parts.
Inputs may be any that keep to these rules, and one draw needn't show every extreme that they name: `session_slots`: each row's entries name every pool entry once. `conv_lengths`: each row's lengths sum to 8.
All inputs are finite; a program needn't handle non-finite values.
Results may differ from a plain program's by a relative error of at most 0.017.
Values may be sent and summed in bfloat16 or wider, within the bound.
No kernel may reach another device: no remote copies, remote signals or barrier semaphores. Data moves between devices by JAX's collectives and lax.ppermute only.
A program may use at most 128 MiB of HBM per device.

v0:
```python
import jax
import jax.numpy as jnp
from jax import lax
from jax.sharding import PartitionSpec as P

HEAD_DIM = 64
STATE = 128
STRETCH = 128


def prefix(value, axis, join, neutral):
    place = lax.axis_index(axis)
    gathered = jax.tree.map(
        lambda a, kind: lax.all_gather(a.astype(kind), axis), value, (jnp.bfloat16, jnp.bfloat16)
    )
    state = jax.tree.map(lambda a, e: jnp.zeros_like(a) + jnp.asarray(e, a.dtype), value, neutral)

    def one(step, state):
        return join(
            state,
            jax.tree.map(
                lambda a, own: lax.dynamic_index_in_dim(a, step, 0, False).astype(own.dtype),
                gathered,
                value,
            ),
        )

    return lax.fori_loop(0, place, one, state)


def combine_pair(earlier, later):
    gain_a, state_a = earlier
    gain_b, state_b = later
    return (gain_a * gain_b, gain_b[:, None, None] * state_a + state_b)


def run_blocks(state_in, priors, flags, totals, block_states):
    running = state_in
    entering = []
    for number in range(flags.shape[0]):
        running = jnp.where(flags[number], priors[number], running)
        entering.append(running)
        running = totals[number][:, None, None] * running + block_states[number]
    return (jnp.stack(entering), running)


def body(
    x_values,
    z_gate,
    write_basis,
    read_basis,
    step_size,
    log_decay,
    cached_states,
    session_slots,
    conv_lengths,
    norm_gain,
    out_weight,
):
    tokens = x_values.shape[1]
    width = x_values.shape[2]
    heads_dev = step_size.shape[2]
    groups_dev = write_basis.shape[2] // STATE
    per_group = heads_dev // groups_dev
    blocks = tokens // STRETCH
    seq_index = lax.axis_index("seq")
    block_ids = seq_index * blocks + jnp.arange(blocks, dtype=jnp.int32)
    lengths_row = conv_lengths[0]
    begins = jnp.cumsum(lengths_row) - lengths_row
    flags = jnp.any(begins[None, :] == block_ids[:, None], axis=1)
    owners = jnp.sum((begins[None, :] <= block_ids[:, None]).astype(jnp.int32), axis=1) - 1
    convs = jnp.arange(lengths_row.shape[0], dtype=jnp.int32)
    slot_ids = jnp.sum(
        jnp.where(convs[None, :] == owners[:, None], session_slots[0][None, :], 0), axis=1
    )
    picker = (convs[None, :] == slot_ids[:, None]).astype(jnp.bfloat16)
    chosen = jnp.einsum(
        "kc,chpn->khpn",
        picker,
        lax.all_gather(cached_states, "seq", axis=3, tiled=True)[0],
        preferred_element_type=jnp.float32,
    )
    values = x_values[0].reshape(blocks, STRETCH, heads_dev, HEAD_DIM)
    writes = write_basis[0].reshape(blocks, STRETCH, groups_dev, STATE)
    reads = read_basis[0].reshape(blocks, STRETCH, groups_dev, STATE)
    steps_b = step_size[0].reshape(blocks, STRETCH, heads_dev)
    logs = log_decay[0].reshape(blocks, STRETCH, heads_dev)
    running_log = jnp.cumsum(logs, axis=1)
    by_head = jnp.transpose(running_log, (0, 2, 1))
    lower = jnp.arange(STRETCH)[:, None] >= jnp.arange(STRETCH)[None, :]
    spread = by_head[:, :, :, None] - by_head[:, :, None, :]
    fading = jnp.where(lower, jnp.exp(jnp.where(lower, spread, 0.0)), 0.0)
    scores = jnp.einsum("cign,cjgn->cgij", reads, writes, preferred_element_type=jnp.float32)
    scores = jnp.repeat(scores, per_group, axis=1)
    mixing = (scores * fading * jnp.transpose(steps_b, (0, 2, 1))[:, :, None, :]).astype(
        jnp.bfloat16
    )
    inner = jnp.einsum("chij,cjhp->cihp", mixing, values, preferred_element_type=jnp.float32)
    to_end = jnp.exp(running_log[:, -1:, :] - running_log) * steps_b
    write_heads = jnp.repeat(writes, per_group, axis=2)
    weighted = (write_heads.astype(jnp.float32) * to_end[:, :, :, None]).astype(jnp.bfloat16)
    block_states = jnp.einsum(
        "cjhp,cjhn->chpn", values, weighted, preferred_element_type=jnp.float32
    )
    totals = jnp.exp(running_log[:, -1, :])
    whole_gain = jnp.prod(totals, axis=0) * (1.0 - jnp.any(flags).astype(jnp.float32))
    zero_state = jnp.zeros((heads_dev, HEAD_DIM, STATE), jnp.float32)
    ones_head = jnp.ones((heads_dev,), jnp.float32)
    unused, device_state = run_blocks(zero_state, chosen, flags, totals, block_states)
    gain_in, state_in = prefix(
        (whole_gain, device_state), "seq", combine_pair, (ones_head, zero_state)
    )
    entering, unused_end = run_blocks(state_in, chosen, flags, totals, block_states)
    read_heads = jnp.repeat(reads, per_group, axis=2).astype(jnp.float32)
    inflow = jnp.exp(running_log)[:, :, :, None] * jnp.einsum(
        "cihn,chpn->cihp", read_heads, entering, precision=lax.Precision.HIGHEST
    )
    mixed = (inner + inflow).reshape(tokens, width)
    gated = mixed * jax.nn.silu(z_gate[0].astype(jnp.float32))
    grouped = gated.reshape(tokens, groups_dev, -1)
    scaled = grouped * lax.rsqrt(jnp.mean(grouped * grouped, axis=2, keepdims=True) + 1e-05)
    normed = (scaled.reshape(tokens, width) * norm_gain).astype(jnp.bfloat16)
    pairs = lax.axis_size("batch")
    batch_index = lax.axis_index("batch")
    part_cols = out_weight.shape[1] // pairs
    own_part = lax.dynamic_slice_in_dim(out_weight, batch_index * part_cols, part_cols, 1)
    both_rows = lax.all_gather(normed, "batch", axis=0, tiled=True)
    partial_value = jnp.dot(
        both_rows,
        lax.all_gather(own_part, "seq", axis=1, tiled=True),
        preferred_element_type=jnp.float32,
    )
    summed = lax.psum_scatter(
        partial_value.astype(jnp.bfloat16), "head", scatter_dimension=1, tiled=True
    )
    spans = summed.shape[1] // part_cols
    sections = summed.reshape(pairs, tokens, spans, 1, part_cols)
    regrouped = lax.all_to_all(sections, "batch", split_axis=0, concat_axis=3, tiled=True)
    return regrouped.reshape(1, tokens, spans * pairs * part_cols)


def solution(mesh):
    placed = (
        P(("groups", "batch"), "seq", "head"),
        P(("groups", "batch"), "seq", "head"),
        P(("groups", "batch"), "seq", "head"),
        P(("groups", "batch"), "seq", "head"),
        P(("groups", "batch"), "seq", "head"),
        P(("groups", "batch"), "seq", "head"),
        P(("groups", "batch"), None, "head", "seq", None),
        P(("groups", "batch"), None),
        P(("groups", "batch"), None),
        P("head"),
        P("head", "seq"),
    )
    return jax.shard_map(
        body,
        mesh=mesh,
        in_specs=placed,
        out_specs=P(("groups", "batch"), "seq", "head"),
        check_vma=False,
    )
```

profile of v0, /device:TPU:3, one launch (start us, length us, event | category | flops | bytes accessed | tf_op | source)
XLA Modules:
  0.0 581.4 jit_solution(16491451261809305525)
XLA Ops:
  6.5 3.7 copy.109
  10.2 0.0 all-gather.6.cloned.1.call-update
  10.3 0.0 all-gather.8.cloned.1.call-start
  10.3 0.9 copy.125
  11.3 0.2 reduce_window_sum.18
  11.5 0.9 copy.104
  12.4 0.1 copy.112
  12.5 0.1 reshape_squeeze.16
  12.7 5.5 reshape.109
  18.2 5.9 %copy.107 = bf16[2,128,64,64]{1,3,2,0:T(8,128)(2,1)S(1)} copy(bf16[2,128,64,64]{3,2,1,0:T(8,128)(2,1)} %reshape.109) | data formatting | bytes 4194304 | tf_op jit(solution)/shard_map/reshape;squeeze | solution.py:83
  24.1 0.2 reduce-window_clone.1
  24.3 0.9 compare_reduce_fusion
  25.3 0.6 fusion.41
  25.9 0.2 fusion.32
  26.1 0.2 fusion.33
  26.3 1.0 broadcast_in_dim.68
  27.3 4.5 fusion.23
  31.9 60.6 %all-gather.6.cloned.1.call-done = bf16[1,4,64,64,128]{4,1,3,2,0:T(4,128)(2,1)} async-done(((bf16[1,4,64,16,128]{4,1,3,2,0:T(4,128)(2,1)}), bf16[1,4,64,64,128]{4,1,3,2,0:T(4,128)(2,1)}) %all-gather.6.cloned.1.call-update) | async-done | bytes 4194320 | tf_op jit(solution)/shard_map/all_gather | solution.py:80
  92.4 4.6 fusion.13
  97.0 4.8 fusion.39
  101.8 1.3 copy-done.1
  103.1 0.6 copy-done.2
  103.7 2.8 fusion.24
  106.6 0.0 all-gather.8.cloned.1.call-update
  106.6 0.0 all-gather.10.cloned.1.call-start
  107.2 0.6 dynamic-slice
  108.4 0.2 dynamic-update-slice
  108.6 7.5 %all-reduce = bf16[256]{0:T(256)(128)(2,1)S(1)} all-reduce(bf16[256]{0:T(256)(128)(2,1)S(1)} %dynamic-update-slice), channel_id=2, replica_groups=mesh['groups'=2,'seq'=4,'head'=2,'batch'=2] {'seq'}, use_global_device_ids=true, to_apply=%add | all-reduce | flops 256 | bytes 1024
  116.2 0.1 reshape.102
  116.3 0.1 copy.108
  116.3 0.1 reshape_squeeze.15
  116.4 0.1 copy.102
  116.5 0.1 copy.105
  116.6 3.3 copy.117
  119.9 3.7 reshape.101
  123.7 0.3 fusion.28
  124.0 1.0 broadcast_in_dim.60
  125.0 0.5 copy-done.6
  125.6 6.1 %fusion = f32[2,64,128,64]{2,3,1,0:T(8,128)} fusion(bf16[2,128,64,64]{1,3,2,0:T(8,128)(2,1)S(1)} %copy-done.6, f32[2,64,128,128]{3,2,1,0:T(8,128)S(1)} %bitcast.108, f32[2,64,128]{2,1,0:T(8,128)S(1)} %copy.105, f32[2,64,128]{2,1,0:T(8,128)S(1)} %copy.102, pred[128,128]{1,0:T(8,128)(4,1)S(1)} %iota_compare_fusion), kind=kOutput, calls=%fused_computation.4 | convolution fusion | flops 281018368 | bytes 14827520 | tf_op jit(solution)/shard_map/chij,cjhp->cihp/dot_general | solution.py:98
  131.6 54.6 %all-gather.8.cloned.1.call-done = bf16[4,64,64,128]{3,2,1,0:T(8,128)(2,1)} async-done(((bf16[1,64,64,128]{3,2,1,0:T(8,128)(2,1)}), bf16[4,64,64,128]{3,2,1,0:T(8,128)(2,1)}) %all-gather.8.cloned.1.call-update) | async-done | bytes 4194320 | tf_op jit(solution)/shard_map/all_gather | solution.py:14
  186.2 0.2 broadcast_in_dim.66
  186.5 6.5 %fusion.27 = (f32[1,64,64,128]{3,2,1,0:T(8,128)}, f32[1,64,64,128]{3,2,1,0:T(8,128)}) fusion(f32[64,64,128]{2,1,0:T(8,128)} %bitcast.104, f32[64,64,128]{2,1,0:T(8,128)S(1)} %get-tuple-element.49, pred[]{:T(512)} %bitcast.9, f32[64,64,128]{2,1,0:T(8,128)} %bitcast.106, f32[2,64,64,128]{3,2,1,0:T(8,128)} %fusion.23, f32[64]{0:T(128)S(1)} %get-tuple-element.69, ...), kind=kLoop, calls=%fused_computation.38 | loop fusion | flops 2097152 | bytes 12583170 | tf_op jit(solution)/shard_map/stack | solution.py:44
  193.0 1.0 broadcast_in_dim.69
  194.0 1.1 copy-done.7
  195.2 10.9 %multiply_reduce_fusion = (f32[2,128,64]{1,2,0:T(8,128)S(1)}, f32[2,128,64,64]{1,3,2,0:T(8,128)S(1)}) fusion(f32[2,128,64,64]{1,0,3,2:T(2,128)S(1)} %copy-done.7, bf16[2,128,64,128]{3,1,2,0:T(8,128)(2,1)S(1)} %bitcast.109, f32[1,64,64,128]{3,2,1,0:T(8,128)} %get-tuple-element.63, f32[1,64,64,128]{3,2,1,0:T(8,128)} %get-tuple-element.62, ...), kind=kOutput, calls=%fused_computation.23 | convolution fusion | flops 1621082112 | bytes 21102592 | tf_op jit(solution)/shard_map/cihn,chpn->cihp/dot_general | solution.py:115
  206.1 0.0 copy-start.11
  206.1 5.8 copy.116
  211.9 0.1 copy.120
  212.0 0.1 reduce_sum.37
  212.1 4.1 fusion.4
  216.1 0.0 all-gather.10.cloned.1.call-update
  216.2 0.3 all-gather.12.cloned.1.call-start
  216.4 4.4 constant_dynamic-slice_fusion
  220.9 0.0 all-gather.12.cloned.1.call-update
  220.9 0.0 reduce-scatter.2.cloned.1.call-start
  221.0 12.3 %all-gather.10.cloned.1.call-done = bf16[512,4096]{0,1:T(8,128)(2,1)} async-done(((bf16[256,4096]{0,1:T(8,128)(2,1)}), bf16[512,4096]{0,1:T(8,128)(2,1)}) %all-gather.10.cloned.1.call-update) | async-done | bytes 4194320 | tf_op jit(solution)/shard_map/all_gather | solution.py:127
  233.2 288.9 %all-gather.12.cloned.1.call-done = bf16[4096,2048]{1,0:T(8,128)(2,1)} async-done(((bf16[4096,512]{1,0:T(8,128)(2,1)}), bf16[4096,2048]{1,0:T(8,128)(2,1)}) %all-gather.12.cloned.1.call-update) | async-done | bytes 16777232 | tf_op jit(solution)/shard_map/all_gather | solution.py:130
  522.2 14.6 %convolution_convert_fusion = bf16[512,2048]{1,0:T(8,128)(2,1)} fusion(bf16[512,4096]{0,1:T(8,128)(2,1)} %all-gather.10.cloned.1.call-done, bf16[4096,2048]{1,0:T(8,128)(2,1)} %all-gather.12.cloned.1.call-done), kind=kOutput, calls=%fused_computation.30 | convolution fusion | flops 8590983168 | bytes 23068672 | tf_op jit(solution)/shard_map/dot_general | solution.py:128
  536.8 0.0 reduce-scatter.2.cloned.1.call-update
  536.8 29.0 %reduce-scatter.2.cloned.1.call-done = bf16[512,1024]{1,0:T(8,128)(2,1)} async-done(((bf16[512,2048]{1,0:T(8,128)(2,1)}), bf16[512,1024]{1,0:T(8,128)(2,1)}) %reduce-scatter.2.cloned.1.call-update) | async-done | bytes 1048592 | tf_op jit(solution)/shard_map/reduce_scatter | solution.py:133
  565.8 1.8 reshape.96
  567.6 4.7 all_to_all.15
  572.4 1.0 copy.122
  573.4 1.4 copy.123
  (41 shorter events, 0.3 us)
Async XLA Ops:
  6.5 6.0 %copy-start.9 = (bf16[1,256,512]{2,1,0:T(8,128)(2,1)S(1)}, bf16[1,256,512]{2,1,0:T(8,128)(2,1)}, u32[]{:S(2)}) copy-start(bf16[1,256,512]{2,1,0:T(8,128)(2,1)} %param.15) | copy-start | bytes 786436
  6.5 6.1 %copy-start.8 = (bf16[1,256,4096]{2,1,0:T(8,128)(2,1)S(1)}, bf16[1,256,4096]{2,1,0:T(8,128)(2,1)}, u32[]{:S(2)}) copy-start(bf16[1,256,4096]{2,1,0:T(8,128)(2,1)} %param.13) | copy-start | bytes 6291460
  6.5 85.9 %all-gather.6.cloned.1.call-start = ((), (), s32[]{:S(2)}) async-start(), calls=%async_computation.2 | async-start | bytes 5242880 | tf_op jit(solution)/shard_map/all_gather | solution.py:80
  10.3 176.0 %all-gather.8.cloned.1.call-start = ((), (), s32[]{:S(2)}) async-start(), calls=%async_computation.3 | async-start | bytes 5242880 | tf_op jit(solution)/shard_map/all_gather | solution.py:14
  18.2 5.9 %copy-start.12 = (s32[1,4]{1,0:T(1,128)S(1)}, s32[1,4]{1,0:T(1,128)}, u32[]{:S(2)}) copy-start(s32[1,4]{1,0:T(1,128)} %param.21) | copy-start | bytes 52
  18.2 7.8 %copy-start.13 = (s32[1,4]{1,0:T(1,128)S(1)}, s32[1,4]{1,0:T(1,128)}, u32[]{:S(2)}) copy-start(s32[1,4]{1,0:T(1,128)} %param.20) | copy-start | bytes 52
  24.1 3.2 copy-start.5
  97.0 6.7 %copy-start = (f32[2,64,64,128]{3,2,1,0:T(8,128)S(1)}, f32[2,64,64,128]{3,2,1,0:T(8,128)}, u32[]{:S(2)}) copy-start(f32[2,64,64,128]{3,2,1,0:T(8,128)} %fusion.23) | copy-start | bytes 12582916
  101.8 1.4 copy-start.1
  101.8 1.9 copy-start.2
  103.7 3.5 copy-start.14
  103.7 12.6 %copy-start.10 = (bf16[1,256,512]{2,1,0:T(8,128)(2,1)S(1)}, bf16[1,256,512]{2,1,0:T(8,128)(2,1)}, u32[]{:S(2)}) copy-start(bf16[1,256,512]{2,1,0:T(8,128)(2,1)} %param.16) | copy-start | bytes 786436
  106.6 126.7 %all-gather.10.cloned.1.call-start = ((), (), s32[]{:S(2)}) async-start(), calls=%async_computation.4 | async-start | bytes 6291456 | tf_op jit(solution)/shard_map/all_gather | solution.py:127
  119.9 5.2 copy-start.3
  124.0 1.6 copy-start.6
  193.0 2.2 copy-start.7
  206.1 6.0 %copy-start.4 = (bf16[1,256,4096]{1,2,0:T(8,128)(2,1)S(1)}, bf16[1,256,4096]{1,2,0:T(8,128)(2,1)}, u32[]{:S(2)}) copy-start(bf16[1,256,4096]{1,2,0:T(8,128)(2,1)} %copy-done.3) | copy-start | bytes 6291460
  206.1 6.0 %copy-start.11 = (f32[4096]{0:T(1024)S(1)}, f32[4096]{0:T(1024)}, u32[]{:S(2)}) copy-start(f32[4096]{0:T(1024)} %param.22) | copy-start | bytes 49156
  216.2 306.0 %all-gather.12.cloned.1.call-start = ((), (), s32[]{:S(2)}) async-start(), calls=%async_computation.5 | async-start | bytes 20971520 | tf_op jit(solution)/shard_map/all_gather | solution.py:130
  220.9 344.9 %reduce-scatter.2.cloned.1.call-start = ((), (), s32[]{:S(2)}) async-start(), calls=%async_computation.6 | async-start | bytes 3145728 | tf_op jit(solution)/shard_map/reduce_scatter | solution.py:133
Sparse Core Ops, SparseCore 0:
  10.4 81.9 all-gather.5
  106.7 79.4 all-gather.7
  216.3 16.9 all-gather.9
  234.7 287.4 all-gather.11
  537.0 28.7 reduce-scatter.1
where the time goes:
time: 584 us; the launch traced here: 581 us
  waiting for transfers between devices  445 us (76%)
  local copies, waits for them, and re-layouts  52.5 us (9%)
  matrix products  41 us (7%)
  other arithmetic  15.2 us (3%)
  between operations  14.6 us (2%)
  blocking collectives  12.3 us (2%)
    all_gather x1, waiting for transfers between devices, body(): lax.all_gather(own_part, 'seq', axis=1, tiled=True)  289 us
    all_gather x1, waiting for transfers between devices, body(): lax.all_gather(cached_states, 'seq', axis=3, tiled=True)[0]  60.6 us
    all_gather x1, waiting for transfers between devices, prefix(): lax.all_gather(a.astype(kind), axis)  54.6 us
    reduce_scatter x1, waiting for transfers between devices, body(): lax.psum_scatter(partial_value.astype(jnp.bfloat16), 'head', scatter_dime...  29 us
    dot_general x1, matrix products, body(): jnp.dot(both_rows, lax.all_gather(own_part, 'seq', axis=1, tiled=True), p...  14.6 us
    unnamed x36, local copies, waits for them, and re-layouts  12.4 us
    all_gather x1, waiting for transfers between devices, body(): both_rows = lax.all_gather(normed, 'batch', axis=0, tiled=True)  12.3 us
  transfers between devices with their start and end apart: 5, of which 5 were waited for; matrix products, arithmetic and copies ran while one was open for 7% of the time, Pallas kernels for 0%

commit v1 on v0

v1 whole, which is shorter than its diff:
```python
import functools

import jax
import jax.numpy as jnp
from jax import lax
from jax.experimental import pallas as pl
from jax.experimental.pallas import tpu as pltpu
from jax.sharding import PartitionSpec as P

HEAD_DIM = 64
STATE = 128
STRETCH = 128
BF = jnp.bfloat16
F32 = jnp.float32
VMEM_LIMIT = 48 * 1024 * 1024


def widen(per_head, width):
    heads = per_head.shape[1]
    high = per_head.astype(BF)
    low = (per_head - high.astype(F32)).astype(BF)
    both = jnp.concatenate([high, low], axis=1)
    place = lax.broadcasted_iota(jnp.int32, (2 * heads, width), 0)
    lane = lax.broadcasted_iota(jnp.int32, (2 * heads, width), 1)
    place = jnp.where(place >= heads, place - heads, place)
    spread = jnp.where(place == lane // (width // heads), 1.0, 0.0).astype(BF)
    return jnp.dot(both, spread, preferred_element_type=F32)


def states_kernel(x_ref, b_ref, end_ref, out_ref):
    width = x_ref.shape[1]
    for c in range(out_ref.shape[0]):
        rows = pl.ds(c * STRETCH, STRETCH)
        scaled = (x_ref[rows, :].astype(F32) * widen(end_ref[0, rows, :], width)).astype(BF)
        out_ref[c] = lax.dot_general(
            scaled, b_ref[rows, :], (((0,), (0,)), ((), ())), preferred_element_type=F32
        )


def block_states_of(x, b, to_end, blocks):
    tokens, width = x.shape
    groups_dev = b.shape[1] // STATE
    per = width // groups_dev
    return pl.pallas_call(
        states_kernel,
        grid=(groups_dev,),
        in_specs=[
            pl.BlockSpec((tokens, per), lambda g: (0, g)),
            pl.BlockSpec((tokens, STATE), lambda g: (0, g)),
            pl.BlockSpec((1, tokens, to_end.shape[2]), lambda g: (g, 0, 0)),
        ],
        out_specs=pl.BlockSpec((blocks, per, STATE), lambda g: (0, g, 0)),
        out_shape=jax.ShapeDtypeStruct((blocks, width, STATE), F32),
        compiler_params=pltpu.CompilerParams(vmem_limit_bytes=VMEM_LIMIT),
        cost_estimate=pl.CostEstimate(
            flops=2 * tokens * width * STATE * 4, bytes_accessed=8 << 20, transcendentals=0
        ),
    )(x, b, to_end)


def mix_kernel(
    code_ref,
    total_ref,
    x_ref,
    z_ref,
    b_ref,
    c_ref,
    run_ref,
    run_t_ref,
    step_t_ref,
    gain_ref,
    carry_ref,
    late_ref,
    early_ref,
    own_ref,
    out_ref,
    state,
    mixed,
):
    block = pl.program_id(0)
    width = x_ref.shape[1]
    heads = run_ref.shape[2]

    @pl.when(block == 0)
    def _():
        @pl.when(code_ref[0] == 0)
        def _():
            state[...] = carry_ref[...].astype(F32)

        @pl.when(code_ref[0] == 1)
        def _():
            state[...] = late_ref[...].astype(F32)

        @pl.when(code_ref[0] == 2)
        def _():
            state[...] = early_ref[...].astype(F32)

    @pl.when(block > 0)
    def _():
        @pl.when(code_ref[1] == 1)
        def _():
            state[...] = late_ref[...].astype(F32)

        @pl.when(code_ref[1] == 0)
        def _():
            for h in range(heads):
                rows = pl.ds(h * HEAD_DIM, HEAD_DIM)
                state[rows, :] = total_ref[h] * state[rows, :] + own_ref[0, rows, :]

    read = c_ref[...]
    scores = lax.dot_general(
        read, b_ref[...], (((1,), (1,)), ((), ())), preferred_element_type=F32
    )
    running = run_ref[0]
    inflow = lax.dot_general(
        read, state[...].astype(BF), (((1,), (1,)), ((), ())), preferred_element_type=F32
    )
    mixed[...] = inflow * widen(jnp.exp(running), width)
    row = lax.broadcasted_iota(jnp.int32, (STRETCH, STRETCH), 0)
    col = lax.broadcasted_iota(jnp.int32, (STRETCH, STRETCH), 1)
    lower = row >= col
    lane = lax.broadcasted_iota(jnp.int32, (STRETCH, 2 * HEAD_DIM), 1)
    for pair in range(heads // 2):
        mixes = []
        for h in (2 * pair, 2 * pair + 1):
            spread = running[:, h : h + 1] - run_t_ref[0, h : h + 1, :]
            fading = jnp.exp(jnp.where(lower, spread, -1e30))
            mixes.append((scores * fading * step_t_ref[0, h : h + 1, :]).astype(BF))
        lanes = pl.ds(pair * 2 * HEAD_DIM, 2 * HEAD_DIM)
        two = x_ref[:, lanes]
        none = jnp.zeros_like(two)
        stacked = jnp.concatenate(
            [jnp.where(lane < HEAD_DIM, two, none), jnp.where(lane < HEAD_DIM, none, two)], axis=0
        )
        mixed[:, lanes] += jnp.dot(
            jnp.concatenate(mixes, axis=1), stacked, preferred_element_type=F32
        )
    gate = z_ref[...].astype(F32)
    gated = mixed[...] * (gate / (1.0 + jnp.exp(-gate)))
    scale = lax.rsqrt(jnp.mean(gated * gated, axis=1, keepdims=True) + 1e-05)
    out_ref[...] = (gated * scale * gain_ref[...]).astype(BF)


def mix_group(g, code, totals, x, z, b, c, run, run_t, step_t, gain, carry, late, early, own):
    tokens, width = x.shape
    groups_dev = b.shape[1] // STATE
    per = width // groups_dev
    heads = run.shape[2]
    smem = pl.BlockSpec(memory_space=pltpu.SMEM)
    states = pl.BlockSpec((per, STATE), lambda i: (g, 0))
    return pl.pallas_call(
        mix_kernel,
        grid=(tokens // STRETCH,),
        in_specs=[
            smem,
            smem,
            pl.BlockSpec((STRETCH, per), lambda i: (i, g)),
            pl.BlockSpec((STRETCH, per), lambda i: (i, g)),
            pl.BlockSpec((STRETCH, STATE), lambda i: (i, g)),
            pl.BlockSpec((STRETCH, STATE), lambda i: (i, g)),
            pl.BlockSpec((1, STRETCH, heads), lambda i: (g, i, 0)),
            pl.BlockSpec((1, heads, STRETCH), lambda i: (g, 0, i)),
            pl.BlockSpec((1, heads, STRETCH), lambda i: (g, 0, i)),
            pl.BlockSpec((1, per), lambda i: (0, g)),
            pl.BlockSpec((per, STATE), lambda i: (0, 0)),
            states,
            states,
            pl.BlockSpec((1, per, STATE), lambda i: (0, g, 0)),
        ],
        out_specs=pl.BlockSpec((STRETCH, per), lambda i: (i, 0)),
        out_shape=jax.ShapeDtypeStruct((tokens, per), BF),
        scratch_shapes=[pltpu.VMEM((per, STATE), F32), pltpu.VMEM((STRETCH, per), F32)],
        compiler_params=pltpu.CompilerParams(vmem_limit_bytes=VMEM_LIMIT),
        cost_estimate=pl.CostEstimate(
            flops=tokens * per * 2 * 1024, bytes_accessed=4 << 20, transcendentals=0
        ),
    )(code, totals, x, z, b, c, run, run_t, step_t, gain, carry, late, early, own)


def project_kernel(count, pick_ref, *refs):
    lhs = refs[:count]
    first, second, out_ref, weight, sem = refs[count:]

    @pl.when(pick_ref[0] == 0)
    def _():
        pltpu.make_async_copy(first, weight, sem).start()

    @pl.when(pick_ref[0] != 0)
    def _():
        pltpu.make_async_copy(second, weight, sem).start()

    pltpu.make_async_copy(first, weight, sem).wait()
    place = 0
    for r in range(4):
        total = None
        for g in range(count // 4):
            own = lhs[g * 4 + r][...]
            depth = own.shape[1]
            part = jnp.dot(
                own, weight[g * depth : (g + 1) * depth, :], preferred_element_type=F32
            )
            total = part if total is None else total + part
        out_ref[place : place + total.shape[0], :] = total.astype(BF)
        place += total.shape[0]


def project(pick, lhs, first, second):
    tokens = 4 * lhs[0].shape[0]
    cols = first.shape[1]
    whole = pl.BlockSpec(memory_space=pltpu.VMEM)
    hbm = pl.BlockSpec(memory_space=pl.ANY)
    return pl.pallas_call(
        functools.partial(project_kernel, len(lhs)),
        in_specs=[pl.BlockSpec(memory_space=pltpu.SMEM)] + [whole] * len(lhs) + [hbm, hbm],
        out_specs=whole,
        out_shape=jax.ShapeDtypeStruct((tokens, cols), BF),
        scratch_shapes=[pltpu.VMEM(first.shape, BF), pltpu.SemaphoreType.DMA],
        compiler_params=pltpu.CompilerParams(vmem_limit_bytes=VMEM_LIMIT),
        cost_estimate=pl.CostEstimate(
            flops=2 * tokens * first.shape[0] * cols, bytes_accessed=11 << 20, transcendentals=0
        ),
    )(pick, *lhs, first, second)


SWAP = [(0, 1), (1, 0)]


def fast_projection(normed, out_weight):
    seq = lax.axis_index("seq")
    head = lax.axis_index("head")
    y = lax.axis_index("groups")
    core = lax.axis_index("batch")
    quarter = out_weight.shape[1] // 4
    own = lax.dynamic_slice_in_dim(out_weight, (2 * y + core) * quarter, quarter, 1)
    one = lax.ppermute(own, "seq", [(0, 1), (1, 0), (2, 3), (3, 2)])
    two_mid = lax.ppermute(own, "seq", [(1, 2), (2, 1)])
    two_end = lax.ppermute(two_mid, "seq", [(1, 0), (2, 3)])
    three_mid = lax.ppermute(one, "seq", [(1, 2), (2, 1)])
    three_end = lax.ppermute(three_mid, "seq", [(1, 0), (2, 3)])

    lhs = []
    for part in normed:
        across = lax.ppermute(part, "groups", SWAP)
        other = lax.ppermute(part, "batch", SWAP)
        other_across = lax.ppermute(across, "batch", SWAP)
        lhs += [part, other, across, other_across]
    zero = jnp.zeros((1,), jnp.int32)
    is_mid = jnp.logical_or(seq == 1, seq == 2).astype(jnp.int32).reshape(1)
    partials = [
        project(zero, lhs, own, own),
        project(zero, lhs, one, one),
        project(is_mid, lhs, two_end, two_mid),
        project(is_mid, lhs, three_end, three_mid),
    ]
    tokens = normed[0].shape[0]
    rows = []
    for number, partial_value in enumerate(partials):
        late = number >= 2
        goal = [(s // 2 + (1 if late else 0)) % 2 for s in range(4)]
        to_goal = [(2 * s + 1 - goal[s], 2 * s + goal[s]) for s in range(4)]
        arrived = lax.ppermute(partial_value, ("seq", "head"), to_goal)
        total = (partial_value.astype(F32) + arrived.astype(F32)).astype(BF)
        total = total.reshape(4, tokens, quarter)
        ends = [2 * s + goal[s] for s in range(4)]
        cross_y = [(a * 8 + e, (1 - a) * 8 + e) for a in (0, 1) for e in ends]
        from_y = lax.ppermute(total[2:], ("groups", "seq", "head"), cross_y)
        cross_core = [(2 * e + a, 2 * e + 1 - a) for a in (0, 1) for e in ends]
        from_core = lax.ppermute(
            jnp.stack([total[1], from_y[1]]), ("seq", "head", "batch"), cross_core
        )
        rows.append((total[0], from_core[0], from_y[0], from_core[1]))
    is_early = head == seq // 2
    swapped = jnp.where(is_early, seq % 2 == 1, seq >= 2)
    first = [jnp.where(is_early, a, b) for a, b in zip(rows[0], rows[2])]
    second = [jnp.where(is_early, a, b) for a, b in zip(rows[1], rows[3])]
    low = [jnp.where(swapped, b, a) for a, b in zip(first, second)]
    high = [jnp.where(swapped, a, b) for a, b in zip(first, second)]
    pieces = []
    for part in (low, high):
        a, b, c, d = part
        p = [jnp.where(core == 0, a, b), jnp.where(core == 0, b, a)]
        q = [jnp.where(core == 0, c, d), jnp.where(core == 0, d, c)]
        pieces += [jnp.where(y == 0, v, w) for v, w in zip(p + q, q + p)]
    return jnp.concatenate(pieces, axis=1)[None]


def plain_projection(normed, out_weight):
    tokens = normed.shape[0]
    pairs = lax.axis_size("batch")
    batch_index = lax.axis_index("batch")
    part_cols = out_weight.shape[1] // pairs
    own_part = lax.dynamic_slice_in_dim(out_weight, batch_index * part_cols, part_cols, 1)
    both_rows = lax.all_gather(normed, "batch", axis=0, tiled=True)
    partial_value = jnp.dot(
        both_rows,
        lax.all_gather(own_part, "seq", axis=1, tiled=True),
        preferred_element_type=F32,
    )
    summed = lax.psum_scatter(partial_value.astype(BF), "head", scatter_dimension=1, tiled=True)
    spans = summed.shape[1] // part_cols
    sections = summed.reshape(pairs, tokens, spans, 1, part_cols)
    regrouped = lax.all_to_all(sections, "batch", split_axis=0, concat_axis=3, tiled=True)
    return regrouped.reshape(1, tokens, spans * pairs * part_cols)


def exchange_states(cached, wanted, seq, size):
    heads, part = cached.shape[1], cached.shape[2]
    pieces = []
    for offset in range(size):
        entry = lax.dynamic_index_in_dim(wanted, (seq + offset) % size, 0, False)
        piece = lax.dynamic_index_in_dim(cached, entry, 0, False)
        if offset:
            piece = lax.ppermute(piece, "seq", [(i, (i + offset) % size) for i in range(size)])
        pieces.append((piece, (seq - offset) % size))
    whole = jnp.zeros((heads, size, part, cached.shape[3]), cached.dtype)
    owner = jnp.arange(size)[None, :, None, None]
    for piece, source in pieces:
        whole = jnp.where(owner == source, piece[:, None], whole)
    return whole.reshape(heads * size * part, cached.shape[3])


def body(
    x_values,
    z_gate,
    write_basis,
    read_basis,
    step_size,
    log_decay,
    cached_states,
    session_slots,
    conv_lengths,
    norm_gain,
    out_weight,
):
    tokens = x_values.shape[1]
    width = x_values.shape[2]
    heads_dev = step_size.shape[2]
    groups_dev = write_basis.shape[2] // STATE
    per_group = heads_dev // groups_dev
    per = width // groups_dev
    blocks = tokens // STRETCH
    size = lax.axis_size("seq")
    seq = lax.axis_index("seq")
    assert blocks == 2

    lengths_row = conv_lengths[0]
    begins = jnp.cumsum(lengths_row) - lengths_row
    all_blocks = jnp.arange(size * blocks, dtype=jnp.int32)
    starts = jnp.any(begins[None, :] == all_blocks[:, None], axis=1)
    owners = jnp.sum((begins[None, :] <= all_blocks[:, None]).astype(jnp.int32), axis=1) - 1
    convs = jnp.arange(lengths_row.shape[0], dtype=jnp.int32)
    slot_ids = jnp.sum(
        jnp.where(convs[None, :] == owners[:, None], session_slots[0][None, :], 0), axis=1
    )
    starts2 = starts.reshape(size, 2)
    slots2 = slot_ids.reshape(size, 2)
    want_late = jnp.where(starts2[:, 1], slots2[:, 1], slots2[:, 0])
    want_early = slots2[:, 0]
    flags = lax.dynamic_index_in_dim(starts2, seq, 0, False)
    late = exchange_states(cached_states[0], want_late, seq, size)
    early = exchange_states(cached_states[0], want_early, seq, size)
    code = jnp.stack(
        [
            jnp.where(flags[0], jnp.where(flags[1], 2, 1), 0),
            jnp.where(flags[1], 1, 0),
        ]
    ).astype(jnp.int32)

    logs = log_decay[0].reshape(blocks, STRETCH, heads_dev)
    running = jnp.cumsum(logs, axis=1)
    totals = jnp.exp(running[:, -1, :])
    to_end = (jnp.exp(running[:, -1:, :] - running)).reshape(tokens, heads_dev) * step_size[0]
    run = running.reshape(tokens, groups_dev, per_group)
    by_group = jnp.transpose(run, (1, 0, 2))
    by_row = jnp.transpose(run, (1, 2, 0))
    step_t = jnp.transpose(step_size[0].reshape(tokens, groups_dev, per_group), (1, 2, 0))
    end_g = jnp.transpose(to_end.reshape(tokens, groups_dev, per_group), (1, 0, 2))

    x, z, b, c = x_values[0], z_gate[0], write_basis[0], read_basis[0]
    own = block_states_of(x, b, end_g, blocks)

    gain_out = jnp.where(jnp.any(flags), 0.0, totals[0] * totals[1])
    keep = jnp.where(flags[1], 0.0, 1.0)
    wide = (heads_dev, HEAD_DIM, STATE)
    prior = jnp.where(jnp.any(flags), late.reshape(wide).astype(F32), 0.0)
    from_late = jnp.where(flags[1], totals[1], totals[0] * totals[1])[:, None, None]
    end_state = (
        from_late * prior
        + (keep * totals[1])[:, None, None] * own[0].reshape(wide)
        + own[1].reshape(wide)
    ).reshape(groups_dev, per, STATE)
    gain_rows = jnp.repeat(gain_out, HEAD_DIM).reshape(groups_dev, per, 1)

    gain = norm_gain.reshape(1, width)
    normed = []
    for g in range(groups_dev):
        carry = jnp.zeros((per, STATE), BF)
        for hop in range(size - 1):
            leaving = (gain_rows[g] * carry.astype(F32) + end_state[g]).astype(BF)
            carry = carry + lax.ppermute(leaving, "seq", [(hop, hop + 1)])
        heads = slice(g * per_group, (g + 1) * per_group)
        normed.append(
            mix_group(
                g, code, totals[0, heads], x, z, b, c, by_group, by_row, step_t, gain,
                carry, late, early, own,
            )
        )
    shared = lax.axis_size("groups") * lax.axis_size("batch")
    if size == 4 and lax.axis_size("head") == 2 and shared == 4 and out_weight.shape[1] == 1024:
        return fast_projection(normed, out_weight)
    return plain_projection(jnp.concatenate(normed, axis=1), out_weight)


def solution(mesh):
    placed = (
        P(("groups", "batch"), "seq", "head"),
        P(("groups", "batch"), "seq", "head"),
        P(("groups", "batch"), "seq", "head"),
        P(("groups", "batch"), "seq", "head"),
        P(("groups", "batch"), "seq", "head"),
        P(("groups", "batch"), "seq", "head"),
        P(("groups", "batch"), None, "head", "seq", None),
        P(("groups", "batch"), None),
        P(("groups", "batch"), None),
        P("head"),
        P("head", "seq"),
    )
    return jax.shard_map(
        body,
        mesh=mesh,
        in_specs=placed,
        out_specs=P(("groups", "batch"), "seq", "head"),
        check_vma=False,
    )
```

time: 584 us -> 345 us (0.59)
  waiting for transfers between devices: 445 us -> 113 us
  starting transfers between devices: 0.39 us -> 104 us
  Pallas kernels: 0 us -> 41.4 us
  matrix products: 41 us -> 0 us
  local copies, waits for them, and re-layouts: 52.5 us -> 32.3 us
  other arithmetic: 15.2 us -> 33.3 us
  blocking collectives: 12.3 us -> 0 us
    all_gather x4 -> x0, waiting for transfers between devices: 416 us -> none  [the longest x1 289 us: body(): lax.all_gather(own_part, 'seq', axis=1, tiled=True)]
    ppermute x0 -> x47, waiting for transfers between devices: none -> 113 us  [the longest x1 35.6 us: fast_projection(): three_end = lax.ppermute(three_mid, 'seq', [(1, 0), (2, 3)])]
    ppermute x0 -> x47, starting transfers between devices: none -> 104 us  [the longest x6 32.4 us: exchange_states(): lax.ppermute(piece, 'seq', [(i, (i + offset) % size) for i in range(size)])]
    pallas_call x0 -> x9, Pallas kernels: none -> 41.4 us  [the longest x4 24.7 us: project(): pl.pallas_call(functools.partial(project_kernel, len(lhs)), in_specs=[pl....]
    dot_general x6 -> x0, matrix products: 41 us -> none  [the longest x1 14.6 us: body(): jnp.dot(both_rows, lax.all_gather(own_part, 'seq', axis=1, tiled=True), p...]
    reduce_scatter x1 -> x0, waiting for transfers between devices: 29 us -> none  [body(): lax.psum_scatter(partial_value.astype(jnp.bfloat16), 'head', scatter_dime...]
    another operation x5 -> x1, local copies, waits for them, and re-layouts: 11.6 us -> 0.09 us  [body(): running = jnp.cumsum(logs, axis=1)]
    broadcast_in_dim x4 -> x20, local copies, waits for them, and re-layouts: 3.35 us -> 13.3 us  [the longest x16 10.6 us: exchange_states(): whole = jnp.where(owner == source, piece[:, None], whole)]
  transfers between devices with their start and end apart: 5 -> 47, of which waited for: 5 -> 19; matrix products, arithmetic and copies ran while one was open for 7% -> 16% of each run, Pallas kernels for 0% -> 12%
where the time goes in v1:
time: 345 us; the launch traced here: 343 us
  waiting for transfers between devices  113 us (33%)
  starting transfers between devices  104 us (30%)
  Pallas kernels  41.4 us (12%)
  other arithmetic  33.3 us (10%)
  local copies, waits for them, and re-layouts  32.3 us (9%)
  between operations  18.8 us (5%)
    ppermute x1, waiting for transfers between devices, fast_projection(): three_end = lax.ppermute(three_mid, 'seq', [(1, 0), (2, 3)])  35.6 us
    ppermute x6, starting transfers between devices, exchange_states(): lax.ppermute(piece, 'seq', [(i, (i + offset) % size) for i in range(size)])  32.4 us
    pallas_call x4, Pallas kernels, project(): pl.pallas_call(functools.partial(project_kernel, len(lhs)), in_specs=[pl....  24.7 us
    ppermute x12, starting transfers between devices, body(): carry = carry + lax.ppermute(leaving, 'seq', [(hop, hop + 1)])  23.9 us
    ppermute x4, waiting for transfers between devices, fast_projection(): across = lax.ppermute(part, 'groups', SWAP)  21.2 us
    ppermute x4, waiting for transfers between devices, fast_projection(): arrived = lax.ppermute(partial_value, ('seq', 'head'), to_goal)  14.3 us
    pallas_call x4, Pallas kernels, mix_group(): pl.pallas_call(mix_kernel, grid=(tokens // STRETCH,), in_specs=[smem, sme...  12 us
    ppermute x6, waiting for transfers between devices, exchange_states(): lax.ppermute(piece, 'seq', [(i, (i + offset) % size) for i in range(size)])  11.8 us
  transfers between devices with their start and end apart: 47, of which 19 were waited for; matrix products, arithmetic and copies ran while one was open for 16% of the time, Pallas kernels for 12%

profile of v1, /device:TPU:3, one launch (start us, length us, event | category | flops | bytes accessed | tf_op | source)
XLA Modules:
  0.0 342.7 jit_solution(11827245976831745252)
XLA Ops:
  0.0 3.2 constant_dynamic-slice_fusion.refs_16_.refs_17_
  3.2 1.3 collective-permute-start.30
  4.5 2.0 collective-permute-start.36
  22.9 1.3 dynamic-slice_bitcast_fusion.3
  24.3 2.2 collective-permute-start
  26.4 1.6 collective-permute-start.1
  33.4 4.7 %shard_map.109.own_ref = f32[2,4096,128]{2,1,0:T(8,128)} custom-call(bf16[256,4096]{1,0:T(8,128)(2,1)S(1)} %bitcast.209, bf16[256,512]{1,0:T(8,128)(2,1)S(1)} %bitcast.214, f32[4,256,16]{2,1,0:T(8,128)S(1)} %copy.31.end_ref), custom_call_target="tpu_custom_call" | custom-call | flops 1073741824 | bytes 8388608 | tf_op jit(solution)/shard_map/pallas_call | solution.py:44
  38.1 4.5 %fusion.31 = (f32[1,4096,128]{2,1,0:T(8,128)}, f32[1,4096,128]{2,1,0:T(8,128)}) fusion(f32[2,4096,128]{2,1,0:T(8,128)} %shard_map.109.own_ref), kind=kLoop, calls=%fused_computation.135 | loop fusion | bytes 8388608 | tf_op jit(solution)/shard_map/slice | solution.py:389
  43.2 1.9 broadcast_select_fusion.13
  51.1 1.3 broadcast_in_dim.201
  55.6 1.3 broadcast_in_dim.214
  57.0 1.3 broadcast_in_dim.218
  58.3 1.3 broadcast_in_dim.219
  59.6 1.3 broadcast_in_dim.199
  61.7 3.3 collective-permute-start.6
  65.0 11.5 %collective-permute-done.1 = bf16[64,16,128]{2,1,0:T(8,128)(2,1)S(1)} collective-permute-done((bf16[64,16,128]{2,1,0:T(8,128)(2,1)}, bf16[64,16,128]{2,1,0:T(8,128)(2,1)S(1)}, u32[]{:S(2)}, u32[]{:S(2)}) %collective-permute-start.1) | collective-permute-done | bytes 262176 | tf_op jit(solution)/shard_map/ppermute | solution.py:313
  76.5 5.4 %add_add_fusion = f32[64,64,128]{2,1,0:T(8,128)S(1)} fusion(f32[64,64,128]{2,1,0:T(8,128)} %bitcast.242, f32[64,64,128]{2,1,0:T(8,128)} %bitcast.241, f32[64]{0:T(128)} %get-tuple-element.67, f32[64]{0:T(128)} %get-tuple-element.66, pred[64]{0:T(512)(128)(4,1)} %broadcast_in_dim.219, pred[64]{0:T(512)(128)(4,1)} %broadcast_in_dim.214, ...), kind=kLoop, calls=%fused_computation | loop fusion | flops 5242880 | bytes 7340801 | tf_op jit(solution)/shard_map/add | solution.py:388
  82.8 6.8 %collective-permute-start.24 = (bf16[1024,128]{1,0:T(8,128)(2,1)S(1)}, bf16[1024,128]{1,0:T(8,128)(2,1)S(1)}, u32[]{:S(2)}, u32[]{:S(2)}) collective-permute-start(bf16[1024,128]{1,0:T(8,128)(2,1)S(1)} %fusion.9), channel_id=1, source_target_pairs={{0,4},{1,5},{2,6},{3,7},{16,20},{17,21},{18,22},{19,23}} | collective-permute-start | bytes 786440 | tf_op jit(solution)/shard_map/ppermute | solution.py:400
  89.9 1.3 collective-permute-start.18
  91.6 1.7 collective-permute-done.24
  93.4 4.1 %collective-permute-start.12 = (bf16[1024,128]{1,0:T(8,128)(2,1)S(1)}, bf16[1024,128]{1,0:T(8,128)(2,1)S(1)}, u32[]{:S(2)}, u32[]{:S(2)}) collective-permute-start(bf16[1024,128]{1,0:T(8,128)(2,1)S(1)} %fusion.15), channel_id=1, source_target_pairs={{0,4},{1,5},{2,6},{3,7},{16,20},{17,21},{18,22},{19,23}} | collective-permute-start | bytes 786440 | tf_op jit(solution)/shard_map/ppermute | solution.py:400
  97.7 1.3 collective-permute-done.18
  99.0 4.1 %collective-permute-start.3 = (bf16[1024,128]{1,0:T(8,128)(2,1)S(1)}, bf16[1024,128]{1,0:T(8,128)(2,1)S(1)}, u32[]{:S(2)}, u32[]{:S(2)}) collective-permute-start(bf16[1024,128]{1,0:T(8,128)(2,1)S(1)} %fusion.18), channel_id=1, source_target_pairs={{0,4},{1,5},{2,6},{3,7},{16,20},{17,21},{18,22},{19,23}} | collective-permute-start | bytes 786440 | tf_op jit(solution)/shard_map/ppermute | solution.py:400
  103.3 1.3 collective-permute-done.12
  105.5 4.7 %collective-permute-done.3 = bf16[1024,128]{1,0:T(8,128)(2,1)S(1)} collective-permute-done((bf16[1024,128]{1,0:T(8,128)(2,1)S(1)}, bf16[1024,128]{1,0:T(8,128)(2,1)S(1)}, u32[]{:S(2)}, u32[]{:S(2)}) %collective-permute-start.3) | collective-permute-done | bytes 262176 | tf_op jit(solution)/shard_map/ppermute | solution.py:400
  115.5 25.3 %collective-permute-start.8 = (bf16[64,16,128]{2,1,0:T(8,128)(2,1)S(1)}, bf16[64,16,128]{2,1,0:T(8,128)(2,1)S(1)}, u32[]{:S(2)}, u32[]{:S(2)}) collective-permute-start(bf16[64,16,128]{2,1,0:T(8,128)(2,1)S(1)} %copy-done.34), channel_id=1, source_target_pairs={{0,4},{4,8},{8,12},{12,0},{1,5},{5,9},{9,13},{13,1},{2,6},{6,10},{... | collective-permute-start | bytes 786440 | tf_op jit(solution)/shard_map/ppermute | solution.py:313
  142.4 1.4 collective-permute-start.20
  144.1 1.4 collective-permute-start.14
  145.5 1.4 collective-permute-start.5
  150.0 6.0 %fusion.2 = (bf16[4096,128]{1,0:T(8,128)(2,1)S(1)}, bf16[4096,128]{1,0:T(8,128)(2,1)S(1)}) fusion(pred[4096]{0:T(1024)(128)(4,1)S(1)} %broadcast_in_dim.238, pred[4096]{0:T(1024)(128)(4,1)S(1)} %broadcast_in_dim.234, pred[4096]{0:T(1024)(128)(4,1)S(1)} %broadcast_in_dim.230, pred[4096]{0:T(1024)(128)(4,1)S(1)} %broadcast_in_dim.226, ...), kind=kLoop, calls=%fused_computation.4 | loop fusion | flops 4194304 | bytes 4210688 | tf_op jit(solution)/shard_map/jit(_where)/select_n | solution.py:318
  156.2 2.0 collective-permute-start.32
  158.2 3.0 shard_map.113.refs_12_
  161.2 1.3 collective-permute-start.28
  164.6 3.0 shard_map.112.refs_8_
  167.6 7.4 %collective-permute-start.27 = (bf16[256,1024]{1,0:T(8,128)(2,1)S(1)}, bf16[256,1024]{1,0:T(8,128)(2,1)S(1)}, u32[]{:S(2)}, u32[]{:S(2)}) collective-permute-start(bf16[256,1024]{1,0:T(8,128)(2,1)S(1)} %shard_map.113.refs_12_), channel_id=1, source_target_pairs={{0,1},{1,0},{2,3},{3,2},{4,5},{5,4},{6,7},{7,6},{8,9},{9,8},{10,11... | collective-permute-start | bytes 1572872 | tf_op jit(solution)/shard_map/ppermute | solution.py:244
  176.3 3.1 shard_map.111.refs_4_
  181.0 7.5 %collective-permute-done.22.refs_10_ = bf16[256,1024]{1,0:T(8,128)(2,1)S(1)} collective-permute-done((bf16[256,1024]{1,0:T(8,128)(2,1)S(1)}, bf16[256,1024]{1,0:T(8,128)(2,1)S(1)}, u32[]{:S(2)}, u32[]{:S(2)}) %collective-permute-start.22) | collective-permute-done | bytes 524320 | tf_op jit(solution)/shard_map/ppermute | solution.py:243
  188.5 1.3 collective-permute-start.15
  190.8 3.0 shard_map.110.refs_0_
  194.4 5.3 %collective-permute-done.16.refs_6_ = bf16[256,1024]{1,0:T(8,128)(2,1)S(1)} collective-permute-done((bf16[256,1024]{1,0:T(8,128)(2,1)S(1)}, bf16[256,1024]{1,0:T(8,128)(2,1)S(1)}, u32[]{:S(2)}, u32[]{:S(2)}) %collective-permute-start.16) | collective-permute-done | bytes 524320 | tf_op jit(solution)/shard_map/ppermute | solution.py:243
  199.7 1.3 collective-permute-start.9
  202.4 8.5 %collective-permute-done.10.refs_2_ = bf16[256,1024]{1,0:T(8,128)(2,1)S(1)} collective-permute-done((bf16[256,1024]{1,0:T(8,128)(2,1)S(1)}, bf16[256,1024]{1,0:T(8,128)(2,1)S(1)}, u32[]{:S(2)}, u32[]{:S(2)}) %collective-permute-start.10) | collective-permute-done | bytes 524320 | tf_op jit(solution)/shard_map/ppermute | solution.py:243
  214.8 6.6 %shard_map.114 = bf16[1024,256]{1,0:T(8,128)(2,1)} custom-call(s32[1]{0:T(128)} %constant.168.clone.1.pick_ref, bf16[256,1024]{1,0:T(8,128)(2,1)S(1)} %shard_map.110.refs_0_, bf16[256,1024]{1,0:T(8,128)(2,1)S(1)} %collective-permute-done.9.refs_1_, bf16[256,1024]{1,0:T(8,128)(2,1)S(1)} %collective-permute-done.10.refs_2_, ...), custom_call_target="tpu_custom_call" | custom-call | flops 2147483648 | bytes 11534336 | tf_op jit(solution)/shard_map/pallas_call | solution.py:212
  221.4 3.0 collective-permute-start.31
  224.4 6.6 %shard_map.116 = bf16[1024,256]{1,0:T(8,128)(2,1)} custom-call(s32[1]{0:T(128)} %constant.168.clone.1.pick_ref, bf16[256,1024]{1,0:T(8,128)(2,1)S(1)} %shard_map.110.refs_0_, bf16[256,1024]{1,0:T(8,128)(2,1)S(1)} %collective-permute-done.9.refs_1_, bf16[256,1024]{1,0:T(8,128)(2,1)S(1)} %collective-permute-done.10.refs_2_, ...), custom_call_target="tpu_custom_call" | custom-call | flops 2147483648 | bytes 11534336 | tf_op jit(solution)/shard_map/pallas_call | solution.py:212
  231.0 2.1 collective-permute-start.35
  233.1 1.7 collective-permute-done.31
  234.8 1.3 add_convert_fusion.3
  236.9 9.2 %collective-permute-done.35 = bf16[1024,256]{1,0:T(8,128)(2,1)} collective-permute-done((bf16[1024,256]{1,0:T(8,128)(2,1)}, bf16[1024,256]{1,0:T(8,128)(2,1)}, u32[]{:S(2)}, u32[]{:S(2)}) %collective-permute-start.35) | collective-permute-done | bytes 524320 | tf_op jit(solution)/shard_map/ppermute | solution.py:261
  246.0 1.3 add_convert_fusion.1
  248.1 11.8 %collective-permute-done.37.refs_16_ = bf16[4096,256]{1,0:T(8,128)(2,1)} collective-permute-done((bf16[4096,256]{1,0:T(8,128)(2,1)}, bf16[4096,256]{1,0:T(8,128)(2,1)}, u32[]{:S(2)}, u32[]{:S(2)}) %collective-permute-start.37) | collective-permute-done | bytes 2097184 | tf_op jit(solution)/shard_map/ppermute | solution.py:237
  259.9 5.8 %shard_map.117 = bf16[1024,256]{1,0:T(8,128)(2,1)S(1)} custom-call(s32[1]{0:T(128)} %bitcast.59.pick_ref, bf16[256,1024]{1,0:T(8,128)(2,1)S(1)} %shard_map.110.refs_0_, bf16[256,1024]{1,0:T(8,128)(2,1)S(1)} %collective-permute-done.9.refs_1_, bf16[256,1024]{1,0:T(8,128)(2,1)S(1)} %collective-permute-done.10.refs_2_, ...), custom_call_target="tpu_custom_call" | custom-call | flops 2147483648 | bytes 11534336 | tf_op jit(solution)/shard_map/pallas_call | solution.py:212
  265.7 1.3 collective-permute-start.38
  267.8 1.4 collective-permute-start.40
  269.2 35.6 %collective-permute-done.33.refs_16_ = bf16[4096,256]{1,0:T(8,128)(2,1)} collective-permute-done((bf16[4096,256]{1,0:T(8,128)(2,1)}, bf16[4096,256]{1,0:T(8,128)(2,1)}, u32[]{:S(2)}, u32[]{:S(2)}) %collective-permute-start.33) | collective-permute-done | bytes 2097184 | tf_op jit(solution)/shard_map/ppermute | solution.py:239
  304.8 5.8 %shard_map.115 = bf16[1024,256]{1,0:T(8,128)(2,1)S(1)} custom-call(s32[1]{0:T(128)} %bitcast.59.pick_ref, bf16[256,1024]{1,0:T(8,128)(2,1)S(1)} %shard_map.110.refs_0_, bf16[256,1024]{1,0:T(8,128)(2,1)S(1)} %collective-permute-done.9.refs_1_, bf16[256,1024]{1,0:T(8,128)(2,1)S(1)} %collective-permute-done.10.refs_2_, ...), custom_call_target="tpu_custom_call" | custom-call | flops 2147483648 | bytes 11534336 | tf_op jit(solution)/shard_map/pallas_call | solution.py:212
  310.6 1.3 collective-permute-start.34
  312.1 2.4 collective-permute-start.45
  315.4 5.4 %collective-permute-done.45 = bf16[2,256,256]{2,1,0:T(8,128)(2,1)S(1)} collective-permute-done((bf16[2,256,256]{2,1,0:T(8,128)(2,1)S(1)}, bf16[2,256,256]{2,1,0:T(8,128)(2,1)S(1)}, u32[]{:S(2)}, u32[]{:S(2)}) %collective-permute-start.45) | collective-permute-done | bytes 262176 | tf_op jit(solution)/shard_map/ppermute | solution.py:266
  321.5 3.4 collective-permute-done.34
  325.1 2.4 collective-permute-start.41
  327.5 4.1 %collective-permute-start.46 = (bf16[2,256,256]{2,1,0:T(8,128)(2,1)S(1)}, bf16[2,256,256]{2,1,0:T(8,128)(2,1)S(1)}, u32[]{:S(2)}, u32[]{:S(2)}) collective-permute-start(bf16[2,256,256]{2,1,0:T(8,128)(2,1)S(1)} %pad_maximum_fusion.3), channel_id=1, source_target_pairs={{2,3},{6,7},{8,9},{12,13},{3,2},{7,6},{9,8},{13,12},{18,19},{22,23... | collective-permute-start | bytes 786440 | tf_op jit(solution)/shard_map/ppermute | solution.py:268
  333.6 4.8 %collective-permute-start.42 = (bf16[2,256,256]{2,1,0:T(8,128)(2,1)S(1)}, bf16[2,256,256]{2,1,0:T(8,128)(2,1)S(1)}, u32[]{:S(2)}, u32[]{:S(2)}) collective-permute-start(bf16[2,256,256]{2,1,0:T(8,128)(2,1)S(1)} %pad_maximum_fusion.1), channel_id=1, source_target_pairs={{2,3},{6,7},{8,9},{12,13},{3,2},{7,6},{9,8},{13,12},{18,19},{22,23... | collective-permute-start | bytes 786440 | tf_op jit(solution)/shard_map/ppermute | solution.py:268
  339.5 1.5 fusion.27
  (270 shorter events, 48.3 us)
Async XLA Ops:
  3.2 152.9 %collective-permute-start.30 = (bf16[4096,256]{1,0:T(8,128)(2,1)}, bf16[4096,256]{1,0:T(8,128)(2,1)}, u32[]{:S(2)}, u32[]{:S(2)}) collective-permute-start(bf16[4096,256]{1,0:T(8,128)(2,1)} %constant_dynamic-slice_fusion.refs_16_.refs_17_), channel_id=1, source_target_pairs={{0,4},{4,0},{8,12},{12,8},{1,5},{5,1},{9,13},{13,9},{2,6},{6,2},{1... | collective-permute-start | bytes 6291464 | tf_op jit(solution)/shard_map/ppermute | solution.py:235
  4.5 196.6 %collective-permute-start.36 = (bf16[4096,256]{1,0:T(8,128)(2,1)}, bf16[4096,256]{1,0:T(8,128)(2,1)}, u32[]{:S(2)}, u32[]{:S(2)}) collective-permute-start(bf16[4096,256]{1,0:T(8,128)(2,1)} %constant_dynamic-slice_fusion.refs_16_.refs_17_), channel_id=1, source_target_pairs={{4,8},{8,4},{5,9},{9,5},{6,10},{10,6},{7,11},{11,7},{20,24},{24,20... | collective-permute-start | bytes 6291464 | tf_op jit(solution)/shard_map/ppermute | solution.py:236
  24.3 37.4 %collective-permute-start = (bf16[64,16,128]{2,1,0:T(8,128)(2,1)}, bf16[64,16,128]{2,1,0:T(8,128)(2,1)S(1)}, u32[]{:S(2)}, u32[]{:S(2)}) collective-permute-start(bf16[64,16,128]{2,1,0:T(8,128)(2,1)} %get-tuple-element.46), channel_id=1, source_target_pairs={{0,12},{4,0},{8,4},{12,8},{1,13},{5,1},{9,5},{13,9},{2,14},{6,2},{... | collective-permute-start | bytes 786440 | tf_op jit(solution)/shard_map/ppermute | solution.py:313
  26.4 50.0 %collective-permute-start.1 = (bf16[64,16,128]{2,1,0:T(8,128)(2,1)}, bf16[64,16,128]{2,1,0:T(8,128)(2,1)S(1)}, u32[]{:S(2)}, u32[]{:S(2)}) collective-permute-start(bf16[64,16,128]{2,1,0:T(8,128)(2,1)} %get-tuple-element.45), channel_id=1, source_target_pairs={{0,8},{4,12},{8,0},{12,4},{1,9},{5,13},{9,1},{13,5},{2,10},{6,14},... | collective-permute-start | bytes 786440 | tf_op jit(solution)/shard_map/ppermute | solution.py:313
  28.0 48.5 %collective-permute-start.2 = (bf16[64,16,128]{2,1,0:T(8,128)(2,1)}, bf16[64,16,128]{2,1,0:T(8,128)(2,1)}, u32[]{:S(2)}, u32[]{:S(2)}) collective-permute-start(bf16[64,16,128]{2,1,0:T(8,128)(2,1)} %get-tuple-element.44), channel_id=1, source_target_pairs={{0,4},{4,8},{8,12},{12,0},{1,5},{5,9},{9,13},{13,1},{2,6},{6,10},{... | collective-permute-start | bytes 786440 | tf_op jit(solution)/shard_map/ppermute | solution.py:313
  38.1 38.4 %copy-start.23 = (bf16[64,16,128]{2,1,0:T(8,128)(2,1)S(1)}, bf16[64,16,128]{2,1,0:T(8,128)(2,1)}, u32[]{:S(2)}) copy-start(bf16[64,16,128]{2,1,0:T(8,128)(2,1)} %get-tuple-element.43) | copy-start | bytes 786436
  61.7 53.8 %collective-permute-start.6 = (bf16[64,16,128]{2,1,0:T(8,128)(2,1)S(1)}, bf16[64,16,128]{2,1,0:T(8,128)(2,1)S(1)}, u32[]{:S(2)}, u32[]{:S(2)}) collective-permute-start(bf16[64,16,128]{2,1,0:T(8,128)(2,1)S(1)} %copy-done.36), channel_id=1, source_target_pairs={{0,12},{4,0},{8,4},{12,8},{1,13},{5,1},{9,5},{13,9},{2,14},{6,2},{... | collective-permute-start | bytes 786440 | tf_op jit(solution)/shard_map/ppermute | solution.py:313
  82.8 10.5 %collective-permute-start.24 = (bf16[1024,128]{1,0:T(8,128)(2,1)S(1)}, bf16[1024,128]{1,0:T(8,128)(2,1)S(1)}, u32[]{:S(2)}, u32[]{:S(2)}) collective-permute-start(bf16[1024,128]{1,0:T(8,128)(2,1)S(1)} %fusion.9), channel_id=1, source_target_pairs={{0,4},{1,5},{2,6},{3,7},{16,20},{17,21},{18,22},{19,23}} | collective-permute-start | bytes 786440 | tf_op jit(solution)/shard_map/ppermute | solution.py:400
  89.9 9.1 %collective-permute-start.18 = (bf16[1024,128]{1,0:T(8,128)(2,1)S(1)}, bf16[1024,128]{1,0:T(8,128)(2,1)S(1)}, u32[]{:S(2)}, u32[]{:S(2)}) collective-permute-start(bf16[1024,128]{1,0:T(8,128)(2,1)S(1)} %fusion.12), channel_id=1, source_target_pairs={{0,4},{1,5},{2,6},{3,7},{16,20},{17,21},{18,22},{19,23}} | collective-permute-start | bytes 786440 | tf_op jit(solution)/shard_map/ppermute | solution.py:400
  93.4 11.2 %collective-permute-start.12 = (bf16[1024,128]{1,0:T(8,128)(2,1)S(1)}, bf16[1024,128]{1,0:T(8,128)(2,1)S(1)}, u32[]{:S(2)}, u32[]{:S(2)}) collective-permute-start(bf16[1024,128]{1,0:T(8,128)(2,1)S(1)} %fusion.15), channel_id=1, source_target_pairs={{0,4},{1,5},{2,6},{3,7},{16,20},{17,21},{18,22},{19,23}} | collective-permute-start | bytes 786440 | tf_op jit(solution)/shard_map/ppermute | solution.py:400
  99.0 11.2 %collective-permute-start.3 = (bf16[1024,128]{1,0:T(8,128)(2,1)S(1)}, bf16[1024,128]{1,0:T(8,128)(2,1)S(1)}, u32[]{:S(2)}, u32[]{:S(2)}) collective-permute-start(bf16[1024,128]{1,0:T(8,128)(2,1)S(1)} %fusion.18), channel_id=1, source_target_pairs={{0,4},{1,5},{2,6},{3,7},{16,20},{17,21},{18,22},{19,23}} | collective-permute-start | bytes 786440 | tf_op jit(solution)/shard_map/ppermute | solution.py:400
  104.6 5.9 %collective-permute-start.25 = (bf16[1024,128]{1,0:T(8,128)(2,1)S(1)}, bf16[1024,128]{1,0:T(8,128)(2,1)S(1)}, u32[]{:S(2)}, u32[]{:S(2)}) collective-permute-start(bf16[1024,128]{1,0:T(8,128)(2,1)S(1)} %fusion.10), channel_id=1, source_target_pairs={{4,8},{5,9},{6,10},{7,11},{20,24},{21,25},{22,26},{23,27}} | collective-permute-start | bytes 786440 | tf_op jit(solution)/shard_map/ppermute | solution.py:400
  110.2 32.2 %collective-permute-start.7 = (bf16[64,16,128]{2,1,0:T(8,128)(2,1)S(1)}, bf16[64,16,128]{2,1,0:T(8,128)(2,1)S(1)}, u32[]{:S(2)}, u32[]{:S(2)}) collective-permute-start(bf16[64,16,128]{2,1,0:T(8,128)(2,1)S(1)} %copy-done.35), channel_id=1, source_target_pairs={{0,8},{4,12},{8,0},{12,4},{1,9},{5,13},{9,1},{13,5},{2,10},{6,14},... | collective-permute-start | bytes 786440 | tf_op jit(solution)/shard_map/ppermute | solution.py:313
  110.4 1.7 collective-permute-start.19
  112.1 34.7 %copy-start.51 = (f32[2,64]{1,0:T(2,128)S(1)}, f32[2,64]{1,0:T(2,128)}, u32[]{:S(2)}) copy-start(f32[2,64]{1,0:T(2,128)} %copy-done.50) | copy-start | bytes 1540
  112.1 36.1 %copy-start.54 = (pred[4]{0:T(512)(128)(4,1)S(1)}, pred[4]{0:T(512)(128)(4,1)}, u32[]{:S(2)}) copy-start(pred[4]{0:T(512)(128)(4,1)} %iota_compare_fusion.6) | copy-start | bytes 16
  112.1 36.3 %copy-start.55 = (pred[4]{0:T(512)(128)(4,1)S(1)}, pred[4]{0:T(512)(128)(4,1)}, u32[]{:S(2)}) copy-start(pred[4]{0:T(512)(128)(4,1)} %iota_compare_fusion.5) | copy-start | bytes 16
  112.1 36.5 %copy-start.57 = (pred[4]{0:T(512)(128)(4,1)S(1)}, pred[4]{0:T(512)(128)(4,1)}, u32[]{:S(2)}) copy-start(pred[4]{0:T(512)(128)(4,1)} %copy-done.56) | copy-start | bytes 16
  112.1 36.7 %copy-start.53 = (pred[4]{0:T(512)(128)(4,1)S(1)}, pred[4]{0:T(512)(128)(4,1)}, u32[]{:S(2)}) copy-start(pred[4]{0:T(512)(128)(4,1)} %iota_compare_fusion.3) | copy-start | bytes 16
  112.2 1.6 collective-permute-start.13
  113.8 27.0 %collective-permute-start.4 = (bf16[1024,128]{1,0:T(8,128)(2,1)S(1)}, bf16[1024,128]{1,0:T(8,128)(2,1)S(1)}, u32[]{:S(2)}, u32[]{:S(2)}) collective-permute-start(bf16[1024,128]{1,0:T(8,128)(2,1)S(1)} %fusion.19), channel_id=1, source_target_pairs={{4,8},{5,9},{6,10},{7,11},{20,24},{21,25},{22,26},{23,27}} | collective-permute-start | bytes 786440 | tf_op jit(solution)/shard_map/ppermute | solution.py:400
  115.5 30.0 %copy-start.37 = (bf16[64,16,128]{2,1,0:T(8,128)(2,1)}, bf16[64,16,128]{2,1,0:T(8,128)(2,1)S(1)}, u32[]{:S(2)}) copy-start(bf16[64,16,128]{2,1,0:T(8,128)(2,1)S(1)} %collective-permute-done.6) | copy-start | bytes 786436
  115.5 28.6 %collective-permute-start.8 = (bf16[64,16,128]{2,1,0:T(8,128)(2,1)S(1)}, bf16[64,16,128]{2,1,0:T(8,128)(2,1)S(1)}, u32[]{:S(2)}, u32[]{:S(2)}) collective-permute-start(bf16[64,16,128]{2,1,0:T(8,128)(2,1)S(1)} %copy-done.34), channel_id=1, source_target_pairs={{0,4},{4,8},{8,12},{12,0},{1,5},{5,9},{9,13},{13,1},{2,6},{6,10},{... | collective-permute-start | bytes 786440 | tf_op jit(solution)/shard_map/ppermute | solution.py:313
  140.8 4.7 %collective-permute-start.26 = (bf16[1024,128]{1,0:T(8,128)(2,1)S(1)}, bf16[1024,128]{1,0:T(8,128)(2,1)S(1)}, u32[]{:S(2)}, u32[]{:S(2)}) collective-permute-start(bf16[1024,128]{1,0:T(8,128)(2,1)S(1)} %get-tuple-element.25), channel_id=1, source_target_pairs={{8,12},{9,13},{10,14},{11,15},{24,28},{25,29},{26,30},{27,31}} | collective-permute-start | bytes 786440 | tf_op jit(solution)/shard_map/ppermute | solution.py:400
  142.4 18.8 %collective-permute-start.20 = (bf16[1024,128]{1,0:T(8,128)(2,1)}, bf16[1024,128]{1,0:T(8,128)(2,1)}, u32[]{:S(2)}, u32[]{:S(2)}) collective-permute-start(bf16[1024,128]{1,0:T(8,128)(2,1)} %get-tuple-element.27), channel_id=1, source_target_pairs={{8,12},{9,13},{10,14},{11,15},{24,28},{25,29},{26,30},{27,31}} | collective-permute-start | bytes 786440 | tf_op jit(solution)/shard_map/ppermute | solution.py:400
  144.1 23.5 %collective-permute-start.14 = (bf16[1024,128]{1,0:T(8,128)(2,1)}, bf16[1024,128]{1,0:T(8,128)(2,1)}, u32[]{:S(2)}, u32[]{:S(2)}) collective-permute-start(bf16[1024,128]{1,0:T(8,128)(2,1)} %get-tuple-element.29), channel_id=1, source_target_pairs={{8,12},{9,13},{10,14},{11,15},{24,28},{25,29},{26,30},{27,31}} | collective-permute-start | bytes 786440 | tf_op jit(solution)/shard_map/ppermute | solution.py:400
  145.5 29.5 %collective-permute-start.5 = (bf16[1024,128]{1,0:T(8,128)(2,1)}, bf16[1024,128]{1,0:T(8,128)(2,1)}, u32[]{:S(2)}, u32[]{:S(2)}) collective-permute-start(bf16[1024,128]{1,0:T(8,128)(2,1)} %get-tuple-element.31), channel_id=1, source_target_pairs={{8,12},{9,13},{10,14},{11,15},{24,28},{25,29},{26,30},{27,31}} | collective-permute-start | bytes 786440 | tf_op jit(solution)/shard_map/ppermute | solution.py:400
  156.2 56.2 %collective-permute-start.32 = (bf16[4096,256]{1,0:T(8,128)(2,1)}, bf16[4096,256]{1,0:T(8,128)(2,1)}, u32[]{:S(2)}, u32[]{:S(2)}) collective-permute-start(bf16[4096,256]{1,0:T(8,128)(2,1)} %collective-permute-done.30.refs_16_.refs_17_), channel_id=1, source_target_pairs={{4,8},{8,4},{5,9},{9,5},{6,10},{10,6},{7,11},{11,7},{20,24},{24,20... | collective-permute-start | bytes 6291464 | tf_op jit(solution)/shard_map/ppermute | solution.py:238
  161.2 18.1 %collective-permute-start.28 = (bf16[256,1024]{1,0:T(8,128)(2,1)S(1)}, bf16[256,1024]{1,0:T(8,128)(2,1)S(1)}, u32[]{:S(2)}, u32[]{:S(2)}) collective-permute-start(bf16[256,1024]{1,0:T(8,128)(2,1)S(1)} %shard_map.113.refs_12_), channel_id=1, source_target_pairs={{0,16},{16,0},{1,17},{17,1},{2,18},{18,2},{3,19},{19,3},{4,20},{20... | collective-permute-start | bytes 1572872 | tf_op jit(solution)/shard_map/ppermute | solution.py:243
  167.6 12.2 %collective-permute-start.27 = (bf16[256,1024]{1,0:T(8,128)(2,1)S(1)}, bf16[256,1024]{1,0:T(8,128)(2,1)S(1)}, u32[]{:S(2)}, u32[]{:S(2)}) collective-permute-start(bf16[256,1024]{1,0:T(8,128)(2,1)S(1)} %shard_map.113.refs_12_), channel_id=1, source_target_pairs={{0,1},{1,0},{2,3},{3,2},{4,5},{5,4},{6,7},{7,6},{8,9},{9,8},{10,11... | collective-permute-start | bytes 1572872 | tf_op jit(solution)/shard_map/ppermute | solution.py:244
  175.0 13.5 %collective-permute-start.22 = (bf16[256,1024]{1,0:T(8,128)(2,1)S(1)}, bf16[256,1024]{1,0:T(8,128)(2,1)S(1)}, u32[]{:S(2)}, u32[]{:S(2)}) collective-permute-start(bf16[256,1024]{1,0:T(8,128)(2,1)S(1)} %shard_map.112.refs_8_), channel_id=1, source_target_pairs={{0,16},{16,0},{1,17},{17,1},{2,18},{18,2},{3,19},{19,3},{4,20},{20... | collective-permute-start | bytes 1572872 | tf_op jit(solution)/shard_map/ppermute | solution.py:243
  179.3 45.0 %copy-start.2 = (bf16[256,1024]{1,0:T(8,128)(2,1)}, bf16[256,1024]{1,0:T(8,128)(2,1)S(1)}, u32[]{:S(2)}) copy-start(bf16[256,1024]{1,0:T(8,128)(2,1)S(1)} %shard_map.111.refs_4_) | copy-start | bytes 1572868
  179.4 14.5 %collective-permute-start.21 = (bf16[256,1024]{1,0:T(8,128)(2,1)S(1)}, bf16[256,1024]{1,0:T(8,128)(2,1)S(1)}, u32[]{:S(2)}, u32[]{:S(2)}) collective-permute-start(bf16[256,1024]{1,0:T(8,128)(2,1)S(1)} %shard_map.112.refs_8_), channel_id=1, source_target_pairs={{0,1},{1,0},{2,3},{3,2},{4,5},{5,4},{6,7},{7,6},{8,9},{9,8},{10,11... | collective-permute-start | bytes 1572872 | tf_op jit(solution)/shard_map/ppermute | solution.py:244
  179.8 19.9 %collective-permute-start.16 = (bf16[256,1024]{1,0:T(8,128)(2,1)S(1)}, bf16[256,1024]{1,0:T(8,128)(2,1)S(1)}, u32[]{:S(2)}, u32[]{:S(2)}) collective-permute-start(bf16[256,1024]{1,0:T(8,128)(2,1)S(1)} %shard_map.111.refs_4_), channel_id=1, source_target_pairs={{0,16},{16,0},{1,17},{17,1},{2,18},{18,2},{3,19},{19,3},{4,20},{20... | collective-permute-start | bytes 1572872 | tf_op jit(solution)/shard_map/ppermute | solution.py:243
  188.5 12.6 %collective-permute-start.15 = (bf16[256,1024]{1,0:T(8,128)(2,1)S(1)}, bf16[256,1024]{1,0:T(8,128)(2,1)S(1)}, u32[]{:S(2)}, u32[]{:S(2)}) collective-permute-start(bf16[256,1024]{1,0:T(8,128)(2,1)S(1)} %shard_map.111.refs_4_), channel_id=1, source_target_pairs={{0,1},{1,0},{2,3},{3,2},{4,5},{5,4},{6,7},{7,6},{8,9},{9,8},{10,11... | collective-permute-start | bytes 1572872 | tf_op jit(solution)/shard_map/ppermute | solution.py:244
  193.8 30.6 %copy-start.7 = (bf16[256,1024]{1,0:T(8,128)(2,1)}, bf16[256,1024]{1,0:T(8,128)(2,1)S(1)}, u32[]{:S(2)}) copy-start(bf16[256,1024]{1,0:T(8,128)(2,1)S(1)} %collective-permute-done.21.refs_9_) | copy-start | bytes 1572868
  193.8 17.1 %collective-permute-start.10 = (bf16[256,1024]{1,0:T(8,128)(2,1)S(1)}, bf16[256,1024]{1,0:T(8,128)(2,1)S(1)}, u32[]{:S(2)}, u32[]{:S(2)}) collective-permute-start(bf16[256,1024]{1,0:T(8,128)(2,1)S(1)} %shard_map.110.refs_0_), channel_id=1, source_target_pairs={{0,16},{16,0},{1,17},{17,1},{2,18},{18,2},{3,19},{19,3},{4,20},{20... | collective-permute-start | bytes 1572872 | tf_op jit(solution)/shard_map/ppermute | solution.py:243
  199.7 12.1 %collective-permute-start.9 = (bf16[256,1024]{1,0:T(8,128)(2,1)S(1)}, bf16[256,1024]{1,0:T(8,128)(2,1)S(1)}, u32[]{:S(2)}, u32[]{:S(2)}) collective-permute-start(bf16[256,1024]{1,0:T(8,128)(2,1)S(1)} %shard_map.110.refs_0_), channel_id=1, source_target_pairs={{0,1},{1,0},{2,3},{3,2},{4,5},{5,4},{6,7},{7,6},{8,9},{9,8},{10,11... | collective-permute-start | bytes 1572872 | tf_op jit(solution)/shard_map/ppermute | solution.py:244
  201.0 10.8 %collective-permute-start.29 = (bf16[256,1024]{1,0:T(8,128)(2,1)S(1)}, bf16[256,1024]{1,0:T(8,128)(2,1)S(1)}, u32[]{:S(2)}, u32[]{:S(2)}) collective-permute-start(bf16[256,1024]{1,0:T(8,128)(2,1)S(1)} %collective-permute-done.28.refs_14_), channel_id=1, source_target_pairs={{0,1},{1,0},{2,3},{3,2},{4,5},{5,4},{6,7},{7,6},{8,9},{9,8},{10,11... | collective-permute-start | bytes 1572872 | tf_op jit(solution)/shard_map/ppermute | solution.py:245
  201.1 58.8 %collective-permute-start.37 = (bf16[4096,256]{1,0:T(8,128)(2,1)}, bf16[4096,256]{1,0:T(8,128)(2,1)}, u32[]{:S(2)}, u32[]{:S(2)}) collective-permute-start(bf16[4096,256]{1,0:T(8,128)(2,1)} %collective-permute-done.36.refs_17_), channel_id=1, source_target_pairs={{4,0},{8,12},{5,1},{9,13},{6,2},{10,14},{7,3},{11,15},{20,16},{24,... | collective-permute-start | bytes 6291464 | tf_op jit(solution)/shard_map/ppermute | solution.py:237
  210.9 2.7 collective-permute-start.23
  211.8 2.3 collective-permute-start.17
  211.9 3.0 collective-permute-start.11
  212.3 92.5 %collective-permute-start.33 = (bf16[4096,256]{1,0:T(8,128)(2,1)}, bf16[4096,256]{1,0:T(8,128)(2,1)}, u32[]{:S(2)}, u32[]{:S(2)}) collective-permute-start(bf16[4096,256]{1,0:T(8,128)(2,1)} %collective-permute-done.32.refs_17_), channel_id=1, source_target_pairs={{4,0},{8,12},{5,1},{9,13},{6,2},{10,14},{7,3},{11,15},{20,16},{24,... | collective-permute-start | bytes 6291464 | tf_op jit(solution)/shard_map/ppermute | solution.py:239
  221.4 13.4 %collective-permute-start.31 = (bf16[1024,256]{1,0:T(8,128)(2,1)}, bf16[1024,256]{1,0:T(8,128)(2,1)}, u32[]{:S(2)}, u32[]{:S(2)}) collective-permute-start(bf16[1024,256]{1,0:T(8,128)(2,1)} %shard_map.114), channel_id=1, source_target_pairs={{2,0},{6,4},{8,10},{12,14},{3,1},{7,5},{9,11},{13,15},{18,16},{22,... | collective-permute-start | bytes 1572872 | tf_op jit(solution)/shard_map/ppermute | solution.py:261
  231.0 15.1 %collective-permute-start.35 = (bf16[1024,256]{1,0:T(8,128)(2,1)}, bf16[1024,256]{1,0:T(8,128)(2,1)}, u32[]{:S(2)}, u32[]{:S(2)}) collective-permute-start(bf16[1024,256]{1,0:T(8,128)(2,1)} %shard_map.116), channel_id=1, source_target_pairs={{2,0},{6,4},{8,10},{12,14},{3,1},{7,5},{9,11},{13,15},{18,16},{22,... | collective-permute-start | bytes 1572872 | tf_op jit(solution)/shard_map/ppermute | solution.py:261
  233.1 26.8 %copy-start.3 = (bf16[256,1024]{1,0:T(8,128)(2,1)S(1)}, bf16[256,1024]{1,0:T(8,128)(2,1)}, u32[]{:S(2)}) copy-start(bf16[256,1024]{1,0:T(8,128)(2,1)} %copy-done.2) | copy-start | bytes 1572868
  233.1 26.8 %copy-start.8 = (bf16[256,1024]{1,0:T(8,128)(2,1)S(1)}, bf16[256,1024]{1,0:T(8,128)(2,1)}, u32[]{:S(2)}) copy-start(bf16[256,1024]{1,0:T(8,128)(2,1)} %copy-done.7) | copy-start | bytes 1572868
  233.1 26.8 %copy-start.10 = (bf16[256,1024]{1,0:T(8,128)(2,1)S(1)}, bf16[256,1024]{1,0:T(8,128)(2,1)}, u32[]{:S(2)}) copy-start(bf16[256,1024]{1,0:T(8,128)(2,1)} %copy-done.9) | copy-start | bytes 1572868
  233.1 26.8 %copy-start.12 = (bf16[256,1024]{1,0:T(8,128)(2,1)S(1)}, bf16[256,1024]{1,0:T(8,128)(2,1)}, u32[]{:S(2)}) copy-start(bf16[256,1024]{1,0:T(8,128)(2,1)} %copy-done.11) | copy-start | bytes 1572868
  236.2 30.8 %collective-permute-start.39 = (bf16[2,256,256]{2,1,0:T(8,128)(2,1)S(1)}, bf16[2,256,256]{2,1,0:T(8,128)(2,1)S(1)}, u32[]{:S(2)}, u32[]{:S(2)}) collective-permute-start(bf16[2,256,256]{2,1,0:T(8,128)(2,1)S(1)} %bitcast.245), channel_id=1, source_target_pairs={{0,16},{4,20},{10,26},{14,30},{16,0},{20,4},{26,10},{30,14},{1,17}... | collective-permute-start | bytes 786440 | tf_op jit(solution)/shard_map/ppermute | solution.py:266
  247.4 21.8 %collective-permute-start.43 = (bf16[2,256,256]{2,1,0:T(8,128)(2,1)S(1)}, bf16[2,256,256]{2,1,0:T(8,128)(2,1)S(1)}, u32[]{:S(2)}, u32[]{:S(2)}) collective-permute-start(bf16[2,256,256]{2,1,0:T(8,128)(2,1)S(1)} %bitcast.244), channel_id=1, source_target_pairs={{0,16},{4,20},{10,26},{14,30},{16,0},{20,4},{26,10},{30,14},{1,17}... | collective-permute-start | bytes 786440 | tf_op jit(solution)/shard_map/ppermute | solution.py:266
  265.7 46.2 %collective-permute-start.38 = (bf16[1024,256]{1,0:T(8,128)(2,1)S(1)}, bf16[1024,256]{1,0:T(8,128)(2,1)S(1)}, u32[]{:S(2)}, u32[]{:S(2)}) collective-permute-start(bf16[1024,256]{1,0:T(8,128)(2,1)S(1)} %shard_map.117), channel_id=1, source_target_pairs={{0,2},{4,6},{10,8},{14,12},{1,3},{5,7},{11,9},{15,13},{16,18},{20,... | collective-permute-start | bytes 1572872 | tf_op jit(solution)/shard_map/ppermute | solution.py:261
  267.0 43.6 %copy-start.42 = (bf16[2,256,256]{2,1,0:T(8,128)(2,1)}, bf16[2,256,256]{2,1,0:T(8,128)(2,1)S(1)}, u32[]{:S(2)}) copy-start(bf16[2,256,256]{2,1,0:T(8,128)(2,1)S(1)} %collective-permute-done.39) | copy-start | bytes 786436
  267.8 70.6 %collective-permute-start.40 = (bf16[2,256,256]{2,1,0:T(8,128)(2,1)}, bf16[2,256,256]{2,1,0:T(8,128)(2,1)}, u32[]{:S(2)}, u32[]{:S(2)}) collective-permute-start(bf16[2,256,256]{2,1,0:T(8,128)(2,1)} %pad_maximum_fusion), channel_id=1, source_target_pairs={{0,1},{4,5},{10,11},{14,15},{1,0},{5,4},{11,10},{15,14},{16,17},{2... | collective-permute-start | bytes 786440 | tf_op jit(solution)/shard_map/ppermute | solution.py:268
  269.2 41.4 %copy-start.32 = (bf16[2,256,256]{2,1,0:T(8,128)(2,1)}, bf16[2,256,256]{2,1,0:T(8,128)(2,1)S(1)}, u32[]{:S(2)}) copy-start(bf16[2,256,256]{2,1,0:T(8,128)(2,1)S(1)} %collective-permute-done.43) | copy-start | bytes 786436
  310.6 14.3 %collective-permute-start.34 = (bf16[1024,256]{1,0:T(8,128)(2,1)S(1)}, bf16[1024,256]{1,0:T(8,128)(2,1)S(1)}, u32[]{:S(2)}, u32[]{:S(2)}) collective-permute-start(bf16[1024,256]{1,0:T(8,128)(2,1)S(1)} %shard_map.115), channel_id=1, source_target_pairs={{0,2},{4,6},{10,8},{14,12},{1,3},{5,7},{11,9},{15,13},{16,18},{20,... | collective-permute-start | bytes 1572872 | tf_op jit(solution)/shard_map/ppermute | solution.py:261
  312.1 8.7 %collective-permute-start.45 = (bf16[2,256,256]{2,1,0:T(8,128)(2,1)S(1)}, bf16[2,256,256]{2,1,0:T(8,128)(2,1)S(1)}, u32[]{:S(2)}, u32[]{:S(2)}) collective-permute-start(bf16[2,256,256]{2,1,0:T(8,128)(2,1)S(1)} %bitcast.246), channel_id=1, source_target_pairs={{2,18},{6,22},{8,24},{12,28},{18,2},{22,6},{24,8},{28,12},{3,19},{... | collective-permute-start | bytes 786440 | tf_op jit(solution)/shard_map/ppermute | solution.py:266
  314.6 24.9 %copy-start.33 = (bf16[2,256,256]{2,1,0:T(8,128)(2,1)S(1)}, bf16[2,256,256]{2,1,0:T(8,128)(2,1)}, u32[]{:S(2)}) copy-start(bf16[2,256,256]{2,1,0:T(8,128)(2,1)} %copy-done.32) | copy-start | bytes 786436
  314.6 24.9 %copy-start.43 = (bf16[2,256,256]{2,1,0:T(8,128)(2,1)S(1)}, bf16[2,256,256]{2,1,0:T(8,128)(2,1)}, u32[]{:S(2)}) copy-start(bf16[2,256,256]{2,1,0:T(8,128)(2,1)} %copy-done.42) | copy-start | bytes 786436
  314.6 23.8 %collective-permute-start.44 = (bf16[2,256,256]{2,1,0:T(8,128)(2,1)S(1)}, bf16[2,256,256]{2,1,0:T(8,128)(2,1)S(1)}, u32[]{:S(2)}, u32[]{:S(2)}) collective-permute-start(bf16[2,256,256]{2,1,0:T(8,128)(2,1)S(1)} %pad_maximum_fusion.2), channel_id=1, source_target_pairs={{0,1},{4,5},{10,11},{14,15},{1,0},{5,4},{11,10},{15,14},{16,17},{2... | collective-permute-start | bytes 786440 | tf_op jit(solution)/shard_map/ppermute | solution.py:268
  325.1 7.8 %collective-permute-start.41 = (bf16[2,256,256]{2,1,0:T(8,128)(2,1)S(1)}, bf16[2,256,256]{2,1,0:T(8,128)(2,1)S(1)}, u32[]{:S(2)}, u32[]{:S(2)}) collective-permute-start(bf16[2,256,256]{2,1,0:T(8,128)(2,1)S(1)} %bitcast.247), channel_id=1, source_target_pairs={{2,18},{6,22},{8,24},{12,28},{18,2},{22,6},{24,8},{28,12},{3,19},{... | collective-permute-start | bytes 786440 | tf_op jit(solution)/shard_map/ppermute | solution.py:266
  327.5 10.9 %collective-permute-start.46 = (bf16[2,256,256]{2,1,0:T(8,128)(2,1)S(1)}, bf16[2,256,256]{2,1,0:T(8,128)(2,1)S(1)}, u32[]{:S(2)}, u32[]{:S(2)}) collective-permute-start(bf16[2,256,256]{2,1,0:T(8,128)(2,1)S(1)} %pad_maximum_fusion.3), channel_id=1, source_target_pairs={{2,3},{6,7},{8,9},{12,13},{3,2},{7,6},{9,8},{13,12},{18,19},{22,23... | collective-permute-start | bytes 786440 | tf_op jit(solution)/shard_map/ppermute | solution.py:268
  333.6 5.9 %collective-permute-start.42 = (bf16[2,256,256]{2,1,0:T(8,128)(2,1)S(1)}, bf16[2,256,256]{2,1,0:T(8,128)(2,1)S(1)}, u32[]{:S(2)}, u32[]{:S(2)}) collective-permute-start(bf16[2,256,256]{2,1,0:T(8,128)(2,1)S(1)} %pad_maximum_fusion.1), channel_id=1, source_target_pairs={{2,3},{6,7},{8,9},{12,13},{3,2},{7,6},{9,8},{13,12},{18,19},{22,23... | collective-permute-start | bytes 786440 | tf_op jit(solution)/shard_map/ppermute | solution.py:268
  (44 other events, 441.8 us)

commit v2 on v1

v2 whole, which is shorter than its diff:
```python
import functools

import jax
import jax.numpy as jnp
from jax import lax
from jax.experimental import pallas as pl
from jax.experimental.pallas import tpu as pltpu
from jax.sharding import PartitionSpec as P

HEAD_DIM = 64
STATE = 128
STRETCH = 128
BF = jnp.bfloat16
F32 = jnp.float32
VMEM_LIMIT = 48 * 1024 * 1024
SMALL = pl.CostEstimate(flops=1000, bytes_accessed=1000, transcendentals=0)


def widen(per_head, width):
    heads = per_head.shape[1]
    high = per_head.astype(BF)
    low = (per_head - high.astype(F32)).astype(BF)
    both = jnp.concatenate([high, low], axis=1)
    place = lax.broadcasted_iota(jnp.int32, (2 * heads, width), 0)
    lane = lax.broadcasted_iota(jnp.int32, (2 * heads, width), 1)
    place = jnp.where(place >= heads, place - heads, place)
    spread = jnp.where(place == lane // (width // heads), 1.0, 0.0).astype(BF)
    return jnp.dot(both, spread, preferred_element_type=F32)


def states_kernel(x_ref, b_ref, end_ref, out_ref):
    width = x_ref.shape[1]
    for c in range(out_ref.shape[0]):
        rows = pl.ds(c * STRETCH, STRETCH)
        scaled = (x_ref[rows, :].astype(F32) * widen(end_ref[0, rows, :], width)).astype(BF)
        out_ref[c] = lax.dot_general(
            scaled, b_ref[rows, :], (((0,), (0,)), ((), ())), preferred_element_type=F32
        )


def block_states_of(x, b, to_end, blocks):
    tokens, width = x.shape
    groups_dev = b.shape[1] // STATE
    per = width // groups_dev
    return pl.pallas_call(
        states_kernel,
        grid=(groups_dev,),
        in_specs=[
            pl.BlockSpec((tokens, per), lambda g: (0, g)),
            pl.BlockSpec((tokens, STATE), lambda g: (0, g)),
            pl.BlockSpec((1, tokens, to_end.shape[2]), lambda g: (g, 0, 0)),
        ],
        out_specs=pl.BlockSpec((blocks, per, STATE), lambda g: (0, g, 0)),
        out_shape=jax.ShapeDtypeStruct((blocks, width, STATE), F32),
        compiler_params=pltpu.CompilerParams(vmem_limit_bytes=VMEM_LIMIT),
        cost_estimate=SMALL,
    )(x, b, to_end)


def pick_kernel(size, seq_ref, lengths_ref, slots_ref, cached, *refs):
    late, early, code_ref, sems = refs[:size], refs[size : 2 * size], refs[2 * size], refs[-1]
    convs = lengths_ref.shape[1]
    begins = [jnp.int32(0)]
    for j in range(convs - 1):
        begins.append(begins[-1] + lengths_ref[0, j])

    def starts(block):
        found = begins[0] == block
        for begin in begins[1:]:
            found = jnp.logical_or(found, begin == block)
        return found

    def slot(block):
        entry = slots_ref[0, 0]
        for j in range(1, convs):
            entry = jnp.where(begins[j] <= block, slots_ref[0, j], entry)
        return entry

    seq = seq_ref[0]
    copies = []
    for offset in range(size):
        target = seq + offset
        target = 2 * jnp.where(target >= size, target - size, target)
        last = jnp.where(starts(target + 1), slot(target + 1), slot(target))
        copies.append(pltpu.make_async_copy(cached.at[0, last], late[offset], sems.at[offset]))
        copies[-1].start()
        copies.append(
            pltpu.make_async_copy(cached.at[0, slot(target)], early[offset], sems.at[size + offset])
        )
        copies[-1].start()
    first = starts(2 * seq)
    second = starts(2 * seq + 1)
    code_ref[0] = jnp.where(first, jnp.where(second, 2, 1), 0).astype(jnp.int32)
    code_ref[1] = jnp.where(second, 1, 0).astype(jnp.int32)
    for copy in copies:
        copy.wait()


def pick_states(seq, lengths, slots, cached, size):
    smem = pl.BlockSpec(memory_space=pltpu.SMEM)
    hbm = pl.BlockSpec(memory_space=pl.ANY)
    piece = jax.ShapeDtypeStruct(cached.shape[2:], cached.dtype)
    out = pl.pallas_call(
        functools.partial(pick_kernel, size),
        in_specs=[smem, smem, smem, hbm],
        out_specs=[hbm] * (2 * size) + [smem],
        out_shape=[piece] * (2 * size) + [jax.ShapeDtypeStruct((2,), jnp.int32)],
        scratch_shapes=[pltpu.SemaphoreType.DMA((2 * size,))],
        cost_estimate=SMALL,
    )(seq.reshape(1), lengths, slots, cached)
    return out[:size], out[size : 2 * size], out[2 * size]


def end_kernel(code_ref, total_ref, late_ref, own_ref, out_ref):
    heads = out_ref.shape[0] // HEAD_DIM
    first = pl.program_id(0) * heads
    plain = jnp.logical_and(code_ref[0] == 0, code_ref[1] == 0)
    for h in range(heads):
        rows = pl.ds(h * HEAD_DIM, HEAD_DIM)
        gain0, gain1 = total_ref[0, first + h], total_ref[1, first + h]
        use_late = jnp.where(plain, 0.0, jnp.where(code_ref[1] == 1, gain1, gain0 * gain1))
        use_own = jnp.where(code_ref[1] == 1, 0.0, gain1)
        out_ref[rows, :] = (
            jnp.where(plain, 0.0, late_ref[rows, :].astype(F32) * use_late)
            + own_ref[0, rows, :] * use_own
            + own_ref[1, rows, :]
        )


def end_states(code, totals, late, own, per):
    width = late.shape[0]
    smem = pl.BlockSpec(memory_space=pltpu.SMEM)
    rows = pl.BlockSpec((per, STATE), lambda g: (g, 0))
    return pl.pallas_call(
        end_kernel,
        grid=(width // per,),
        in_specs=[smem, smem, rows, pl.BlockSpec((2, per, STATE), lambda g: (0, g, 0))],
        out_specs=rows,
        out_shape=jax.ShapeDtypeStruct((width, STATE), F32),
        cost_estimate=SMALL,
    )(code, totals, late, own)


def leave_kernel(place, code_ref, total_ref, carry_ref, end_ref, out_ref):
    heads = out_ref.shape[0] // HEAD_DIM
    first = (place + pl.program_id(0)) * heads
    passes = jnp.logical_and(code_ref[0] == 0, code_ref[1] == 0)
    for h in range(heads):
        rows = pl.ds(h * HEAD_DIM, HEAD_DIM)
        gain = jnp.where(passes, total_ref[0, first + h] * total_ref[1, first + h], 0.0)
        out_ref[rows, :] = (carry_ref[rows, :].astype(F32) * gain + end_ref[rows, :]).astype(BF)


def leaving_state(place, code, totals, carry, ends, per):
    smem = pl.BlockSpec(memory_space=pltpu.SMEM)
    rows = pl.BlockSpec((per, STATE), lambda g: (g, 0))
    return pl.pallas_call(
        functools.partial(leave_kernel, place),
        grid=(carry.shape[0] // per,),
        in_specs=[smem, smem, rows, pl.BlockSpec((per, STATE), lambda g: (place + g, 0))],
        out_specs=rows,
        out_shape=jax.ShapeDtypeStruct(carry.shape, BF),
        cost_estimate=SMALL,
    )(code, totals, carry, ends)


def mix_kernel(
    place,
    code_ref,
    total_ref,
    x_ref,
    z_ref,
    b_ref,
    c_ref,
    run_ref,
    run_t_ref,
    step_t_ref,
    gain_ref,
    carry_ref,
    late_ref,
    early_ref,
    own_ref,
    out_ref,
    state,
    mixed,
):
    block = pl.program_id(1)
    width = x_ref.shape[1]
    heads = run_ref.shape[2]
    head = (place + pl.program_id(0)) * heads

    @pl.when(block == 0)
    def _():
        @pl.when(code_ref[0] == 0)
        def _():
            state[...] = carry_ref[...].astype(F32)

        @pl.when(code_ref[0] == 1)
        def _():
            state[...] = late_ref[...].astype(F32)

        @pl.when(code_ref[0] == 2)
        def _():
            state[...] = early_ref[...].astype(F32)

    @pl.when(block > 0)
    def _():
        @pl.when(code_ref[1] == 1)
        def _():
            state[...] = late_ref[...].astype(F32)

        @pl.when(code_ref[1] == 0)
        def _():
            for h in range(heads):
                rows = pl.ds(h * HEAD_DIM, HEAD_DIM)
                state[rows, :] = total_ref[0, head + h] * state[rows, :] + own_ref[0, rows, :]

    read = c_ref[...]
    scores = lax.dot_general(
        read, b_ref[...], (((1,), (1,)), ((), ())), preferred_element_type=F32
    )
    running = run_ref[0]
    inflow = lax.dot_general(
        read, state[...].astype(BF), (((1,), (1,)), ((), ())), preferred_element_type=F32
    )
    mixed[...] = inflow * widen(jnp.exp(running), width)
    row = lax.broadcasted_iota(jnp.int32, (STRETCH, STRETCH), 0)
    col = lax.broadcasted_iota(jnp.int32, (STRETCH, STRETCH), 1)
    lower = row >= col
    lane = lax.broadcasted_iota(jnp.int32, (STRETCH, 2 * HEAD_DIM), 1)
    for pair in range(heads // 2):
        mixes = []
        for h in (2 * pair, 2 * pair + 1):
            spread = running[:, h : h + 1] - run_t_ref[0, h : h + 1, :]
            fading = jnp.exp(jnp.where(lower, spread, -1e30))
            mixes.append((scores * fading * step_t_ref[0, h : h + 1, :]).astype(BF))
        lanes = pl.ds(pair * 2 * HEAD_DIM, 2 * HEAD_DIM)
        two = x_ref[:, lanes]
        none = jnp.zeros_like(two)
        stacked = jnp.concatenate(
            [jnp.where(lane < HEAD_DIM, two, none), jnp.where(lane < HEAD_DIM, none, two)], axis=0
        )
        mixed[:, lanes] += jnp.dot(
            jnp.concatenate(mixes, axis=1), stacked, preferred_element_type=F32
        )
    gate = z_ref[...].astype(F32)
    gated = mixed[...] * (gate / (1.0 + jnp.exp(-gate)))
    scale = lax.rsqrt(jnp.mean(gated * gated, axis=1, keepdims=True) + 1e-05)
    out_ref[...] = (gated * scale * gain_ref[...]).astype(BF)


def mix_groups(place, count, code, totals, x, z, b, c, run, run_t, step_t, gain, carry, late, early, own):
    tokens, width = x.shape
    groups_dev = b.shape[1] // STATE
    per = width // groups_dev
    heads = run.shape[2]
    smem = pl.BlockSpec(memory_space=pltpu.SMEM)
    states = pl.BlockSpec((per, STATE), lambda g, i: (place + g, 0))
    wide = pl.BlockSpec((STRETCH, per), lambda g, i: (i, place + g))
    basis = pl.BlockSpec((STRETCH, STATE), lambda g, i: (i, place + g))
    rows = pl.BlockSpec((1, heads, STRETCH), lambda g, i: (place + g, 0, i))
    return pl.pallas_call(
        functools.partial(mix_kernel, place),
        grid=(count, tokens // STRETCH),
        in_specs=[
            smem,
            smem,
            wide,
            wide,
            basis,
            basis,
            pl.BlockSpec((1, STRETCH, heads), lambda g, i: (place + g, i, 0)),
            rows,
            rows,
            pl.BlockSpec((1, per), lambda g, i: (0, place + g)),
            pl.BlockSpec((per, STATE), lambda g, i: (g, 0)),
            states,
            states,
            pl.BlockSpec((1, per, STATE), lambda g, i: (0, place + g, 0)),
        ],
        out_specs=pl.BlockSpec((STRETCH, per), lambda g, i: (i, g)),
        out_shape=jax.ShapeDtypeStruct((tokens, count * per), BF),
        scratch_shapes=[pltpu.VMEM((per, STATE), F32), pltpu.VMEM((STRETCH, per), F32)],
        compiler_params=pltpu.CompilerParams(vmem_limit_bytes=VMEM_LIMIT),
        cost_estimate=SMALL,
    )(code, totals, x, z, b, c, run, run_t, step_t, gain, carry, late, early, own)


def project_kernel(count, picks, seq_ref, *refs):
    lhs = refs[: 4 * count]
    arrays = refs[4 * count : -3]
    out_ref, weight, sems = refs[-3:]
    depth = lhs[0].shape[1]
    cols = weight.shape[2]
    for n, block in enumerate(picks):
        for half, where in enumerate(block):
            for choice in sorted(set(where)):
                mine = [s for s, other in enumerate(where) if other == choice]
                hit = seq_ref[0] == mine[0]
                for s in mine[1:]:
                    hit = jnp.logical_or(hit, seq_ref[0] == s)

                @pl.when(hit)
                def _(n=n, half=half, choice=choice):
                    pltpu.make_async_copy(
                        arrays[choice[0]].at[pl.ds(choice[1], depth)],
                        weight.at[n, pl.ds(half * depth, depth)],
                        sems.at[n],
                    ).start()

    for n in range(len(picks)):
        pltpu.make_async_copy(weight.at[n], weight.at[n], sems.at[n]).wait()
        for r in range(4):
            total = None
            for half in range(count):
                part = jnp.dot(
                    lhs[4 * half + r][...],
                    weight[n, half * depth : (half + 1) * depth, :],
                    preferred_element_type=F32,
                )
                total = part if total is None else total + part
            rows = total.shape[0]
            out_ref[r * rows : (r + 1) * rows, n * cols : (n + 1) * cols] = total.astype(BF)


def project(seq, lhs, arrays, picks):
    count = len(lhs) // 4
    tokens = 4 * lhs[0].shape[0]
    cols = arrays[0].shape[1]
    depth = lhs[0].shape[1]
    whole = pl.BlockSpec(memory_space=pltpu.VMEM)
    hbm = pl.BlockSpec(memory_space=pl.ANY)
    return pl.pallas_call(
        functools.partial(project_kernel, count, picks),
        in_specs=[pl.BlockSpec(memory_space=pltpu.SMEM)]
        + [whole] * len(lhs)
        + [hbm] * len(arrays),
        out_specs=whole,
        out_shape=jax.ShapeDtypeStruct((tokens, len(picks) * cols), BF),
        scratch_shapes=[
            pltpu.VMEM((len(picks), count * depth, cols), BF),
            pltpu.SemaphoreType.DMA((len(picks),)),
        ],
        compiler_params=pltpu.CompilerParams(vmem_limit_bytes=VMEM_LIMIT),
        cost_estimate=SMALL,
    )(seq.reshape(1), *lhs, *arrays)


SWAP = [(0, 1), (1, 0)]


def after(value, *others):
    return lax.optimization_barrier((value, *others))[0]


def finish_fast(seq, head, y, core, early_sums, late_sums, tokens, quarter):
    is_early = head == seq // 2
    swapped = jnp.where(is_early, seq % 2 == 1, seq >= 2)
    first = [jnp.where(is_early, a, b) for a, b in zip(early_sums[0], late_sums[0])]
    second = [jnp.where(is_early, a, b) for a, b in zip(early_sums[1], late_sums[1])]
    low = [jnp.where(swapped, b, a) for a, b in zip(first, second)]
    high = [jnp.where(swapped, a, b) for a, b in zip(first, second)]
    pieces = []
    for part in (low, high):
        a, b, c, d = part
        p = [jnp.where(core == 0, a, b), jnp.where(core == 0, b, a)]
        q = [jnp.where(core == 0, c, d), jnp.where(core == 0, d, c)]
        pieces += [jnp.where(y == 0, v, w) for v, w in zip(p + q, q + p)]
    return jnp.concatenate(pieces, axis=1)[None]


def to_rows(partial_value, late, tokens):
    goal = [(s // 2 + (1 if late else 0)) % 2 for s in range(4)]
    to_goal = [(2 * s + 1 - goal[s], 2 * s + goal[s]) for s in range(4)]
    arrived = lax.ppermute(partial_value, ("seq", "head"), to_goal)
    total = (partial_value.astype(F32) + arrived.astype(F32)).astype(BF)
    total = total.reshape(4, tokens, total.shape[1])
    ends = [2 * s + goal[s] for s in range(4)]
    cross_y = [(a * 8 + e, (1 - a) * 8 + e) for a in (0, 1) for e in ends]
    from_y = lax.ppermute(total[2:], ("groups", "seq", "head"), cross_y)
    cross_core = [(2 * e + a, 2 * e + 1 - a) for a in (0, 1) for e in ends]
    from_core = lax.ppermute(
        jnp.stack([total[1], from_y[1]]), ("seq", "head", "batch"), cross_core
    )
    return total[0], from_core[0], from_y[0], from_core[1]


def plain_projection(normed, out_weight):
    tokens = normed.shape[0]
    pairs = lax.axis_size("batch")
    batch_index = lax.axis_index("batch")
    part_cols = out_weight.shape[1] // pairs
    own_part = lax.dynamic_slice_in_dim(out_weight, batch_index * part_cols, part_cols, 1)
    both_rows = lax.all_gather(normed, "batch", axis=0, tiled=True)
    partial_value = jnp.dot(
        both_rows,
        lax.all_gather(own_part, "seq", axis=1, tiled=True),
        preferred_element_type=F32,
    )
    summed = lax.psum_scatter(partial_value.astype(BF), "head", scatter_dimension=1, tiled=True)
    spans = summed.shape[1] // part_cols
    sections = summed.reshape(pairs, tokens, spans, 1, part_cols)
    regrouped = lax.all_to_all(sections, "batch", split_axis=0, concat_axis=3, tiled=True)
    return regrouped.reshape(1, tokens, spans * pairs * part_cols)


def exchange_states(payload, seq, size):
    heads, part, state = payload[0].shape
    whole = jnp.zeros((heads, size, part, state), payload[0].dtype)
    owner = jnp.arange(size)[None, :, None, None]
    for offset, piece in enumerate(payload):
        if offset:
            piece = lax.ppermute(piece, "seq", [(i, (i + offset) % size) for i in range(size)])
        whole = jnp.where(owner == (seq - offset) % size, piece[:, None], whole)
    return whole.reshape(heads * size * part, state)


def body(
    x_values,
    z_gate,
    write_basis,
    read_basis,
    step_size,
    log_decay,
    cached_states,
    session_slots,
    conv_lengths,
    norm_gain,
    out_weight,
):
    tokens = x_values.shape[1]
    width = x_values.shape[2]
    heads_dev = step_size.shape[2]
    groups_dev = write_basis.shape[2] // STATE
    per_group = heads_dev // groups_dev
    per = width // groups_dev
    blocks = tokens // STRETCH
    size = lax.axis_size("seq")
    seq = lax.axis_index("seq")
    assert blocks == 2

    shared = lax.axis_size("groups") * lax.axis_size("batch")
    fast = (
        size == 4
        and lax.axis_size("head") == 2
        and shared == 4
        and out_weight.shape == (4096, 1024)
        and groups_dev == 4
    )
    late_out, early_out, code = pick_states(
        seq, conv_lengths, session_slots, cached_states, size
    )
    late = exchange_states(late_out, seq, size)
    head = lax.axis_index("head")
    y = lax.axis_index("groups")
    core = lax.axis_index("batch")
    if fast:
        quarter = out_weight.shape[1] // 4
        half = out_weight.shape[0] // 2
        w_own = lax.dynamic_slice_in_dim(
            after(out_weight, code), (2 * y + core) * quarter, quarter, 1
        )
        w_side = lax.ppermute(w_own, "seq", [(1, 0), (3, 2), (2, 3)])
        w_mid = lax.ppermute(w_own, "seq", [(1, 2), (2, 1)])

    logs = log_decay[0].reshape(blocks, STRETCH, heads_dev)
    running = jnp.cumsum(logs, axis=1)
    totals = jnp.exp(running[:, -1, :])
    to_end = (jnp.exp(running[:, -1:, :] - running)).reshape(tokens, heads_dev) * step_size[0]
    run = running.reshape(tokens, groups_dev, per_group)
    by_group = jnp.transpose(run, (1, 0, 2))
    by_row = jnp.transpose(run, (1, 2, 0))
    step_t = jnp.transpose(step_size[0].reshape(tokens, groups_dev, per_group), (1, 2, 0))
    end_g = jnp.transpose(to_end.reshape(tokens, groups_dev, per_group), (1, 0, 2))

    x, z, b, c = x_values[0], z_gate[0], write_basis[0], read_basis[0]
    own = block_states_of(x, b, end_g, blocks)

    ends = end_states(code, totals, late, own, per)
    count = 2 if groups_dev % 2 == 0 else 1
    chunks = groups_dev // count
    span = count * per
    arrived = [[] for _ in range(chunks)]
    leaving = [ends[n * span : (n + 1) * span].astype(BF) for n in range(chunks)]
    early_out = [after(piece, leaving[0]) for piece in early_out]
    early = None
    for hop in range(size - 1):
        for n in range(chunks):
            if hop:
                leaving[n] = leaving_state(n * count, code, totals, arrived[n][-1], ends, per)
            arrived[n].append(lax.ppermute(leaving[n], "seq", [(hop, hop + 1)]))
        if early is None:
            early = exchange_states(early_out, seq, size)
        if fast and hop == 0:
            w_first = lax.ppermute(after(w_own, arrived[-1][0]), "seq", [(0, 1)])
        if fast and hop == 1:
            w_side, w_mid, arrived[0][1] = lax.optimization_barrier(
                (w_side, w_mid, arrived[0][1])
            )
            w_two = lax.ppermute(w_mid[:half], "seq", [(1, 0), (2, 3)])
            w_two_left = lax.ppermute(w_mid[half:], "seq", [(1, 0)])
            w_three_mid = lax.ppermute(w_side, "seq", [(2, 1)])
    if fast:
        w_two_right = lax.ppermute(after(w_mid[half:], arrived[-1][-1]), "seq", [(2, 3)])
        w_first, arrived[0][-1] = lax.optimization_barrier((w_first, arrived[0][-1]))
        w_first_mid = lax.ppermute(w_first, "seq", [(1, 2)])
        w_three_left = lax.ppermute(w_three_mid, "seq", [(1, 0)])
        w_three_right = lax.ppermute(w_first_mid, "seq", [(2, 3)])

    gain = norm_gain.reshape(1, width)
    normed = []
    for n in range(chunks):
        carry = functools.reduce(jnp.add, arrived[n])
        normed.append(
            mix_groups(
                n * count, count, code, totals, x, z, b, c, by_group, by_row, step_t, gain,
                carry, late, early, own,
            )
        )
    if not fast:
        return plain_projection(jnp.concatenate(normed, axis=1), out_weight)

    lhs = []
    for part in normed:
        across = lax.ppermute(part, "groups", SWAP)
        other = lax.ppermute(part, "batch", SWAP)
        other_across = lax.ppermute(across, "batch", SWAP)
        lhs += [part, other, across, other_across]
    one = project(
        seq,
        lhs,
        [w_own, w_side, w_first],
        [
            [[(0, 0)] * 4, [(0, half)] * 4],
            [[(1, 0), (2, 0), (1, 0), (1, 0)], [(1, half), (2, half), (1, half), (1, half)]],
        ],
    )
    two = project(
        seq,
        lhs,
        [w_two, w_two_left, w_two_right, w_mid],
        [[[(0, 0), (3, 0), (3, 0), (0, 0)], [(1, 0), (3, half), (3, half), (2, 0)]]],
    )
    arrays = [w_three_left, w_three_mid, w_first_mid, w_three_right]
    three = project(
        seq,
        lhs,
        arrays,
        [[[(s, 0) for s in range(4)], [(s, half) for s in range(4)]]],
    )
    sums = [to_rows(one, False, tokens), to_rows(two, True, tokens), to_rows(three, True, tokens)]
    early_sums = [[v[:, :quarter] for v in sums[0]], [v[:, quarter:] for v in sums[0]]]
    return finish_fast(seq, head, y, core, early_sums, sums[1:], tokens, quarter)


def solution(mesh):
    placed = (
        P(("groups", "batch"), "seq", "head"),
        P(("groups", "batch"), "seq", "head"),
        P(("groups", "batch"), "seq", "head"),
        P(("groups", "batch"), "seq", "head"),
        P(("groups", "batch"), "seq", "head"),
        P(("groups", "batch"), "seq", "head"),
        P(("groups", "batch"), None, "head", "seq", None),
        P(("groups", "batch"), None),
        P(("groups", "batch"), None),
        P("head"),
        P("head", "seq"),
    )
    return jax.shard_map(
        body,
        mesh=mesh,
        in_specs=placed,
        out_specs=P(("groups", "batch"), "seq", "head"),
        check_vma=False,
    )
```

time: 345 us -> 417 us (1.21)
  waiting for transfers between devices: 113 us -> 187 us
  Pallas kernels: 41.4 us -> 114 us
  starting transfers between devices: 104 us -> 79.4 us
  local copies, waits for them, and re-layouts: 32.3 us -> 13.9 us
  between operations: 18.8 us -> 0.94 us
  other arithmetic: 33.3 us -> 20.1 us
    ppermute x41 -> x31, waiting for transfers between devices: 101 us -> 175 us  [the longest x6 59.6 us: body(): arrived[n].append(lax.ppermute(leaving[n], 'seq', [(hop, hop + 1)]))]
    pallas_call x8 -> x11, Pallas kernels: 36.7 us -> 109 us  [the longest x1 65.9 us: pick_states(): pl.pallas_call(functools.partial(pick_kernel, size), in_specs=[smem, smem...]
    ppermute x6, starting transfers between devices: 32.4 us -> 17.5 us  [exchange_states(): lax.ppermute(piece, 'seq', [(i, (i + offset) % size) for i in range(size)])]
    broadcast_in_dim x20 -> x8, local copies, waits for them, and re-layouts: 13.3 us -> 0.81 us  [exchange_states(): whole = jnp.where(owner == (seq - offset) % size, piece[:, None], whole)]
    ppermute x41 -> x31, starting transfers between devices: 71.9 us -> 61.9 us  [the longest x6 15.5 us: body(): arrived[n].append(lax.ppermute(leaving[n], 'seq', [(hop, hop + 1)]))]
    convert_element_type x16 -> x3, other arithmetic: 8.3 us -> 0.59 us  [to_rows(): total = (partial_value.astype(F32) + arrived.astype(F32)).astype(BF)]
    add x5 -> x2, other arithmetic: 8.56 us -> 2.43 us  [body(): carry = functools.reduce(jnp.add, arrived[n])]
  transfers between devices with their start and end apart: 47 -> 37, of which waited for: 19 -> 15; matrix products, arithmetic and copies ran while one was open for 16% -> 7% of each run, Pallas kernels for 12% -> 12%
where the time goes in v2:
time: 417 us; the launch traced here: 415 us
  waiting for transfers between devices  187 us (45%)
  Pallas kernels  114 us (27%)
  starting transfers between devices  79.4 us (19%)
  other arithmetic  20.1 us (5%)
  local copies, waits for them, and re-layouts  13.9 us (3%)
    pallas_call x1, Pallas kernels, pick_states(): pl.pallas_call(functools.partial(pick_kernel, size), in_specs=[smem, smem...  65.9 us
    ppermute x6, waiting for transfers between devices, body(): arrived[n].append(lax.ppermute(leaving[n], 'seq', [(hop, hop + 1)]))  59.6 us
    ppermute x2, waiting for transfers between devices, body(): across = lax.ppermute(part, 'groups', SWAP)  34.5 us
    ppermute x3, waiting for transfers between devices, to_rows(): arrived = lax.ppermute(partial_value, ('seq', 'head'), to_goal)  23.2 us
    ppermute x1, waiting for transfers between devices, body(): w_two_left = lax.ppermute(w_mid[half:], 'seq', [(1, 0)])  20.2 us
    pallas_call x3, Pallas kernels, project(): pl.pallas_call(functools.partial(project_kernel, count, picks), in_specs=...  19.9 us
    ppermute x1, waiting for transfers between devices, body(): w_two = lax.ppermute(w_mid[:half], 'seq', [(1, 0), (2, 3)])  17.6 us
    ppermute x6, starting transfers between devices, exchange_states(): lax.ppermute(piece, 'seq', [(i, (i + offset) % size) for i in range(size)])  17.5 us
  transfers between devices with their start and end apart: 37, of which 15 were waited for; matrix products, arithmetic and copies ran while one was open for 7% of the time, Pallas kernels for 12%

profile of v2, /device:TPU:3, one launch (start us, length us, event | category | flops | bytes accessed | tf_op | source)
XLA Modules:
  0.0 415.2 jit_solution(13007683825608453600)
XLA Ops:
  0.0 65.9 %shard_map.109 = (bf16[64,16,128]{2,1,0:T(8,128)(2,1)}, bf16[64,16,128]{2,1,0:T(8,128)(2,1)}, bf16[64,16,128]{2,1,0:T(8,128)(2,1)}, bf16[64,16,128]{2,1,0:T(8,12...) custom-call(s32[1]{0:T(128)} %bitcast.seq_ref, ...), custom_call_target="tpu_custom_call" | custom-call | flops 1000 | bytes 1000 | tf_op jit(solution)/shard_map/pallas_call | solution.py:103
  65.9 1.3 collective-permute-start.2
  67.3 2.3 collective-permute-start.1
  69.6 1.1 collective-permute-start
  70.6 3.2 constant_dynamic-slice_fusion.refs_8_
  73.9 1.3 collective-permute-start.4
  76.3 4.7 %shard_map.110.own_ref = f32[2,4096,128]{2,1,0:T(8,128)} custom-call(bf16[256,4096]{1,0:T(8,128)(2,1)S(1)} %bitcast.125, bf16[256,512]{1,0:T(8,128)(2,1)S(1)} %bitcast.126, f32[4,256,16]{2,1,0:T(8,128)S(1)} %copy.21.end_ref), custom_call_target="tpu_custom_call" | custom-call | flops 1000 | bytes 1000 | tf_op jit(solution)/shard_map/pallas_call | solution.py:45
  82.4 5.3 %collective-permute-done.1 = bf16[64,16,128]{2,1,0:T(8,128)(2,1)} collective-permute-done((bf16[64,16,128]{2,1,0:T(8,128)(2,1)}, bf16[64,16,128]{2,1,0:T(8,128)(2,1)}, u32[]{:S(2)}, u32[]{:S(2)}) %collective-permute-start.1) | collective-permute-done | bytes 262176 | tf_op jit(solution)/shard_map/ppermute | solution.py:413
  87.7 6.3 %fusion.5.late_ref = bf16[4096,128]{1,0:T(8,128)(2,1)} fusion(pred[4096]{0:T(1024)(128)(4,1)S(1)} %broadcast_in_dim.139, pred[4096]{0:T(1024)(128)(4,1)S(1)} %broadcast_in_dim.134, pred[4096]{0:T(1024)(128)(4,1)S(1)} %broadcast_in_dim.129, pred[4096]{0:T(1024)(128)(4,1)S(1)} %broadcast_in_dim.124, bf16[64,16,128]{2,1,0:T(8,128)(2,1)S(1)} %copy-done.27, ...), kind=kLoop, calls=%fused_computation.8 | loop fusion | flops 2097152 | bytes 2113536 | tf_op jit(solution)/shard_map/jit(_where)/select_n | solution.py:414
  94.8 4.6 %shard_map.111.end_ref = f32[4096,128]{1,0:T(8,128)} custom-call(s32[2]{0:T(128)} %get-tuple-element.26.code_ref, f32[2,64]{1,0:T(2,128)} %exp.8.total_ref, bf16[4096,128]{1,0:T(8,128)(2,1)} %fusion.5.late_ref, f32[2,4096,128]{2,1,0:T(8,128)} %shard_map.110.own_ref), custom_call_target="tpu_custom_call" | custom-call | flops 1000 | bytes 1000 | tf_op jit(solution)/shard_map/pallas_call | solution.py:134
  99.4 1.7 convert.4
  101.9 8.9 %collective-permute-start.7 = (bf16[2048,128]{1,0:T(8,128)(2,1)S(1)}, bf16[2048,128]{1,0:T(8,128)(2,1)S(1)}, u32[]{:S(2)}, u32[]{:S(2)}) collective-permute-start(bf16[2048,128]{1,0:T(8,128)(2,1)S(1)} %get-tuple-element.60), channel_id=1, source_target_pairs={{0,4},{1,5},{2,6},{3,7},{16,20},{17,21},{18,22},{19,23}} | collective-permute-start | bytes 1572872 | tf_op jit(solution)/shard_map/ppermute | solution.py:491
  110.9 10.7 %collective-permute-done.7.carry_ref = bf16[2048,128]{1,0:T(8,128)(2,1)S(1)} collective-permute-done((bf16[2048,128]{1,0:T(8,128)(2,1)S(1)}, bf16[2048,128]{1,0:T(8,128)(2,1)S(1)}, u32[]{:S(2)}, u32[]{:S(2)}) %collective-permute-start.7) | collective-permute-done | bytes 524320 | tf_op jit(solution)/shard_map/ppermute | solution.py:491
  121.6 5.4 %collective-permute-start.8 = (bf16[4096,256]{1,0:T(8,128)(2,1)}, bf16[4096,256]{1,0:T(8,128)(2,1)}, u32[]{:S(2)}, u32[]{:S(2)}) collective-permute-start(bf16[4096,256]{1,0:T(8,128)(2,1)} %constant_dynamic-slice_fusion.refs_8_), channel_id=1, source_target_pairs={{0,4},{1,5},{2,6},{3,7},{16,20},{17,21},{18,22},{19,23}} | collective-permute-start | bytes 6291464 | tf_op jit(solution)/shard_map/ppermute | solution.py:495
  127.0 1.3 collective-permute-start.3
  128.4 2.2 shard_map.115
  130.5 1.5 collective-permute-start.16
  132.0 48.9 %collective-permute-done.3.carry_ref = bf16[2048,128]{1,0:T(8,128)(2,1)S(1)} collective-permute-done((bf16[2048,128]{1,0:T(8,128)(2,1)}, bf16[2048,128]{1,0:T(8,128)(2,1)S(1)}, u32[]{:S(2)}, u32[]{:S(2)}) %collective-permute-start.3) | collective-permute-done | bytes 524320 | tf_op jit(solution)/shard_map/ppermute | solution.py:491
  181.7 2.1 shard_map.112
  184.5 2.2 shard_map.116
  186.7 1.5 collective-permute-start.17
  188.1 8.6 %collective-permute-start.12 = (bf16[64,16,128]{2,1,0:T(8,128)(2,1)}, bf16[64,16,128]{2,1,0:T(8,128)(2,1)}, u32[]{:S(2)}, u32[]{:S(2)}) collective-permute-start(bf16[64,16,128]{2,1,0:T(8,128)(2,1)} %get-tuple-element.40), channel_id=1, source_target_pairs={{0,4},{4,8},{8,12},{12,0},{1,5},{5,9},{9,13},{13,1},{2,6},{6,10},{... | collective-permute-start | bytes 786440 | tf_op jit(solution)/shard_map/ppermute | solution.py:413
  196.7 1.9 collective-permute-start.11
  198.6 2.3 collective-permute-start.10
  200.9 2.1 shard_map.113
  203.1 1.6 collective-permute-start.9
  204.9 3.1 collective-permute-done.11
  208.0 3.0 collective-permute-done.10
  211.0 5.5 %fusion.2.early_ref = bf16[4096,128]{1,0:T(8,128)(2,1)S(1)} fusion(pred[4096]{0:T(1024)(128)(4,1)S(1)} %broadcast_in_dim.139, pred[4096]{0:T(1024)(128)(4,1)S(1)} %broadcast_in_dim.134, pred[4096]{0:T(1024)(128)(4,1)S(1)} %broadcast_in_dim.129, pred[4096]{0:T(1024)(128)(4,1)S(1)} %broadcast_in_dim.124, bf16[64,16,128]{2,1,0:T(8,128)(2,1)} %get-tuple-element.42, ...), kind=kLoop, calls=%fused_computation.4 | loop fusion | flops 2097152 | bytes 2113536 | tf_op jit(solution)/shard_map/jit(_where)/select_n | solution.py:414
  216.5 1.3 add_add_fusion.carry_ref
  217.9 5.3 %shard_map.117.refs_4_ = bf16[256,2048]{1,0:T(8,128)(2,1)S(1)} custom-call(s32[2]{0:T(128)S(1)} %copy-done.9, f32[2,64]{1,0:T(2,128)S(1)} %copy-done.8, bf16[256,4096]{1,0:T(8,128)(2,1)} %bitcast.123, bf16[256,4096]{1,0:T(8,128)(2,1)} %bitcast.139, bf16[256,512]{1,0:T(8,128)(2,1)S(1)} %bitcast.127, bf16[256,512]{1,0:T(8,128)(2,1)S(1)} %bitcast.132, ...), custom_call_target="tpu_custom_call" | custom-call | flops 1000 | bytes 1000 | tf_op jit(solution)/shard_map/pallas_call | solution.py:262
  223.2 3.9 collective-permute-start.18
  227.1 1.3 collective-permute-start.19
  228.4 1.2 add_add_fusion.1.carry_ref
  229.5 5.2 %shard_map.114.refs_0_ = bf16[256,2048]{1,0:T(8,128)(2,1)S(1)} custom-call(s32[2]{0:T(128)S(1)} %copy-done.9, f32[2,64]{1,0:T(2,128)S(1)} %copy-done.8, bf16[256,4096]{1,0:T(8,128)(2,1)} %bitcast.124, bf16[256,4096]{1,0:T(8,128)(2,1)} %bitcast.140, bf16[256,512]{1,0:T(8,128)(2,1)S(1)} %bitcast.128, bf16[256,512]{1,0:T(8,128)(2,1)S(1)} %bitcast.133, ...), custom_call_target="tpu_custom_call" | custom-call | flops 1000 | bytes 1000 | tf_op jit(solution)/shard_map/pallas_call | solution.py:262
  235.9 2.0 collective-permute-start.24
  238.5 13.3 %collective-permute-done.19.refs_6_ = bf16[256,2048]{1,0:T(8,128)(2,1)S(1)} collective-permute-done((bf16[256,2048]{1,0:T(8,128)(2,1)S(1)}, bf16[256,2048]{1,0:T(8,128)(2,1)S(1)}, u32[]{:S(2)}, u32[]{:S(2)}) %collective-permute-start.19) | collective-permute-done | bytes 1048608 | tf_op jit(solution)/shard_map/ppermute | solution.py:525
  251.8 1.3 collective-permute-start.20
  253.1 21.2 %collective-permute-done.14.refs_2_ = bf16[256,2048]{1,0:T(8,128)(2,1)S(1)} collective-permute-done((bf16[256,2048]{1,0:T(8,128)(2,1)S(1)}, bf16[256,2048]{1,0:T(8,128)(2,1)S(1)}, u32[]{:S(2)}, u32[]{:S(2)}) %collective-permute-start.14) | collective-permute-done | bytes 1048608 | tf_op jit(solution)/shard_map/ppermute | solution.py:525
  275.2 1.1 fusion.12
  276.3 1.3 collective-permute-start.27
  277.6 1.4 collective-permute-start.28
  279.8 1.3 collective-permute-start.23
  281.1 2.0 collective-permute-start.25
  283.1 8.4 %shard_map.118 = bf16[1024,512]{1,0:T(8,128)(2,1)S(1)} custom-call(s32[1]{0:T(128)} %bitcast.seq_ref, bf16[256,2048]{1,0:T(8,128)(2,1)S(1)} %shard_map.114.refs_0_, bf16[256,2048]{1,0:T(8,128)(2,1)S(1)} %collective-permute-done.13.refs_1_, bf16[256,2048]{1,0:T(8,128)(2,1)S(1)} %collective-permute-done.14.refs_2_, ...), custom_call_target="tpu_custom_call" | custom-call | flops 1000 | bytes 1000 | tf_op jit(solution)/shard_map/pallas_call | solution.py:333
  291.5 17.6 %collective-permute-done.27.refs_8_ = bf16[2048,256]{1,0:T(8,128)(2,1)S(1)} collective-permute-done((bf16[2048,256]{1,0:T(8,128)(2,1)}, bf16[2048,256]{1,0:T(8,128)(2,1)S(1)}, u32[]{:S(2)}, u32[]{:S(2)}) %collective-permute-start.27) | collective-permute-done | bytes 1048608 | tf_op jit(solution)/shard_map/ppermute | solution.py:500
  309.1 2.2 collective-permute-start.21
  311.3 20.2 %collective-permute-done.28.refs_9_ = bf16[2048,256]{1,0:T(8,128)(2,1)S(1)} collective-permute-done((bf16[2048,256]{1,0:T(8,128)(2,1)S(1)}, bf16[2048,256]{1,0:T(8,128)(2,1)S(1)}, u32[]{:S(2)}, u32[]{:S(2)}) %collective-permute-start.28) | collective-permute-done | bytes 1048608 | tf_op jit(solution)/shard_map/ppermute | solution.py:501
  332.5 1.0 copy-done.24
  333.5 5.7 %shard_map.120 = bf16[1024,256]{1,0:T(8,128)(2,1)S(1)} custom-call(s32[1]{0:T(128)} %bitcast.seq_ref, bf16[256,2048]{1,0:T(8,128)(2,1)S(1)} %shard_map.114.refs_0_, bf16[256,2048]{1,0:T(8,128)(2,1)S(1)} %collective-permute-done.13.refs_1_, bf16[256,2048]{1,0:T(8,128)(2,1)S(1)} %collective-permute-done.14.refs_2_, ...), custom_call_target="tpu_custom_call" | custom-call | flops 1000 | bytes 1000 | tf_op jit(solution)/shard_map/pallas_call | solution.py:333
  339.3 1.3 collective-permute-start.30
  341.6 12.2 %collective-permute-done.30 = bf16[1024,256]{1,0:T(8,128)(2,1)S(1)} collective-permute-done((bf16[1024,256]{1,0:T(8,128)(2,1)S(1)}, bf16[1024,256]{1,0:T(8,128)(2,1)S(1)}, u32[]{:S(2)}, u32[]{:S(2)}) %collective-permute-start.30) | collective-permute-done | bytes 524320 | tf_op jit(solution)/shard_map/ppermute | solution.py:375
  354.0 3.2 collective-permute-start.35
  357.2 4.9 %collective-permute-done.35 = bf16[2,256,256]{2,1,0:T(8,128)(2,1)S(1)} collective-permute-done((bf16[2,256,256]{2,1,0:T(8,128)(2,1)S(1)}, bf16[2,256,256]{2,1,0:T(8,128)(2,1)S(1)}, u32[]{:S(2)}, u32[]{:S(2)}) %collective-permute-start.35) | collective-permute-done | bytes 262176 | tf_op jit(solution)/shard_map/ppermute | solution.py:380
  362.1 14.4 %collective-permute-done.23.refs_8_ = bf16[4096,256]{1,0:T(8,128)(2,1)S(1)} collective-permute-done((bf16[4096,256]{1,0:T(8,128)(2,1)S(1)}, bf16[4096,256]{1,0:T(8,128)(2,1)S(1)}, u32[]{:S(2)}, u32[]{:S(2)}) %collective-permute-start.23) | collective-permute-done | bytes 2097184 | tf_op jit(solution)/shard_map/ppermute | solution.py:507
  376.5 1.3 copy-done.15
  377.8 5.7 %shard_map.119 = bf16[1024,256]{1,0:T(8,128)(2,1)S(1)} custom-call(s32[1]{0:T(128)} %bitcast.seq_ref, bf16[256,2048]{1,0:T(8,128)(2,1)S(1)} %shard_map.114.refs_0_, bf16[256,2048]{1,0:T(8,128)(2,1)S(1)} %collective-permute-done.13.refs_1_, bf16[256,2048]{1,0:T(8,128)(2,1)S(1)} %collective-permute-done.14.refs_2_, ...), custom_call_target="tpu_custom_call" | custom-call | flops 1000 | bytes 1000 | tf_op jit(solution)/shard_map/pallas_call | solution.py:333
  383.6 1.3 collective-permute-start.26
  385.8 1.6 collective-permute-start.32
  387.4 10.9 %collective-permute-done.26 = bf16[1024,256]{1,0:T(8,128)(2,1)S(1)} collective-permute-done((bf16[1024,256]{1,0:T(8,128)(2,1)S(1)}, bf16[1024,256]{1,0:T(8,128)(2,1)S(1)}, u32[]{:S(2)}, u32[]{:S(2)}) %collective-permute-start.26) | collective-permute-done | bytes 524320 | tf_op jit(solution)/shard_map/ppermute | solution.py:375
  398.5 3.1 collective-permute-start.33
  402.4 3.6 collective-permute-start.36
  407.5 4.3 %collective-permute-start.34 = (bf16[2,256,256]{2,1,0:T(8,128)(2,1)}, bf16[2,256,256]{2,1,0:T(8,128)(2,1)S(1)}, u32[]{:S(2)}, u32[]{:S(2)}) collective-permute-start(bf16[2,256,256]{2,1,0:T(8,128)(2,1)} %pad_maximum_fusion.1), channel_id=1, source_target_pairs={{2,3},{6,7},{8,9},{12,13},{3,2},{7,6},{9,8},{13,12},{18,19},{22,23... | collective-permute-start | bytes 786440 | tf_op jit(solution)/shard_map/ppermute | solution.py:382
  411.8 1.1 slice_bitcast_fusion.2
  (139 shorter events, 16.7 us)
Async XLA Ops:
  65.9 16.5 %collective-permute-start.2 = (bf16[64,16,128]{2,1,0:T(8,128)(2,1)}, bf16[64,16,128]{2,1,0:T(8,128)(2,1)S(1)}, u32[]{:S(2)}, u32[]{:S(2)}) collective-permute-start(bf16[64,16,128]{2,1,0:T(8,128)(2,1)} %get-tuple-element.29), channel_id=1, source_target_pairs={{0,4},{4,8},{8,12},{12,0},{1,5},{5,9},{9,13},{13,1},{2,6},{6,10},{... | collective-permute-start | bytes 786440 | tf_op jit(solution)/shard_map/ppermute | solution.py:413
  67.3 20.4 %collective-permute-start.1 = (bf16[64,16,128]{2,1,0:T(8,128)(2,1)}, bf16[64,16,128]{2,1,0:T(8,128)(2,1)}, u32[]{:S(2)}, u32[]{:S(2)}) collective-permute-start(bf16[64,16,128]{2,1,0:T(8,128)(2,1)} %get-tuple-element.28), channel_id=1, source_target_pairs={{0,8},{4,12},{8,0},{12,4},{1,9},{5,13},{9,1},{13,5},{2,10},{6,14},... | collective-permute-start | bytes 786440 | tf_op jit(solution)/shard_map/ppermute | solution.py:413
  69.6 18.1 %collective-permute-start = (bf16[64,16,128]{2,1,0:T(8,128)(2,1)}, bf16[64,16,128]{2,1,0:T(8,128)(2,1)}, u32[]{:S(2)}, u32[]{:S(2)}) collective-permute-start(bf16[64,16,128]{2,1,0:T(8,128)(2,1)} %get-tuple-element.27), channel_id=1, source_target_pairs={{0,12},{4,0},{8,4},{12,8},{1,13},{5,1},{9,5},{13,9},{2,14},{6,2},{... | collective-permute-start | bytes 786440 | tf_op jit(solution)/shard_map/ppermute | solution.py:413
  70.6 4.5 %copy-start.28 = (f32[1,256,64]{1,2,0:T(8,128)S(1)}, f32[1,256,64]{1,2,0:T(8,128)}, u32[]{:S(2)}) copy-start(f32[1,256,64]{1,2,0:T(8,128)} %param.16) | copy-start | bytes 196612
  70.6 5.3 %copy-start.6 = (f32[1,256,64]{1,2,0:T(8,128)S(1)}, f32[1,256,64]{1,2,0:T(8,128)}, u32[]{:S(2)}) copy-start(f32[1,256,64]{1,2,0:T(8,128)} %param.15) | copy-start | bytes 196612
  70.6 5.6 %copy-start = (bf16[1,256,4096]{2,1,0:T(8,128)(2,1)S(1)}, bf16[1,256,4096]{2,1,0:T(8,128)(2,1)}, u32[]{:S(2)}) copy-start(bf16[1,256,4096]{2,1,0:T(8,128)(2,1)} %param.11) | copy-start | bytes 6291460
  70.6 5.6 %copy-start.4 = (bf16[1,256,512]{2,1,0:T(8,128)(2,1)S(1)}, bf16[1,256,512]{2,1,0:T(8,128)(2,1)}, u32[]{:S(2)}) copy-start(bf16[1,256,512]{2,1,0:T(8,128)(2,1)} %param.13) | copy-start | bytes 786436
  73.9 122.8 %collective-permute-start.4 = (bf16[4096,256]{1,0:T(8,128)(2,1)}, bf16[4096,256]{1,0:T(8,128)(2,1)}, u32[]{:S(2)}, u32[]{:S(2)}) collective-permute-start(bf16[4096,256]{1,0:T(8,128)(2,1)} %constant_dynamic-slice_fusion.refs_8_), channel_id=1, source_target_pairs={{4,0},{12,8},{8,12},{5,1},{13,9},{9,13},{6,2},{14,10},{10,14},{7,3... | collective-permute-start | bytes 6291464 | tf_op jit(solution)/shard_map/ppermute | solution.py:463
  76.2 11.4 %copy-start.27 = (bf16[64,16,128]{2,1,0:T(8,128)(2,1)S(1)}, bf16[64,16,128]{2,1,0:T(8,128)(2,1)}, u32[]{:S(2)}) copy-start(bf16[64,16,128]{2,1,0:T(8,128)(2,1)} %get-tuple-element.30) | copy-start | bytes 786436
  94.0 104.6 %collective-permute-start.5 = (bf16[4096,256]{1,0:T(8,128)(2,1)}, bf16[4096,256]{1,0:T(8,128)(2,1)S(1)}, u32[]{:S(2)}, u32[]{:S(2)}) collective-permute-start(bf16[4096,256]{1,0:T(8,128)(2,1)} %constant_dynamic-slice_fusion.refs_8_), channel_id=1, source_target_pairs={{4,8},{8,4},{5,9},{9,5},{6,10},{10,6},{7,11},{11,7},{20,24},{24,20... | collective-permute-start | bytes 6291464 | tf_op jit(solution)/shard_map/ppermute | solution.py:464
  101.9 19.7 %collective-permute-start.7 = (bf16[2048,128]{1,0:T(8,128)(2,1)S(1)}, bf16[2048,128]{1,0:T(8,128)(2,1)S(1)}, u32[]{:S(2)}, u32[]{:S(2)}) collective-permute-start(bf16[2048,128]{1,0:T(8,128)(2,1)S(1)} %get-tuple-element.60), channel_id=1, source_target_pairs={{0,4},{1,5},{2,6},{3,7},{16,20},{17,21},{18,22},{19,23}} | collective-permute-start | bytes 1572872 | tf_op jit(solution)/shard_map/ppermute | solution.py:491
  121.6 6.7 %copy-start.18 = (bf16[2048,128]{1,0:T(8,128)(2,1)}, bf16[2048,128]{1,0:T(8,128)(2,1)S(1)}, u32[]{:S(2)}) copy-start(bf16[2048,128]{1,0:T(8,128)(2,1)S(1)} %collective-permute-done.7.carry_ref) | copy-start | bytes 1572868
  121.6 106.7 %collective-permute-start.8 = (bf16[4096,256]{1,0:T(8,128)(2,1)}, bf16[4096,256]{1,0:T(8,128)(2,1)}, u32[]{:S(2)}, u32[]{:S(2)}) collective-permute-start(bf16[4096,256]{1,0:T(8,128)(2,1)} %constant_dynamic-slice_fusion.refs_8_), channel_id=1, source_target_pairs={{0,4},{1,5},{2,6},{3,7},{16,20},{17,21},{18,22},{19,23}} | collective-permute-start | bytes 6291464 | tf_op jit(solution)/shard_map/ppermute | solution.py:495
  127.0 53.8 %collective-permute-start.3 = (bf16[2048,128]{1,0:T(8,128)(2,1)}, bf16[2048,128]{1,0:T(8,128)(2,1)S(1)}, u32[]{:S(2)}, u32[]{:S(2)}) collective-permute-start(bf16[2048,128]{1,0:T(8,128)(2,1)} %get-tuple-element.59), channel_id=1, source_target_pairs={{0,4},{1,5},{2,6},{3,7},{16,20},{17,21},{18,22},{19,23}} | collective-permute-start | bytes 1572872 | tf_op jit(solution)/shard_map/ppermute | solution.py:491
  130.5 54.0 %collective-permute-start.16 = (bf16[2048,128]{1,0:T(8,128)(2,1)}, bf16[2048,128]{1,0:T(8,128)(2,1)}, u32[]{:S(2)}, u32[]{:S(2)}) collective-permute-start(bf16[2048,128]{1,0:T(8,128)(2,1)} %shard_map.115), channel_id=1, source_target_pairs={{4,8},{5,9},{6,10},{7,11},{20,24},{21,25},{22,26},{23,27}} | collective-permute-start | bytes 1572872 | tf_op jit(solution)/shard_map/ppermute | solution.py:491
  183.8 4.3 %collective-permute-start.6 = (bf16[2048,128]{1,0:T(8,128)(2,1)}, bf16[2048,128]{1,0:T(8,128)(2,1)S(1)}, u32[]{:S(2)}, u32[]{:S(2)}) collective-permute-start(bf16[2048,128]{1,0:T(8,128)(2,1)} %shard_map.112), channel_id=1, source_target_pairs={{4,8},{5,9},{6,10},{7,11},{20,24},{21,25},{22,26},{23,27}} | collective-permute-start | bytes 1572872 | tf_op jit(solution)/shard_map/ppermute | solution.py:491
  186.7 29.8 %collective-permute-start.17 = (bf16[2048,128]{1,0:T(8,128)(2,1)}, bf16[2048,128]{1,0:T(8,128)(2,1)}, u32[]{:S(2)}, u32[]{:S(2)}) collective-permute-start(bf16[2048,128]{1,0:T(8,128)(2,1)} %shard_map.116), channel_id=1, source_target_pairs={{8,12},{9,13},{10,14},{11,15},{24,28},{25,29},{26,30},{27,31}} | collective-permute-start | bytes 1572872 | tf_op jit(solution)/shard_map/ppermute | solution.py:491
  188.1 12.8 %copy-start.20 = (bf16[2048,128]{1,0:T(8,128)(2,1)}, bf16[2048,128]{1,0:T(8,128)(2,1)S(1)}, u32[]{:S(2)}) copy-start(bf16[2048,128]{1,0:T(8,128)(2,1)S(1)} %collective-permute-done.6.carry_ref) | copy-start | bytes 1572868
  188.1 14.9 %collective-permute-start.12 = (bf16[64,16,128]{2,1,0:T(8,128)(2,1)}, bf16[64,16,128]{2,1,0:T(8,128)(2,1)}, u32[]{:S(2)}, u32[]{:S(2)}) collective-permute-start(bf16[64,16,128]{2,1,0:T(8,128)(2,1)} %get-tuple-element.40), channel_id=1, source_target_pairs={{0,4},{4,8},{8,12},{12,0},{1,5},{5,9},{9,13},{13,1},{2,6},{6,10},{... | collective-permute-start | bytes 786440 | tf_op jit(solution)/shard_map/ppermute | solution.py:413
  196.7 11.3 %collective-permute-start.11 = (bf16[64,16,128]{2,1,0:T(8,128)(2,1)}, bf16[64,16,128]{2,1,0:T(8,128)(2,1)}, u32[]{:S(2)}, u32[]{:S(2)}) collective-permute-start(bf16[64,16,128]{2,1,0:T(8,128)(2,1)} %get-tuple-element.38), channel_id=1, source_target_pairs={{0,8},{4,12},{8,0},{12,4},{1,9},{5,13},{9,1},{13,5},{2,10},{6,14},... | collective-permute-start | bytes 786440 | tf_op jit(solution)/shard_map/ppermute | solution.py:413
  198.6 76.6 %copy-start.13 = (bf16[4096,256]{1,0:T(8,128)(2,1)}, bf16[4096,256]{1,0:T(8,128)(2,1)S(1)}, u32[]{:S(2)}) copy-start(bf16[4096,256]{1,0:T(8,128)(2,1)S(1)} %collective-permute-done.5.refs_11_) | copy-start | bytes 6291460
  198.6 12.4 %collective-permute-start.10 = (bf16[64,16,128]{2,1,0:T(8,128)(2,1)}, bf16[64,16,128]{2,1,0:T(8,128)(2,1)}, u32[]{:S(2)}, u32[]{:S(2)}) collective-permute-start(bf16[64,16,128]{2,1,0:T(8,128)(2,1)} %get-tuple-element.36), channel_id=1, source_target_pairs={{0,12},{4,0},{8,4},{12,8},{1,13},{5,1},{9,5},{13,9},{2,14},{6,2},{... | collective-permute-start | bytes 786440 | tf_op jit(solution)/shard_map/ppermute | solution.py:413
  203.0 13.5 %copy-start.19 = (bf16[2048,128]{1,0:T(8,128)(2,1)S(1)}, bf16[2048,128]{1,0:T(8,128)(2,1)}, u32[]{:S(2)}) copy-start(bf16[2048,128]{1,0:T(8,128)(2,1)} %copy-done.18) | copy-start | bytes 1572868
  203.1 25.3 %collective-permute-start.9 = (bf16[2048,128]{1,0:T(8,128)(2,1)}, bf16[2048,128]{1,0:T(8,128)(2,1)}, u32[]{:S(2)}, u32[]{:S(2)}) collective-permute-start(bf16[2048,128]{1,0:T(8,128)(2,1)} %shard_map.113), channel_id=1, source_target_pairs={{8,12},{9,13},{10,14},{11,15},{24,28},{25,29},{26,30},{27,31}} | collective-permute-start | bytes 1572872 | tf_op jit(solution)/shard_map/ppermute | solution.py:491
  204.9 12.9 %copy-start.3 = (bf16[4096,128]{1,0:T(8,128)(2,1)S(1)}, bf16[4096,128]{1,0:T(8,128)(2,1)}, u32[]{:S(2)}) copy-start(bf16[4096,128]{1,0:T(8,128)(2,1)} %fusion.5.late_ref) | copy-start | bytes 3145732
  204.9 12.9 %copy-start.5 = (bf16[1,256,512]{2,1,0:T(8,128)(2,1)S(1)}, bf16[1,256,512]{2,1,0:T(8,128)(2,1)}, u32[]{:S(2)}) copy-start(bf16[1,256,512]{2,1,0:T(8,128)(2,1)} %param.14) | copy-start | bytes 786436
  204.9 12.9 %copy-start.7 = (f32[4096]{0:T(1024)S(1)}, f32[4096]{0:T(1024)}, u32[]{:S(2)}) copy-start(f32[4096]{0:T(1024)} %param.20) | copy-start | bytes 49156
  204.9 12.9 %copy-start.8 = (f32[2,64]{1,0:T(2,128)S(1)}, f32[2,64]{1,0:T(2,128)}, u32[]{:S(2)}) copy-start(f32[2,64]{1,0:T(2,128)} %exp.8.total_ref) | copy-start | bytes 1540
  204.9 12.9 %copy-start.9 = (s32[2]{0:T(128)S(1)}, s32[2]{0:T(128)}, u32[]{:S(2)}) copy-start(s32[2]{0:T(128)} %get-tuple-element.26.code_ref) | copy-start | bytes 28
  217.9 10.5 %copy-start.17 = (bf16[2048,128]{1,0:T(8,128)(2,1)S(1)}, bf16[2048,128]{1,0:T(8,128)(2,1)}, u32[]{:S(2)}) copy-start(bf16[2048,128]{1,0:T(8,128)(2,1)} %copy-done.16) | copy-start | bytes 1572868
  217.9 10.5 %copy-start.21 = (bf16[2048,128]{1,0:T(8,128)(2,1)S(1)}, bf16[2048,128]{1,0:T(8,128)(2,1)}, u32[]{:S(2)}) copy-start(bf16[2048,128]{1,0:T(8,128)(2,1)} %copy-done.20) | copy-start | bytes 1572868
  223.2 11.6 %copy-start.1 = (bf16[256,2048]{1,0:T(8,128)(2,1)}, bf16[256,2048]{1,0:T(8,128)(2,1)S(1)}, u32[]{:S(2)}) copy-start(bf16[256,2048]{1,0:T(8,128)(2,1)S(1)} %shard_map.117.refs_4_) | copy-start | bytes 3145732
  223.2 14.7 %collective-permute-start.18 = (bf16[256,2048]{1,0:T(8,128)(2,1)S(1)}, bf16[256,2048]{1,0:T(8,128)(2,1)S(1)}, u32[]{:S(2)}, u32[]{:S(2)}) collective-permute-start(bf16[256,2048]{1,0:T(8,128)(2,1)S(1)} %shard_map.117.refs_4_), channel_id=1, source_target_pairs={{0,1},{1,0},{2,3},{3,2},{4,5},{5,4},{6,7},{7,6},{8,9},{9,8},{10,11... | collective-permute-start | bytes 3145736 | tf_op jit(solution)/shard_map/ppermute | solution.py:526
  227.1 24.7 %collective-permute-start.19 = (bf16[256,2048]{1,0:T(8,128)(2,1)S(1)}, bf16[256,2048]{1,0:T(8,128)(2,1)S(1)}, u32[]{:S(2)}, u32[]{:S(2)}) collective-permute-start(bf16[256,2048]{1,0:T(8,128)(2,1)S(1)} %shard_map.117.refs_4_), channel_id=1, source_target_pairs={{0,16},{16,0},{1,17},{17,1},{2,18},{18,2},{3,19},{19,3},{4,20},{20... | collective-permute-start | bytes 3145736 | tf_op jit(solution)/shard_map/ppermute | solution.py:525
  234.8 39.5 %collective-permute-start.14 = (bf16[256,2048]{1,0:T(8,128)(2,1)S(1)}, bf16[256,2048]{1,0:T(8,128)(2,1)S(1)}, u32[]{:S(2)}, u32[]{:S(2)}) collective-permute-start(bf16[256,2048]{1,0:T(8,128)(2,1)S(1)} %shard_map.114.refs_0_), channel_id=1, source_target_pairs={{0,16},{16,0},{1,17},{17,1},{2,18},{18,2},{3,19},{19,3},{4,20},{20... | collective-permute-start | bytes 3145736 | tf_op jit(solution)/shard_map/ppermute | solution.py:525
  235.1 44.0 %collective-permute-start.22 = (bf16[4096,256]{1,0:T(8,128)(2,1)}, bf16[4096,256]{1,0:T(8,128)(2,1)S(1)}, u32[]{:S(2)}, u32[]{:S(2)}) collective-permute-start(bf16[4096,256]{1,0:T(8,128)(2,1)} %collective-permute-done.4.refs_9_), channel_id=1, source_target_pairs={{8,4},{9,5},{10,6},{11,7},{24,20},{25,21},{26,22},{27,23}} | collective-permute-start | bytes 6291464 | tf_op jit(solution)/shard_map/ppermute | solution.py:502
  235.9 45.3 %collective-permute-start.24 = (bf16[4096,256]{1,0:T(8,128)(2,1)}, bf16[4096,256]{1,0:T(8,128)(2,1)}, u32[]{:S(2)}, u32[]{:S(2)}) collective-permute-start(bf16[4096,256]{1,0:T(8,128)(2,1)} %collective-permute-done.8.refs_10_), channel_id=1, source_target_pairs={{4,8},{5,9},{6,10},{7,11},{20,24},{21,25},{22,26},{23,27}} | collective-permute-start | bytes 6291464 | tf_op jit(solution)/shard_map/ppermute | solution.py:506
  237.9 38.4 %copy-start.10 = (bf16[256,2048]{1,0:T(8,128)(2,1)}, bf16[256,2048]{1,0:T(8,128)(2,1)S(1)}, u32[]{:S(2)}) copy-start(bf16[256,2048]{1,0:T(8,128)(2,1)S(1)} %collective-permute-done.18.refs_5_) | copy-start | bytes 3145732
  237.9 38.4 %collective-permute-start.13 = (bf16[256,2048]{1,0:T(8,128)(2,1)S(1)}, bf16[256,2048]{1,0:T(8,128)(2,1)S(1)}, u32[]{:S(2)}, u32[]{:S(2)}) collective-permute-start(bf16[256,2048]{1,0:T(8,128)(2,1)S(1)} %shard_map.114.refs_0_), channel_id=1, source_target_pairs={{0,1},{1,0},{2,3},{3,2},{4,5},{5,4},{6,7},{7,6},{8,9},{9,8},{10,11... | collective-permute-start | bytes 3145736 | tf_op jit(solution)/shard_map/ppermute | solution.py:526
  251.8 24.4 %copy-start.11 = (bf16[256,2048]{1,0:T(8,128)(2,1)}, bf16[256,2048]{1,0:T(8,128)(2,1)S(1)}, u32[]{:S(2)}) copy-start(bf16[256,2048]{1,0:T(8,128)(2,1)S(1)} %collective-permute-done.19.refs_6_) | copy-start | bytes 3145732
  251.8 25.8 %collective-permute-start.20 = (bf16[256,2048]{1,0:T(8,128)(2,1)S(1)}, bf16[256,2048]{1,0:T(8,128)(2,1)S(1)}, u32[]{:S(2)}, u32[]{:S(2)}) collective-permute-start(bf16[256,2048]{1,0:T(8,128)(2,1)S(1)} %collective-permute-done.19.refs_6_), channel_id=1, source_target_pairs={{0,1},{1,0},{2,3},{3,2},{4,5},{5,4},{6,7},{7,6},{8,9},{9,8},{10,11... | collective-permute-start | bytes 3145736 | tf_op jit(solution)/shard_map/ppermute | solution.py:527
  274.3 5.5 %collective-permute-start.15 = (bf16[256,2048]{1,0:T(8,128)(2,1)S(1)}, bf16[256,2048]{1,0:T(8,128)(2,1)S(1)}, u32[]{:S(2)}, u32[]{:S(2)}) collective-permute-start(bf16[256,2048]{1,0:T(8,128)(2,1)S(1)} %collective-permute-done.14.refs_2_), channel_id=1, source_target_pairs={{0,1},{1,0},{2,3},{3,2},{4,5},{5,4},{6,7},{7,6},{8,9},{9,8},{10,11... | collective-permute-start | bytes 3145736 | tf_op jit(solution)/shard_map/ppermute | solution.py:527
  276.3 32.8 %collective-permute-start.27 = (bf16[2048,256]{1,0:T(8,128)(2,1)}, bf16[2048,256]{1,0:T(8,128)(2,1)S(1)}, u32[]{:S(2)}, u32[]{:S(2)}) collective-permute-start(bf16[2048,256]{1,0:T(8,128)(2,1)} %get-tuple-element.58), channel_id=1, source_target_pairs={{4,0},{8,12},{5,1},{9,13},{6,2},{10,14},{7,3},{11,15},{20,16},{24,... | collective-permute-start | bytes 3145736 | tf_op jit(solution)/shard_map/ppermute | solution.py:500
  277.6 56.0 %copy-start.2 = (bf16[256,2048]{1,0:T(8,128)(2,1)S(1)}, bf16[256,2048]{1,0:T(8,128)(2,1)}, u32[]{:S(2)}) copy-start(bf16[256,2048]{1,0:T(8,128)(2,1)} %copy-done.1) | copy-start | bytes 3145732
  277.6 5.5 %copy-start.12 = (bf16[256,2048]{1,0:T(8,128)(2,1)}, bf16[256,2048]{1,0:T(8,128)(2,1)S(1)}, u32[]{:S(2)}) copy-start(bf16[256,2048]{1,0:T(8,128)(2,1)S(1)} %collective-permute-done.20.refs_7_) | copy-start | bytes 3145732
  277.6 53.9 %collective-permute-start.28 = (bf16[2048,256]{1,0:T(8,128)(2,1)S(1)}, bf16[2048,256]{1,0:T(8,128)(2,1)S(1)}, u32[]{:S(2)}, u32[]{:S(2)}) collective-permute-start(bf16[2048,256]{1,0:T(8,128)(2,1)S(1)} %get-tuple-element.46), channel_id=1, source_target_pairs={{4,0},{5,1},{6,2},{7,3},{20,16},{21,17},{22,18},{23,19}} | collective-permute-start | bytes 3145736 | tf_op jit(solution)/shard_map/ppermute | solution.py:501
  279.1 12.4 %copy-start.14 = (bf16[4096,256]{1,0:T(8,128)(2,1)}, bf16[4096,256]{1,0:T(8,128)(2,1)S(1)}, u32[]{:S(2)}) copy-start(bf16[4096,256]{1,0:T(8,128)(2,1)S(1)} %collective-permute-done.22.refs_9_) | copy-start | bytes 6291460
  279.1 52.5 %collective-permute-start.29 = (bf16[2048,256]{1,0:T(8,128)(2,1)S(1)}, bf16[2048,256]{1,0:T(8,128)(2,1)S(1)}, u32[]{:S(2)}, u32[]{:S(2)}) collective-permute-start(bf16[2048,256]{1,0:T(8,128)(2,1)S(1)} %get-tuple-element.46), channel_id=1, source_target_pairs={{8,12},{9,13},{10,14},{11,15},{24,28},{25,29},{26,30},{27,31}} | collective-permute-start | bytes 3145736 | tf_op jit(solution)/shard_map/ppermute | solution.py:504
  279.8 96.7 %collective-permute-start.23 = (bf16[4096,256]{1,0:T(8,128)(2,1)S(1)}, bf16[4096,256]{1,0:T(8,128)(2,1)S(1)}, u32[]{:S(2)}, u32[]{:S(2)}) collective-permute-start(bf16[4096,256]{1,0:T(8,128)(2,1)S(1)} %collective-permute-done.22.refs_9_), channel_id=1, source_target_pairs={{4,0},{5,1},{6,2},{7,3},{20,16},{21,17},{22,18},{23,19}} | collective-permute-start | bytes 6291464 | tf_op jit(solution)/shard_map/ppermute | solution.py:507
  281.1 95.4 %collective-permute-start.25 = (bf16[4096,256]{1,0:T(8,128)(2,1)}, bf16[4096,256]{1,0:T(8,128)(2,1)}, u32[]{:S(2)}, u32[]{:S(2)}) collective-permute-start(bf16[4096,256]{1,0:T(8,128)(2,1)} %collective-permute-done.24.refs_10_), channel_id=1, source_target_pairs={{8,12},{9,13},{10,14},{11,15},{24,28},{25,29},{26,30},{27,31}} | collective-permute-start | bytes 6291464 | tf_op jit(solution)/shard_map/ppermute | solution.py:508
  309.1 22.5 %copy-start.22 = (bf16[2048,256]{1,0:T(8,128)(2,1)}, bf16[2048,256]{1,0:T(8,128)(2,1)S(1)}, u32[]{:S(2)}) copy-start(bf16[2048,256]{1,0:T(8,128)(2,1)S(1)} %collective-permute-done.27.refs_8_) | copy-start | bytes 3145732
  309.1 31.5 %collective-permute-start.21 = (bf16[1024,512]{1,0:T(8,128)(2,1)S(1)}, bf16[1024,512]{1,0:T(8,128)(2,1)S(1)}, u32[]{:S(2)}, u32[]{:S(2)}) collective-permute-start(bf16[1024,512]{1,0:T(8,128)(2,1)S(1)} %shard_map.118), channel_id=1, source_target_pairs={{2,0},{6,4},{8,10},{12,14},{3,1},{7,5},{9,11},{13,15},{18,16},{22,... | collective-permute-start | bytes 3145736 | tf_op jit(solution)/shard_map/ppermute | solution.py:375
  339.3 14.6 %collective-permute-start.30 = (bf16[1024,256]{1,0:T(8,128)(2,1)S(1)}, bf16[1024,256]{1,0:T(8,128)(2,1)S(1)}, u32[]{:S(2)}, u32[]{:S(2)}) collective-permute-start(bf16[1024,256]{1,0:T(8,128)(2,1)S(1)} %shard_map.120), channel_id=1, source_target_pairs={{0,2},{4,6},{10,8},{14,12},{1,3},{5,7},{11,9},{15,13},{16,18},{20,... | collective-permute-start | bytes 1572872 | tf_op jit(solution)/shard_map/ppermute | solution.py:375
  340.9 44.0 %collective-permute-start.31 = (bf16[2,256,512]{2,1,0:T(8,128)(2,1)S(1)}, bf16[2,256,512]{2,1,0:T(8,128)(2,1)S(1)}, u32[]{:S(2)}, u32[]{:S(2)}) collective-permute-start(bf16[2,256,512]{2,1,0:T(8,128)(2,1)S(1)} %bitcast.141), channel_id=1, source_target_pairs={{0,16},{4,20},{10,26},{14,30},{16,0},{20,4},{26,10},{30,14},{1,17}... | collective-permute-start | bytes 1572872 | tf_op jit(solution)/shard_map/ppermute | solution.py:380
  354.0 8.0 %collective-permute-start.35 = (bf16[2,256,256]{2,1,0:T(8,128)(2,1)S(1)}, bf16[2,256,256]{2,1,0:T(8,128)(2,1)S(1)}, u32[]{:S(2)}, u32[]{:S(2)}) collective-permute-start(bf16[2,256,256]{2,1,0:T(8,128)(2,1)S(1)} %bitcast.144), channel_id=1, source_target_pairs={{2,18},{6,22},{8,24},{12,28},{18,2},{22,6},{24,8},{28,12},{3,19},{... | collective-permute-start | bytes 786440 | tf_op jit(solution)/shard_map/ppermute | solution.py:380
  362.1 21.5 %copy-start.25 = (bf16[2,256,256]{2,1,0:T(8,128)(2,1)}, bf16[2,256,256]{2,1,0:T(8,128)(2,1)S(1)}, u32[]{:S(2)}) copy-start(bf16[2,256,256]{2,1,0:T(8,128)(2,1)S(1)} %collective-permute-done.35) | copy-start | bytes 786436
  376.5 1.3 copy-start.15
  383.6 14.8 %collective-permute-start.26 = (bf16[1024,256]{1,0:T(8,128)(2,1)S(1)}, bf16[1024,256]{1,0:T(8,128)(2,1)S(1)}, u32[]{:S(2)}, u32[]{:S(2)}) collective-permute-start(bf16[1024,256]{1,0:T(8,128)(2,1)S(1)} %shard_map.119), channel_id=1, source_target_pairs={{0,2},{4,6},{10,8},{14,12},{1,3},{5,7},{11,9},{15,13},{16,18},{20,... | collective-permute-start | bytes 1572872 | tf_op jit(solution)/shard_map/ppermute | solution.py:375
  384.9 16.8 %slice-start = ((bf16[2,256,256]{2,1,0:T(8,128)(2,1)}), bf16[1,256,256]{2,1,0:T(8,128)(2,1)S(1)}, s32[]{:S(2)}) async-start(bf16[2,256,256]{2,1,0:T(8,128)(2,1)} %copy-done.25), calls=%async_computation | async-start | bytes 262144 | tf_op jit(solution)/shard_map/slice | solution.py:383
  385.8 27.3 %copy-start.26 = (bf16[2,256,256]{2,1,0:T(8,128)(2,1)S(1)}, bf16[2,256,256]{2,1,0:T(8,128)(2,1)}, u32[]{:S(2)}) copy-start(bf16[2,256,256]{2,1,0:T(8,128)(2,1)} %copy-done.25) | copy-start | bytes 786436
  385.8 26.0 %collective-permute-start.32 = (bf16[2,256,512]{2,1,0:T(8,128)(2,1)}, bf16[2,256,512]{2,1,0:T(8,128)(2,1)}, u32[]{:S(2)}, u32[]{:S(2)}) collective-permute-start(bf16[2,256,512]{2,1,0:T(8,128)(2,1)} %pad_maximum_fusion), channel_id=1, source_target_pairs={{0,1},{4,5},{10,11},{14,15},{1,0},{5,4},{11,10},{15,14},{16,17},{2... | collective-permute-start | bytes 1572872 | tf_op jit(solution)/shard_map/ppermute | solution.py:382
  398.5 8.3 %collective-permute-start.33 = (bf16[2,256,256]{2,1,0:T(8,128)(2,1)S(1)}, bf16[2,256,256]{2,1,0:T(8,128)(2,1)S(1)}, u32[]{:S(2)}, u32[]{:S(2)}) collective-permute-start(bf16[2,256,256]{2,1,0:T(8,128)(2,1)S(1)} %bitcast.143), channel_id=1, source_target_pairs={{2,18},{6,22},{8,24},{12,28},{18,2},{22,6},{24,8},{28,12},{3,19},{... | collective-permute-start | bytes 786440 | tf_op jit(solution)/shard_map/ppermute | solution.py:380
  402.4 10.5 %collective-permute-start.36 = (bf16[2,256,256]{2,1,0:T(8,128)(2,1)}, bf16[2,256,256]{2,1,0:T(8,128)(2,1)S(1)}, u32[]{:S(2)}, u32[]{:S(2)}) collective-permute-start(bf16[2,256,256]{2,1,0:T(8,128)(2,1)} %pad_maximum_fusion.2), channel_id=1, source_target_pairs={{2,3},{6,7},{8,9},{12,13},{3,2},{7,6},{9,8},{13,12},{18,19},{22,23... | collective-permute-start | bytes 786440 | tf_op jit(solution)/shard_map/ppermute | solution.py:382
  407.5 5.6 %collective-permute-start.34 = (bf16[2,256,256]{2,1,0:T(8,128)(2,1)}, bf16[2,256,256]{2,1,0:T(8,128)(2,1)S(1)}, u32[]{:S(2)}, u32[]{:S(2)}) collective-permute-start(bf16[2,256,256]{2,1,0:T(8,128)(2,1)} %pad_maximum_fusion.1), channel_id=1, source_target_pairs={{2,3},{6,7},{8,9},{12,13},{3,2},{7,6},{9,8},{13,12},{18,19},{22,23... | collective-permute-start | bytes 786440 | tf_op jit(solution)/shard_map/ppermute | solution.py:382
  (4 other events, 3.8 us)

commit v3 on v2

--- a/solution.py
+++ b/solution.py
@@ -10,9 +10,10 @@
 HEAD_DIM = 64
 STATE = 128
 STRETCH = 128
+PIECES = 2
 BF = jnp.bfloat16
 F32 = jnp.float32
-VMEM_LIMIT = 48 * 1024 * 1024
+VMEM_LIMIT = 56 * 1024 * 1024
 SMALL = pl.CostEstimate(flops=1000, bytes_accessed=1000, transcendentals=0)
 
 
@@ -53,7 +54,9 @@
         out_specs=pl.BlockSpec((blocks, per, STATE), lambda g: (0, g, 0)),
         out_shape=jax.ShapeDtypeStruct((blocks, width, STATE), F32),
         compiler_params=pltpu.CompilerParams(vmem_limit_bytes=VMEM_LIMIT),
-        cost_estimate=SMALL,
+        cost_estimate=pl.CostEstimate(
+            flops=2 * tokens * width * STATE, bytes_accessed=16 << 20, transcendentals=0
+        ),
     )(x, b, to_end)
 
 
@@ -99,11 +102,12 @@
 def pick_states(seq, lengths, slots, cached, size):
     smem = pl.BlockSpec(memory_space=pltpu.SMEM)
     hbm = pl.BlockSpec(memory_space=pl.ANY)
+    whole = pl.BlockSpec(memory_space=pltpu.VMEM)
     piece = jax.ShapeDtypeStruct(cached.shape[2:], cached.dtype)
     out = pl.pallas_call(
         functools.partial(pick_kernel, size),
         in_specs=[smem, smem, smem, hbm],
-        out_specs=[hbm] * (2 * size) + [smem],
+        out_specs=[whole] * (2 * size) + [smem],
         out_shape=[piece] * (2 * size) + [jax.ShapeDtypeStruct((2,), jnp.int32)],
         scratch_shapes=[pltpu.SemaphoreType.DMA((2 * size,))],
         cost_estimate=SMALL,
@@ -111,34 +115,90 @@
     return out[:size], out[size : 2 * size], out[2 * size]
 
 
-def end_kernel(code_ref, total_ref, late_ref, own_ref, out_ref):
-    heads = out_ref.shape[0] // HEAD_DIM
-    first = pl.program_id(0) * heads
+def gather_kernel(size, seq_ref, *refs):
+    out_ref = refs[-1]
+    part = refs[0].shape[1]
+    for offset in range(size):
+        source = seq_ref[0] - offset
+        source = jnp.where(source < 0, source + size, source)
+        out_ref[:, pl.ds(pl.multiple_of(source * part, part), part), :] = refs[offset][...]
+
+
+def put_together(pieces, seq, size):
+    heads, part, state = pieces[0].shape
+    if part % 16 == 0:
+        step = min(heads, 16)
+        piece = pl.BlockSpec((step, part, state), lambda g: (g, 0, 0))
+        whole = pl.pallas_call(
+            functools.partial(gather_kernel, size),
+            grid=(heads // step,),
+            in_specs=[pl.BlockSpec(memory_space=pltpu.SMEM)] + [piece] * size,
+            out_specs=pl.BlockSpec((step, size * part, state), lambda g: (g, 0, 0)),
+            out_shape=jax.ShapeDtypeStruct((heads, size * part, state), pieces[0].dtype),
+            compiler_params=pltpu.CompilerParams(vmem_limit_bytes=VMEM_LIMIT),
+            cost_estimate=SMALL,
+        )(seq.reshape(1), *pieces)
+    else:
+        whole = jnp.zeros((heads, size, part, state), pieces[0].dtype)
+        owner = jnp.arange(size)[None, :, None, None]
+        for offset, piece in enumerate(pieces):
+            whole = jnp.where(owner == (seq - offset) % size, piece[:, None], whole)
+    return whole.reshape(heads * size * part, state)
+
+
+def end_kernel(size, seq_ref, code_ref, total_ref, own_ref, *refs):
+    pieces, late_ref, end_ref = refs[:size], refs[size], refs[size + 1]
+    leaves = refs[size + 2 :]
+    group = pl.program_id(0)
+    heads = end_ref.shape[0] // HEAD_DIM
+    first = group * heads
     plain = jnp.logical_and(code_ref[0] == 0, code_ref[1] == 0)
+    gather_kernel(size, seq_ref, *pieces, late_ref)
     for h in range(heads):
         rows = pl.ds(h * HEAD_DIM, HEAD_DIM)
         gain0, gain1 = total_ref[0, first + h], total_ref[1, first + h]
         use_late = jnp.where(plain, 0.0, jnp.where(code_ref[1] == 1, gain1, gain0 * gain1))
         use_own = jnp.where(code_ref[1] == 1, 0.0, gain1)
-        out_ref[rows, :] = (
-            jnp.where(plain, 0.0, late_ref[rows, :].astype(F32) * use_late)
+        end_ref[rows, :] = (
+            jnp.where(plain, 0.0, late_ref[h].astype(F32) * use_late)
             + own_ref[0, rows, :] * use_own
             + own_ref[1, rows, :]
         )
-
-
-def end_states(code, totals, late, own, per):
-    width = late.shape[0]
+    for n, leave_ref in enumerate(leaves):
+
+        @pl.when(group == n)
+        def _(leave_ref=leave_ref):
+            leave_ref[...] = end_ref[...].astype(BF)
+
+
+def end_states(seq, code, totals, pieces, own, per):
+    size = len(pieces)
+    heads_dev, part, state = pieces[0].shape
+    width = own.shape[1]
+    groups = width // per
+    heads = heads_dev // groups
+    if part % 16:
+        pieces = [put_together(pieces, seq, size).reshape(heads_dev, size * part, state)]
+        size, part = 1, size * part
+        seq = jnp.zeros_like(seq)
     smem = pl.BlockSpec(memory_space=pltpu.SMEM)
     rows = pl.BlockSpec((per, STATE), lambda g: (g, 0))
-    return pl.pallas_call(
-        end_kernel,
-        grid=(width // per,),
-        in_specs=[smem, smem, rows, pl.BlockSpec((2, per, STATE), lambda g: (0, g, 0))],
-        out_specs=rows,
-        out_shape=jax.ShapeDtypeStruct((width, STATE), F32),
+    late, ends, *leaves = pl.pallas_call(
+        functools.partial(end_kernel, size),
+        grid=(groups,),
+        in_specs=[smem, smem, smem, pl.BlockSpec((2, per, STATE), lambda g: (0, g, 0))]
+        + [pl.BlockSpec((heads, part, state), lambda g: (g, 0, 0))] * size,
+        out_specs=[pl.BlockSpec((heads, size * part, state), lambda g: (g, 0, 0)), rows]
+        + [pl.BlockSpec((per, STATE), lambda g: (0, 0))] * groups,
+        out_shape=[
+            jax.ShapeDtypeStruct((heads_dev, size * part, state), BF),
+            jax.ShapeDtypeStruct((width, STATE), F32),
+        ]
+        + [jax.ShapeDtypeStruct((per, STATE), BF)] * groups,
+        compiler_params=pltpu.CompilerParams(vmem_limit_bytes=VMEM_LIMIT),
         cost_estimate=SMALL,
-    )(code, totals, late, own)
+    )(seq.reshape(1), code, totals, own, *pieces)
+    return late.reshape(width, state), ends, leaves
 
 
 def leave_kernel(place, code_ref, total_ref, carry_ref, end_ref, out_ref):
@@ -160,6 +220,7 @@
         in_specs=[smem, smem, rows, pl.BlockSpec((per, STATE), lambda g: (place + g, 0))],
         out_specs=rows,
         out_shape=jax.ShapeDtypeStruct(carry.shape, BF),
+        compiler_params=pltpu.CompilerParams(vmem_limit_bytes=VMEM_LIMIT),
         cost_estimate=SMALL,
     )(code, totals, carry, ends)
 
@@ -286,64 +347,59 @@
     )(code, totals, x, z, b, c, run, run_t, step_t, gain, carry, late, early, own)
 
 
-def project_kernel(count, picks, seq_ref, *refs):
-    lhs = refs[: 4 * count]
-    arrays = refs[4 * count : -3]
-    out_ref, weight, sems = refs[-3:]
-    depth = lhs[0].shape[1]
-    cols = weight.shape[2]
-    for n, block in enumerate(picks):
-        for half, where in enumerate(block):
-            for choice in sorted(set(where)):
-                mine = [s for s, other in enumerate(where) if other == choice]
-                hit = seq_ref[0] == mine[0]
-                for s in mine[1:]:
-                    hit = jnp.logical_or(hit, seq_ref[0] == s)
-
-                @pl.when(hit)
-                def _(n=n, half=half, choice=choice):
-                    pltpu.make_async_copy(
-                        arrays[choice[0]].at[pl.ds(choice[1], depth)],
-                        weight.at[n, pl.ds(half * depth, depth)],
-                        sems.at[n],
-                    ).start()
-
-    for n in range(len(picks)):
-        pltpu.make_async_copy(weight.at[n], weight.at[n], sems.at[n]).wait()
+def project_kernel(first_ref, *refs):
+    weights, out_ref, rows_all, weight, total, sems = refs[-6:]
+    lhs = refs[:-6]
+    tokens, depth = lhs[0].shape
+    cols = weights.shape[2]
+    parts = len(lhs) // 4
+    for part in range(parts):
+        span = pl.ds(part * depth, depth)
         for r in range(4):
-            total = None
-            for half in range(count):
-                part = jnp.dot(
-                    lhs[4 * half + r][...],
-                    weight[n, half * depth : (half + 1) * depth, :],
-                    preferred_element_type=F32,
-                )
-                total = part if total is None else total + part
-            rows = total.shape[0]
-            out_ref[r * rows : (r + 1) * rows, n * cols : (n + 1) * cols] = total.astype(BF)
-
-
-def project(seq, lhs, arrays, picks):
-    count = len(lhs) // 4
+            pltpu.make_async_copy(
+                lhs[4 * part + r],
+                rows_all.at[part, pl.ds(r * tokens, tokens)],
+                sems.at[0, part],
+            ).start()
+        for n in range(2):
+            pltpu.make_async_copy(
+                weights.at[first_ref[0] + n, span],
+                weight.at[part, :, pl.ds(n * cols, cols)],
+                sems.at[1, part],
+            ).start()
+    for part in range(parts):
+        pltpu.make_async_copy(rows_all.at[part], rows_all.at[part], sems.at[0, part]).wait()
+        pltpu.make_async_copy(weight.at[part], weight.at[part], sems.at[1, part]).wait()
+        for r in range(4):
+            span = pl.ds(r * tokens, tokens)
+            product = jnp.dot(rows_all[part, span, :], weight[part], preferred_element_type=F32)
+            if part == 0:
+                total[span, :] = product
+            elif part < parts - 1:
+                total[span, :] += product
+            else:
+                out_ref[span, :] = (total[span, :] + product).astype(BF)
+
+
+def project(first, lhs, weights):
+    parts = len(lhs) // 4
     tokens = 4 * lhs[0].shape[0]
-    cols = arrays[0].shape[1]
-    depth = lhs[0].shape[1]
-    whole = pl.BlockSpec(memory_space=pltpu.VMEM)
+    depth, cols = weights.shape[1:]
     hbm = pl.BlockSpec(memory_space=pl.ANY)
     return pl.pallas_call(
-        functools.partial(project_kernel, count, picks),
-        in_specs=[pl.BlockSpec(memory_space=pltpu.SMEM)]
-        + [whole] * len(lhs)
-        + [hbm] * len(arrays),
-        out_specs=whole,
-        out_shape=jax.ShapeDtypeStruct((tokens, len(picks) * cols), BF),
+        project_kernel,
+        in_specs=[pl.BlockSpec(memory_space=pltpu.SMEM)] + [hbm] * (len(lhs) + 1),
+        out_specs=pl.BlockSpec(memory_space=pltpu.VMEM),
+        out_shape=jax.ShapeDtypeStruct((tokens, 2 * cols), BF),
         scratch_shapes=[
-            pltpu.VMEM((len(picks), count * depth, cols), BF),
-            pltpu.SemaphoreType.DMA((len(picks),)),
+            pltpu.VMEM((parts, tokens, depth // parts), BF),
+            pltpu.VMEM((parts, depth // parts, 2 * cols), BF),
+            pltpu.VMEM((tokens, 2 * cols), F32),
+            pltpu.SemaphoreType.DMA((2, parts)),
         ],
         compiler_params=pltpu.CompilerParams(vmem_limit_bytes=VMEM_LIMIT),
         cost_estimate=SMALL,
-    )(seq.reshape(1), *lhs, *arrays)
+    )(first.reshape(1), *lhs, weights)
 
 
 SWAP = [(0, 1), (1, 0)]
@@ -353,36 +409,20 @@
     return lax.optimization_barrier((value, *others))[0]
 
 
-def finish_fast(seq, head, y, core, early_sums, late_sums, tokens, quarter):
-    is_early = head == seq // 2
-    swapped = jnp.where(is_early, seq % 2 == 1, seq >= 2)
-    first = [jnp.where(is_early, a, b) for a, b in zip(early_sums[0], late_sums[0])]
-    second = [jnp.where(is_early, a, b) for a, b in zip(early_sums[1], late_sums[1])]
-    low = [jnp.where(swapped, b, a) for a, b in zip(first, second)]
-    high = [jnp.where(swapped, a, b) for a, b in zip(first, second)]
-    pieces = []
-    for part in (low, high):
-        a, b, c, d = part
-        p = [jnp.where(core == 0, a, b), jnp.where(core == 0, b, a)]
-        q = [jnp.where(core == 0, c, d), jnp.where(core == 0, d, c)]
-        pieces += [jnp.where(y == 0, v, w) for v, w in zip(p + q, q + p)]
-    return jnp.concatenate(pieces, axis=1)[None]
-
-
-def to_rows(partial_value, late, tokens):
-    goal = [(s // 2 + (1 if late else 0)) % 2 for s in range(4)]
-    to_goal = [(2 * s + 1 - goal[s], 2 * s + goal[s]) for s in range(4)]
-    arrived = lax.ppermute(partial_value, ("seq", "head"), to_goal)
-    total = (partial_value.astype(F32) + arrived.astype(F32)).astype(BF)
+def to_rows(own, others, tokens):
+    arrived = lax.ppermute(others, "head", SWAP)
+    total = (own.astype(F32) + arrived.astype(F32)).astype(BF)
     total = total.reshape(4, tokens, total.shape[1])
-    ends = [2 * s + goal[s] for s in range(4)]
-    cross_y = [(a * 8 + e, (1 - a) * 8 + e) for a in (0, 1) for e in ends]
-    from_y = lax.ppermute(total[2:], ("groups", "seq", "head"), cross_y)
-    cross_core = [(2 * e + a, 2 * e + 1 - a) for a in (0, 1) for e in ends]
-    from_core = lax.ppermute(
-        jnp.stack([total[1], from_y[1]]), ("seq", "head", "batch"), cross_core
-    )
+    from_y = lax.ppermute(total[2:], "groups", SWAP)
+    from_core = lax.ppermute(jnp.stack([total[1], from_y[1]]), "batch", SWAP)
     return total[0], from_core[0], from_y[0], from_core[1]
+
+
+def in_order(y, core, parts):
+    a, b, c, d = parts
+    p = [jnp.where(core == 0, a, b), jnp.where(core == 0, b, a)]
+    q = [jnp.where(core == 0, c, d), jnp.where(core == 0, d, c)]
+    return [jnp.where(y == 0, v, w) for v, w in zip(p + q, q + p)]
 
 
 def plain_projection(normed, out_weight):
@@ -405,14 +445,12 @@
 
 
 def exchange_states(payload, seq, size):
-    heads, part, state = payload[0].shape
-    whole = jnp.zeros((heads, size, part, state), payload[0].dtype)
-    owner = jnp.arange(size)[None, :, None, None]
-    for offset, piece in enumerate(payload):
-        if offset:
-            piece = lax.ppermute(piece, "seq", [(i, (i + offset) % size) for i in range(size)])
-        whole = jnp.where(owner == (seq - offset) % size, piece[:, None], whole)
-    return whole.reshape(heads * size * part, state)
+    return [
+        lax.ppermute(piece, "seq", [(i, (i + offset) % size) for i in range(size)])
+        if offset
+        else piece
+        for offset, piece in enumerate(payload)
+    ]
 
 
 def body(
@@ -450,18 +488,19 @@
     late_out, early_out, code = pick_states(
         seq, conv_lengths, session_slots, cached_states, size
     )
-    late = exchange_states(late_out, seq, size)
+    late_pieces = exchange_states(late_out, seq, size)
     head = lax.axis_index("head")
     y = lax.axis_index("groups")
     core = lax.axis_index("batch")
     if fast:
         quarter = out_weight.shape[1] // 4
-        half = out_weight.shape[0] // 2
-        w_own = lax.dynamic_slice_in_dim(
-            after(out_weight, code), (2 * y + core) * quarter, quarter, 1
-        )
-        w_side = lax.ppermute(w_own, "seq", [(1, 0), (3, 2), (2, 3)])
-        w_mid = lax.ppermute(w_own, "seq", [(1, 2), (2, 1)])
+        piece = quarter // PIECES
+        w_own = [
+            lax.dynamic_slice_in_dim(
+                out_weight, (2 * y + core) * quarter + k * piece, piece, 1
+            )
+            for k in range(PIECES)
+        ]
 
     logs = log_decay[0].reshape(blocks, STRETCH, heads_dev)
     running = jnp.cumsum(logs, axis=1)
@@ -476,36 +515,25 @@
     x, z, b, c = x_values[0], z_gate[0], write_basis[0], read_basis[0]
     own = block_states_of(x, b, end_g, blocks)
 
-    ends = end_states(code, totals, late, own, per)
-    count = 2 if groups_dev % 2 == 0 else 1
+    count = 1
     chunks = groups_dev // count
-    span = count * per
     arrived = [[] for _ in range(chunks)]
-    leaving = [ends[n * span : (n + 1) * span].astype(BF) for n in range(chunks)]
-    early_out = [after(piece, leaving[0]) for piece in early_out]
-    early = None
+    late, ends, leaving = end_states(seq, code, totals, late_pieces, own, per)
+    early_pieces = exchange_states([after(piece, own) for piece in early_out], seq, size)
+    weights = None
     for hop in range(size - 1):
         for n in range(chunks):
             if hop:
-                leaving[n] = leaving_state(n * count, code, totals, arrived[n][-1], ends, per)
+                leaving[n] = leaving_state(
+                    n * count, code, totals, arrived[n][-1], ends, per
+                )
             arrived[n].append(lax.ppermute(leaving[n], "seq", [(hop, hop + 1)]))
-        if early is None:
-            early = exchange_states(early_out, seq, size)
-        if fast and hop == 0:
-            w_first = lax.ppermute(after(w_own, arrived[-1][0]), "seq", [(0, 1)])
-        if fast and hop == 1:
-            w_side, w_mid, arrived[0][1] = lax.optimization_barrier(
-                (w_side, w_mid, arrived[0][1])
-            )
-            w_two = lax.ppermute(w_mid[:half], "seq", [(1, 0), (2, 3)])
-            w_two_left = lax.ppermute(w_mid[half:], "seq", [(1, 0)])
-            w_three_mid = lax.ppermute(w_side, "seq", [(2, 1)])
-    if fast:
-        w_two_right = lax.ppermute(after(w_mid[half:], arrived[-1][-1]), "seq", [(2, 3)])
-        w_first, arrived[0][-1] = lax.optimization_barrier((w_first, arrived[0][-1]))
-        w_first_mid = lax.ppermute(w_first, "seq", [(1, 2)])
-        w_three_left = lax.ppermute(w_three_mid, "seq", [(1, 0)])
-        w_three_right = lax.ppermute(w_first_mid, "seq", [(2, 3)])
+        if fast and weights is None:
+            weights = [
+                lax.all_gather(after(part, arrived[0][0], *early_pieces), "seq", axis=0)
+                for part in w_own
+            ]
+    early = put_together(early_pieces, seq, size)
 
     gain = norm_gain.reshape(1, width)
     normed = []
@@ -526,31 +554,18 @@
         other = lax.ppermute(part, "batch", SWAP)
         other_across = lax.ppermute(across, "batch", SWAP)
         lhs += [part, other, across, other_across]
-    one = project(
-        seq,
-        lhs,
-        [w_own, w_side, w_first],
-        [
-            [[(0, 0)] * 4, [(0, half)] * 4],
-            [[(1, 0), (2, 0), (1, 0), (1, 0)], [(1, half), (2, half), (1, half), (1, half)]],
-        ],
-    )
-    two = project(
-        seq,
-        lhs,
-        [w_two, w_two_left, w_two_right, w_mid],
-        [[[(0, 0), (3, 0), (3, 0), (0, 0)], [(1, 0), (3, half), (3, half), (2, 0)]]],
-    )
-    arrays = [w_three_left, w_three_mid, w_first_mid, w_three_right]
-    three = project(
-        seq,
-        lhs,
-        arrays,
-        [[[(s, 0) for s in range(4)], [(s, half) for s in range(4)]]],
-    )
-    sums = [to_rows(one, False, tokens), to_rows(two, True, tokens), to_rows(three, True, tokens)]
-    early_sums = [[v[:, :quarter] for v in sums[0]], [v[:, quarter:] for v in sums[0]]]
-    return finish_fast(seq, head, y, core, early_sums, sums[1:], tokens, quarter)
+    sides = []
+    for part in weights:
+        others = project(2 - 2 * head, lhs, part)
+        mine = project(2 * head, lhs, part)
+        sides.append(in_order(y, core, to_rows(mine, others, tokens)))
+    pieces = [
+        sides[k][q][:, block * piece : (block + 1) * piece]
+        for block in range(2)
+        for q in range(4)
+        for k in range(PIECES)
+    ]
+    return jnp.concatenate(pieces, axis=1)[None]
 
 
 def solution(mesh):

time: 417 us -> 291 us (0.70)
  waiting for transfers between devices: 187 us -> 119 us
  Pallas kernels: 114 us -> 73.4 us
  starting transfers between devices: 79.4 us -> 61.3 us
  other arithmetic: 20.1 us -> 5.51 us
  between operations: 0.94 us -> 14.1 us
    ppermute x19 -> x6, waiting for transfers between devices: 81.2 us -> 6.79 us  [the longest x2 5.7 us: to_rows(): from_y = lax.ppermute(total[2:], 'groups', SWAP)]
    all_gather x0 -> x2, waiting for transfers between devices: none -> 64.9 us  [body(): lax.all_gather(after(part, arrived[0][0], *early_pieces), 'seq', axis=0)]
    pallas_call x1, Pallas kernels: 65.9 us -> 3.81 us  [pick_states(): pl.pallas_call(functools.partial(pick_kernel, size), in_specs=[smem, smem...]
    ppermute x6 -> x12, waiting for transfers between devices: 59.6 us -> 15.4 us  [body(): arrived[n].append(lax.ppermute(leaving[n], 'seq', [(hop, hop + 1)]))]
    ppermute x19 -> x6, starting transfers between devices: 38.2 us -> 8.47 us  [the longest x2 5.29 us: to_rows(): from_core = lax.ppermute(jnp.stack([total[1], from_y[1]]), 'batch', SWAP)]
    ppermute x6 -> x12, starting transfers between devices: 15.5 us -> 30.3 us  [body(): arrived[n].append(lax.ppermute(leaving[n], 'seq', [(hop, hop + 1)]))]
    select_n x2, other arithmetic: 11.9 us -> 0.1 us  [in_order(): return [jnp.where(y == 0, v, w) for v, w in zip(p + q, q + p)]]
    ppermute x6, starting transfers between devices: 17.5 us -> 7.99 us  [exchange_states(): lax.ppermute(piece, 'seq', [(i, (i + offset) % size) for i in range(size)])]
  transfers between devices with their start and end apart: 37 -> 38, of which waited for: 15 -> 12; matrix products, arithmetic and copies ran while one was open for 7% -> 4% of each run, Pallas kernels for 12% -> 24%
where the time goes in v3:
time: 291 us; the launch traced here: 288 us
  waiting for transfers between devices  119 us (41%)
  Pallas kernels  73.4 us (25%)
  starting transfers between devices  61.3 us (21%)
  local copies, waits for them, and re-layouts  14.2 us (5%)
  between operations  14.1 us (5%)
  other arithmetic  5.51 us (2%)
    all_gather x2, waiting for transfers between devices, body(): lax.all_gather(after(part, arrived[0][0], *early_pieces), 'seq', axis=0)  64.9 us
    ppermute x12, starting transfers between devices, body(): arrived[n].append(lax.ppermute(leaving[n], 'seq', [(hop, hop + 1)]))  30.3 us
    ppermute x4, waiting for transfers between devices, body(): across = lax.ppermute(part, 'groups', SWAP)  25.3 us
    pallas_call x4, Pallas kernels, project(): pl.pallas_call(project_kernel, in_specs=[pl.BlockSpec(memory_space=pltpu....  22.7 us
    pallas_call x4, Pallas kernels, mix_groups(): pl.pallas_call(functools.partial(mix_kernel, place), grid=(count, tokens...  16.8 us
    pallas_call x8, Pallas kernels, leaving_state(): pl.pallas_call(functools.partial(leave_kernel, place), grid=(carry.shape[...  15.5 us
    ppermute x12, waiting for transfers between devices, body(): arrived[n].append(lax.ppermute(leaving[n], 'seq', [(hop, hop + 1)]))  15.4 us
    ppermute x6, starting transfers between devices, exchange_states(): lax.ppermute(piece, 'seq', [(i, (i + offset) % size) for i in range(size)])  7.99 us
  transfers between devices with their start and end apart: 38, of which 12 were waited for; matrix products, arithmetic and copies ran while one was open for 4% of the time, Pallas kernels for 24%

profile of v3, /device:TPU:3, one launch (start us, length us, event | category | flops | bytes accessed | tf_op | source)
XLA Modules:
  0.0 287.8 jit_solution(17995709261820035597)
XLA Ops:
  6.5 3.8 %shard_map.109 = (bf16[64,16,128]{2,1,0:T(8,128)(2,1)}, bf16[64,16,128]{2,1,0:T(8,128)(2,1)}, bf16[64,16,128]{2,1,0:T(8,128)(2,1)}, bf16[64,16,128]{2,1,0:T(8,12...) custom-call(s32[1]{0:T(128)} %bitcast.1.seq_ref, ...), custom_call_target="tpu_custom_call" | custom-call | flops 1000 | bytes 1000 | tf_op jit(solution)/shard_map/pallas_call | solution.py:107
  10.4 1.4 collective-permute-start
  11.7 2.2 collective-permute-start.1
  14.0 1.0 collective-permute-start.2
  15.0 0.9 copy.20
  16.7 0.9 multiply_bitcast_fusion
  17.5 1.0 copy.15.end_ref
  18.5 6.1 %shard_map.110.own_ref = f32[2,4096,128]{2,1,0:T(8,128)} custom-call(bf16[256,4096]{1,0:T(8,128)(2,1)} %bitcast.72, bf16[256,512]{1,0:T(8,128)(2,1)} %bitcast.93, f32[4,256,16]{2,1,0:T(8,128)} %copy.15.end_ref), custom_call_target="tpu_custom_call" | custom-call | flops 268435456 | bytes 16777216 | tf_op jit(solution)/shard_map/pallas_call | solution.py:46
  25.8 2.8 collective-permute-start.8
  28.6 4.3 %collective-permute-done.1.refs_2_ = bf16[64,16,128]{2,1,0:T(8,128)(2,1)S(1)} collective-permute-done((bf16[64,16,128]{2,1,0:T(8,128)(2,1)}, bf16[64,16,128]{2,1,0:T(8,128)(2,1)S(1)}, u32[]{:S(2)}, u32[]{:S(2)}) %collective-permute-start.1) | collective-permute-done | bytes 262176 | tf_op jit(solution)/shard_map/ppermute | solution.py:449
  32.9 0.7 copy-done.29
  33.7 5.1 %shard_map.111 = (bf16[64,64,128]{2,1,0:T(8,128)(2,1)}, f32[4096,128]{1,0:T(8,128)}, bf16[1024,128]{1,0:T(8,128)(2,1)}, bf16[1024,128]{1,0:T(8,128)(2,1)}, bf16[...) custom-call(s32[1]{0:T(128)} %bitcast.1.seq_ref, s32[2]{0:T(128)} %get-tuple-element.26.code_ref, f32[2,64]{1,0:T(2,128)} %exp.8.total_ref, ...), custom_call_target="tpu_custom_call" | custom-call | flops 1000 | bytes 1000 | tf_op jit(solution)/shard_map/pallas_call | solution.py:186
  38.9 18.2 %collective-permute-start.3 = (bf16[1024,128]{1,0:T(8,128)(2,1)}, bf16[1024,128]{1,0:T(8,128)(2,1)S(1)}, u32[]{:S(2)}, u32[]{:S(2)}) collective-permute-start(bf16[1024,128]{1,0:T(8,128)(2,1)} %get-tuple-element.31), channel_id=1, source_target_pairs={{0,4},{1,5},{2,6},{3,7},{16,20},{17,21},{18,22},{19,23}} | collective-permute-start | bytes 786440 | tf_op jit(solution)/shard_map/ppermute | solution.py:530
  57.1 3.0 %constant_dynamic-slice_fusion = (bf16[4096,128]{1,0:T(8,128)(2,1)}, bf16[4096,128]{1,0:T(8,128)(2,1)}) fusion(bf16[4096,1024]{1,0:T(8,128)(2,1)} %param.21, s32[]{:T(128)S(6)} %select_n.98, s32[]{:T(128)S(6)} %select_n.92), kind=kLoop, calls=%fused_computation.45 | loop fusion | bytes 4194312 | tf_op jit(solution)/shard_map/dynamic_slice | solution.py:499
  60.1 2.3 collective-permute-done.3.carry_ref
  63.2 4.0 %collective-permute-start.12 = (bf16[1024,128]{1,0:T(8,128)(2,1)S(1)}, bf16[1024,128]{1,0:T(8,128)(2,1)S(1)}, u32[]{:S(2)}, u32[]{:S(2)}) collective-permute-start(bf16[1024,128]{1,0:T(8,128)(2,1)S(1)} %copy-done.37), channel_id=1, source_target_pairs={{0,4},{1,5},{2,6},{3,7},{16,20},{17,21},{18,22},{19,23}} | collective-permute-start | bytes 786440 | tf_op jit(solution)/shard_map/ppermute | solution.py:530
  67.2 1.3 collective-permute-start.18
  68.6 1.3 collective-permute-start.24
  69.9 2.0 shard_map.112
  73.3 2.0 shard_map.116
  75.9 5.1 %collective-permute-done.18.carry_ref = bf16[1024,128]{1,0:T(8,128)(2,1)S(1)} collective-permute-done((bf16[1024,128]{1,0:T(8,128)(2,1)S(1)}, bf16[1024,128]{1,0:T(8,128)(2,1)S(1)}, u32[]{:S(2)}, u32[]{:S(2)}) %collective-permute-start.18) | collective-permute-done | bytes 262176 | tf_op jit(solution)/shard_map/ppermute | solution.py:530
  81.8 1.9 shard_map.119
  84.4 7.9 %collective-permute-done.24.carry_ref = bf16[1024,128]{1,0:T(8,128)(2,1)S(1)} collective-permute-done((bf16[1024,128]{1,0:T(8,128)(2,1)S(1)}, bf16[1024,128]{1,0:T(8,128)(2,1)S(1)}, u32[]{:S(2)}, u32[]{:S(2)}) %collective-permute-start.24) | collective-permute-done | bytes 262176 | tf_op jit(solution)/shard_map/ppermute | solution.py:530
  93.0 1.9 shard_map.122
  96.3 1.9 shard_map.113
  99.6 1.9 shard_map.117
  101.5 0.8 collective-permute-start.14
  102.4 1.0 copy.16.run_ref
  103.4 3.4 %shard_map.114 = bf16[64,64,128]{2,1,0:T(8,128)(2,1)} custom-call(s32[1]{0:T(128)} %bitcast.1.seq_ref, bf16[64,16,128]{2,1,0:T(8,128)(2,1)} %get-tuple-element.35.refs_0_, bf16[64,16,128]{2,1,0:T(8,128)(2,1)} %copy-done.25, bf16[64,16,128]{2,1,0:T(8,128)(2,1)} %copy-done.26, bf16[64,16,128]{2,1,0:T(8,128)(2,1)} %copy-done.27), custom_call_target="tpu_custom_call" | custom-call | flops 1000 | bytes 1000 | tf_op jit(solution)/shard_map/pallas_call | solution.py:132
  107.5 1.9 shard_map.120
  110.1 0.7 copy-done.19
  110.8 1.9 shard_map.123
  113.4 0.7 add_add_fusion.3.carry_ref
  114.1 4.2 %shard_map.115.refs_0_ = bf16[256,1024]{1,0:T(8,128)(2,1)} custom-call(s32[2]{0:T(128)} %get-tuple-element.26.code_ref, f32[2,64]{1,0:T(2,128)} %exp.8.total_ref, bf16[256,4096]{1,0:T(8,128)(2,1)} %bitcast.73, bf16[256,4096]{1,0:T(8,128)(2,1)} %bitcast.77, bf16[256,512]{1,0:T(8,128)(2,1)} %bitcast.94, bf16[256,512]{1,0:T(8,128)(2,1)} %bitcast.98, ...), custom_call_target="tpu_custom_call" | custom-call | flops 1000 | bytes 1000 | tf_op jit(solution)/shard_map/pallas_call | solution.py:323
  118.4 6.4 %collective-permute-start.9 = (bf16[256,1024]{1,0:T(8,128)(2,1)}, bf16[256,1024]{1,0:T(8,128)(2,1)S(1)}, u32[]{:S(2)}, u32[]{:S(2)}) collective-permute-start(bf16[256,1024]{1,0:T(8,128)(2,1)} %shard_map.115.refs_0_), channel_id=1, source_target_pairs={{0,1},{1,0},{2,3},{3,2},{4,5},{5,4},{6,7},{7,6},{8,9},{9,8},{10,11... | collective-permute-start | bytes 1572872 | tf_op jit(solution)/shard_map/ppermute | solution.py:554
  124.7 1.3 collective-permute-start.10
  126.1 0.7 add_add_fusion.2.carry_ref
  126.9 4.2 %shard_map.118.refs_4_ = bf16[256,1024]{1,0:T(8,128)(2,1)} custom-call(s32[2]{0:T(128)} %get-tuple-element.26.code_ref, f32[2,64]{1,0:T(2,128)} %exp.8.total_ref, bf16[256,4096]{1,0:T(8,128)(2,1)} %bitcast.74, bf16[256,4096]{1,0:T(8,128)(2,1)} %bitcast.78, bf16[256,512]{1,0:T(8,128)(2,1)} %bitcast.95, bf16[256,512]{1,0:T(8,128)(2,1)} %bitcast.99, ...), custom_call_target="tpu_custom_call" | custom-call | flops 1000 | bytes 1000 | tf_op jit(solution)/shard_map/pallas_call | solution.py:323
  131.6 0.8 add_add_fusion.1.carry_ref
  132.4 0.8 add_add_fusion.carry_ref
  133.1 4.2 %shard_map.121.refs_8_ = bf16[256,1024]{1,0:T(8,128)(2,1)} custom-call(s32[2]{0:T(128)} %get-tuple-element.26.code_ref, f32[2,64]{1,0:T(2,128)} %exp.8.total_ref, bf16[256,4096]{1,0:T(8,128)(2,1)} %bitcast.75, bf16[256,4096]{1,0:T(8,128)(2,1)} %bitcast.79, bf16[256,512]{1,0:T(8,128)(2,1)} %bitcast.96, bf16[256,512]{1,0:T(8,128)(2,1)} %bitcast.100, ...), custom_call_target="tpu_custom_call" | custom-call | flops 1000 | bytes 1000 | tf_op jit(solution)/shard_map/pallas_call | solution.py:323
  137.8 4.2 %shard_map.124.refs_12_ = bf16[256,1024]{1,0:T(8,128)(2,1)} custom-call(s32[2]{0:T(128)} %get-tuple-element.26.code_ref, f32[2,64]{1,0:T(2,128)} %exp.8.total_ref, bf16[256,4096]{1,0:T(8,128)(2,1)} %bitcast.76, bf16[256,4096]{1,0:T(8,128)(2,1)} %bitcast.80, bf16[256,512]{1,0:T(8,128)(2,1)} %bitcast.97, bf16[256,512]{1,0:T(8,128)(2,1)} %bitcast.101, ...), custom_call_target="tpu_custom_call" | custom-call | flops 1000 | bytes 1000 | tf_op jit(solution)/shard_map/pallas_call | solution.py:323
  142.0 1.4 collective-permute-start.22
  144.2 5.5 %collective-permute-done.16.refs_6_ = bf16[256,1024]{1,0:T(8,128)(2,1)S(1)} collective-permute-done((bf16[256,1024]{1,0:T(8,128)(2,1)}, bf16[256,1024]{1,0:T(8,128)(2,1)S(1)}, u32[]{:S(2)}, u32[]{:S(2)}) %collective-permute-start.16) | collective-permute-done | bytes 524320 | tf_op jit(solution)/shard_map/ppermute | solution.py:553
  149.7 1.3 collective-permute-start.11
  151.1 9.9 %collective-permute-done.22.refs_10_ = bf16[256,1024]{1,0:T(8,128)(2,1)} collective-permute-done((bf16[256,1024]{1,0:T(8,128)(2,1)S(1)}, bf16[256,1024]{1,0:T(8,128)(2,1)}, u32[]{:S(2)}, u32[]{:S(2)}) %collective-permute-start.22) | collective-permute-done | bytes 524320 | tf_op jit(solution)/shard_map/ppermute | solution.py:553
  161.0 1.3 collective-permute-start.23
  162.3 9.9 %collective-permute-done.28.refs_14_ = bf16[256,1024]{1,0:T(8,128)(2,1)} collective-permute-done((bf16[256,1024]{1,0:T(8,128)(2,1)}, bf16[256,1024]{1,0:T(8,128)(2,1)}, u32[]{:S(2)}, u32[]{:S(2)}) %collective-permute-start.28) | collective-permute-done | bytes 524320 | tf_op jit(solution)/shard_map/ppermute | solution.py:553
  172.2 0.9 collective-permute-start.29
  173.1 1.8 collective-permute-done.29.refs_15_
  175.0 5.9 %shard_map.126 = bf16[1024,256]{1,0:T(8,128)(2,1)} custom-call(s32[1]{0:T(128)} %bitcast.18.first_ref, bf16[256,1024]{1,0:T(8,128)(2,1)} %shard_map.115.refs_0_, bf16[256,1024]{1,0:T(8,128)(2,1)} %copy-done.1, bf16[256,1024]{1,0:T(8,128)(2,1)} %copy-done.2, bf16[256,1024]{1,0:T(8,128)(2,1)} %collective-permute-done.11.refs_3_, ...), custom_call_target="tpu_custom_call" | custom-call | flops 1000 | bytes 1000 | tf_op jit(solution)/shard_map/pallas_call | solution.py:389
  181.3 64.9 %all-gather.7.cloned.1.call-done = bf16[16384,128]{1,0:T(8,128)(2,1)} async-done(((bf16[4096,128]{1,0:T(8,128)(2,1)}), bf16[16384,128]{1,0:T(8,128)(2,1)}) %all-gather.7.cloned.1.call-update) | async-done | bytes 4194320 | tf_op jit(solution)/shard_map/all_gather | solution.py:533
  246.3 5.5 %shard_map.128 = bf16[1024,256]{1,0:T(8,128)(2,1)} custom-call(s32[1]{0:T(128)} %bitcast.18.first_ref, bf16[256,1024]{1,0:T(8,128)(2,1)} %shard_map.115.refs_0_, bf16[256,1024]{1,0:T(8,128)(2,1)} %copy-done.1, bf16[256,1024]{1,0:T(8,128)(2,1)} %copy-done.2, bf16[256,1024]{1,0:T(8,128)(2,1)} %collective-permute-done.11.refs_3_, ...), custom_call_target="tpu_custom_call" | custom-call | flops 1000 | bytes 1000 | tf_op jit(solution)/shard_map/pallas_call | solution.py:389
  252.4 5.6 %shard_map.125 = bf16[1024,256]{1,0:T(8,128)(2,1)} custom-call(s32[1]{0:T(128)} %bitcast.first_ref, bf16[256,1024]{1,0:T(8,128)(2,1)} %shard_map.115.refs_0_, bf16[256,1024]{1,0:T(8,128)(2,1)} %copy-done.1, bf16[256,1024]{1,0:T(8,128)(2,1)} %copy-done.2, bf16[256,1024]{1,0:T(8,128)(2,1)} %collective-permute-done.11.refs_3_, ...), custom_call_target="tpu_custom_call" | custom-call | flops 1000 | bytes 1000 | tf_op jit(solution)/shard_map/pallas_call | solution.py:389
  257.9 5.8 %shard_map.127 = bf16[1024,256]{1,0:T(8,128)(2,1)} custom-call(s32[1]{0:T(128)} %bitcast.first_ref, bf16[256,1024]{1,0:T(8,128)(2,1)} %shard_map.115.refs_0_, bf16[256,1024]{1,0:T(8,128)(2,1)} %copy-done.1, bf16[256,1024]{1,0:T(8,128)(2,1)} %copy-done.2, bf16[256,1024]{1,0:T(8,128)(2,1)} %collective-permute-done.11.refs_3_, ...), custom_call_target="tpu_custom_call" | custom-call | flops 1000 | bytes 1000 | tf_op jit(solution)/shard_map/pallas_call | solution.py:389
  263.9 1.3 collective-permute-start.31
  265.1 1.2 add_convert_fusion
  266.3 0.9 collective-permute-start.34
  267.3 3.5 %collective-permute-done.31 = bf16[2,256,256]{2,1,0:T(8,128)(2,1)S(1)} collective-permute-done((bf16[2,256,256]{2,1,0:T(8,128)(2,1)S(1)}, bf16[2,256,256]{2,1,0:T(8,128)(2,1)S(1)}, u32[]{:S(2)}, u32[]{:S(2)}) %collective-permute-start.31) | collective-permute-done | bytes 262176 | tf_op jit(solution)/shard_map/ppermute | solution.py:416
  270.9 3.4 %collective-permute-start.32 = (bf16[2,256,256]{2,1,0:T(8,128)(2,1)S(1)}, bf16[2,256,256]{2,1,0:T(8,128)(2,1)S(1)}, u32[]{:S(2)}, u32[]{:S(2)}) collective-permute-start(bf16[2,256,256]{2,1,0:T(8,128)(2,1)S(1)} %pad_maximum_fusion), channel_id=1, source_target_pairs={{0,1},{1,0},{2,3},{3,2},{4,5},{5,4},{6,7},{7,6},{8,9},{9,8},{10,11... | collective-permute-start | bytes 786440 | tf_op jit(solution)/shard_map/ppermute | solution.py:417
  274.2 2.2 collective-permute-done.34
  276.5 1.9 collective-permute-start.35
  278.5 1.1 collective-permute-done.35
  280.0 1.0 copy-done.31
  (155 shorter events, 15.1 us)
Async XLA Ops:
  6.5 168.5 %all-gather.5.cloned.1.call-start = ((), (), s32[]{:S(2)}) async-start(), calls=%async_computation | async-start | bytes 5242880 | tf_op jit(solution)/shard_map/all_gather | solution.py:533
  10.4 15.4 %collective-permute-start = (bf16[64,16,128]{2,1,0:T(8,128)(2,1)}, bf16[64,16,128]{2,1,0:T(8,128)(2,1)S(1)}, u32[]{:S(2)}, u32[]{:S(2)}) collective-permute-start(bf16[64,16,128]{2,1,0:T(8,128)(2,1)} %get-tuple-element.28), channel_id=1, source_target_pairs={{0,4},{4,8},{8,12},{12,0},{1,5},{5,9},{9,13},{13,1},{2,6},{6,10},{... | collective-permute-start | bytes 786440 | tf_op jit(solution)/shard_map/ppermute | solution.py:449
  11.7 21.1 %collective-permute-start.1 = (bf16[64,16,128]{2,1,0:T(8,128)(2,1)}, bf16[64,16,128]{2,1,0:T(8,128)(2,1)S(1)}, u32[]{:S(2)}, u32[]{:S(2)}) collective-permute-start(bf16[64,16,128]{2,1,0:T(8,128)(2,1)} %get-tuple-element.29), channel_id=1, source_target_pairs={{0,8},{4,12},{8,0},{12,4},{1,9},{5,13},{9,1},{13,5},{2,10},{6,14},... | collective-permute-start | bytes 786440 | tf_op jit(solution)/shard_map/ppermute | solution.py:449
  14.0 18.9 %collective-permute-start.2 = (bf16[64,16,128]{2,1,0:T(8,128)(2,1)}, bf16[64,16,128]{2,1,0:T(8,128)(2,1)S(1)}, u32[]{:S(2)}, u32[]{:S(2)}) collective-permute-start(bf16[64,16,128]{2,1,0:T(8,128)(2,1)} %get-tuple-element.30), channel_id=1, source_target_pairs={{0,12},{4,0},{8,4},{12,8},{1,13},{5,1},{9,5},{13,9},{2,14},{6,2},{... | collective-permute-start | bytes 786440 | tf_op jit(solution)/shard_map/ppermute | solution.py:449
  16.3 8.4 %copy-start.34 = (bf16[64,16,128]{2,1,0:T(8,128)(2,1)S(1)}, bf16[64,16,128]{2,1,0:T(8,128)(2,1)}, u32[]{:S(2)}) copy-start(bf16[64,16,128]{2,1,0:T(8,128)(2,1)} %get-tuple-element.37) | copy-start | bytes 786436
  16.3 8.8 %copy-start.33 = (bf16[64,16,128]{2,1,0:T(8,128)(2,1)S(1)}, bf16[64,16,128]{2,1,0:T(8,128)(2,1)}, u32[]{:S(2)}) copy-start(bf16[64,16,128]{2,1,0:T(8,128)(2,1)} %get-tuple-element.39) | copy-start | bytes 786436
  16.3 9.5 %copy-start.32 = (bf16[64,16,128]{2,1,0:T(8,128)(2,1)S(1)}, bf16[64,16,128]{2,1,0:T(8,128)(2,1)}, u32[]{:S(2)}) copy-start(bf16[64,16,128]{2,1,0:T(8,128)(2,1)} %get-tuple-element.41) | copy-start | bytes 786436
  16.4 86.0 %copy-start.7 = (f32[256,4,16]{0,2,1:T(8,128)}, f32[256,4,16]{0,2,1:T(8,128)S(1)}, u32[]{:S(2)}) copy-start(f32[256,4,16]{0,2,1:T(8,128)S(1)} %reshape.52) | copy-start | bytes 196612
  24.7 35.4 %collective-permute-start.6 = (bf16[64,16,128]{2,1,0:T(8,128)(2,1)S(1)}, bf16[64,16,128]{2,1,0:T(8,128)(2,1)S(1)}, u32[]{:S(2)}, u32[]{:S(2)}) collective-permute-start(bf16[64,16,128]{2,1,0:T(8,128)(2,1)S(1)} %copy-done.34), channel_id=1, source_target_pairs={{0,4},{4,8},{8,12},{12,0},{1,5},{5,9},{9,13},{13,1},{2,6},{6,10},{... | collective-permute-start | bytes 786440 | tf_op jit(solution)/shard_map/ppermute | solution.py:449
  25.1 35.0 %collective-permute-start.7 = (bf16[64,16,128]{2,1,0:T(8,128)(2,1)S(1)}, bf16[64,16,128]{2,1,0:T(8,128)(2,1)S(1)}, u32[]{:S(2)}, u32[]{:S(2)}) collective-permute-start(bf16[64,16,128]{2,1,0:T(8,128)(2,1)S(1)} %copy-done.33), channel_id=1, source_target_pairs={{0,8},{4,12},{8,0},{12,4},{1,9},{5,13},{9,1},{13,5},{2,10},{6,14},... | collective-permute-start | bytes 786440 | tf_op jit(solution)/shard_map/ppermute | solution.py:449
  25.8 7.1 %copy-start.28 = (bf16[64,16,128]{2,1,0:T(8,128)(2,1)}, bf16[64,16,128]{2,1,0:T(8,128)(2,1)S(1)}, u32[]{:S(2)}) copy-start(bf16[64,16,128]{2,1,0:T(8,128)(2,1)S(1)} %collective-permute-done.refs_1_) | copy-start | bytes 786436
  25.8 34.3 %collective-permute-start.8 = (bf16[64,16,128]{2,1,0:T(8,128)(2,1)S(1)}, bf16[64,16,128]{2,1,0:T(8,128)(2,1)S(1)}, u32[]{:S(2)}, u32[]{:S(2)}) collective-permute-start(bf16[64,16,128]{2,1,0:T(8,128)(2,1)S(1)} %copy-done.32), channel_id=1, source_target_pairs={{0,12},{4,0},{8,4},{12,8},{1,13},{5,1},{9,5},{13,9},{2,14},{6,2},{... | collective-permute-start | bytes 786440 | tf_op jit(solution)/shard_map/ppermute | solution.py:449
  38.8 24.4 %copy-start.37 = (bf16[1024,128]{1,0:T(8,128)(2,1)S(1)}, bf16[1024,128]{1,0:T(8,128)(2,1)}, u32[]{:S(2)}) copy-start(bf16[1024,128]{1,0:T(8,128)(2,1)} %get-tuple-element.42) | copy-start | bytes 786436
  38.8 28.4 %copy-start.36 = (bf16[1024,128]{1,0:T(8,128)(2,1)S(1)}, bf16[1024,128]{1,0:T(8,128)(2,1)}, u32[]{:S(2)}) copy-start(bf16[1024,128]{1,0:T(8,128)(2,1)} %get-tuple-element.43) | copy-start | bytes 786436
  38.9 29.7 %copy-start.35 = (bf16[1024,128]{1,0:T(8,128)(2,1)S(1)}, bf16[1024,128]{1,0:T(8,128)(2,1)}, u32[]{:S(2)}) copy-start(bf16[1024,128]{1,0:T(8,128)(2,1)} %get-tuple-element.44) | copy-start | bytes 786436
  38.9 23.6 %collective-permute-start.3 = (bf16[1024,128]{1,0:T(8,128)(2,1)}, bf16[1024,128]{1,0:T(8,128)(2,1)S(1)}, u32[]{:S(2)}, u32[]{:S(2)}) collective-permute-start(bf16[1024,128]{1,0:T(8,128)(2,1)} %get-tuple-element.31), channel_id=1, source_target_pairs={{0,4},{1,5},{2,6},{3,7},{16,20},{17,21},{18,22},{19,23}} | collective-permute-start | bytes 786440 | tf_op jit(solution)/shard_map/ppermute | solution.py:530
  60.1 23.6 %copy-start.25 = (bf16[64,16,128]{2,1,0:T(8,128)(2,1)}, bf16[64,16,128]{2,1,0:T(8,128)(2,1)S(1)}, u32[]{:S(2)}) copy-start(bf16[64,16,128]{2,1,0:T(8,128)(2,1)S(1)} %collective-permute-done.6.refs_1_) | copy-start | bytes 786436
  60.1 23.6 %copy-start.26 = (bf16[64,16,128]{2,1,0:T(8,128)(2,1)}, bf16[64,16,128]{2,1,0:T(8,128)(2,1)S(1)}, u32[]{:S(2)}) copy-start(bf16[64,16,128]{2,1,0:T(8,128)(2,1)S(1)} %collective-permute-done.7.refs_2_) | copy-start | bytes 786436
  60.1 23.6 %copy-start.27 = (bf16[64,16,128]{2,1,0:T(8,128)(2,1)}, bf16[64,16,128]{2,1,0:T(8,128)(2,1)S(1)}, u32[]{:S(2)}) copy-start(bf16[64,16,128]{2,1,0:T(8,128)(2,1)S(1)} %collective-permute-done.8.refs_3_) | copy-start | bytes 786436
  62.4 7.5 %copy-start.9 = (bf16[1024,128]{1,0:T(8,128)(2,1)}, bf16[1024,128]{1,0:T(8,128)(2,1)S(1)}, u32[]{:S(2)}) copy-start(bf16[1024,128]{1,0:T(8,128)(2,1)S(1)} %collective-permute-done.3.carry_ref) | copy-start | bytes 786436
  62.4 183.8 %all-gather.7.cloned.1.call-start = ((), (), s32[]{:S(2)}) async-start(), calls=%async_computation.1 | async-start | bytes 5242880 | tf_op jit(solution)/shard_map/all_gather | solution.py:533
  63.2 9.3 %collective-permute-start.12 = (bf16[1024,128]{1,0:T(8,128)(2,1)S(1)}, bf16[1024,128]{1,0:T(8,128)(2,1)S(1)}, u32[]{:S(2)}, u32[]{:S(2)}) collective-permute-start(bf16[1024,128]{1,0:T(8,128)(2,1)S(1)} %copy-done.37), channel_id=1, source_target_pairs={{0,4},{1,5},{2,6},{3,7},{16,20},{17,21},{18,22},{19,23}} | collective-permute-start | bytes 786440 | tf_op jit(solution)/shard_map/ppermute | solution.py:530
  67.2 13.8 %collective-permute-start.18 = (bf16[1024,128]{1,0:T(8,128)(2,1)S(1)}, bf16[1024,128]{1,0:T(8,128)(2,1)S(1)}, u32[]{:S(2)}, u32[]{:S(2)}) collective-permute-start(bf16[1024,128]{1,0:T(8,128)(2,1)S(1)} %copy-done.36), channel_id=1, source_target_pairs={{0,4},{1,5},{2,6},{3,7},{16,20},{17,21},{18,22},{19,23}} | collective-permute-start | bytes 786440 | tf_op jit(solution)/shard_map/ppermute | solution.py:530
  68.6 23.7 %collective-permute-start.24 = (bf16[1024,128]{1,0:T(8,128)(2,1)S(1)}, bf16[1024,128]{1,0:T(8,128)(2,1)S(1)}, u32[]{:S(2)}, u32[]{:S(2)}) collective-permute-start(bf16[1024,128]{1,0:T(8,128)(2,1)S(1)} %copy-done.35), channel_id=1, source_target_pairs={{0,4},{1,5},{2,6},{3,7},{16,20},{17,21},{18,22},{19,23}} | collective-permute-start | bytes 786440 | tf_op jit(solution)/shard_map/ppermute | solution.py:530
  71.9 23.7 %collective-permute-start.4 = (bf16[1024,128]{1,0:T(8,128)(2,1)}, bf16[1024,128]{1,0:T(8,128)(2,1)S(1)}, u32[]{:S(2)}, u32[]{:S(2)}) collective-permute-start(bf16[1024,128]{1,0:T(8,128)(2,1)} %shard_map.112), channel_id=1, source_target_pairs={{4,8},{5,9},{6,10},{7,11},{20,24},{21,25},{22,26},{23,27}} | collective-permute-start | bytes 786440 | tf_op jit(solution)/shard_map/ppermute | solution.py:530
  75.2 23.6 %collective-permute-start.13 = (bf16[1024,128]{1,0:T(8,128)(2,1)}, bf16[1024,128]{1,0:T(8,128)(2,1)S(1)}, u32[]{:S(2)}, u32[]{:S(2)}) collective-permute-start(bf16[1024,128]{1,0:T(8,128)(2,1)} %shard_map.116), channel_id=1, source_target_pairs={{4,8},{5,9},{6,10},{7,11},{20,24},{21,25},{22,26},{23,27}} | collective-permute-start | bytes 786440 | tf_op jit(solution)/shard_map/ppermute | solution.py:530
  83.7 23.1 %collective-permute-start.19 = (bf16[1024,128]{1,0:T(8,128)(2,1)}, bf16[1024,128]{1,0:T(8,128)(2,1)S(1)}, u32[]{:S(2)}, u32[]{:S(2)}) collective-permute-start(bf16[1024,128]{1,0:T(8,128)(2,1)} %shard_map.119), channel_id=1, source_target_pairs={{4,8},{5,9},{6,10},{7,11},{20,24},{21,25},{22,26},{23,27}} | collective-permute-start | bytes 786440 | tf_op jit(solution)/shard_map/ppermute | solution.py:530
  94.9 15.2 %collective-permute-start.25 = (bf16[1024,128]{1,0:T(8,128)(2,1)}, bf16[1024,128]{1,0:T(8,128)(2,1)S(1)}, u32[]{:S(2)}, u32[]{:S(2)}) collective-permute-start(bf16[1024,128]{1,0:T(8,128)(2,1)} %shard_map.122), channel_id=1, source_target_pairs={{4,8},{5,9},{6,10},{7,11},{20,24},{21,25},{22,26},{23,27}} | collective-permute-start | bytes 786440 | tf_op jit(solution)/shard_map/ppermute | solution.py:530
  98.2 15.2 %collective-permute-start.5 = (bf16[1024,128]{1,0:T(8,128)(2,1)}, bf16[1024,128]{1,0:T(8,128)(2,1)S(1)}, u32[]{:S(2)}, u32[]{:S(2)}) collective-permute-start(bf16[1024,128]{1,0:T(8,128)(2,1)} %shard_map.113), channel_id=1, source_target_pairs={{8,12},{9,13},{10,14},{11,15},{24,28},{25,29},{26,30},{27,31}} | collective-permute-start | bytes 786440 | tf_op jit(solution)/shard_map/ppermute | solution.py:530
  101.5 11.8 %copy-start.10 = (bf16[1024,128]{1,0:T(8,128)(2,1)S(1)}, bf16[1024,128]{1,0:T(8,128)(2,1)}, u32[]{:S(2)}) copy-start(bf16[1024,128]{1,0:T(8,128)(2,1)} %copy-done.9) | copy-start | bytes 786436
  101.5 11.8 %copy-start.24 = (bf16[1024,128]{1,0:T(8,128)(2,1)S(1)}, bf16[1024,128]{1,0:T(8,128)(2,1)}, u32[]{:S(2)}) copy-start(bf16[1024,128]{1,0:T(8,128)(2,1)} %copy-done.23) | copy-start | bytes 786436
  101.5 24.6 %collective-permute-start.14 = (bf16[1024,128]{1,0:T(8,128)(2,1)}, bf16[1024,128]{1,0:T(8,128)(2,1)S(1)}, u32[]{:S(2)}, u32[]{:S(2)}) collective-permute-start(bf16[1024,128]{1,0:T(8,128)(2,1)} %shard_map.117), channel_id=1, source_target_pairs={{8,12},{9,13},{10,14},{11,15},{24,28},{25,29},{26,30},{27,31}} | collective-permute-start | bytes 786440 | tf_op jit(solution)/shard_map/ppermute | solution.py:530
  109.4 22.1 %collective-permute-start.20 = (bf16[1024,128]{1,0:T(8,128)(2,1)}, bf16[1024,128]{1,0:T(8,128)(2,1)S(1)}, u32[]{:S(2)}, u32[]{:S(2)}) collective-permute-start(bf16[1024,128]{1,0:T(8,128)(2,1)} %shard_map.120), channel_id=1, source_target_pairs={{8,12},{9,13},{10,14},{11,15},{24,28},{25,29},{26,30},{27,31}} | collective-permute-start | bytes 786440 | tf_op jit(solution)/shard_map/ppermute | solution.py:530
  112.7 19.7 %collective-permute-start.26 = (bf16[1024,128]{1,0:T(8,128)(2,1)}, bf16[1024,128]{1,0:T(8,128)(2,1)S(1)}, u32[]{:S(2)}, u32[]{:S(2)}) collective-permute-start(bf16[1024,128]{1,0:T(8,128)(2,1)} %shard_map.123), channel_id=1, source_target_pairs={{8,12},{9,13},{10,14},{11,15},{24,28},{25,29},{26,30},{27,31}} | collective-permute-start | bytes 786440 | tf_op jit(solution)/shard_map/ppermute | solution.py:530
  114.1 12.0 %copy-start.16 = (bf16[1024,128]{1,0:T(8,128)(2,1)S(1)}, bf16[1024,128]{1,0:T(8,128)(2,1)}, u32[]{:S(2)}) copy-start(bf16[1024,128]{1,0:T(8,128)(2,1)} %copy-done.15) | copy-start | bytes 786436
  114.1 12.0 %copy-start.22 = (bf16[1024,128]{1,0:T(8,128)(2,1)S(1)}, bf16[1024,128]{1,0:T(8,128)(2,1)}, u32[]{:S(2)}) copy-start(bf16[1024,128]{1,0:T(8,128)(2,1)} %copy-done.21) | copy-start | bytes 786436
  118.4 23.6 %collective-permute-start.9 = (bf16[256,1024]{1,0:T(8,128)(2,1)}, bf16[256,1024]{1,0:T(8,128)(2,1)S(1)}, u32[]{:S(2)}, u32[]{:S(2)}) collective-permute-start(bf16[256,1024]{1,0:T(8,128)(2,1)} %shard_map.115.refs_0_), channel_id=1, source_target_pairs={{0,1},{1,0},{2,3},{3,2},{4,5},{5,4},{6,7},{7,6},{8,9},{9,8},{10,11... | collective-permute-start | bytes 1572872 | tf_op jit(solution)/shard_map/ppermute | solution.py:554
  124.7 18.7 %collective-permute-start.10 = (bf16[256,1024]{1,0:T(8,128)(2,1)}, bf16[256,1024]{1,0:T(8,128)(2,1)S(1)}, u32[]{:S(2)}, u32[]{:S(2)}) collective-permute-start(bf16[256,1024]{1,0:T(8,128)(2,1)} %shard_map.115.refs_0_), channel_id=1, source_target_pairs={{0,16},{16,0},{1,17},{17,1},{2,18},{18,2},{3,19},{19,3},{4,20},{20... | collective-permute-start | bytes 1572872 | tf_op jit(solution)/shard_map/ppermute | solution.py:553
  126.8 4.7 %copy-start.14 = (bf16[1024,128]{1,0:T(8,128)(2,1)S(1)}, bf16[1024,128]{1,0:T(8,128)(2,1)}, u32[]{:S(2)}) copy-start(bf16[1024,128]{1,0:T(8,128)(2,1)} %copy-done.13) | copy-start | bytes 786436
  126.8 4.7 %copy-start.18 = (bf16[1024,128]{1,0:T(8,128)(2,1)S(1)}, bf16[1024,128]{1,0:T(8,128)(2,1)}, u32[]{:S(2)}) copy-start(bf16[1024,128]{1,0:T(8,128)(2,1)} %copy-done.17) | copy-start | bytes 786436
  126.8 5.5 %copy-start.12 = (bf16[1024,128]{1,0:T(8,128)(2,1)S(1)}, bf16[1024,128]{1,0:T(8,128)(2,1)}, u32[]{:S(2)}) copy-start(bf16[1024,128]{1,0:T(8,128)(2,1)} %copy-done.11) | copy-start | bytes 786436
  126.8 5.5 %copy-start.20 = (bf16[1024,128]{1,0:T(8,128)(2,1)S(1)}, bf16[1024,128]{1,0:T(8,128)(2,1)}, u32[]{:S(2)}) copy-start(bf16[1024,128]{1,0:T(8,128)(2,1)} %copy-done.19) | copy-start | bytes 786436
  131.1 12.4 %collective-permute-start.15 = (bf16[256,1024]{1,0:T(8,128)(2,1)}, bf16[256,1024]{1,0:T(8,128)(2,1)S(1)}, u32[]{:S(2)}, u32[]{:S(2)}) collective-permute-start(bf16[256,1024]{1,0:T(8,128)(2,1)} %shard_map.118.refs_4_), channel_id=1, source_target_pairs={{0,1},{1,0},{2,3},{3,2},{4,5},{5,4},{6,7},{7,6},{8,9},{9,8},{10,11... | collective-permute-start | bytes 1572872 | tf_op jit(solution)/shard_map/ppermute | solution.py:554
  131.4 18.2 %collective-permute-start.16 = (bf16[256,1024]{1,0:T(8,128)(2,1)}, bf16[256,1024]{1,0:T(8,128)(2,1)S(1)}, u32[]{:S(2)}, u32[]{:S(2)}) collective-permute-start(bf16[256,1024]{1,0:T(8,128)(2,1)} %shard_map.118.refs_4_), channel_id=1, source_target_pairs={{0,16},{16,0},{1,17},{17,1},{2,18},{18,2},{3,19},{19,3},{4,20},{20... | collective-permute-start | bytes 1572872 | tf_op jit(solution)/shard_map/ppermute | solution.py:553
  137.3 13.7 %collective-permute-start.21 = (bf16[256,1024]{1,0:T(8,128)(2,1)}, bf16[256,1024]{1,0:T(8,128)(2,1)S(1)}, u32[]{:S(2)}, u32[]{:S(2)}) collective-permute-start(bf16[256,1024]{1,0:T(8,128)(2,1)} %shard_map.121.refs_8_), channel_id=1, source_target_pairs={{0,1},{1,0},{2,3},{3,2},{4,5},{5,4},{6,7},{7,6},{8,9},{9,8},{10,11... | collective-permute-start | bytes 1572872 | tf_op jit(solution)/shard_map/ppermute | solution.py:554
  142.0 33.0 %copy-start.1 = (bf16[256,1024]{1,0:T(8,128)(2,1)}, bf16[256,1024]{1,0:T(8,128)(2,1)S(1)}, u32[]{:S(2)}) copy-start(bf16[256,1024]{1,0:T(8,128)(2,1)S(1)} %collective-permute-done.9.refs_1_) | copy-start | bytes 1572868
  142.0 19.0 %collective-permute-start.22 = (bf16[256,1024]{1,0:T(8,128)(2,1)S(1)}, bf16[256,1024]{1,0:T(8,128)(2,1)}, u32[]{:S(2)}, u32[]{:S(2)}) collective-permute-start(bf16[256,1024]{1,0:T(8,128)(2,1)S(1)} %copy-done), channel_id=1, source_target_pairs={{0,16},{16,0},{1,17},{17,1},{2,18},{18,2},{3,19},{19,3},{4,20},{20... | collective-permute-start | bytes 1572872 | tf_op jit(solution)/shard_map/ppermute | solution.py:553
  143.4 31.6 %copy-start.2 = (bf16[256,1024]{1,0:T(8,128)(2,1)}, bf16[256,1024]{1,0:T(8,128)(2,1)S(1)}, u32[]{:S(2)}) copy-start(bf16[256,1024]{1,0:T(8,128)(2,1)S(1)} %collective-permute-done.10.refs_2_) | copy-start | bytes 1572868
  143.4 28.8 %collective-permute-start.28 = (bf16[256,1024]{1,0:T(8,128)(2,1)}, bf16[256,1024]{1,0:T(8,128)(2,1)}, u32[]{:S(2)}, u32[]{:S(2)}) collective-permute-start(bf16[256,1024]{1,0:T(8,128)(2,1)} %shard_map.124.refs_12_), channel_id=1, source_target_pairs={{0,16},{16,0},{1,17},{17,1},{2,18},{18,2},{3,19},{19,3},{4,20},{20... | collective-permute-start | bytes 1572872 | tf_op jit(solution)/shard_map/ppermute | solution.py:553
  143.5 31.5 %copy-start.3 = (bf16[256,1024]{1,0:T(8,128)(2,1)}, bf16[256,1024]{1,0:T(8,128)(2,1)S(1)}, u32[]{:S(2)}) copy-start(bf16[256,1024]{1,0:T(8,128)(2,1)S(1)} %collective-permute-done.15.refs_5_) | copy-start | bytes 1572868
  143.5 29.6 %collective-permute-start.27 = (bf16[256,1024]{1,0:T(8,128)(2,1)}, bf16[256,1024]{1,0:T(8,128)(2,1)}, u32[]{:S(2)}, u32[]{:S(2)}) collective-permute-start(bf16[256,1024]{1,0:T(8,128)(2,1)} %shard_map.124.refs_12_), channel_id=1, source_target_pairs={{0,1},{1,0},{2,3},{3,2},{4,5},{5,4},{6,7},{7,6},{8,9},{9,8},{10,11... | collective-permute-start | bytes 1572872 | tf_op jit(solution)/shard_map/ppermute | solution.py:554
  149.7 25.3 %copy-start.4 = (bf16[256,1024]{1,0:T(8,128)(2,1)}, bf16[256,1024]{1,0:T(8,128)(2,1)S(1)}, u32[]{:S(2)}) copy-start(bf16[256,1024]{1,0:T(8,128)(2,1)S(1)} %collective-permute-done.16.refs_6_) | copy-start | bytes 1572868
  149.7 23.4 %collective-permute-start.11 = (bf16[256,1024]{1,0:T(8,128)(2,1)S(1)}, bf16[256,1024]{1,0:T(8,128)(2,1)}, u32[]{:S(2)}, u32[]{:S(2)}) collective-permute-start(bf16[256,1024]{1,0:T(8,128)(2,1)S(1)} %collective-permute-done.10.refs_2_), channel_id=1, source_target_pairs={{0,1},{1,0},{2,3},{3,2},{4,5},{5,4},{6,7},{7,6},{8,9},{9,8},{10,11... | collective-permute-start | bytes 1572872 | tf_op jit(solution)/shard_map/ppermute | solution.py:555
  151.0 24.0 %copy-start.5 = (bf16[256,1024]{1,0:T(8,128)(2,1)}, bf16[256,1024]{1,0:T(8,128)(2,1)S(1)}, u32[]{:S(2)}) copy-start(bf16[256,1024]{1,0:T(8,128)(2,1)S(1)} %collective-permute-done.21.refs_9_) | copy-start | bytes 1572868
  151.0 22.1 %collective-permute-start.17 = (bf16[256,1024]{1,0:T(8,128)(2,1)S(1)}, bf16[256,1024]{1,0:T(8,128)(2,1)}, u32[]{:S(2)}, u32[]{:S(2)}) collective-permute-start(bf16[256,1024]{1,0:T(8,128)(2,1)S(1)} %collective-permute-done.16.refs_6_), channel_id=1, source_target_pairs={{0,1},{1,0},{2,3},{3,2},{4,5},{5,4},{6,7},{7,6},{8,9},{9,8},{10,11... | collective-permute-start | bytes 1572872 | tf_op jit(solution)/shard_map/ppermute | solution.py:555
  161.0 12.1 %collective-permute-start.23 = (bf16[256,1024]{1,0:T(8,128)(2,1)}, bf16[256,1024]{1,0:T(8,128)(2,1)S(1)}, u32[]{:S(2)}, u32[]{:S(2)}) collective-permute-start(bf16[256,1024]{1,0:T(8,128)(2,1)} %collective-permute-done.22.refs_10_), channel_id=1, source_target_pairs={{0,1},{1,0},{2,3},{3,2},{4,5},{5,4},{6,7},{7,6},{8,9},{9,8},{10,11... | collective-permute-start | bytes 1572872 | tf_op jit(solution)/shard_map/ppermute | solution.py:555
  172.2 2.7 collective-permute-start.29
  180.9 82.8 %collective-permute-start.30 = (bf16[1024,256]{1,0:T(8,128)(2,1)}, bf16[1024,256]{1,0:T(8,128)(2,1)S(1)}, u32[]{:S(2)}, u32[]{:S(2)}) collective-permute-start(bf16[1024,256]{1,0:T(8,128)(2,1)} %shard_map.126), channel_id=1, source_target_pairs={{0,2},{2,0},{1,3},{3,1},{4,6},{6,4},{5,7},{7,5},{8,10},{10,8},{9,1... | collective-permute-start | bytes 1572872 | tf_op jit(solution)/shard_map/ppermute | solution.py:413
  251.8 13.4 %collective-permute-start.33 = (bf16[1024,256]{1,0:T(8,128)(2,1)}, bf16[1024,256]{1,0:T(8,128)(2,1)S(1)}, u32[]{:S(2)}, u32[]{:S(2)}) collective-permute-start(bf16[1024,256]{1,0:T(8,128)(2,1)} %shard_map.128), channel_id=1, source_target_pairs={{0,2},{2,0},{1,3},{3,1},{4,6},{6,4},{5,7},{7,5},{8,10},{10,8},{9,1... | collective-permute-start | bytes 1572872 | tf_op jit(solution)/shard_map/ppermute | solution.py:413
  257.9 5.8 %copy-start.8 = (bf16[1024,256]{1,0:T(8,128)(2,1)S(1)}, bf16[1024,256]{1,0:T(8,128)(2,1)}, u32[]{:S(2)}) copy-start(bf16[1024,256]{1,0:T(8,128)(2,1)} %shard_map.125) | copy-start | bytes 1572868
  263.9 6.9 %collective-permute-start.31 = (bf16[2,256,256]{2,1,0:T(8,128)(2,1)S(1)}, bf16[2,256,256]{2,1,0:T(8,128)(2,1)S(1)}, u32[]{:S(2)}, u32[]{:S(2)}) collective-permute-start(bf16[2,256,256]{2,1,0:T(8,128)(2,1)S(1)} %bitcast.118), channel_id=1, source_target_pairs={{0,16},{16,0},{1,17},{17,1},{2,18},{18,2},{3,19},{19,3},{4,20},{20... | collective-permute-start | bytes 786440 | tf_op jit(solution)/shard_map/ppermute | solution.py:416
  266.3 10.1 %collective-permute-start.34 = (bf16[2,256,256]{2,1,0:T(8,128)(2,1)S(1)}, bf16[2,256,256]{2,1,0:T(8,128)(2,1)S(1)}, u32[]{:S(2)}, u32[]{:S(2)}) collective-permute-start(bf16[2,256,256]{2,1,0:T(8,128)(2,1)S(1)} %bitcast.117), channel_id=1, source_target_pairs={{0,16},{16,0},{1,17},{17,1},{2,18},{18,2},{3,19},{19,3},{4,20},{20... | collective-permute-start | bytes 786440 | tf_op jit(solution)/shard_map/ppermute | solution.py:416
  270.9 7.5 %collective-permute-start.32 = (bf16[2,256,256]{2,1,0:T(8,128)(2,1)S(1)}, bf16[2,256,256]{2,1,0:T(8,128)(2,1)S(1)}, u32[]{:S(2)}, u32[]{:S(2)}) collective-permute-start(bf16[2,256,256]{2,1,0:T(8,128)(2,1)S(1)} %pad_maximum_fusion), channel_id=1, source_target_pairs={{0,1},{1,0},{2,3},{3,2},{4,5},{5,4},{6,7},{7,6},{8,9},{9,8},{10,11... | collective-permute-start | bytes 786440 | tf_op jit(solution)/shard_map/ppermute | solution.py:417
  276.5 3.1 %collective-permute-start.35 = (bf16[2,256,256]{2,1,0:T(8,128)(2,1)S(1)}, bf16[2,256,256]{2,1,0:T(8,128)(2,1)S(1)}, u32[]{:S(2)}, u32[]{:S(2)}) collective-permute-start(bf16[2,256,256]{2,1,0:T(8,128)(2,1)S(1)} %pad_maximum_fusion.1), channel_id=1, source_target_pairs={{0,1},{1,0},{2,3},{3,2},{4,5},{5,4},{6,7},{7,6},{8,9},{9,8},{10,11... | collective-permute-start | bytes 786440 | tf_op jit(solution)/shard_map/ppermute | solution.py:417
  (12 other events, 14.0 us)
Sparse Core Ops, SparseCore 0:
  62.6 89.8 all-gather.4
  154.0 92.1 all-gather.6

commit v4 on v3

v4 whole, which is shorter than its diff:
```python
import functools

import jax
import jax.numpy as jnp
from jax import lax
from jax.experimental import pallas as pl
from jax.experimental.pallas import tpu as pltpu
from jax.sharding import PartitionSpec as P

HEAD_DIM = 64
STATE = 128
STRETCH = 128
PIECES = 2
BF = jnp.bfloat16
F32 = jnp.float32
VMEM_LIMIT = 56 * 1024 * 1024
SMALL = pl.CostEstimate(flops=1000, bytes_accessed=1000, transcendentals=0)


def widen(per_head, width):
    heads = per_head.shape[1]
    high = per_head.astype(BF)
    low = (per_head - high.astype(F32)).astype(BF)
    both = jnp.concatenate([high, low], axis=1)
    place = lax.broadcasted_iota(jnp.int32, (2 * heads, width), 0)
    lane = lax.broadcasted_iota(jnp.int32, (2 * heads, width), 1)
    place = jnp.where(place >= heads, place - heads, place)
    spread = jnp.where(place == lane // (width // heads), 1.0, 0.0).astype(BF)
    return jnp.dot(both, spread, preferred_element_type=F32)


def states_kernel(x_ref, b_ref, end_ref, out_ref):
    width = x_ref.shape[1]
    for c in range(out_ref.shape[0]):
        rows = pl.ds(c * STRETCH, STRETCH)
        scaled = (x_ref[rows, :].astype(F32) * widen(end_ref[0, rows, :], width)).astype(BF)
        out_ref[c] = lax.dot_general(
            scaled, b_ref[rows, :], (((0,), (0,)), ((), ())), preferred_element_type=F32
        )


def block_states_of(x, b, to_end, blocks):
    tokens, width = x.shape
    groups_dev = b.shape[1] // STATE
    per = width // groups_dev
    return pl.pallas_call(
        states_kernel,
        grid=(groups_dev,),
        in_specs=[
            pl.BlockSpec((tokens, per), lambda g: (0, g)),
            pl.BlockSpec((tokens, STATE), lambda g: (0, g)),
            pl.BlockSpec((1, tokens, to_end.shape[2]), lambda g: (g, 0, 0)),
        ],
        out_specs=pl.BlockSpec((blocks, per, STATE), lambda g: (0, g, 0)),
        out_shape=jax.ShapeDtypeStruct((blocks, width, STATE), F32),
        compiler_params=pltpu.CompilerParams(vmem_limit_bytes=VMEM_LIMIT),
        cost_estimate=pl.CostEstimate(
            flops=2 * tokens * width * STATE, bytes_accessed=16 << 20, transcendentals=0
        ),
    )(x, b, to_end)


def row_starts(lengths_ref, slots_ref):
    convs = lengths_ref.shape[1]
    begins = [jnp.int32(0)]
    for j in range(convs - 1):
        begins.append(begins[-1] + lengths_ref[0, j])

    def starts(block):
        found = begins[0] == block
        for begin in begins[1:]:
            found = jnp.logical_or(found, begin == block)
        return found

    def slot(block):
        entry = slots_ref[0, 0]
        for j in range(1, convs):
            entry = jnp.where(begins[j] <= block, slots_ref[0, j], entry)
        return entry

    return starts, slot


def along(seq, offset, size):
    place = seq + offset
    return jnp.where(place >= size, place - size, place)


def second_kernel(size, seq_ref, lengths_ref, slots_ref, cached, *refs):
    pieces, code_ref, sems = refs[:size], refs[size], refs[-1]
    starts, slot = row_starts(lengths_ref, slots_ref)
    seq = seq_ref[0]
    copies = []
    for offset in range(size):
        entry = slot(2 * along(seq, offset, size) + 1)
        copies.append(pltpu.make_async_copy(cached.at[0, entry], pieces[offset], sems.at[offset]))
        copies[-1].start()
    code_ref[0] = jnp.where(starts(2 * seq + 1), 1, 0).astype(jnp.int32)
    for copy in copies:
        copy.wait()


def second_states(seq, lengths, slots, cached, size):
    smem = pl.BlockSpec(memory_space=pltpu.SMEM)
    whole = pl.BlockSpec(memory_space=pltpu.VMEM)
    piece = jax.ShapeDtypeStruct(cached.shape[2:], cached.dtype)
    *pieces, code = pl.pallas_call(
        functools.partial(second_kernel, size),
        in_specs=[smem, smem, smem, pl.BlockSpec(memory_space=pl.ANY)],
        out_specs=[whole] * size + [smem],
        out_shape=[piece] * size + [jax.ShapeDtypeStruct((1,), jnp.int32)],
        scratch_shapes=[pltpu.SemaphoreType.DMA((size,))],
        cost_estimate=SMALL,
    )(seq.reshape(1), lengths, slots, cached)
    return pieces, code


def split_kernel(size, seq_ref, code_ref, total_ref, gain_ref, own_ref, *refs):
    pieces, added = refs[:size], refs[size]
    group = pl.program_id(0)
    per = own_ref.shape[1]
    heads = per // HEAD_DIM
    part = HEAD_DIM // size
    for h in range(heads):
        rows = pl.ds(h * HEAD_DIM, HEAD_DIM)
        gain = jnp.where(code_ref[0] == 1, 0.0, total_ref[1, group * heads + h])
        added[rows, :] = (own_ref[0, rows, :] * gain + own_ref[1, rows, :]).astype(BF)
    for d in range(size):
        start = along(seq_ref[0], d, size) * part
        for h in range(heads):
            rows = pl.ds(pl.multiple_of(h * HEAD_DIM + start, part), part)
            pieces[d][group * heads + h] = added[rows, :]

    @pl.when(group == 0)
    def _():
        for piece in pieces:
            piece[piece.shape[0] - 1] = gain_ref[...]


def split_states(seq, code, totals, gains, own, per, size):
    width = own.shape[1]
    heads_dev = width // HEAD_DIM
    smem = pl.BlockSpec(memory_space=pltpu.SMEM)
    whole = pl.BlockSpec(memory_space=pltpu.VMEM)
    shape = (heads_dev + 1, HEAD_DIM // size, STATE)
    return pl.pallas_call(
        functools.partial(split_kernel, size),
        grid=(width // per,),
        in_specs=[smem, smem, smem, whole, pl.BlockSpec((2, per, STATE), lambda g: (0, g, 0))],
        out_specs=[pl.BlockSpec(shape, lambda g: (0, 0, 0))] * size,
        out_shape=[jax.ShapeDtypeStruct(shape, BF)] * size,
        scratch_shapes=[pltpu.VMEM((per, STATE), BF)],
        compiler_params=pltpu.CompilerParams(vmem_limit_bytes=VMEM_LIMIT),
        cost_estimate=SMALL,
    )(seq.reshape(1), code, totals, gains, own)


def enter_kernel(size, seq_ref, lengths_ref, slots_ref, cached_ref, *refs):
    pieces, outs, added, entering = refs[:size], refs[size : 2 * size], refs[-2], refs[-1]
    starts, slot = row_starts(lengths_ref, slots_ref)
    seq = seq_ref[0]
    heads_dev = cached_ref.shape[2]
    for d in range(size):
        source = seq - d
        added[jnp.where(source < 0, source + size, source)] = pieces[d][...]
    for t in range(size):
        if t:
            second = starts(2 * t - 1)
            before = slot(2 * t - 1)
            first = starts(2 * t)

            @pl.when(first)
            def _(t=t):
                entering[t] = cached_ref[0, slot(2 * t)]

            @pl.when(jnp.logical_not(first))
            def _(t=t, second=second, before=before):
                high = added[t - 1, heads_dev].astype(F32)
                gains = high[0:1, :] + high[1:2, :]
                for h in range(heads_dev):
                    both = gains[:, h : h + 1]
                    last = gains[:, heads_dev + h : heads_dev + h + 1]
                    old = jnp.where(
                        second,
                        cached_ref[0, before, h].astype(F32) * last,
                        entering[t - 1, h].astype(F32) * both,
                    )
                    entering[t, h] = (old + added[t - 1, h].astype(F32)).astype(BF)

        else:
            entering[0] = cached_ref[0, slot(0)]
    for d in range(size):
        outs[d][...] = entering[along(seq, d, size)]


def entering_states(seq, lengths, slots, cached, pieces):
    size = len(pieces)
    shape = cached.shape[2:]
    smem = pl.BlockSpec(memory_space=pltpu.SMEM)
    whole = pl.BlockSpec(memory_space=pltpu.VMEM)
    return pl.pallas_call(
        functools.partial(enter_kernel, size),
        in_specs=[smem, smem, smem] + [whole] * (size + 1),
        out_specs=[whole] * size,
        out_shape=[jax.ShapeDtypeStruct(shape, BF)] * size,
        scratch_shapes=[
            pltpu.VMEM((size,) + pieces[0].shape, BF),
            pltpu.VMEM((size,) + shape, BF),
        ],
        compiler_params=pltpu.CompilerParams(vmem_limit_bytes=VMEM_LIMIT),
        cost_estimate=SMALL,
    )(seq.reshape(1), lengths, slots, cached, *pieces)


def plain_entering(seq, lengths, slots, cached, totals, own, size):
    heads_dev, part = cached.shape[2:4]
    begins = jnp.cumsum(lengths[0]) - lengths[0]
    blocks = jnp.arange(2 * size, dtype=jnp.int32)
    starts = jnp.any(begins[None, :] == blocks[:, None], axis=1)
    owners = jnp.sum((begins[None, :] <= blocks[:, None]).astype(jnp.int32), axis=1) - 1
    entries = jnp.take(cached[0], jnp.take(slots[0], owners), axis=0)
    second = lax.all_to_all(entries[1::2], "seq", 0, 0, tiled=True)
    code = lax.dynamic_index_in_dim(starts, 2 * seq + 1, 0, True).astype(jnp.int32)
    states = own.reshape(2, heads_dev, HEAD_DIM, STATE)
    keep = jnp.where(code[0] == 1, 0.0, totals[1])[:, None, None]
    added = (keep * states[0] + states[1]).astype(BF)
    added = jnp.transpose(added.reshape(heads_dev, size, part, STATE), (1, 0, 2, 3))
    added = lax.all_to_all(added, "seq", 0, 0, tiled=True)
    gains = lax.all_gather(totals, "seq")
    entering = [entries[0]]
    for t in range(1, size):
        last = gains[t - 1, 1][:, None, None]
        both = (gains[t - 1, 0] * gains[t - 1, 1])[:, None, None]
        old = jnp.where(
            starts[2 * t - 1],
            entries[2 * t - 1].astype(F32) * last,
            entering[-1].astype(F32) * both,
        )
        carry = (old + added[t - 1].astype(F32)).astype(BF)
        entering.append(jnp.where(starts[2 * t], entries[2 * t], carry))
    entering = lax.all_to_all(jnp.stack(entering), "seq", 0, 0, tiled=True)
    whole = [
        jnp.transpose(v, (1, 0, 2, 3)).reshape(heads_dev, HEAD_DIM, STATE)
        for v in (entering, second)
    ]
    return whole[0], whole[1], code


def mix_kernel(
    place,
    size,
    seq_ref,
    code_ref,
    total_ref,
    x_ref,
    z_ref,
    b_ref,
    c_ref,
    run_ref,
    run_t_ref,
    step_t_ref,
    gain_ref,
    own_ref,
    *refs,
):
    entered, second = refs[:size], refs[size : 2 * size]
    out_ref, state, mixed = refs[2 * size :]
    block = pl.program_id(1)
    width = x_ref.shape[1]
    heads = run_ref.shape[2]
    head = (place + pl.program_id(0)) * heads

    def put(pieces):
        part = pieces[0].shape[1]
        for d in range(size):
            source = seq_ref[0] - d
            source = jnp.where(source < 0, source + size, source)
            start = pl.multiple_of(source * part, part)
            for h in range(heads):
                state[pl.ds(h * HEAD_DIM + start, part), :] = pieces[d][h].astype(F32)

    @pl.when(block == 0)
    def _():
        put(entered)

    @pl.when(block > 0)
    def _():
        @pl.when(code_ref[0] == 1)
        def _():
            put(second)

        @pl.when(code_ref[0] == 0)
        def _():
            for h in range(heads):
                rows = pl.ds(h * HEAD_DIM, HEAD_DIM)
                state[rows, :] = total_ref[0, head + h] * state[rows, :] + own_ref[0, rows, :]

    read = c_ref[...]
    scores = lax.dot_general(
        read, b_ref[...], (((1,), (1,)), ((), ())), preferred_element_type=F32
    )
    running = run_ref[0]
    inflow = lax.dot_general(
        read, state[...].astype(BF), (((1,), (1,)), ((), ())), preferred_element_type=F32
    )
    mixed[...] = inflow * widen(jnp.exp(running), width)
    row = lax.broadcasted_iota(jnp.int32, (STRETCH, STRETCH), 0)
    col = lax.broadcasted_iota(jnp.int32, (STRETCH, STRETCH), 1)
    lower = row >= col
    lane = lax.broadcasted_iota(jnp.int32, (STRETCH, 2 * HEAD_DIM), 1)
    for pair in range(heads // 2):
        mixes = []
        for h in (2 * pair, 2 * pair + 1):
            spread = running[:, h : h + 1] - run_t_ref[0, h : h + 1, :]
            fading = jnp.exp(jnp.where(lower, spread, -1e30))
            mixes.append((scores * fading * step_t_ref[0, h : h + 1, :]).astype(BF))
        lanes = pl.ds(pair * 2 * HEAD_DIM, 2 * HEAD_DIM)
        two = x_ref[:, lanes]
        none = jnp.zeros_like(two)
        stacked = jnp.concatenate(
            [jnp.where(lane < HEAD_DIM, two, none), jnp.where(lane < HEAD_DIM, none, two)], axis=0
        )
        mixed[:, lanes] += jnp.dot(
            jnp.concatenate(mixes, axis=1), stacked, preferred_element_type=F32
        )
    gate = z_ref[...].astype(F32)
    gated = mixed[...] * (gate / (1.0 + jnp.exp(-gate)))
    scale = lax.rsqrt(jnp.mean(gated * gated, axis=1, keepdims=True) + 1e-05)
    out_ref[...] = (gated * scale * gain_ref[...]).astype(BF)


def mix_groups(place, seq, code, totals, x, z, b, c, run, run_t, step_t, gain, own, entered, second):
    tokens, width = x.shape
    groups_dev = b.shape[1] // STATE
    per = width // groups_dev
    heads = run.shape[2]
    size = len(entered)
    smem = pl.BlockSpec(memory_space=pltpu.SMEM)
    piece = pl.BlockSpec((heads,) + entered[0].shape[1:], lambda g, i: (place + g, 0, 0))
    wide = pl.BlockSpec((STRETCH, per), lambda g, i: (i, place + g))
    basis = pl.BlockSpec((STRETCH, STATE), lambda g, i: (i, place + g))
    rows = pl.BlockSpec((1, heads, STRETCH), lambda g, i: (place + g, 0, i))
    return pl.pallas_call(
        functools.partial(mix_kernel, place, size),
        grid=(1, tokens // STRETCH),
        in_specs=[
            smem,
            smem,
            smem,
            wide,
            wide,
            basis,
            basis,
            pl.BlockSpec((1, STRETCH, heads), lambda g, i: (place + g, i, 0)),
            rows,
            rows,
            pl.BlockSpec((1, per), lambda g, i: (0, place + g)),
            pl.BlockSpec((1, per, STATE), lambda g, i: (0, place + g, 0)),
        ]
        + [piece] * (2 * size),
        out_specs=pl.BlockSpec((STRETCH, per), lambda g, i: (i, g)),
        out_shape=jax.ShapeDtypeStruct((tokens, per), BF),
        scratch_shapes=[pltpu.VMEM((per, STATE), F32), pltpu.VMEM((STRETCH, per), F32)],
        compiler_params=pltpu.CompilerParams(vmem_limit_bytes=VMEM_LIMIT),
        cost_estimate=SMALL,
    )(seq.reshape(1), code, totals, x, z, b, c, run, run_t, step_t, gain, own, *entered, *second)


def project_kernel(first_ref, *refs):
    weights, near_ref, far_ref, rows_all, weight, total, sems = refs[-7:]
    lhs = refs[:-7]
    tokens, depth = lhs[0].shape
    cols = weights.shape[2]
    parts = len(lhs) // 4
    for part in range(parts):
        span = pl.ds(part * depth, depth)
        for r in range(4):
            pltpu.make_async_copy(
                lhs[4 * part + r],
                rows_all.at[part, pl.ds(r * tokens, tokens)],
                sems.at[0, part],
            ).start()
        for n in range(2):
            pltpu.make_async_copy(
                weights.at[first_ref[0] + n, span],
                weight.at[part, :, pl.ds(n * cols, cols)],
                sems.at[1, part],
            ).start()
    for part in range(parts):
        pltpu.make_async_copy(rows_all.at[part], rows_all.at[part], sems.at[0, part]).wait()
        pltpu.make_async_copy(weight.at[part], weight.at[part], sems.at[1, part]).wait()
        for r in range(4):
            span = pl.ds(r * tokens, tokens)
            product = jnp.dot(rows_all[part, span, :], weight[part], preferred_element_type=F32)
            if part == 0:
                total[span, :] = product
            elif part < parts - 1:
                total[span, :] += product
            else:
                out_ref = far_ref if r >= 2 else near_ref
                out_ref[pl.ds(r % 2 * tokens, tokens), :] = (total[span, :] + product).astype(BF)


def project(first, lhs, weights):
    parts = len(lhs) // 4
    tokens = 4 * lhs[0].shape[0]
    depth, cols = weights.shape[1:]
    hbm = pl.BlockSpec(memory_space=pl.ANY)
    return pl.pallas_call(
        project_kernel,
        in_specs=[pl.BlockSpec(memory_space=pltpu.SMEM)] + [hbm] * (len(lhs) + 1),
        out_specs=[pl.BlockSpec(memory_space=pltpu.VMEM)] * 2,
        out_shape=[jax.ShapeDtypeStruct((tokens // 2, 2 * cols), BF)] * 2,
        scratch_shapes=[
            pltpu.VMEM((parts, tokens, depth // parts), BF),
            pltpu.VMEM((parts, depth // parts, 2 * cols), BF),
            pltpu.VMEM((tokens, 2 * cols), F32),
            pltpu.SemaphoreType.DMA((2, parts)),
        ],
        compiler_params=pltpu.CompilerParams(vmem_limit_bytes=VMEM_LIMIT),
        cost_estimate=SMALL,
    )(first.reshape(1), *lhs, weights)


SWAP = [(0, 1), (1, 0)]


def after(value, *others):
    return lax.optimization_barrier((value, *others))[0]


def to_rows(own, others, tokens):
    far, near = [
        (own[k].astype(F32) + lax.ppermute(others[k], "head", SWAP).astype(F32)).astype(BF)
        for k in (1, 0)
    ]
    from_y = lax.ppermute(far, "groups", SWAP).reshape(2, tokens, -1)
    near = near.reshape(2, tokens, -1)
    from_core = lax.ppermute(jnp.stack([near[1], from_y[1]]), "batch", SWAP)
    return near[0], from_core[0], from_y[0], from_core[1]


def in_order(y, core, parts):
    a, b, c, d = parts
    p = [jnp.where(core == 0, a, b), jnp.where(core == 0, b, a)]
    q = [jnp.where(core == 0, c, d), jnp.where(core == 0, d, c)]
    return [jnp.where(y == 0, v, w) for v, w in zip(p + q, q + p)]


def plain_projection(normed, out_weight):
    tokens = normed.shape[0]
    pairs = lax.axis_size("batch")
    batch_index = lax.axis_index("batch")
    part_cols = out_weight.shape[1] // pairs
    own_part = lax.dynamic_slice_in_dim(out_weight, batch_index * part_cols, part_cols, 1)
    both_rows = lax.all_gather(normed, "batch", axis=0, tiled=True)
    partial_value = jnp.dot(
        both_rows,
        lax.all_gather(own_part, "seq", axis=1, tiled=True),
        preferred_element_type=F32,
    )
    summed = lax.psum_scatter(partial_value.astype(BF), "head", scatter_dimension=1, tiled=True)
    spans = summed.shape[1] // part_cols
    sections = summed.reshape(pairs, tokens, spans, 1, part_cols)
    regrouped = lax.all_to_all(sections, "batch", split_axis=0, concat_axis=3, tiled=True)
    return regrouped.reshape(1, tokens, spans * pairs * part_cols)


def exchange_states(payload, seq, size):
    return [
        lax.ppermute(piece, "seq", [(i, (i + offset) % size) for i in range(size)])
        if offset
        else piece
        for offset, piece in enumerate(payload)
    ]


def body(
    x_values,
    z_gate,
    write_basis,
    read_basis,
    step_size,
    log_decay,
    cached_states,
    session_slots,
    conv_lengths,
    norm_gain,
    out_weight,
):
    tokens = x_values.shape[1]
    width = x_values.shape[2]
    heads_dev = step_size.shape[2]
    groups_dev = write_basis.shape[2] // STATE
    per_group = heads_dev // groups_dev
    per = width // groups_dev
    blocks = tokens // STRETCH
    size = lax.axis_size("seq")
    seq = lax.axis_index("seq")
    assert blocks == 2

    shared = lax.axis_size("groups") * lax.axis_size("batch")
    fast = (
        size == 4
        and lax.axis_size("head") == 2
        and shared == 4
        and out_weight.shape == (4096, 1024)
        and groups_dev == 4
    )
    kernels = HEAD_DIM // size % 16 == 0 and 2 * heads_dev <= STATE
    if kernels:
        second, code = second_states(seq, conv_lengths, session_slots, cached_states, size)
        second = exchange_states(second, seq, size)
    head = lax.axis_index("head")
    y = lax.axis_index("groups")
    core = lax.axis_index("batch")

    logs = log_decay[0].reshape(blocks, STRETCH, heads_dev)
    running = jnp.cumsum(logs, axis=1)
    totals = jnp.exp(running[:, -1, :])
    to_end = (jnp.exp(running[:, -1:, :] - running)).reshape(tokens, heads_dev) * step_size[0]
    run = running.reshape(tokens, groups_dev, per_group)
    by_group = jnp.transpose(run, (1, 0, 2))
    by_row = jnp.transpose(run, (1, 2, 0))
    step_t = jnp.transpose(step_size[0].reshape(tokens, groups_dev, per_group), (1, 2, 0))
    end_g = jnp.transpose(to_end.reshape(tokens, groups_dev, per_group), (1, 0, 2))

    x, z, b, c = x_values[0], z_gate[0], write_basis[0], read_basis[0]
    own = block_states_of(x, b, end_g, blocks)
    if fast:
        quarter = out_weight.shape[1] // 4
        piece = quarter // PIECES
        w_own = [
            lax.dynamic_slice_in_dim(
                out_weight, (2 * y + core) * quarter + k * piece, piece, 1
            )
            for k in range(PIECES)
        ]

    if kernels:
        both = jnp.concatenate([totals[0] * totals[1], totals[1]])
        both = jnp.pad(both, (0, STATE - 2 * heads_dev))
        high = both.astype(BF)
        low = (both - high.astype(F32)).astype(BF)
        gains = jnp.pad(jnp.stack([high, low]), ((0, HEAD_DIM // size - 2), (0, 0)))
        added = split_states(seq, code, totals, gains, own, per, size)
        added = exchange_states([after(v, *second) for v in added], seq, size)
        entered = entering_states(seq, conv_lengths, session_slots, cached_states, added)
        entered = exchange_states(entered, seq, size)
    else:
        one, two, code = plain_entering(
            seq, conv_lengths, session_slots, cached_states, totals, own, size
        )
        entered, second = [one], [two]
    where = seq if kernels else jnp.zeros_like(seq)
    if fast:
        weights = [lax.all_gather(part, "seq", axis=0) for part in w_own]
    gain = norm_gain.reshape(1, width)
    normed = [
        mix_groups(
            g, where, code, totals, x, z, b, c, by_group, by_row, step_t, gain, own, entered, second
        )
        for g in range(groups_dev)
    ]
    if not fast:
        return plain_projection(jnp.concatenate(normed, axis=1), out_weight)

    lhs = []
    for part in normed:
        across = lax.ppermute(part, "groups", SWAP)
        other = lax.ppermute(part, "batch", SWAP)
        other_across = lax.ppermute(across, "batch", SWAP)
        lhs += [part, other, across, other_across]
    sides = []
    done = []
    for part in weights:
        others = project(2 - 2 * head, lhs, after(part, *done))
        mine = project(2 * head, lhs, after(part, *others) if done else part)
        done = mine
        sides.append(in_order(y, core, to_rows(mine, others, tokens)))
    pieces = [
        sides[k][q][:, block * piece : (block + 1) * piece]
        for block in range(2)
        for q in range(4)
        for k in range(PIECES)
    ]
    return jnp.concatenate(pieces, axis=1)[None]


def solution(mesh):
    placed = (
        P(("groups", "batch"), "seq", "head"),
        P(("groups", "batch"), "seq", "head"),
        P(("groups", "batch"), "seq", "head"),
        P(("groups", "batch"), "seq", "head"),
        P(("groups", "batch"), "seq", "head"),
        P(("groups", "batch"), "seq", "head"),
        P(("groups", "batch"), None, "head", "seq", None),
        P(("groups", "batch"), None),
        P(("groups", "batch"), None),
        P("head"),
        P("head", "seq"),
    )
    return jax.shard_map(
        body,
        mesh=mesh,
        in_specs=placed,
        out_specs=P(("groups", "batch"), "seq", "head"),
        check_vma=False,
    )
```

time: 291 us -> 263 us (0.904)
  Pallas kernels: 73.4 us -> 57.4 us
  waiting for transfers between devices: 119 us -> 105 us
  starting transfers between devices: 61.3 us -> 71.6 us
  local copies, waits for them, and re-layouts: 14.2 us -> 8.45 us
    all_gather x2, waiting for transfers between devices: 64.9 us -> 7.74 us  [body(): weights = [lax.all_gather(part, 'seq', axis=0) for part in w_own]]
    ppermute x6 -> x9, waiting for transfers between devices: 4.32 us -> 58.7 us  [exchange_states(): lax.ppermute(piece, 'seq', [(i, (i + offset) % size) for i in range(size)])]
    ppermute x6 -> x9, starting transfers between devices: 7.99 us -> 57.3 us  [exchange_states(): lax.ppermute(piece, 'seq', [(i, (i + offset) % size) for i in range(size)])]
    ppermute x18 -> x8, starting transfers between devices: 38.8 us -> 5.7 us  [the longest x4 2.13 us: to_rows(): lax.ppermute(others[k], 'head', SWAP).astype(F32)]
    pallas_call x15 -> x7, Pallas kernels: 44.6 us -> 29.5 us  [the longest x4 18.7 us: mix_groups(): pl.pallas_call(functools.partial(mix_kernel, place, size), grid=(1, token...]
    ppermute x18 -> x8, waiting for transfers between devices: 22.1 us -> 9.91 us  [the longest x4 8.69 us: to_rows(): lax.ppermute(others[k], 'head', SWAP).astype(F32)]
    ppermute x4, starting transfers between devices: 7.86 us -> 2.01 us  [body(): other = lax.ppermute(part, 'batch', SWAP)]
    unnamed x91 -> x63, local copies, waits for them, and re-layouts: 7.09 us -> 2.8 us
  transfers between devices with their start and end apart: 38 -> 31, of which waited for: 12 -> 14; matrix products, arithmetic and copies ran while one was open for 4% -> 2% of each run, Pallas kernels for 24% -> 22%
where the time goes in v4:
time: 263 us; the launch traced here: 260 us
  waiting for transfers between devices  105 us (40%)
  starting transfers between devices  71.6 us (27%)
  Pallas kernels  57.4 us (22%)
  between operations  13.9 us (5%)
  local copies, waits for them, and re-layouts  8.45 us (3%)
  other arithmetic  3.27 us (1%)
    ppermute x9, waiting for transfers between devices, exchange_states(): lax.ppermute(piece, 'seq', [(i, (i + offset) % size) for i in range(size)])  58.7 us
    ppermute x9, starting transfers between devices, exchange_states(): lax.ppermute(piece, 'seq', [(i, (i + offset) % size) for i in range(size)])  57.3 us
    ppermute x4, waiting for transfers between devices, body(): across = lax.ppermute(part, 'groups', SWAP)  26.3 us
    pallas_call x4, Pallas kernels, project(): pl.pallas_call(project_kernel, in_specs=[pl.BlockSpec(memory_space=pltpu....  21.7 us
    pallas_call x4, Pallas kernels, mix_groups(): pl.pallas_call(functools.partial(mix_kernel, place, size), grid=(1, token...  18.7 us
    ppermute x4, waiting for transfers between devices, to_rows(): lax.ppermute(others[k], 'head', SWAP).astype(F32)  8.69 us
    all_gather x2, waiting for transfers between devices, body(): weights = [lax.all_gather(part, 'seq', axis=0) for part in w_own]  7.74 us
    pallas_call x1, Pallas kernels, block_states_of(): pl.pallas_call(states_kernel, grid=(groups_dev,), in_specs=[pl.BlockSpec(...  6.17 us
  transfers between devices with their start and end apart: 31, of which 14 were waited for; matrix products, arithmetic and copies ran while one was open for 2% of the time, Pallas kernels for 22%

profile of v4, /device:TPU:3, one launch (start us, length us, event | category | flops | bytes accessed | tf_op | source)
XLA Modules:
  0.0 259.9 jit_solution(10366845829122085797)
XLA Ops:
  6.5 3.0 %constant_dynamic-slice_fusion = (bf16[4096,128]{1,0:T(8,128)(2,1)}, bf16[4096,128]{1,0:T(8,128)(2,1)}) fusion(bf16[4096,1024]{1,0:T(8,128)(2,1)} %param.21, s32[]{:T(128)S(6)} %select_n.82, s32[]{:T(128)S(6)} %select_n.78), kind=kLoop, calls=%fused_computation.54 | loop fusion | bytes 4194312 | tf_op jit(solution)/shard_map/dynamic_slice | solution.py:534
  9.7 0.7 all-gather.7.cloned.1.call-update
  10.4 2.9 %shard_map.109 = (bf16[64,16,128]{2,1,0:T(8,128)(2,1)}, bf16[64,16,128]{2,1,0:T(8,128)(2,1)}, bf16[64,16,128]{2,1,0:T(8,128)(2,1)}, bf16[64,16,128]{2,1,0:T(8,128)(2,1)}, s32[1]{0:T(128)}) custom-call(s32[1]{0:T(128)} %bitcast.1.seq_ref, s32[1,4]{1,0:T(1,128)} %lengths_ref.3, s32[1,4]{1,0:T(1,128)} %slots_ref.3, bf16[1,4,64,16,128]{4,3,2,1,0:T(8,128)(2,1)} %cached_ref.1), custom_call_target="tpu_custom_call" | custom-call | flops 1000 | bytes 1000 | tf_op jit(solution)/shard_map/pallas_call | solution.py:107
  13.2 1.3 collective-permute-start
  14.6 2.3 collective-permute-start.1
  16.9 1.1 collective-permute-start.2
  18.1 0.2 reduce_window_sum.11
  18.6 0.1 sub.26
  18.9 1.0 copy.15.end_ref
  19.9 6.2 %shard_map.110.own_ref = f32[2,4096,128]{2,1,0:T(8,128)} custom-call(bf16[256,4096]{1,0:T(8,128)(2,1)} %bitcast.88, bf16[256,512]{1,0:T(8,128)(2,1)} %bitcast.101, f32[4,256,16]{2,1,0:T(8,128)} %copy.15.end_ref), custom_call_target="tpu_custom_call" | custom-call | flops 268435456 | bytes 16777216 | tf_op jit(solution)/shard_map/pallas_call | solution.py:46
  26.2 0.6 fusion.2.gain_ref
  26.8 4.7 %shard_map.111 = (bf16[65,16,128]{2,1,0:T(8,128)(2,1)}, bf16[65,16,128]{2,1,0:T(8,128)(2,1)}, bf16[65,16,128]{2,1,0:T(8,128)(2,1)}, bf16[65,16,128]{2,1,0:T(8,128)(2,1)}) custom-call(s32[1]{0:T(128)} %bitcast.1.seq_ref, s32[1]{0:T(128)} %get-tuple-element.32.code_ref, f32[2,64]{1,0:T(2,128)} %copy-done.21, bf16[16,128]{1,0:T(8,128)(2,1)} %fusion.2.gain_ref, ...), custom_call_target="tpu_custom_call" | custom-call | flops 1000 | bytes 1000 | tf_op jit(solution)/shard_map/pallas_call | solution.py:146
  31.5 14.6 %collective-permute-done.1.refs_6_ = bf16[64,16,128]{2,1,0:T(8,128)(2,1)S(1)} collective-permute-done((bf16[64,16,128]{2,1,0:T(8,128)(2,1)}, bf16[64,16,128]{2,1,0:T(8,128)(2,1)S(1)}, u32[]{:S(2)}, u32[]{:S(2)}) %collective-permute-start.1) | collective-permute-done | bytes 262176 | tf_op jit(solution)/shard_map/ppermute | solution.py:471
  46.0 28.0 %collective-permute-start.3 = (bf16[65,16,128]{2,1,0:T(8,128)(2,1)}, bf16[65,16,128]{2,1,0:T(8,128)(2,1)S(1)}, u32[]{:S(2)}, u32[]{:S(2)}) collective-permute-start(bf16[65,16,128]{2,1,0:T(8,128)(2,1)} %get-tuple-element.40), channel_id=1, source_target_pairs={{0,4},{4,8},{8,12},{12,0},{1,5},{5,9},{9,13},{13,1},{2,6},{6,10},{... | collective-permute-start | bytes 798728 | tf_op jit(solution)/shard_map/ppermute | solution.py:471
  74.0 2.1 collective-permute-start.5
  76.1 8.9 %collective-permute-done.3.refs_1_ = bf16[65,16,128]{2,1,0:T(8,128)(2,1)S(1)} collective-permute-done((bf16[65,16,128]{2,1,0:T(8,128)(2,1)}, bf16[65,16,128]{2,1,0:T(8,128)(2,1)S(1)}, u32[]{:S(2)}, u32[]{:S(2)}) %collective-permute-start.3) | collective-permute-done | bytes 266272 | tf_op jit(solution)/shard_map/ppermute | solution.py:471
  85.0 15.2 %collective-permute-done.4.refs_2_ = bf16[65,16,128]{2,1,0:T(8,128)(2,1)S(1)} collective-permute-done((bf16[65,16,128]{2,1,0:T(8,128)(2,1)}, bf16[65,16,128]{2,1,0:T(8,128)(2,1)S(1)}, u32[]{:S(2)}, u32[]{:S(2)}) %collective-permute-start.4) | collective-permute-done | bytes 266272 | tf_op jit(solution)/shard_map/ppermute | solution.py:471
  100.3 2.4 collective-permute-done.5.refs_3_
  102.7 0.7 copy-done.17
  103.4 3.3 %shard_map.112 = (bf16[64,16,128]{2,1,0:T(8,128)(2,1)}, bf16[64,16,128]{2,1,0:T(8,128)(2,1)}, bf16[64,16,128]{2,1,0:T(8,128)(2,1)}, bf16[64,16,128]{2,1,0:T(8,128)(2,1)}) custom-call(s32[1]{0:T(128)} %bitcast.1.seq_ref, s32[1,4]{1,0:T(1,128)} %lengths_ref.3, s32[1,4]{1,0:T(1,128)} %slots_ref.3, bf16[1,4,64,16,128]{4,3,2,1,0:T(8,128)(2,1)} %cached_ref.1, ...), custom_call_target="tpu_custom_call" | custom-call | flops 1000 | bytes 1000 | tf_op jit(solution)/shard_map/pallas_call | solution.py:201
  106.6 19.3 %collective-permute-start.6 = (bf16[64,16,128]{2,1,0:T(8,128)(2,1)}, bf16[64,16,128]{2,1,0:T(8,128)(2,1)S(1)}, u32[]{:S(2)}, u32[]{:S(2)}) collective-permute-start(bf16[64,16,128]{2,1,0:T(8,128)(2,1)} %get-tuple-element.46), channel_id=1, source_target_pairs={{0,4},{4,8},{8,12},{12,0},{1,5},{5,9},{9,13},{13,1},{2,6},{6,10},{... | collective-permute-start | bytes 786440 | tf_op jit(solution)/shard_map/ppermute | solution.py:471
  126.0 3.1 %collective-permute-start.7 = (bf16[64,16,128]{2,1,0:T(8,128)(2,1)}, bf16[64,16,128]{2,1,0:T(8,128)(2,1)S(1)}, u32[]{:S(2)}, u32[]{:S(2)}) collective-permute-start(bf16[64,16,128]{2,1,0:T(8,128)(2,1)} %get-tuple-element.47), channel_id=1, source_target_pairs={{0,8},{4,12},{8,0},{12,4},{1,9},{5,13},{9,1},{13,5},{2,10},{6,14},... | collective-permute-start | bytes 786440 | tf_op jit(solution)/shard_map/ppermute | solution.py:471
  129.1 1.0 copy.16.run_ref
  130.1 5.2 %collective-permute-done.6.refs_1_ = bf16[64,16,128]{2,1,0:T(8,128)(2,1)S(1)} collective-permute-done((bf16[64,16,128]{2,1,0:T(8,128)(2,1)}, bf16[64,16,128]{2,1,0:T(8,128)(2,1)S(1)}, u32[]{:S(2)}, u32[]{:S(2)}) %collective-permute-start.6) | collective-permute-done | bytes 262176 | tf_op jit(solution)/shard_map/ppermute | solution.py:471
  135.3 12.5 %collective-permute-done.7.refs_2_ = bf16[64,16,128]{2,1,0:T(8,128)(2,1)S(1)} collective-permute-done((bf16[64,16,128]{2,1,0:T(8,128)(2,1)}, bf16[64,16,128]{2,1,0:T(8,128)(2,1)S(1)}, u32[]{:S(2)}, u32[]{:S(2)}) %collective-permute-start.7) | collective-permute-done | bytes 262176 | tf_op jit(solution)/shard_map/ppermute | solution.py:471
  147.8 0.7 copy-done.11
  148.5 4.8 %shard_map.113.refs_0_ = bf16[256,1024]{1,0:T(8,128)(2,1)} custom-call(s32[1]{0:T(128)} %bitcast.1.seq_ref, s32[1]{0:T(128)} %get-tuple-element.32.code_ref, f32[2,64]{1,0:T(2,128)} %copy-done.21, bf16[256,4096]{1,0:T(8,128)(2,1)} %bitcast.89, bf16[256,4096]{1,0:T(8,128)(2,1)} %bitcast.93, bf16[256,512]{1,0:T(8,128)(2,1)} %bitcast.102, ...), custom_call_target="tpu_custom_call" | custom-call | flops 1000 | bytes 1000 | tf_op jit(solution)/shard_map/pallas_call | solution.py:343
  153.3 0.5 collective-permute-start.9
  153.8 1.3 collective-permute-start.10
  155.1 4.6 %shard_map.114.refs_4_ = bf16[256,1024]{1,0:T(8,128)(2,1)} custom-call(s32[1]{0:T(128)} %bitcast.1.seq_ref, s32[1]{0:T(128)} %get-tuple-element.32.code_ref, f32[2,64]{1,0:T(2,128)} %copy-done.21, bf16[256,4096]{1,0:T(8,128)(2,1)} %bitcast.90, bf16[256,4096]{1,0:T(8,128)(2,1)} %bitcast.94, bf16[256,512]{1,0:T(8,128)(2,1)} %bitcast.103, ...), custom_call_target="tpu_custom_call" | custom-call | flops 1000 | bytes 1000 | tf_op jit(solution)/shard_map/pallas_call | solution.py:343
  159.7 0.4 collective-permute-start.12
  160.1 0.2 collective-permute-start.13
  160.3 4.6 %shard_map.115.refs_8_ = bf16[256,1024]{1,0:T(8,128)(2,1)} custom-call(s32[1]{0:T(128)} %bitcast.1.seq_ref, s32[1]{0:T(128)} %get-tuple-element.32.code_ref, f32[2,64]{1,0:T(2,128)} %copy-done.21, bf16[256,4096]{1,0:T(8,128)(2,1)} %bitcast.91, bf16[256,4096]{1,0:T(8,128)(2,1)} %bitcast.95, bf16[256,512]{1,0:T(8,128)(2,1)} %bitcast.104, ...), custom_call_target="tpu_custom_call" | custom-call | flops 1000 | bytes 1000 | tf_op jit(solution)/shard_map/pallas_call | solution.py:343
  165.0 0.5 collective-permute-start.15
  165.5 4.6 %shard_map.116.refs_12_ = bf16[256,1024]{1,0:T(8,128)(2,1)} custom-call(s32[1]{0:T(128)} %bitcast.1.seq_ref, s32[1]{0:T(128)} %get-tuple-element.32.code_ref, f32[2,64]{1,0:T(2,128)} %copy-done.21, bf16[256,4096]{1,0:T(8,128)(2,1)} %bitcast.92, bf16[256,4096]{1,0:T(8,128)(2,1)} %bitcast.96, bf16[256,512]{1,0:T(8,128)(2,1)} %bitcast.105, ...), custom_call_target="tpu_custom_call" | custom-call | flops 1000 | bytes 1000 | tf_op jit(solution)/shard_map/pallas_call | solution.py:343
  170.1 1.3 collective-permute-start.16
  171.5 0.2 collective-permute-start.19
  171.7 0.6 collective-permute-start.18
  172.3 6.5 %collective-permute-done.13.refs_6_ = bf16[256,1024]{1,0:T(8,128)(2,1)S(1)} collective-permute-done((bf16[256,1024]{1,0:T(8,128)(2,1)}, bf16[256,1024]{1,0:T(8,128)(2,1)S(1)}, u32[]{:S(2)}, u32[]{:S(2)}) %collective-permute-start.13) | collective-permute-done | bytes 524320 | tf_op jit(solution)/shard_map/ppermute | solution.py:570
  178.8 1.2 collective-permute-start.11
  180.2 9.9 %collective-permute-done.16.refs_10_ = bf16[256,1024]{1,0:T(8,128)(2,1)} collective-permute-done((bf16[256,1024]{1,0:T(8,128)(2,1)S(1)}, bf16[256,1024]{1,0:T(8,128)(2,1)}, u32[]{:S(2)}, u32[]{:S(2)}) %collective-permute-start.16) | collective-permute-done | bytes 524320 | tf_op jit(solution)/shard_map/ppermute | solution.py:570
  190.1 1.3 collective-permute-start.17
  191.4 9.9 %collective-permute-done.19.refs_14_ = bf16[256,1024]{1,0:T(8,128)(2,1)} collective-permute-done((bf16[256,1024]{1,0:T(8,128)(2,1)}, bf16[256,1024]{1,0:T(8,128)(2,1)}, u32[]{:S(2)}, u32[]{:S(2)}) %collective-permute-start.19) | collective-permute-done | bytes 524320 | tf_op jit(solution)/shard_map/ppermute | solution.py:570
  201.3 0.9 collective-permute-start.20
  202.2 1.8 collective-permute-done.20.refs_15_
  204.1 5.4 %shard_map.118 = (bf16[512,256]{1,0:T(8,128)(2,1)}, bf16[512,256]{1,0:T(8,128)(2,1)}) custom-call(s32[1]{0:T(128)} %bitcast.16.first_ref, bf16[256,1024]{1,0:T(8,128)(2,1)} %shard_map.113.refs_0_, bf16[256,1024]{1,0:T(8,128)(2,1)} %copy-done.1, bf16[256,1024]{1,0:T(8,128)(2,1)} %copy-done.2, bf16[256,1024]{1,0:T(8,128)(2,1)} %collective-permute-done.11.refs_3_, ...), custom_call_target="tpu_custom_call" | custom-call | flops 1000 | bytes 1000 | tf_op jit(solution)/shard_map/pallas_call | solution.py:409
  209.5 0.3 collective-permute-start.22
  209.9 5.4 %shard_map.117 = (bf16[512,256]{1,0:T(8,128)(2,1)}, bf16[512,256]{1,0:T(8,128)(2,1)}) custom-call(s32[1]{0:T(128)} %bitcast.first_ref, bf16[256,1024]{1,0:T(8,128)(2,1)} %shard_map.113.refs_0_, bf16[256,1024]{1,0:T(8,128)(2,1)} %copy-done.1, bf16[256,1024]{1,0:T(8,128)(2,1)} %copy-done.2, bf16[256,1024]{1,0:T(8,128)(2,1)} %collective-permute-done.11.refs_3_, ...), custom_call_target="tpu_custom_call" | custom-call | flops 1000 | bytes 1000 | tf_op jit(solution)/shard_map/pallas_call | solution.py:409
  215.3 7.7 %all-gather.7.cloned.1.call-done = bf16[16384,128]{1,0:T(8,128)(2,1)} async-done(((bf16[4096,128]{1,0:T(8,128)(2,1)}), bf16[16384,128]{1,0:T(8,128)(2,1)}) %all-gather.7.cloned.1.call-update) | async-done | bytes 4194320 | tf_op jit(solution)/shard_map/all_gather | solution.py:557
  223.0 5.5 %shard_map.119 = (bf16[512,256]{1,0:T(8,128)(2,1)}, bf16[512,256]{1,0:T(8,128)(2,1)}) custom-call(s32[1]{0:T(128)} %bitcast.16.first_ref, bf16[256,1024]{1,0:T(8,128)(2,1)} %shard_map.113.refs_0_, bf16[256,1024]{1,0:T(8,128)(2,1)} %copy-done.1, bf16[256,1024]{1,0:T(8,128)(2,1)} %copy-done.2, bf16[256,1024]{1,0:T(8,128)(2,1)} %collective-permute-done.11.refs_3_, ...), custom_call_target="tpu_custom_call" | custom-call | flops 1000 | bytes 1000 | tf_op jit(solution)/shard_map/pallas_call | solution.py:409
  228.5 0.3 collective-permute-start.26
  228.8 1.2 collective-permute-start.25
  230.0 0.3 collective-permute-start.21
  230.3 5.4 %shard_map.120 = (bf16[512,256]{1,0:T(8,128)(2,1)}, bf16[512,256]{1,0:T(8,128)(2,1)}) custom-call(s32[1]{0:T(128)} %bitcast.first_ref, bf16[256,1024]{1,0:T(8,128)(2,1)} %shard_map.113.refs_0_, bf16[256,1024]{1,0:T(8,128)(2,1)} %copy-done.1, bf16[256,1024]{1,0:T(8,128)(2,1)} %copy-done.2, bf16[256,1024]{1,0:T(8,128)(2,1)} %collective-permute-done.11.refs_3_, ...), custom_call_target="tpu_custom_call" | custom-call | flops 1000 | bytes 1000 | tf_op jit(solution)/shard_map/pallas_call | solution.py:409
  235.8 1.3 collective-permute-start.23
  237.1 1.0 add_convert_fusion
  238.1 0.3 collective-permute-start.27
  238.5 8.7 %collective-permute-done.21 = bf16[512,256]{1,0:T(8,128)(2,1)S(1)} collective-permute-done((bf16[512,256]{1,0:T(8,128)(2,1)S(1)}, bf16[512,256]{1,0:T(8,128)(2,1)S(1)}, u32[]{:S(2)}, u32[]{:S(2)}) %collective-permute-start.21) | collective-permute-done | bytes 262176 | tf_op jit(solution)/shard_map/ppermute | solution.py:434
  247.2 1.0 add_convert_fusion.1
  248.3 1.7 collective-permute-start.24
  250.0 0.3 collective-permute-start.28
  250.4 0.8 collective-permute-done.24
  251.2 0.4 collective-permute-done.28
  252.1 1.0 copy-done.22
  (105 shorter events, 1.6 us)
Async XLA Ops:
  6.5 11.4 %copy-start.20 = (f32[1,256,64]{1,2,0:T(8,128)S(1)}, f32[1,256,64]{1,2,0:T(8,128)}, u32[]{:S(2)}) copy-start(f32[1,256,64]{1,2,0:T(8,128)} %param.16) | copy-start | bytes 196612
  6.5 195.7 %all-gather.5.cloned.1.call-start = ((), (), s32[]{:S(2)}) async-start(), calls=%async_computation | async-start | bytes 5242880 | tf_op jit(solution)/shard_map/all_gather | solution.py:557
  6.5 12.2 %copy-start.14 = (f32[1,256,64]{1,2,0:T(8,128)S(1)}, f32[1,256,64]{1,2,0:T(8,128)}, u32[]{:S(2)}) copy-start(f32[1,256,64]{1,2,0:T(8,128)} %param.15) | copy-start | bytes 196612
  9.6 213.4 %all-gather.7.cloned.1.call-start = ((), (), s32[]{:S(2)}) async-start(), calls=%async_computation.1 | async-start | bytes 5242880 | tf_op jit(solution)/shard_map/all_gather | solution.py:557
  13.2 18.2 %collective-permute-start = (bf16[64,16,128]{2,1,0:T(8,128)(2,1)}, bf16[64,16,128]{2,1,0:T(8,128)(2,1)S(1)}, u32[]{:S(2)}, u32[]{:S(2)}) collective-permute-start(bf16[64,16,128]{2,1,0:T(8,128)(2,1)} %get-tuple-element.35), channel_id=1, source_target_pairs={{0,4},{4,8},{8,12},{12,0},{1,5},{5,9},{9,13},{13,1},{2,6},{6,10},{... | collective-permute-start | bytes 786440 | tf_op jit(solution)/shard_map/ppermute | solution.py:471
  14.6 31.4 %collective-permute-start.1 = (bf16[64,16,128]{2,1,0:T(8,128)(2,1)}, bf16[64,16,128]{2,1,0:T(8,128)(2,1)S(1)}, u32[]{:S(2)}, u32[]{:S(2)}) collective-permute-start(bf16[64,16,128]{2,1,0:T(8,128)(2,1)} %get-tuple-element.36), channel_id=1, source_target_pairs={{0,8},{4,12},{8,0},{12,4},{1,9},{5,13},{9,1},{13,5},{2,10},{6,14},... | collective-permute-start | bytes 786440 | tf_op jit(solution)/shard_map/ppermute | solution.py:471
  16.9 29.1 %collective-permute-start.2 = (bf16[64,16,128]{2,1,0:T(8,128)(2,1)}, bf16[64,16,128]{2,1,0:T(8,128)(2,1)S(1)}, u32[]{:S(2)}, u32[]{:S(2)}) collective-permute-start(bf16[64,16,128]{2,1,0:T(8,128)(2,1)} %get-tuple-element.37), channel_id=1, source_target_pairs={{0,12},{4,0},{8,4},{12,8},{1,13},{5,1},{9,5},{13,9},{2,14},{6,2},{... | collective-permute-start | bytes 786440 | tf_op jit(solution)/shard_map/ppermute | solution.py:471
  18.4 8.4 %copy-start.21 = (f32[2,64]{1,0:T(2,128)}, f32[2,64]{1,0:T(2,128)S(1)}, u32[]{:S(2)}) copy-start(f32[2,64]{1,0:T(2,128)S(1)} %exp.8.total_ref) | copy-start | bytes 1540
  18.5 110.5 %copy-start.13 = (f32[256,4,16]{0,2,1:T(8,128)}, f32[256,4,16]{0,2,1:T(8,128)S(1)}, u32[]{:S(2)}) copy-start(f32[256,4,16]{0,2,1:T(8,128)S(1)} %reshape.114) | copy-start | bytes 196612
  31.5 116.3 %copy-start.7 = (bf16[64,16,128]{2,1,0:T(8,128)(2,1)}, bf16[64,16,128]{2,1,0:T(8,128)(2,1)S(1)}, u32[]{:S(2)}) copy-start(bf16[64,16,128]{2,1,0:T(8,128)(2,1)S(1)} %collective-permute-done.refs_5_) | copy-start | bytes 786436
  46.0 101.7 %copy-start.8 = (bf16[64,16,128]{2,1,0:T(8,128)(2,1)}, bf16[64,16,128]{2,1,0:T(8,128)(2,1)S(1)}, u32[]{:S(2)}) copy-start(bf16[64,16,128]{2,1,0:T(8,128)(2,1)S(1)} %collective-permute-done.1.refs_6_) | copy-start | bytes 786436
  46.0 101.7 %copy-start.9 = (bf16[64,16,128]{2,1,0:T(8,128)(2,1)}, bf16[64,16,128]{2,1,0:T(8,128)(2,1)S(1)}, u32[]{:S(2)}) copy-start(bf16[64,16,128]{2,1,0:T(8,128)(2,1)S(1)} %collective-permute-done.2.refs_7_) | copy-start | bytes 786436
  46.0 39.0 %collective-permute-start.3 = (bf16[65,16,128]{2,1,0:T(8,128)(2,1)}, bf16[65,16,128]{2,1,0:T(8,128)(2,1)S(1)}, u32[]{:S(2)}, u32[]{:S(2)}) collective-permute-start(bf16[65,16,128]{2,1,0:T(8,128)(2,1)} %get-tuple-element.40), channel_id=1, source_target_pairs={{0,4},{4,8},{8,12},{12,0},{1,5},{5,9},{9,13},{13,1},{2,6},{6,10},{... | collective-permute-start | bytes 798728 | tf_op jit(solution)/shard_map/ppermute | solution.py:471
  74.0 26.2 %collective-permute-start.4 = (bf16[65,16,128]{2,1,0:T(8,128)(2,1)}, bf16[65,16,128]{2,1,0:T(8,128)(2,1)S(1)}, u32[]{:S(2)}, u32[]{:S(2)}) collective-permute-start(bf16[65,16,128]{2,1,0:T(8,128)(2,1)} %get-tuple-element.42), channel_id=1, source_target_pairs={{0,8},{4,12},{8,0},{12,4},{1,9},{5,13},{9,1},{13,5},{2,10},{6,14},... | collective-permute-start | bytes 798728 | tf_op jit(solution)/shard_map/ppermute | solution.py:471
  74.0 28.6 %collective-permute-start.5 = (bf16[65,16,128]{2,1,0:T(8,128)(2,1)}, bf16[65,16,128]{2,1,0:T(8,128)(2,1)S(1)}, u32[]{:S(2)}, u32[]{:S(2)}) collective-permute-start(bf16[65,16,128]{2,1,0:T(8,128)(2,1)} %get-tuple-element.44), channel_id=1, source_target_pairs={{0,12},{4,0},{8,4},{12,8},{1,13},{5,1},{9,5},{13,9},{2,14},{6,2},{... | collective-permute-start | bytes 798728 | tf_op jit(solution)/shard_map/ppermute | solution.py:471
  85.0 17.6 %copy-start.15 = (bf16[65,16,128]{2,1,0:T(8,128)(2,1)}, bf16[65,16,128]{2,1,0:T(8,128)(2,1)S(1)}, u32[]{:S(2)}) copy-start(bf16[65,16,128]{2,1,0:T(8,128)(2,1)S(1)} %collective-permute-done.3.refs_1_) | copy-start | bytes 798724
  100.3 2.4 copy-start.16
  102.7 0.7 copy-start.17
  106.6 28.6 %collective-permute-start.6 = (bf16[64,16,128]{2,1,0:T(8,128)(2,1)}, bf16[64,16,128]{2,1,0:T(8,128)(2,1)S(1)}, u32[]{:S(2)}, u32[]{:S(2)}) collective-permute-start(bf16[64,16,128]{2,1,0:T(8,128)(2,1)} %get-tuple-element.46), channel_id=1, source_target_pairs={{0,4},{4,8},{8,12},{12,0},{1,5},{5,9},{9,13},{13,1},{2,6},{6,10},{... | collective-permute-start | bytes 786440 | tf_op jit(solution)/shard_map/ppermute | solution.py:471
  126.0 21.8 %collective-permute-start.7 = (bf16[64,16,128]{2,1,0:T(8,128)(2,1)}, bf16[64,16,128]{2,1,0:T(8,128)(2,1)S(1)}, u32[]{:S(2)}, u32[]{:S(2)}) collective-permute-start(bf16[64,16,128]{2,1,0:T(8,128)(2,1)} %get-tuple-element.47), channel_id=1, source_target_pairs={{0,8},{4,12},{8,0},{12,4},{1,9},{5,13},{9,1},{13,5},{2,10},{6,14},... | collective-permute-start | bytes 786440 | tf_op jit(solution)/shard_map/ppermute | solution.py:471
  129.1 18.7 %collective-permute-start.8 = (bf16[64,16,128]{2,1,0:T(8,128)(2,1)}, bf16[64,16,128]{2,1,0:T(8,128)(2,1)S(1)}, u32[]{:S(2)}, u32[]{:S(2)}) collective-permute-start(bf16[64,16,128]{2,1,0:T(8,128)(2,1)} %get-tuple-element.48), channel_id=1, source_target_pairs={{0,12},{4,0},{8,4},{12,8},{1,13},{5,1},{9,5},{13,9},{2,14},{6,2},{... | collective-permute-start | bytes 786440 | tf_op jit(solution)/shard_map/ppermute | solution.py:471
  135.2 12.5 %copy-start.10 = (bf16[64,16,128]{2,1,0:T(8,128)(2,1)}, bf16[64,16,128]{2,1,0:T(8,128)(2,1)S(1)}, u32[]{:S(2)}) copy-start(bf16[64,16,128]{2,1,0:T(8,128)(2,1)S(1)} %collective-permute-done.6.refs_1_) | copy-start | bytes 786436
  147.7 0.7 copy-start.11
  147.7 0.8 copy-start.12
  153.3 16.8 %collective-permute-start.9 = (bf16[256,1024]{1,0:T(8,128)(2,1)}, bf16[256,1024]{1,0:T(8,128)(2,1)S(1)}, u32[]{:S(2)}, u32[]{:S(2)}) collective-permute-start(bf16[256,1024]{1,0:T(8,128)(2,1)} %shard_map.113.refs_0_), channel_id=1, source_target_pairs={{0,1},{1,0},{2,3},{3,2},{4,5},{5,4},{6,7},{7,6},{8,9},{9,8},{10,11... | collective-permute-start | bytes 1572872 | tf_op jit(solution)/shard_map/ppermute | solution.py:571
  153.8 17.7 %collective-permute-start.10 = (bf16[256,1024]{1,0:T(8,128)(2,1)}, bf16[256,1024]{1,0:T(8,128)(2,1)S(1)}, u32[]{:S(2)}, u32[]{:S(2)}) collective-permute-start(bf16[256,1024]{1,0:T(8,128)(2,1)} %shard_map.113.refs_0_), channel_id=1, source_target_pairs={{0,16},{16,0},{1,17},{17,1},{2,18},{18,2},{3,19},{19,3},{4,20},{20... | collective-permute-start | bytes 1572872 | tf_op jit(solution)/shard_map/ppermute | solution.py:570
  159.7 12.0 %collective-permute-start.12 = (bf16[256,1024]{1,0:T(8,128)(2,1)}, bf16[256,1024]{1,0:T(8,128)(2,1)S(1)}, u32[]{:S(2)}, u32[]{:S(2)}) collective-permute-start(bf16[256,1024]{1,0:T(8,128)(2,1)} %shard_map.114.refs_4_), channel_id=1, source_target_pairs={{0,1},{1,0},{2,3},{3,2},{4,5},{5,4},{6,7},{7,6},{8,9},{9,8},{10,11... | collective-permute-start | bytes 1572872 | tf_op jit(solution)/shard_map/ppermute | solution.py:571
  160.1 18.7 %collective-permute-start.13 = (bf16[256,1024]{1,0:T(8,128)(2,1)}, bf16[256,1024]{1,0:T(8,128)(2,1)S(1)}, u32[]{:S(2)}, u32[]{:S(2)}) collective-permute-start(bf16[256,1024]{1,0:T(8,128)(2,1)} %shard_map.114.refs_4_), channel_id=1, source_target_pairs={{0,16},{16,0},{1,17},{17,1},{2,18},{18,2},{3,19},{19,3},{4,20},{20... | collective-permute-start | bytes 1572872 | tf_op jit(solution)/shard_map/ppermute | solution.py:570
  165.0 5.1 %copy-start = (bf16[256,1024]{1,0:T(8,128)(2,1)S(1)}, bf16[256,1024]{1,0:T(8,128)(2,1)}, u32[]{:S(2)}) copy-start(bf16[256,1024]{1,0:T(8,128)(2,1)} %shard_map.115.refs_8_) | copy-start | bytes 1572868
  165.0 15.1 %collective-permute-start.15 = (bf16[256,1024]{1,0:T(8,128)(2,1)}, bf16[256,1024]{1,0:T(8,128)(2,1)S(1)}, u32[]{:S(2)}, u32[]{:S(2)}) collective-permute-start(bf16[256,1024]{1,0:T(8,128)(2,1)} %shard_map.115.refs_8_), channel_id=1, source_target_pairs={{0,1},{1,0},{2,3},{3,2},{4,5},{5,4},{6,7},{7,6},{8,9},{9,8},{10,11... | collective-permute-start | bytes 1572872 | tf_op jit(solution)/shard_map/ppermute | solution.py:571
  170.1 33.9 %copy-start.1 = (bf16[256,1024]{1,0:T(8,128)(2,1)}, bf16[256,1024]{1,0:T(8,128)(2,1)S(1)}, u32[]{:S(2)}) copy-start(bf16[256,1024]{1,0:T(8,128)(2,1)S(1)} %collective-permute-done.9.refs_1_) | copy-start | bytes 1572868
  170.1 19.9 %collective-permute-start.16 = (bf16[256,1024]{1,0:T(8,128)(2,1)S(1)}, bf16[256,1024]{1,0:T(8,128)(2,1)}, u32[]{:S(2)}, u32[]{:S(2)}) collective-permute-start(bf16[256,1024]{1,0:T(8,128)(2,1)S(1)} %copy-done), channel_id=1, source_target_pairs={{0,16},{16,0},{1,17},{17,1},{2,18},{18,2},{3,19},{19,3},{4,20},{20... | collective-permute-start | bytes 1572872 | tf_op jit(solution)/shard_map/ppermute | solution.py:570
  171.5 32.6 %copy-start.2 = (bf16[256,1024]{1,0:T(8,128)(2,1)}, bf16[256,1024]{1,0:T(8,128)(2,1)S(1)}, u32[]{:S(2)}) copy-start(bf16[256,1024]{1,0:T(8,128)(2,1)S(1)} %collective-permute-done.10.refs_2_) | copy-start | bytes 1572868
  171.5 29.8 %collective-permute-start.19 = (bf16[256,1024]{1,0:T(8,128)(2,1)}, bf16[256,1024]{1,0:T(8,128)(2,1)}, u32[]{:S(2)}, u32[]{:S(2)}) collective-permute-start(bf16[256,1024]{1,0:T(8,128)(2,1)} %shard_map.116.refs_12_), channel_id=1, source_target_pairs={{0,16},{16,0},{1,17},{17,1},{2,18},{18,2},{3,19},{19,3},{4,20},{20... | collective-permute-start | bytes 1572872 | tf_op jit(solution)/shard_map/ppermute | solution.py:570
  171.7 32.4 %copy-start.3 = (bf16[256,1024]{1,0:T(8,128)(2,1)}, bf16[256,1024]{1,0:T(8,128)(2,1)S(1)}, u32[]{:S(2)}) copy-start(bf16[256,1024]{1,0:T(8,128)(2,1)S(1)} %collective-permute-done.12.refs_5_) | copy-start | bytes 1572868
  171.7 30.5 %collective-permute-start.18 = (bf16[256,1024]{1,0:T(8,128)(2,1)}, bf16[256,1024]{1,0:T(8,128)(2,1)}, u32[]{:S(2)}, u32[]{:S(2)}) collective-permute-start(bf16[256,1024]{1,0:T(8,128)(2,1)} %shard_map.116.refs_12_), channel_id=1, source_target_pairs={{0,1},{1,0},{2,3},{3,2},{4,5},{5,4},{6,7},{7,6},{8,9},{9,8},{10,11... | collective-permute-start | bytes 1572872 | tf_op jit(solution)/shard_map/ppermute | solution.py:571
  178.8 25.2 %copy-start.4 = (bf16[256,1024]{1,0:T(8,128)(2,1)}, bf16[256,1024]{1,0:T(8,128)(2,1)S(1)}, u32[]{:S(2)}) copy-start(bf16[256,1024]{1,0:T(8,128)(2,1)S(1)} %collective-permute-done.13.refs_6_) | copy-start | bytes 1572868
  178.8 23.3 %collective-permute-start.11 = (bf16[256,1024]{1,0:T(8,128)(2,1)S(1)}, bf16[256,1024]{1,0:T(8,128)(2,1)}, u32[]{:S(2)}, u32[]{:S(2)}) collective-permute-start(bf16[256,1024]{1,0:T(8,128)(2,1)S(1)} %collective-permute-done.10.refs_2_), channel_id=1, source_target_pairs={{0,1},{1,0},{2,3},{3,2},{4,5},{5,4},{6,7},{7,6},{8,9},{9,8},{10,11... | collective-permute-start | bytes 1572872 | tf_op jit(solution)/shard_map/ppermute | solution.py:572
  180.1 24.0 %copy-start.5 = (bf16[256,1024]{1,0:T(8,128)(2,1)}, bf16[256,1024]{1,0:T(8,128)(2,1)S(1)}, u32[]{:S(2)}) copy-start(bf16[256,1024]{1,0:T(8,128)(2,1)S(1)} %collective-permute-done.15.refs_9_) | copy-start | bytes 1572868
  180.1 22.1 %collective-permute-start.14 = (bf16[256,1024]{1,0:T(8,128)(2,1)S(1)}, bf16[256,1024]{1,0:T(8,128)(2,1)}, u32[]{:S(2)}, u32[]{:S(2)}) collective-permute-start(bf16[256,1024]{1,0:T(8,128)(2,1)S(1)} %collective-permute-done.13.refs_6_), channel_id=1, source_target_pairs={{0,1},{1,0},{2,3},{3,2},{4,5},{5,4},{6,7},{7,6},{8,9},{9,8},{10,11... | collective-permute-start | bytes 1572872 | tf_op jit(solution)/shard_map/ppermute | solution.py:572
  190.1 12.1 %collective-permute-start.17 = (bf16[256,1024]{1,0:T(8,128)(2,1)}, bf16[256,1024]{1,0:T(8,128)(2,1)S(1)}, u32[]{:S(2)}, u32[]{:S(2)}) collective-permute-start(bf16[256,1024]{1,0:T(8,128)(2,1)} %collective-permute-done.16.refs_10_), channel_id=1, source_target_pairs={{0,1},{1,0},{2,3},{3,2},{4,5},{5,4},{6,7},{7,6},{8,9},{9,8},{10,11... | collective-permute-start | bytes 1572872 | tf_op jit(solution)/shard_map/ppermute | solution.py:572
  201.3 2.8 %collective-permute-start.20 = (bf16[256,1024]{1,0:T(8,128)(2,1)}, bf16[256,1024]{1,0:T(8,128)(2,1)}, u32[]{:S(2)}, u32[]{:S(2)}) collective-permute-start(bf16[256,1024]{1,0:T(8,128)(2,1)} %collective-permute-done.19.refs_14_), channel_id=1, source_target_pairs={{0,1},{1,0},{2,3},{3,2},{4,5},{5,4},{6,7},{7,6},{8,9},{9,8},{10,11... | collective-permute-start | bytes 1572872 | tf_op jit(solution)/shard_map/ppermute | solution.py:572
  202.2 1.9 copy-start.6
  209.5 26.2 %collective-permute-start.22 = (bf16[512,256]{1,0:T(8,128)(2,1)}, bf16[512,256]{1,0:T(8,128)(2,1)S(1)}, u32[]{:S(2)}, u32[]{:S(2)}) collective-permute-start(bf16[512,256]{1,0:T(8,128)(2,1)} %get-tuple-element.52), channel_id=1, source_target_pairs={{0,2},{2,0},{1,3},{3,1},{4,6},{6,4},{5,7},{7,5},{8,10},{10,8},{9,1... | collective-permute-start | bytes 786440 | tf_op jit(solution)/shard_map/ppermute | solution.py:434
  223.0 7.0 %copy-start.23 = (bf16[512,256]{1,0:T(8,128)(2,1)S(1)}, bf16[512,256]{1,0:T(8,128)(2,1)}, u32[]{:S(2)}) copy-start(bf16[512,256]{1,0:T(8,128)(2,1)} %get-tuple-element.50) | copy-start | bytes 786436
  228.5 8.6 %collective-permute-start.26 = (bf16[512,256]{1,0:T(8,128)(2,1)}, bf16[512,256]{1,0:T(8,128)(2,1)S(1)}, u32[]{:S(2)}, u32[]{:S(2)}) collective-permute-start(bf16[512,256]{1,0:T(8,128)(2,1)} %get-tuple-element.55), channel_id=1, source_target_pairs={{0,2},{2,0},{1,3},{3,1},{4,6},{6,4},{5,7},{7,5},{8,10},{10,8},{9,1... | collective-permute-start | bytes 786440 | tf_op jit(solution)/shard_map/ppermute | solution.py:434
  228.8 18.4 %collective-permute-start.25 = (bf16[512,256]{1,0:T(8,128)(2,1)}, bf16[512,256]{1,0:T(8,128)(2,1)S(1)}, u32[]{:S(2)}, u32[]{:S(2)}) collective-permute-start(bf16[512,256]{1,0:T(8,128)(2,1)} %get-tuple-element.54), channel_id=1, source_target_pairs={{0,2},{2,0},{1,3},{3,1},{4,6},{6,4},{5,7},{7,5},{8,10},{10,8},{9,1... | collective-permute-start | bytes 786440 | tf_op jit(solution)/shard_map/ppermute | solution.py:434
  230.0 5.7 %copy-start.19 = (bf16[512,256]{1,0:T(8,128)(2,1)S(1)}, bf16[512,256]{1,0:T(8,128)(2,1)}, u32[]{:S(2)}) copy-start(bf16[512,256]{1,0:T(8,128)(2,1)} %get-tuple-element.51) | copy-start | bytes 786436
  230.0 17.1 %copy-start.18 = (bf16[512,256]{1,0:T(8,128)(2,1)S(1)}, bf16[512,256]{1,0:T(8,128)(2,1)}, u32[]{:S(2)}) copy-start(bf16[512,256]{1,0:T(8,128)(2,1)} %get-tuple-element.49) | copy-start | bytes 786436
  230.0 17.1 %collective-permute-start.21 = (bf16[512,256]{1,0:T(8,128)(2,1)S(1)}, bf16[512,256]{1,0:T(8,128)(2,1)S(1)}, u32[]{:S(2)}, u32[]{:S(2)}) collective-permute-start(bf16[512,256]{1,0:T(8,128)(2,1)S(1)} %copy-done.23), channel_id=1, source_target_pairs={{0,2},{2,0},{1,3},{3,1},{4,6},{6,4},{5,7},{7,5},{8,10},{10,8},{9,1... | collective-permute-start | bytes 786440 | tf_op jit(solution)/shard_map/ppermute | solution.py:434
  235.8 12.4 %collective-permute-start.23 = (bf16[512,256]{1,0:T(8,128)(2,1)S(1)}, bf16[512,256]{1,0:T(8,128)(2,1)S(1)}, u32[]{:S(2)}, u32[]{:S(2)}) collective-permute-start(bf16[512,256]{1,0:T(8,128)(2,1)S(1)} %add_convert_fusion.2), channel_id=1, source_target_pairs={{0,16},{16,0},{1,17},{17,1},{2,18},{18,2},{3,19},{19,3},{4,20},{20... | collective-permute-start | bytes 786440 | tf_op jit(solution)/shard_map/ppermute | solution.py:437
  238.1 11.9 %collective-permute-start.27 = (bf16[512,256]{1,0:T(8,128)(2,1)S(1)}, bf16[512,256]{1,0:T(8,128)(2,1)S(1)}, u32[]{:S(2)}, u32[]{:S(2)}) collective-permute-start(bf16[512,256]{1,0:T(8,128)(2,1)S(1)} %add_convert_fusion), channel_id=1, source_target_pairs={{0,16},{16,0},{1,17},{17,1},{2,18},{18,2},{3,19},{19,3},{4,20},{20... | collective-permute-start | bytes 786440 | tf_op jit(solution)/shard_map/ppermute | solution.py:437
  248.3 2.8 %collective-permute-start.24 = (bf16[2,256,256]{2,1,0:T(8,128)(2,1)S(1)}, bf16[2,256,256]{2,1,0:T(8,128)(2,1)S(1)}, u32[]{:S(2)}, u32[]{:S(2)}) collective-permute-start(bf16[2,256,256]{2,1,0:T(8,128)(2,1)S(1)} %pad_maximum_fusion), channel_id=1, source_target_pairs={{0,1},{1,0},{2,3},{3,2},{4,5},{5,4},{6,7},{7,6},{8,9},{9,8},{10,11... | collective-permute-start | bytes 786440 | tf_op jit(solution)/shard_map/ppermute | solution.py:439
  250.0 1.6 collective-permute-start.28
  252.1 1.0 copy-start.22
Sparse Core Ops, SparseCore 0:
  9.7 133.1 all-gather.4
  144.5 78.5 all-gather.6

commit v5 on v4

--- a/solution.py
+++ b/solution.py
@@ -366,17 +366,20 @@
     )(seq.reshape(1), code, totals, x, z, b, c, run, run_t, step_t, gain, own, *entered, *second)
 
 
-def project_kernel(first_ref, *refs):
-    weights, near_ref, far_ref, rows_all, weight, total, sems = refs[-7:]
-    lhs = refs[:-7]
+def project_kernel(outs, first_ref, *refs):
+    rows_all, weight, total, sems = refs[-4:]
+    out_refs = refs[-4 - outs : -4]
+    weights = refs[-5 - outs]
+    lhs = refs[: -5 - outs]
     tokens, depth = lhs[0].shape
     cols = weights.shape[2]
-    parts = len(lhs) // 4
+    parts = weight.shape[0]
+    count = len(lhs) // parts
     for part in range(parts):
         span = pl.ds(part * depth, depth)
-        for r in range(4):
+        for r in range(count):
             pltpu.make_async_copy(
-                lhs[4 * part + r],
+                lhs[count * part + r],
                 rows_all.at[part, pl.ds(r * tokens, tokens)],
                 sems.at[0, part],
             ).start()
@@ -389,7 +392,7 @@
     for part in range(parts):
         pltpu.make_async_copy(rows_all.at[part], rows_all.at[part], sems.at[0, part]).wait()
         pltpu.make_async_copy(weight.at[part], weight.at[part], sems.at[1, part]).wait()
-        for r in range(4):
+        for r in range(count):
             span = pl.ds(r * tokens, tokens)
             product = jnp.dot(rows_all[part, span, :], weight[part], preferred_element_type=F32)
             if part == 0:
@@ -397,20 +400,22 @@
             elif part < parts - 1:
                 total[span, :] += product
             else:
-                out_ref = far_ref if r >= 2 else near_ref
-                out_ref[pl.ds(r % 2 * tokens, tokens), :] = (total[span, :] + product).astype(BF)
-
-
-def project(first, lhs, weights):
-    parts = len(lhs) // 4
-    tokens = 4 * lhs[0].shape[0]
+                each = count // outs
+                place = pl.ds(r % each * tokens, tokens)
+                out_refs[r // each][place, :] = (total[span, :] + product).astype(BF)
+
+
+def project(first, lhs, weights, outs):
+    parts = len(lhs)
+    flat = [rows for part in lhs for rows in part]
+    tokens = len(lhs[0]) * flat[0].shape[0]
     depth, cols = weights.shape[1:]
     hbm = pl.BlockSpec(memory_space=pl.ANY)
     return pl.pallas_call(
-        project_kernel,
-        in_specs=[pl.BlockSpec(memory_space=pltpu.SMEM)] + [hbm] * (len(lhs) + 1),
-        out_specs=[pl.BlockSpec(memory_space=pltpu.VMEM)] * 2,
-        out_shape=[jax.ShapeDtypeStruct((tokens // 2, 2 * cols), BF)] * 2,
+        functools.partial(project_kernel, outs),
+        in_specs=[pl.BlockSpec(memory_space=pltpu.SMEM)] + [hbm] * (len(flat) + 1),
+        out_specs=[pl.BlockSpec(memory_space=pltpu.VMEM)] * outs,
+        out_shape=[jax.ShapeDtypeStruct((tokens // outs, 2 * cols), BF)] * outs,
         scratch_shapes=[
             pltpu.VMEM((parts, tokens, depth // parts), BF),
             pltpu.VMEM((parts, depth // parts, 2 * cols), BF),
@@ -418,8 +423,12 @@
             pltpu.SemaphoreType.DMA((2, parts)),
         ],
         compiler_params=pltpu.CompilerParams(vmem_limit_bytes=VMEM_LIMIT),
-        cost_estimate=SMALL,
-    )(first.reshape(1), *lhs, weights)
+        cost_estimate=pl.CostEstimate(
+            flops=4 * tokens * depth * cols,
+            bytes_accessed=2 * depth * (tokens + 2 * cols),
+            transcendentals=0,
+        ),
+    )(first.reshape(1), *flat, weights)
 
 
 SWAP = [(0, 1), (1, 0)]
@@ -429,11 +438,11 @@
     return lax.optimization_barrier((value, *others))[0]
 
 
-def to_rows(own, others, tokens):
-    far, near = [
-        (own[k].astype(F32) + lax.ppermute(others[k], "head", SWAP).astype(F32)).astype(BF)
-        for k in (1, 0)
-    ]
+def to_rows(own, others, tokens, near_first):
+    far = lax.ppermute(others[1], "head", SWAP)
+    near = lax.ppermute(others[0] if near_first else after(others[0], far), "head", SWAP)
+    far = (own[1].astype(F32) + far.astype(F32)).astype(BF)
+    near = (own[0].astype(F32) + near.astype(F32)).astype(BF)
     from_y = lax.ppermute(far, "groups", SWAP).reshape(2, tokens, -1)
     near = near.reshape(2, tokens, -1)
     from_core = lax.ppermute(jnp.stack([near[1], from_y[1]]), "batch", SWAP)
@@ -565,19 +574,28 @@
     if not fast:
         return plain_projection(jnp.concatenate(normed, axis=1), out_weight)
 
-    lhs = []
-    for part in normed:
-        across = lax.ppermute(part, "groups", SWAP)
-        other = lax.ppermute(part, "batch", SWAP)
-        other_across = lax.ppermute(across, "batch", SWAP)
-        lhs += [part, other, across, other_across]
-    sides = []
-    done = []
-    for part in weights:
-        others = project(2 - 2 * head, lhs, after(part, *done))
-        mine = project(2 * head, lhs, after(part, *others) if done else part)
-        done = mine
-        sides.append(in_order(y, core, to_rows(mine, others, tokens)))
+    theirs, mine = 2 - 2 * head, 2 * head
+    crossed = [lax.ppermute(part, "groups", SWAP) for part in normed]
+    near = []
+    for n, part in enumerate(normed):
+        tied = after(part, *crossed[max(n - 2, 0) : n - 1]) if n > 1 else part
+        near.append([part, lax.ppermute(tied, "batch", SWAP)])
+    near_others = project(theirs, near, weights[0], 1)
+    near_mine = project(mine, near, weights[0], 1)
+    far = []
+    for across in crossed:
+        across = after(across, *near_mine)
+        far.append([across, lax.ppermute(across, "batch", SWAP)])
+    far_others = project(theirs, far, weights[0], 1)
+    lhs = [a + b for a, b in zip(near, far)]
+    far_mine = project(mine, far, after(weights[0], *far_others), 1)
+    last = after(weights[1], *far_mine)
+    last_others = project(theirs, lhs, last, 2)
+    last_mine = project(mine, lhs, after(last, *last_others), 2)
+    sides = [
+        in_order(y, core, to_rows(near_mine + far_mine, near_others + far_others, tokens, True)),
+        in_order(y, core, to_rows(last_mine, last_others, tokens, False)),
+    ]
     pieces = [
         sides[k][q][:, block * piece : (block + 1) * piece]
         for block in range(2)

time: 263 us -> 259 us (0.985)
  waiting for transfers between devices: 105 us -> 90.3 us
  Pallas kernels: 57.4 us -> 63.3 us
  starting transfers between devices: 71.6 us -> 74.5 us
    ppermute x16, waiting for transfers between devices: 36.9 us -> 21.9 us  [the longest x4 19.2 us: body(): crossed = [lax.ppermute(part, 'groups', SWAP) for part in normed]]
    pallas_call x4 -> x6, Pallas kernels: 21.7 us -> 26.7 us  [project(): pl.pallas_call(functools.partial(project_kernel, outs), in_specs=[pl.Bloc...]
    ppermute x2, starting transfers between devices: 1.97 us -> 4.74 us  [to_rows(): from_core = lax.ppermute(jnp.stack([near[1], from_y[1]]), 'batch', SWAP)]
  transfers between devices with their start and end apart: 31 -> 31, of which waited for: 14 -> 16; matrix products, arithmetic and copies ran while one was open for 2% -> 3% of each run, Pallas kernels for 22% -> 25%
where the time goes in v5:
time: 259 us; the launch traced here: 257 us
  waiting for transfers between devices  90.3 us (35%)
  starting transfers between devices  74.5 us (29%)
  Pallas kernels  63.3 us (24%)
  between operations  13.9 us (5%)
  local copies, waits for them, and re-layouts  10.4 us (4%)
  other arithmetic  4.32 us (2%)
    ppermute x9, waiting for transfers between devices, exchange_states(): lax.ppermute(piece, 'seq', [(i, (i + offset) % size) for i in range(size)])  58.3 us
    ppermute x9, starting transfers between devices, exchange_states(): lax.ppermute(piece, 'seq', [(i, (i + offset) % size) for i in range(size)])  57.3 us
    pallas_call x6, Pallas kernels, project(): pl.pallas_call(functools.partial(project_kernel, outs), in_specs=[pl.Bloc...  26.7 us
    ppermute x4, waiting for transfers between devices, body(): crossed = [lax.ppermute(part, 'groups', SWAP) for part in normed]  19.2 us
    pallas_call x4, Pallas kernels, mix_groups(): pl.pallas_call(functools.partial(mix_kernel, place, size), grid=(1, token...  19.1 us
    all_gather x2, waiting for transfers between devices, body(): weights = [lax.all_gather(part, 'seq', axis=0) for part in w_own]  7.2 us
    pallas_call x1, Pallas kernels, block_states_of(): pl.pallas_call(states_kernel, grid=(groups_dev,), in_specs=[pl.BlockSpec(...  6.2 us
  transfers between devices with their start and end apart: 31, of which 16 were waited for; matrix products, arithmetic and copies ran while one was open for 3% of the time, Pallas kernels for 25%

profile of v5, /device:TPU:3, one launch (start us, length us, event | category | flops | bytes accessed | tf_op | source)
XLA Modules:
  0.0 256.7 jit_solution(5579365205556288506)
XLA Ops:
  6.5 3.0 %constant_dynamic-slice_fusion = (bf16[4096,128]{1,0:T(8,128)(2,1)}, bf16[4096,128]{1,0:T(8,128)(2,1)}) fusion(bf16[4096,1024]{1,0:T(8,128)(2,1)} %param.21, s32[]{:T(128)S(6)} %select_n.82, s32[]{:T(128)S(6)} %select_n.78), kind=kLoop, calls=%fused_computation.54 | loop fusion | bytes 4194312 | tf_op jit(solution)/shard_map/dynamic_slice | solution.py:543
  9.7 0.7 all-gather.7.cloned.1.call-update
  10.4 2.9 %shard_map.109 = (bf16[64,16,128]{2,1,0:T(8,128)(2,1)}, bf16[64,16,128]{2,1,0:T(8,128)(2,1)}, bf16[64,16,128]{2,1,0:T(8,128)(2,1)}, bf16[64,16,128]{2,1,0:T(8,128)(2,1)}, s32[1]{0:T(128)}) custom-call(s32[1]{0:T(128)} %bitcast.1.seq_ref, s32[1,4]{1,0:T(1,128)} %lengths_ref.3, s32[1,4]{1,0:T(1,128)} %slots_ref.3, bf16[1,4,64,16,128]{4,3,2,1,0:T(8,128)(2,1)} %cached_ref.1), custom_call_target="tpu_custom_call" | custom-call | flops 1000 | bytes 1000 | tf_op jit(solution)/shard_map/pallas_call | solution.py:107
  13.2 1.3 collective-permute-start
  14.6 2.3 collective-permute-start.1
  16.9 1.1 collective-permute-start.2
  18.9 1.0 copy.15.end_ref
  19.9 6.2 %shard_map.110.own_ref = f32[2,4096,128]{2,1,0:T(8,128)} custom-call(bf16[256,4096]{1,0:T(8,128)(2,1)} %bitcast.92, bf16[256,512]{1,0:T(8,128)(2,1)} %bitcast.103, f32[4,256,16]{2,1,0:T(8,128)} %copy.15.end_ref), custom_call_target="tpu_custom_call" | custom-call | flops 268435456 | bytes 16777216 | tf_op jit(solution)/shard_map/pallas_call | solution.py:46
  26.2 0.6 fusion.2.gain_ref
  26.8 4.8 %shard_map.111 = (bf16[65,16,128]{2,1,0:T(8,128)(2,1)}, bf16[65,16,128]{2,1,0:T(8,128)(2,1)}, bf16[65,16,128]{2,1,0:T(8,128)(2,1)}, bf16[65,16,128]{2,1,0:T(8,128)(2,1)}) custom-call(s32[1]{0:T(128)} %bitcast.1.seq_ref, s32[1]{0:T(128)} %get-tuple-element.36.code_ref, f32[2,64]{1,0:T(2,128)} %copy-done.24, bf16[16,128]{1,0:T(8,128)(2,1)} %fusion.2.gain_ref, ...), custom_call_target="tpu_custom_call" | custom-call | flops 1000 | bytes 1000 | tf_op jit(solution)/shard_map/pallas_call | solution.py:146
  31.6 14.4 %collective-permute-done.1.refs_6_ = bf16[64,16,128]{2,1,0:T(8,128)(2,1)S(1)} collective-permute-done((bf16[64,16,128]{2,1,0:T(8,128)(2,1)}, bf16[64,16,128]{2,1,0:T(8,128)(2,1)S(1)}, u32[]{:S(2)}, u32[]{:S(2)}) %collective-permute-start.1) | collective-permute-done | bytes 262176 | tf_op jit(solution)/shard_map/ppermute | solution.py:480
  46.0 28.0 %collective-permute-start.3 = (bf16[65,16,128]{2,1,0:T(8,128)(2,1)}, bf16[65,16,128]{2,1,0:T(8,128)(2,1)S(1)}, u32[]{:S(2)}, u32[]{:S(2)}) collective-permute-start(bf16[65,16,128]{2,1,0:T(8,128)(2,1)} %get-tuple-element.44), channel_id=1, source_target_pairs={{0,4},{4,8},{8,12},{12,0},{1,5},{5,9},{9,13},{13,1},{2,6},{6,10},{... | collective-permute-start | bytes 798728 | tf_op jit(solution)/shard_map/ppermute | solution.py:480
  74.0 2.1 collective-permute-start.5
  76.1 8.9 %collective-permute-done.3.refs_1_ = bf16[65,16,128]{2,1,0:T(8,128)(2,1)S(1)} collective-permute-done((bf16[65,16,128]{2,1,0:T(8,128)(2,1)}, bf16[65,16,128]{2,1,0:T(8,128)(2,1)S(1)}, u32[]{:S(2)}, u32[]{:S(2)}) %collective-permute-start.3) | collective-permute-done | bytes 266272 | tf_op jit(solution)/shard_map/ppermute | solution.py:480
  85.0 15.2 %collective-permute-done.4.refs_2_ = bf16[65,16,128]{2,1,0:T(8,128)(2,1)S(1)} collective-permute-done((bf16[65,16,128]{2,1,0:T(8,128)(2,1)}, bf16[65,16,128]{2,1,0:T(8,128)(2,1)S(1)}, u32[]{:S(2)}, u32[]{:S(2)}) %collective-permute-start.4) | collective-permute-done | bytes 266272 | tf_op jit(solution)/shard_map/ppermute | solution.py:480
  100.3 2.4 collective-permute-done.5.refs_3_
  102.7 0.7 copy-done.22
  103.4 3.5 %shard_map.112 = (bf16[64,16,128]{2,1,0:T(8,128)(2,1)}, bf16[64,16,128]{2,1,0:T(8,128)(2,1)}, bf16[64,16,128]{2,1,0:T(8,128)(2,1)}, bf16[64,16,128]{2,1,0:T(8,128)(2,1)}) custom-call(s32[1]{0:T(128)} %bitcast.1.seq_ref, s32[1,4]{1,0:T(1,128)} %lengths_ref.3, s32[1,4]{1,0:T(1,128)} %slots_ref.3, bf16[1,4,64,16,128]{4,3,2,1,0:T(8,128)(2,1)} %cached_ref.1, ...), custom_call_target="tpu_custom_call" | custom-call | flops 1000 | bytes 1000 | tf_op jit(solution)/shard_map/pallas_call | solution.py:201
  106.9 19.3 %collective-permute-start.6 = (bf16[64,16,128]{2,1,0:T(8,128)(2,1)}, bf16[64,16,128]{2,1,0:T(8,128)(2,1)S(1)}, u32[]{:S(2)}, u32[]{:S(2)}) collective-permute-start(bf16[64,16,128]{2,1,0:T(8,128)(2,1)} %get-tuple-element.50), channel_id=1, source_target_pairs={{0,4},{4,8},{8,12},{12,0},{1,5},{5,9},{9,13},{13,1},{2,6},{6,10},{... | collective-permute-start | bytes 786440 | tf_op jit(solution)/shard_map/ppermute | solution.py:480
  126.2 3.1 %collective-permute-start.7 = (bf16[64,16,128]{2,1,0:T(8,128)(2,1)}, bf16[64,16,128]{2,1,0:T(8,128)(2,1)S(1)}, u32[]{:S(2)}, u32[]{:S(2)}) collective-permute-start(bf16[64,16,128]{2,1,0:T(8,128)(2,1)} %get-tuple-element.51), channel_id=1, source_target_pairs={{0,8},{4,12},{8,0},{12,4},{1,9},{5,13},{9,1},{13,5},{2,10},{6,14},... | collective-permute-start | bytes 786440 | tf_op jit(solution)/shard_map/ppermute | solution.py:480
  129.3 1.0 copy.16.run_ref
  130.3 5.7 %collective-permute-done.6.refs_1_ = bf16[64,16,128]{2,1,0:T(8,128)(2,1)S(1)} collective-permute-done((bf16[64,16,128]{2,1,0:T(8,128)(2,1)}, bf16[64,16,128]{2,1,0:T(8,128)(2,1)S(1)}, u32[]{:S(2)}, u32[]{:S(2)}) %collective-permute-start.6) | collective-permute-done | bytes 262176 | tf_op jit(solution)/shard_map/ppermute | solution.py:480
  136.0 11.7 %collective-permute-done.7.refs_2_ = bf16[64,16,128]{2,1,0:T(8,128)(2,1)S(1)} collective-permute-done((bf16[64,16,128]{2,1,0:T(8,128)(2,1)}, bf16[64,16,128]{2,1,0:T(8,128)(2,1)S(1)}, u32[]{:S(2)}, u32[]{:S(2)}) %collective-permute-start.7) | collective-permute-done | bytes 262176 | tf_op jit(solution)/shard_map/ppermute | solution.py:480
  147.8 0.7 copy-done.15
  148.5 4.9 %shard_map.113.refs_0_ = bf16[256,1024]{1,0:T(8,128)(2,1)} custom-call(s32[1]{0:T(128)} %bitcast.1.seq_ref, s32[1]{0:T(128)} %get-tuple-element.36.code_ref, f32[2,64]{1,0:T(2,128)} %copy-done.24, bf16[256,4096]{1,0:T(8,128)(2,1)} %bitcast.93, bf16[256,4096]{1,0:T(8,128)(2,1)} %bitcast.97, bf16[256,512]{1,0:T(8,128)(2,1)} %bitcast.104, ...), custom_call_target="tpu_custom_call" | custom-call | flops 1000 | bytes 1000 | tf_op jit(solution)/shard_map/pallas_call | solution.py:343
  153.4 1.3 collective-permute-start.11
  154.8 4.7 %shard_map.114.refs_2_.refs_4_ = bf16[256,1024]{1,0:T(8,128)(2,1)} custom-call(s32[1]{0:T(128)} %bitcast.1.seq_ref, s32[1]{0:T(128)} %get-tuple-element.36.code_ref, f32[2,64]{1,0:T(2,128)} %copy-done.24, bf16[256,4096]{1,0:T(8,128)(2,1)} %bitcast.94, bf16[256,4096]{1,0:T(8,128)(2,1)} %bitcast.98, bf16[256,512]{1,0:T(8,128)(2,1)} %bitcast.105, ...), custom_call_target="tpu_custom_call" | custom-call | flops 1000 | bytes 1000 | tf_op jit(solution)/shard_map/pallas_call | solution.py:343
  159.8 0.9 collective-permute-start.9
  160.7 4.7 %shard_map.115.refs_4_.refs_8_ = bf16[256,1024]{1,0:T(8,128)(2,1)} custom-call(s32[1]{0:T(128)} %bitcast.1.seq_ref, s32[1]{0:T(128)} %get-tuple-element.36.code_ref, f32[2,64]{1,0:T(2,128)} %copy-done.24, bf16[256,4096]{1,0:T(8,128)(2,1)} %bitcast.95, bf16[256,4096]{1,0:T(8,128)(2,1)} %bitcast.99, bf16[256,512]{1,0:T(8,128)(2,1)} %bitcast.106, ...), custom_call_target="tpu_custom_call" | custom-call | flops 1000 | bytes 1000 | tf_op jit(solution)/shard_map/pallas_call | solution.py:343
  165.5 4.8 %shard_map.116.refs_6_.refs_12_ = bf16[256,1024]{1,0:T(8,128)(2,1)} custom-call(s32[1]{0:T(128)} %bitcast.1.seq_ref, s32[1]{0:T(128)} %get-tuple-element.36.code_ref, f32[2,64]{1,0:T(2,128)} %copy-done.24, bf16[256,4096]{1,0:T(8,128)(2,1)} %bitcast.96, bf16[256,4096]{1,0:T(8,128)(2,1)} %bitcast.100, bf16[256,512]{1,0:T(8,128)(2,1)} %bitcast.107, ...), custom_call_target="tpu_custom_call" | custom-call | flops 1000 | bytes 1000 | tf_op jit(solution)/shard_map/pallas_call | solution.py:343
  170.3 0.6 collective-permute-start.12
  170.8 7.3 %collective-permute-done.13.refs_2_.refs_6_ = bf16[256,1024]{1,0:T(8,128)(2,1)S(1)} collective-permute-done((bf16[256,1024]{1,0:T(8,128)(2,1)}, bf16[256,1024]{1,0:T(8,128)(2,1)S(1)}, u32[]{:S(2)}, u32[]{:S(2)}) %collective-permute-start.13) | collective-permute-done | bytes 524320 | tf_op jit(solution)/shard_map/ppermute | solution.py:578
  178.2 1.1 collective-permute-start.14
  179.3 1.3 collective-permute-start.18
  180.8 0.4 collective-permute-done.14.refs_7_.refs_13_
  181.8 4.0 %shard_map.118 = bf16[512,256]{1,0:T(8,128)(2,1)} custom-call(s32[1]{0:T(128)} %bitcast.16.first_ref, bf16[256,1024]{1,0:T(8,128)(2,1)} %shard_map.113.refs_0_, bf16[256,1024]{1,0:T(8,128)(2,1)} %copy-done.4, bf16[256,1024]{1,0:T(8,128)(2,1)} %shard_map.114.refs_2_.refs_4_, bf16[256,1024]{1,0:T(8,128)(2,1)} %copy-done.5, ...), custom_call_target="tpu_custom_call" | custom-call | flops 1073741824 | bytes 6291456 | tf_op jit(solution)/shard_map/pallas_call | solution.py:414
  185.8 0.3 collective-permute-start.15
  186.1 4.0 %shard_map.117 = bf16[512,256]{1,0:T(8,128)(2,1)} custom-call(s32[1]{0:T(128)} %bitcast.first_ref, bf16[256,1024]{1,0:T(8,128)(2,1)} %shard_map.113.refs_0_, bf16[256,1024]{1,0:T(8,128)(2,1)} %copy-done.4, bf16[256,1024]{1,0:T(8,128)(2,1)} %shard_map.114.refs_2_.refs_4_, bf16[256,1024]{1,0:T(8,128)(2,1)} %copy-done.5, ...), custom_call_target="tpu_custom_call" | custom-call | flops 1073741824 | bytes 6291456 | tf_op jit(solution)/shard_map/pallas_call | solution.py:414
  190.1 0.9 collective-permute-start.16
  191.1 1.9 collective-permute-done.18.refs_4_.refs_10_
  192.9 1.2 collective-permute-start.19
  194.1 10.1 %collective-permute-done.20.refs_6_.refs_14_ = bf16[256,1024]{1,0:T(8,128)(2,1)} collective-permute-done((bf16[256,1024]{1,0:T(8,128)(2,1)}, bf16[256,1024]{1,0:T(8,128)(2,1)}, u32[]{:S(2)}, u32[]{:S(2)}) %collective-permute-start.20) | collective-permute-done | bytes 524320 | tf_op jit(solution)/shard_map/ppermute | solution.py:578
  204.2 0.8 collective-permute-start.21
  205.0 1.1 add_convert_fusion.3
  206.1 0.6 collective-permute-done.21.refs_7_.refs_15_
  207.2 0.8 copy-done.10
  208.0 4.0 %shard_map.119 = bf16[512,256]{1,0:T(8,128)(2,1)} custom-call(s32[1]{0:T(128)} %bitcast.16.first_ref, bf16[256,1024]{1,0:T(8,128)(2,1)} %copy-done.2, bf16[256,1024]{1,0:T(8,128)(2,1)} %copy-done.7, bf16[256,1024]{1,0:T(8,128)(2,1)} %copy-done.3, bf16[256,1024]{1,0:T(8,128)(2,1)} %copy-done.8, bf16[256,1024]{1,0:T(8,128)(2,1)} %collective-permute-done.18.refs_4_.refs_10_, ...), custom_call_target="tpu_custom_call" | custom-call | flops 1073741824 | bytes 6291456 | tf_op jit(solution)/shard_map/pallas_call | solution.py:414
  212.0 0.3 collective-permute-start.22
  212.3 4.0 %shard_map.120 = bf16[512,256]{1,0:T(8,128)(2,1)} custom-call(s32[1]{0:T(128)} %bitcast.first_ref, bf16[256,1024]{1,0:T(8,128)(2,1)} %copy-done.2, bf16[256,1024]{1,0:T(8,128)(2,1)} %copy-done.7, bf16[256,1024]{1,0:T(8,128)(2,1)} %copy-done.3, bf16[256,1024]{1,0:T(8,128)(2,1)} %copy-done.8, bf16[256,1024]{1,0:T(8,128)(2,1)} %collective-permute-done.18.refs_4_.refs_10_, ...), custom_call_target="tpu_custom_call" | custom-call | flops 1073741824 | bytes 6291456 | tf_op jit(solution)/shard_map/pallas_call | solution.py:414
  216.3 7.2 %all-gather.7.cloned.1.call-done = bf16[16384,128]{1,0:T(8,128)(2,1)} async-done(((bf16[4096,128]{1,0:T(8,128)(2,1)}), bf16[16384,128]{1,0:T(8,128)(2,1)}) %all-gather.7.cloned.1.call-update) | async-done | bytes 4194320 | tf_op jit(solution)/shard_map/all_gather | solution.py:566
  223.5 5.5 %shard_map.121 = (bf16[512,256]{1,0:T(8,128)(2,1)}, bf16[512,256]{1,0:T(8,128)(2,1)}) custom-call(s32[1]{0:T(128)} %bitcast.16.first_ref, bf16[256,1024]{1,0:T(8,128)(2,1)} %shard_map.113.refs_0_, bf16[256,1024]{1,0:T(8,128)(2,1)} %copy-done.4, bf16[256,1024]{1,0:T(8,128)(2,1)} %copy-done.2, bf16[256,1024]{1,0:T(8,128)(2,1)} %copy-done.7, ...), custom_call_target="tpu_custom_call" | custom-call | flops 2147483648 | bytes 10485760 | tf_op jit(solution)/shard_map/pallas_call | solution.py:414
  229.0 0.3 collective-permute-start.25
  229.4 1.3 collective-permute-start.23
  230.7 5.4 %shard_map.122 = (bf16[512,256]{1,0:T(8,128)(2,1)}, bf16[512,256]{1,0:T(8,128)(2,1)}) custom-call(s32[1]{0:T(128)} %bitcast.first_ref, bf16[256,1024]{1,0:T(8,128)(2,1)} %shard_map.113.refs_0_, bf16[256,1024]{1,0:T(8,128)(2,1)} %copy-done.4, bf16[256,1024]{1,0:T(8,128)(2,1)} %copy-done.2, bf16[256,1024]{1,0:T(8,128)(2,1)} %copy-done.7, ...), custom_call_target="tpu_custom_call" | custom-call | flops 2147483648 | bytes 10485760 | tf_op jit(solution)/shard_map/pallas_call | solution.py:414
  236.4 1.0 collective-permute-start.26
  237.4 1.0 add_convert_fusion
  238.4 0.6 collective-permute-start.27
  239.0 2.2 collective-permute-start.24
  241.2 1.4 collective-permute-done.26
  242.6 1.0 add_convert_fusion.1
  243.6 1.1 collective-permute-done.27
  244.7 2.5 collective-permute-start.28
  247.4 1.1 collective-permute-done.28
  248.9 1.0 copy-done.25
  (113 shorter events, 3.8 us)
Async XLA Ops:
  6.5 11.4 %copy-start.23 = (f32[1,256,64]{1,2,0:T(8,128)S(1)}, f32[1,256,64]{1,2,0:T(8,128)}, u32[]{:S(2)}) copy-start(f32[1,256,64]{1,2,0:T(8,128)} %param.16) | copy-start | bytes 196612
  6.5 174.6 %all-gather.5.cloned.1.call-start = ((), (), s32[]{:S(2)}) async-start(), calls=%async_computation | async-start | bytes 5242880 | tf_op jit(solution)/shard_map/all_gather | solution.py:566
  6.5 12.2 %copy-start.18 = (f32[1,256,64]{1,2,0:T(8,128)S(1)}, f32[1,256,64]{1,2,0:T(8,128)}, u32[]{:S(2)}) copy-start(f32[1,256,64]{1,2,0:T(8,128)} %param.15) | copy-start | bytes 196612
  9.6 213.9 %all-gather.7.cloned.1.call-start = ((), (), s32[]{:S(2)}) async-start(), calls=%async_computation.1 | async-start | bytes 5242880 | tf_op jit(solution)/shard_map/all_gather | solution.py:566
  13.2 18.3 %collective-permute-start = (bf16[64,16,128]{2,1,0:T(8,128)(2,1)}, bf16[64,16,128]{2,1,0:T(8,128)(2,1)S(1)}, u32[]{:S(2)}, u32[]{:S(2)}) collective-permute-start(bf16[64,16,128]{2,1,0:T(8,128)(2,1)} %get-tuple-element.39), channel_id=1, source_target_pairs={{0,4},{4,8},{8,12},{12,0},{1,5},{5,9},{9,13},{13,1},{2,6},{6,10},{... | collective-permute-start | bytes 786440 | tf_op jit(solution)/shard_map/ppermute | solution.py:480
  14.6 31.4 %collective-permute-start.1 = (bf16[64,16,128]{2,1,0:T(8,128)(2,1)}, bf16[64,16,128]{2,1,0:T(8,128)(2,1)S(1)}, u32[]{:S(2)}, u32[]{:S(2)}) collective-permute-start(bf16[64,16,128]{2,1,0:T(8,128)(2,1)} %get-tuple-element.40), channel_id=1, source_target_pairs={{0,8},{4,12},{8,0},{12,4},{1,9},{5,13},{9,1},{13,5},{2,10},{6,14},... | collective-permute-start | bytes 786440 | tf_op jit(solution)/shard_map/ppermute | solution.py:480
  16.9 29.1 %collective-permute-start.2 = (bf16[64,16,128]{2,1,0:T(8,128)(2,1)}, bf16[64,16,128]{2,1,0:T(8,128)(2,1)S(1)}, u32[]{:S(2)}, u32[]{:S(2)}) collective-permute-start(bf16[64,16,128]{2,1,0:T(8,128)(2,1)} %get-tuple-element.41), channel_id=1, source_target_pairs={{0,12},{4,0},{8,4},{12,8},{1,13},{5,1},{9,5},{13,9},{2,14},{6,2},{... | collective-permute-start | bytes 786440 | tf_op jit(solution)/shard_map/ppermute | solution.py:480
  18.4 8.4 %copy-start.24 = (f32[2,64]{1,0:T(2,128)}, f32[2,64]{1,0:T(2,128)S(1)}, u32[]{:S(2)}) copy-start(f32[2,64]{1,0:T(2,128)S(1)} %exp.8.total_ref) | copy-start | bytes 1540
  18.5 110.8 %copy-start.17 = (f32[256,4,16]{0,2,1:T(8,128)}, f32[256,4,16]{0,2,1:T(8,128)S(1)}, u32[]{:S(2)}) copy-start(f32[256,4,16]{0,2,1:T(8,128)S(1)} %reshape.116) | copy-start | bytes 196612
  31.6 116.1 %copy-start.11 = (bf16[64,16,128]{2,1,0:T(8,128)(2,1)}, bf16[64,16,128]{2,1,0:T(8,128)(2,1)S(1)}, u32[]{:S(2)}) copy-start(bf16[64,16,128]{2,1,0:T(8,128)(2,1)S(1)} %collective-permute-done.refs_5_) | copy-start | bytes 786436
  46.0 101.7 %copy-start.12 = (bf16[64,16,128]{2,1,0:T(8,128)(2,1)}, bf16[64,16,128]{2,1,0:T(8,128)(2,1)S(1)}, u32[]{:S(2)}) copy-start(bf16[64,16,128]{2,1,0:T(8,128)(2,1)S(1)} %collective-permute-done.1.refs_6_) | copy-start | bytes 786436
  46.0 101.7 %copy-start.13 = (bf16[64,16,128]{2,1,0:T(8,128)(2,1)}, bf16[64,16,128]{2,1,0:T(8,128)(2,1)S(1)}, u32[]{:S(2)}) copy-start(bf16[64,16,128]{2,1,0:T(8,128)(2,1)S(1)} %collective-permute-done.2.refs_7_) | copy-start | bytes 786436
  46.0 39.0 %collective-permute-start.3 = (bf16[65,16,128]{2,1,0:T(8,128)(2,1)}, bf16[65,16,128]{2,1,0:T(8,128)(2,1)S(1)}, u32[]{:S(2)}, u32[]{:S(2)}) collective-permute-start(bf16[65,16,128]{2,1,0:T(8,128)(2,1)} %get-tuple-element.44), channel_id=1, source_target_pairs={{0,4},{4,8},{8,12},{12,0},{1,5},{5,9},{9,13},{13,1},{2,6},{6,10},{... | collective-permute-start | bytes 798728 | tf_op jit(solution)/shard_map/ppermute | solution.py:480
  74.0 26.2 %collective-permute-start.4 = (bf16[65,16,128]{2,1,0:T(8,128)(2,1)}, bf16[65,16,128]{2,1,0:T(8,128)(2,1)S(1)}, u32[]{:S(2)}, u32[]{:S(2)}) collective-permute-start(bf16[65,16,128]{2,1,0:T(8,128)(2,1)} %get-tuple-element.46), channel_id=1, source_target_pairs={{0,8},{4,12},{8,0},{12,4},{1,9},{5,13},{9,1},{13,5},{2,10},{6,14},... | collective-permute-start | bytes 798728 | tf_op jit(solution)/shard_map/ppermute | solution.py:480
  74.0 28.6 %collective-permute-start.5 = (bf16[65,16,128]{2,1,0:T(8,128)(2,1)}, bf16[65,16,128]{2,1,0:T(8,128)(2,1)S(1)}, u32[]{:S(2)}, u32[]{:S(2)}) collective-permute-start(bf16[65,16,128]{2,1,0:T(8,128)(2,1)} %get-tuple-element.48), channel_id=1, source_target_pairs={{0,12},{4,0},{8,4},{12,8},{1,13},{5,1},{9,5},{13,9},{2,14},{6,2},{... | collective-permute-start | bytes 798728 | tf_op jit(solution)/shard_map/ppermute | solution.py:480
  85.0 17.6 %copy-start.20 = (bf16[65,16,128]{2,1,0:T(8,128)(2,1)}, bf16[65,16,128]{2,1,0:T(8,128)(2,1)S(1)}, u32[]{:S(2)}) copy-start(bf16[65,16,128]{2,1,0:T(8,128)(2,1)S(1)} %collective-permute-done.3.refs_1_) | copy-start | bytes 798724
  100.3 2.4 copy-start.21
  102.7 0.7 copy-start.22
  106.9 29.1 %collective-permute-start.6 = (bf16[64,16,128]{2,1,0:T(8,128)(2,1)}, bf16[64,16,128]{2,1,0:T(8,128)(2,1)S(1)}, u32[]{:S(2)}, u32[]{:S(2)}) collective-permute-start(bf16[64,16,128]{2,1,0:T(8,128)(2,1)} %get-tuple-element.50), channel_id=1, source_target_pairs={{0,4},{4,8},{8,12},{12,0},{1,5},{5,9},{9,13},{13,1},{2,6},{6,10},{... | collective-permute-start | bytes 786440 | tf_op jit(solution)/shard_map/ppermute | solution.py:480
  126.2 21.5 %collective-permute-start.7 = (bf16[64,16,128]{2,1,0:T(8,128)(2,1)}, bf16[64,16,128]{2,1,0:T(8,128)(2,1)S(1)}, u32[]{:S(2)}, u32[]{:S(2)}) collective-permute-start(bf16[64,16,128]{2,1,0:T(8,128)(2,1)} %get-tuple-element.51), channel_id=1, source_target_pairs={{0,8},{4,12},{8,0},{12,4},{1,9},{5,13},{9,1},{13,5},{2,10},{6,14},... | collective-permute-start | bytes 786440 | tf_op jit(solution)/shard_map/ppermute | solution.py:480
  129.3 18.4 %collective-permute-start.8 = (bf16[64,16,128]{2,1,0:T(8,128)(2,1)}, bf16[64,16,128]{2,1,0:T(8,128)(2,1)S(1)}, u32[]{:S(2)}, u32[]{:S(2)}) collective-permute-start(bf16[64,16,128]{2,1,0:T(8,128)(2,1)} %get-tuple-element.52), channel_id=1, source_target_pairs={{0,12},{4,0},{8,4},{12,8},{1,13},{5,1},{9,5},{13,9},{2,14},{6,2},{... | collective-permute-start | bytes 786440 | tf_op jit(solution)/shard_map/ppermute | solution.py:480
  136.0 11.8 %copy-start.14 = (bf16[64,16,128]{2,1,0:T(8,128)(2,1)}, bf16[64,16,128]{2,1,0:T(8,128)(2,1)S(1)}, u32[]{:S(2)}) copy-start(bf16[64,16,128]{2,1,0:T(8,128)(2,1)S(1)} %collective-permute-done.6.refs_1_) | copy-start | bytes 786436
  147.7 0.7 copy-start.15
  147.7 0.8 copy-start.16
  153.4 6.3 %copy-start = (bf16[256,1024]{1,0:T(8,128)(2,1)S(1)}, bf16[256,1024]{1,0:T(8,128)(2,1)}, u32[]{:S(2)}) copy-start(bf16[256,1024]{1,0:T(8,128)(2,1)} %shard_map.113.refs_0_) | copy-start | bytes 1572868
  153.4 16.8 %collective-permute-start.11 = (bf16[256,1024]{1,0:T(8,128)(2,1)}, bf16[256,1024]{1,0:T(8,128)(2,1)S(1)}, u32[]{:S(2)}, u32[]{:S(2)}) collective-permute-start(bf16[256,1024]{1,0:T(8,128)(2,1)} %shard_map.113.refs_0_), channel_id=1, source_target_pairs={{0,16},{16,0},{1,17},{17,1},{2,18},{18,2},{3,19},{19,3},{4,20},{20... | collective-permute-start | bytes 1572872 | tf_op jit(solution)/shard_map/ppermute | solution.py:578
  159.5 18.7 %collective-permute-start.13 = (bf16[256,1024]{1,0:T(8,128)(2,1)}, bf16[256,1024]{1,0:T(8,128)(2,1)S(1)}, u32[]{:S(2)}, u32[]{:S(2)}) collective-permute-start(bf16[256,1024]{1,0:T(8,128)(2,1)} %shard_map.114.refs_2_.refs_4_), channel_id=1, source_target_pairs={{0,16},{16,0},{1,17},{17,1},{2,18},{18,2},{3,19},{19,3},{4,20},{20... | collective-permute-start | bytes 1572872 | tf_op jit(solution)/shard_map/ppermute | solution.py:578
  159.8 20.8 %collective-permute-start.9 = (bf16[256,1024]{1,0:T(8,128)(2,1)S(1)}, bf16[256,1024]{1,0:T(8,128)(2,1)S(1)}, u32[]{:S(2)}, u32[]{:S(2)}) collective-permute-start(bf16[256,1024]{1,0:T(8,128)(2,1)S(1)} %copy-done), channel_id=1, source_target_pairs={{0,1},{1,0},{2,3},{3,2},{4,5},{5,4},{6,7},{7,6},{8,9},{9,8},{10,11... | collective-permute-start | bytes 1572872 | tf_op jit(solution)/shard_map/ppermute | solution.py:582
  160.7 20.0 %collective-permute-start.10 = (bf16[256,1024]{1,0:T(8,128)(2,1)}, bf16[256,1024]{1,0:T(8,128)(2,1)S(1)}, u32[]{:S(2)}, u32[]{:S(2)}) collective-permute-start(bf16[256,1024]{1,0:T(8,128)(2,1)} %shard_map.114.refs_2_.refs_4_), channel_id=1, source_target_pairs={{0,1},{1,0},{2,3},{3,2},{4,5},{5,4},{6,7},{7,6},{8,9},{9,8},{10,11... | collective-permute-start | bytes 1572872 | tf_op jit(solution)/shard_map/ppermute | solution.py:582
  165.4 4.8 %copy-start.1 = (bf16[256,1024]{1,0:T(8,128)(2,1)S(1)}, bf16[256,1024]{1,0:T(8,128)(2,1)}, u32[]{:S(2)}) copy-start(bf16[256,1024]{1,0:T(8,128)(2,1)} %shard_map.115.refs_4_.refs_8_) | copy-start | bytes 1572868
  170.3 19.8 %copy-start.2 = (bf16[256,1024]{1,0:T(8,128)(2,1)}, bf16[256,1024]{1,0:T(8,128)(2,1)S(1)}, u32[]{:S(2)}) copy-start(bf16[256,1024]{1,0:T(8,128)(2,1)S(1)} %collective-permute-done.11.refs_0_.refs_2_) | copy-start | bytes 1572868
  170.3 10.5 %collective-permute-start.12 = (bf16[256,1024]{1,0:T(8,128)(2,1)S(1)}, bf16[256,1024]{1,0:T(8,128)(2,1)S(1)}, u32[]{:S(2)}, u32[]{:S(2)}) collective-permute-start(bf16[256,1024]{1,0:T(8,128)(2,1)S(1)} %copy-done.1), channel_id=1, source_target_pairs={{0,1},{1,0},{2,3},{3,2},{4,5},{5,4},{6,7},{7,6},{8,9},{9,8},{10,11... | collective-permute-start | bytes 1572872 | tf_op jit(solution)/shard_map/ppermute | solution.py:582
  178.1 12.8 %copy-start.3 = (bf16[256,1024]{1,0:T(8,128)(2,1)}, bf16[256,1024]{1,0:T(8,128)(2,1)S(1)}, u32[]{:S(2)}) copy-start(bf16[256,1024]{1,0:T(8,128)(2,1)S(1)} %collective-permute-done.13.refs_2_.refs_6_) | copy-start | bytes 1572868
  178.2 3.0 %collective-permute-start.14 = (bf16[256,1024]{1,0:T(8,128)(2,1)}, bf16[256,1024]{1,0:T(8,128)(2,1)}, u32[]{:S(2)}, u32[]{:S(2)}) collective-permute-start(bf16[256,1024]{1,0:T(8,128)(2,1)} %shard_map.116.refs_6_.refs_12_), channel_id=1, source_target_pairs={{0,1},{1,0},{2,3},{3,2},{4,5},{5,4},{6,7},{7,6},{8,9},{9,8},{10,11... | collective-permute-start | bytes 1572872 | tf_op jit(solution)/shard_map/ppermute | solution.py:582
  179.3 13.7 %collective-permute-start.18 = (bf16[256,1024]{1,0:T(8,128)(2,1)S(1)}, bf16[256,1024]{1,0:T(8,128)(2,1)}, u32[]{:S(2)}, u32[]{:S(2)}) collective-permute-start(bf16[256,1024]{1,0:T(8,128)(2,1)S(1)} %copy-done.1), channel_id=1, source_target_pairs={{0,16},{16,0},{1,17},{17,1},{2,18},{18,2},{3,19},{19,3},{4,20},{20... | collective-permute-start | bytes 1572872 | tf_op jit(solution)/shard_map/ppermute | solution.py:578
  180.5 0.8 copy-start.4
  180.5 23.6 %collective-permute-start.20 = (bf16[256,1024]{1,0:T(8,128)(2,1)}, bf16[256,1024]{1,0:T(8,128)(2,1)}, u32[]{:S(2)}, u32[]{:S(2)}) collective-permute-start(bf16[256,1024]{1,0:T(8,128)(2,1)} %shard_map.116.refs_6_.refs_12_), channel_id=1, source_target_pairs={{0,16},{16,0},{1,17},{17,1},{2,18},{18,2},{3,19},{19,3},{4,20},{20... | collective-permute-start | bytes 1572872 | tf_op jit(solution)/shard_map/ppermute | solution.py:578
  180.8 0.8 copy-start.5
  180.8 1.0 copy-start.6
  185.8 19.2 %collective-permute-start.15 = (bf16[512,256]{1,0:T(8,128)(2,1)}, bf16[512,256]{1,0:T(8,128)(2,1)}, u32[]{:S(2)}, u32[]{:S(2)}) collective-permute-start(bf16[512,256]{1,0:T(8,128)(2,1)} %shard_map.118), channel_id=1, source_target_pairs={{0,2},{2,0},{1,3},{3,1},{4,6},{6,4},{5,7},{7,5},{8,10},{10,8},{9,1... | collective-permute-start | bytes 786440 | tf_op jit(solution)/shard_map/ppermute | solution.py:443
  190.1 16.0 %collective-permute-start.16 = (bf16[256,1024]{1,0:T(8,128)(2,1)S(1)}, bf16[256,1024]{1,0:T(8,128)(2,1)S(1)}, u32[]{:S(2)}, u32[]{:S(2)}) collective-permute-start(bf16[256,1024]{1,0:T(8,128)(2,1)S(1)} %collective-permute-done.11.refs_0_.refs_2_), channel_id=1, source_target_pairs={{0,1},{1,0},{2,3},{3,2},{4,5},{5,4},{6,7},{7,6},{8,9},{9,8},{10,11... | collective-permute-start | bytes 1572872 | tf_op jit(solution)/shard_map/ppermute | solution.py:588
  191.0 15.1 %collective-permute-start.17 = (bf16[256,1024]{1,0:T(8,128)(2,1)S(1)}, bf16[256,1024]{1,0:T(8,128)(2,1)S(1)}, u32[]{:S(2)}, u32[]{:S(2)}) collective-permute-start(bf16[256,1024]{1,0:T(8,128)(2,1)S(1)} %collective-permute-done.13.refs_2_.refs_6_), channel_id=1, source_target_pairs={{0,1},{1,0},{2,3},{3,2},{4,5},{5,4},{6,7},{7,6},{8,9},{9,8},{10,11... | collective-permute-start | bytes 1572872 | tf_op jit(solution)/shard_map/ppermute | solution.py:588
  192.9 13.2 %collective-permute-start.19 = (bf16[256,1024]{1,0:T(8,128)(2,1)}, bf16[256,1024]{1,0:T(8,128)(2,1)S(1)}, u32[]{:S(2)}, u32[]{:S(2)}) collective-permute-start(bf16[256,1024]{1,0:T(8,128)(2,1)} %collective-permute-done.18.refs_4_.refs_10_), channel_id=1, source_target_pairs={{0,1},{1,0},{2,3},{3,2},{4,5},{5,4},{6,7},{7,6},{8,9},{9,8},{10,11... | collective-permute-start | bytes 1572872 | tf_op jit(solution)/shard_map/ppermute | solution.py:588
  204.2 2.5 collective-permute-start.21
  206.1 0.8 copy-start.7
  206.1 0.9 copy-start.8
  206.1 1.1 copy-start.9
  207.2 0.8 copy-start.10
  212.0 17.3 %collective-permute-start.22 = (bf16[512,256]{1,0:T(8,128)(2,1)}, bf16[512,256]{1,0:T(8,128)(2,1)S(1)}, u32[]{:S(2)}, u32[]{:S(2)}) collective-permute-start(bf16[512,256]{1,0:T(8,128)(2,1)} %shard_map.119), channel_id=1, source_target_pairs={{0,2},{2,0},{1,3},{3,1},{4,6},{6,4},{5,7},{7,5},{8,10},{10,8},{9,1... | collective-permute-start | bytes 786440 | tf_op jit(solution)/shard_map/ppermute | solution.py:442
  223.5 5.8 %copy-start.19 = (bf16[512,256]{1,0:T(8,128)(2,1)S(1)}, bf16[512,256]{1,0:T(8,128)(2,1)}, u32[]{:S(2)}) copy-start(bf16[512,256]{1,0:T(8,128)(2,1)} %shard_map.120) | copy-start | bytes 786436
  229.0 7.4 %collective-permute-start.25 = (bf16[512,256]{1,0:T(8,128)(2,1)}, bf16[512,256]{1,0:T(8,128)(2,1)S(1)}, u32[]{:S(2)}, u32[]{:S(2)}) collective-permute-start(bf16[512,256]{1,0:T(8,128)(2,1)} %get-tuple-element.62), channel_id=1, source_target_pairs={{0,2},{2,0},{1,3},{3,1},{4,6},{6,4},{5,7},{7,5},{8,10},{10,8},{9,1... | collective-permute-start | bytes 786440 | tf_op jit(solution)/shard_map/ppermute | solution.py:442
  229.4 7.0 %copy-start.26 = (bf16[512,256]{1,0:T(8,128)(2,1)S(1)}, bf16[512,256]{1,0:T(8,128)(2,1)}, u32[]{:S(2)}) copy-start(bf16[512,256]{1,0:T(8,128)(2,1)} %get-tuple-element.65) | copy-start | bytes 786436
  229.4 9.5 %collective-permute-start.23 = (bf16[512,256]{1,0:T(8,128)(2,1)S(1)}, bf16[512,256]{1,0:T(8,128)(2,1)S(1)}, u32[]{:S(2)}, u32[]{:S(2)}) collective-permute-start(bf16[512,256]{1,0:T(8,128)(2,1)S(1)} %add_convert_fusion.2), channel_id=1, source_target_pairs={{0,16},{16,0},{1,17},{17,1},{2,18},{18,2},{3,19},{19,3},{4,20},{20... | collective-permute-start | bytes 786440 | tf_op jit(solution)/shard_map/ppermute | solution.py:446
  236.4 6.2 %collective-permute-start.26 = (bf16[512,256]{1,0:T(8,128)(2,1)S(1)}, bf16[512,256]{1,0:T(8,128)(2,1)S(1)}, u32[]{:S(2)}, u32[]{:S(2)}) collective-permute-start(bf16[512,256]{1,0:T(8,128)(2,1)S(1)} %copy-done.26), channel_id=1, source_target_pairs={{0,2},{2,0},{1,3},{3,1},{4,6},{6,4},{5,7},{7,5},{8,10},{10,8},{9,1... | collective-permute-start | bytes 786440 | tf_op jit(solution)/shard_map/ppermute | solution.py:443
  238.4 6.3 %collective-permute-start.27 = (bf16[512,256]{1,0:T(8,128)(2,1)S(1)}, bf16[512,256]{1,0:T(8,128)(2,1)S(1)}, u32[]{:S(2)}, u32[]{:S(2)}) collective-permute-start(bf16[512,256]{1,0:T(8,128)(2,1)S(1)} %add_convert_fusion), channel_id=1, source_target_pairs={{0,16},{16,0},{1,17},{17,1},{2,18},{18,2},{3,19},{19,3},{4,20},{20... | collective-permute-start | bytes 786440 | tf_op jit(solution)/shard_map/ppermute | solution.py:446
  239.0 8.3 %collective-permute-start.24 = (bf16[2,256,256]{2,1,0:T(8,128)(2,1)S(1)}, bf16[2,256,256]{2,1,0:T(8,128)(2,1)S(1)}, u32[]{:S(2)}, u32[]{:S(2)}) collective-permute-start(bf16[2,256,256]{2,1,0:T(8,128)(2,1)S(1)} %pad_maximum_fusion), channel_id=1, source_target_pairs={{0,1},{1,0},{2,3},{3,2},{4,5},{5,4},{6,7},{7,6},{8,9},{9,8},{10,11... | collective-permute-start | bytes 786440 | tf_op jit(solution)/shard_map/ppermute | solution.py:448
  244.7 3.7 %collective-permute-start.28 = (bf16[2,256,256]{2,1,0:T(8,128)(2,1)S(1)}, bf16[2,256,256]{2,1,0:T(8,128)(2,1)S(1)}, u32[]{:S(2)}, u32[]{:S(2)}) collective-permute-start(bf16[2,256,256]{2,1,0:T(8,128)(2,1)S(1)} %pad_maximum_fusion.1), channel_id=1, source_target_pairs={{0,1},{1,0},{2,3},{3,2},{4,5},{5,4},{6,7},{7,6},{8,9},{9,8},{10,11... | collective-permute-start | bytes 786440 | tf_op jit(solution)/shard_map/ppermute | solution.py:448
  248.9 1.0 copy-start.25
Sparse Core Ops, SparseCore 0:
  9.7 132.8 all-gather.4
  144.2 79.2 all-gather.6

commit v6 on v5

--- a/solution.py
+++ b/solution.py
@@ -383,9 +383,9 @@
                 rows_all.at[part, pl.ds(r * tokens, tokens)],
                 sems.at[0, part],
             ).start()
-        for n in range(2):
+        for n in range(weight.shape[2] // cols):
             pltpu.make_async_copy(
-                weights.at[first_ref[0] + n, span],
+                weights.at[first_ref[n // 2] + n % 2, span],
                 weight.at[part, :, pl.ds(n * cols, cols)],
                 sems.at[1, part],
             ).start()
@@ -400,35 +400,40 @@
             elif part < parts - 1:
                 total[span, :] += product
             else:
-                each = count // outs
+                product = (total[span, :] + product).astype(BF)
+                wide = product.shape[1] // (2 * cols)
+                each = count // (outs // wide)
                 place = pl.ds(r % each * tokens, tokens)
-                out_refs[r // each][place, :] = (total[span, :] + product).astype(BF)
-
-
-def project(first, lhs, weights, outs):
+                for n in range(wide):
+                    out_refs[r // each + n][place, :] = product[:, 2 * n * cols : 2 * (n + 1) * cols]
+
+
+def project(firsts, lhs, weights, outs):
     parts = len(lhs)
     flat = [rows for part in lhs for rows in part]
     tokens = len(lhs[0]) * flat[0].shape[0]
     depth, cols = weights.shape[1:]
+    width = 2 * cols * len(firsts)
+    rows = tokens if len(firsts) > 1 else tokens // outs
     hbm = pl.BlockSpec(memory_space=pl.ANY)
     return pl.pallas_call(
         functools.partial(project_kernel, outs),
         in_specs=[pl.BlockSpec(memory_space=pltpu.SMEM)] + [hbm] * (len(flat) + 1),
         out_specs=[pl.BlockSpec(memory_space=pltpu.VMEM)] * outs,
-        out_shape=[jax.ShapeDtypeStruct((tokens // outs, 2 * cols), BF)] * outs,
+        out_shape=[jax.ShapeDtypeStruct((rows, 2 * cols), BF)] * outs,
         scratch_shapes=[
             pltpu.VMEM((parts, tokens, depth // parts), BF),
-            pltpu.VMEM((parts, depth // parts, 2 * cols), BF),
-            pltpu.VMEM((tokens, 2 * cols), F32),
+            pltpu.VMEM((parts, depth // parts, width), BF),
+            pltpu.VMEM((tokens, width), F32),
             pltpu.SemaphoreType.DMA((2, parts)),
         ],
         compiler_params=pltpu.CompilerParams(vmem_limit_bytes=VMEM_LIMIT),
         cost_estimate=pl.CostEstimate(
-            flops=4 * tokens * depth * cols,
-            bytes_accessed=2 * depth * (tokens + 2 * cols),
+            flops=2 * tokens * depth * width,
+            bytes_accessed=2 * depth * (tokens + width),
             transcendentals=0,
         ),
-    )(first.reshape(1), *flat, weights)
+    )(jnp.stack(firsts), *flat, weights)
 
 
 SWAP = [(0, 1), (1, 0)]
@@ -442,6 +447,8 @@
     far = lax.ppermute(others[1], "head", SWAP)
     near = lax.ppermute(others[0] if near_first else after(others[0], far), "head", SWAP)
     far = (own[1].astype(F32) + far.astype(F32)).astype(BF)
+    if near_first:
+        near = after(near, own[1])
     near = (own[0].astype(F32) + near.astype(F32)).astype(BF)
     from_y = lax.ppermute(far, "groups", SWAP).reshape(2, tokens, -1)
     near = near.reshape(2, tokens, -1)
@@ -580,20 +587,19 @@
     for n, part in enumerate(normed):
         tied = after(part, *crossed[max(n - 2, 0) : n - 1]) if n > 1 else part
         near.append([part, lax.ppermute(tied, "batch", SWAP)])
-    near_others = project(theirs, near, weights[0], 1)
-    near_mine = project(mine, near, weights[0], 1)
+    (near_others,) = project([theirs], near, weights[0], 1)
+    (near_mine,) = project([mine], near, weights[0], 1)
     far = []
     for across in crossed:
-        across = after(across, *near_mine)
+        across = after(across, near_mine)
         far.append([across, lax.ppermute(across, "batch", SWAP)])
-    far_others = project(theirs, far, weights[0], 1)
+    far_others, far_mine = project([theirs, mine], far, weights[0], 2)
     lhs = [a + b for a, b in zip(near, far)]
-    far_mine = project(mine, far, after(weights[0], *far_others), 1)
-    last = after(weights[1], *far_mine)
-    last_others = project(theirs, lhs, last, 2)
-    last_mine = project(mine, lhs, after(last, *last_others), 2)
+    last = after(weights[1], far_mine)
+    last_others = project([theirs], lhs, last, 2)
+    last_mine = project([mine], lhs, after(last, *last_others), 2)
     sides = [
-        in_order(y, core, to_rows(near_mine + far_mine, near_others + far_others, tokens, True)),
+        in_order(y, core, to_rows([near_mine, far_mine], [near_others, far_others], tokens, True)),
         in_order(y, core, to_rows(last_mine, last_others, tokens, False)),
     ]
     pieces = [

time: 259 us -> 259 us (level)
  Pallas kernels: 63.3 us -> 60.5 us
    ppermute x4, waiting for transfers between devices: 19.2 us -> 23.8 us  [body(): crossed = [lax.ppermute(part, 'groups', SWAP) for part in normed]]
    pallas_call x6 -> x5, Pallas kernels: 26.7 us -> 24.4 us  [project(): pl.pallas_call(functools.partial(project_kernel, outs), in_specs=[pl.Bloc...]
    unnamed x69 -> x71, local copies, waits for them, and re-layouts: 4.73 us -> 5.55 us
  transfers between devices with their start and end apart: 31 -> 31, of which waited for: 16 -> 15; matrix products, arithmetic and copies ran while one was open for 3% -> 3% of each run, Pallas kernels for 25% -> 24%
where the time goes in v6:
time: 259 us; the launch traced here: 257 us
  waiting for transfers between devices  92 us (36%)
  starting transfers between devices  75.2 us (29%)
  Pallas kernels  60.5 us (23%)
  between operations  13.9 us (5%)
  local copies, waits for them, and re-layouts  11.2 us (4%)
  other arithmetic  3.9 us (2%)
    ppermute x9, waiting for transfers between devices, exchange_states(): lax.ppermute(piece, 'seq', [(i, (i + offset) % size) for i in range(size)])  58.7 us
    ppermute x9, starting transfers between devices, exchange_states(): lax.ppermute(piece, 'seq', [(i, (i + offset) % size) for i in range(size)])  57.2 us
    pallas_call x5, Pallas kernels, project(): pl.pallas_call(functools.partial(project_kernel, outs), in_specs=[pl.Bloc...  24.4 us
    ppermute x4, waiting for transfers between devices, body(): crossed = [lax.ppermute(part, 'groups', SWAP) for part in normed]  23.8 us
    pallas_call x4, Pallas kernels, mix_groups(): pl.pallas_call(functools.partial(mix_kernel, place, size), grid=(1, token...  19 us
    pallas_call x1, Pallas kernels, block_states_of(): pl.pallas_call(states_kernel, grid=(groups_dev,), in_specs=[pl.BlockSpec(...  6.16 us
    unnamed x71, local copies, waits for them, and re-layouts  5.55 us
  transfers between devices with their start and end apart: 31, of which 15 were waited for; matrix products, arithmetic and copies ran while one was open for 3% of the time, Pallas kernels for 24%

profile of v6, /device:TPU:3, one launch (start us, length us, event | category | flops | bytes accessed | tf_op | source)
XLA Modules:
  0.0 256.8 jit_solution(17024792662924416880)
XLA Ops:
  6.5 3.1 %constant_dynamic-slice_fusion = (bf16[4096,128]{1,0:T(8,128)(2,1)}, bf16[4096,128]{1,0:T(8,128)(2,1)}) fusion(bf16[4096,1024]{1,0:T(8,128)(2,1)} %param.21, s32[]{:T(128)S(6)} %select_n.82, s32[]{:T(128)S(6)} %select_n.78), kind=kLoop, calls=%fused_computation.55 | loop fusion | bytes 4194312 | tf_op jit(solution)/shard_map/dynamic_slice | solution.py:550
  9.7 0.7 all-gather.7.cloned.1.call-update
  10.4 2.9 %shard_map.109 = (bf16[64,16,128]{2,1,0:T(8,128)(2,1)}, bf16[64,16,128]{2,1,0:T(8,128)(2,1)}, bf16[64,16,128]{2,1,0:T(8,128)(2,1)}, bf16[64,16,128]{2,1,0:T(8,128)(2,1)}, s32[1]{0:T(128)}) custom-call(s32[1]{0:T(128)} %bitcast.1.seq_ref, s32[1,4]{1,0:T(1,128)} %lengths_ref.3, s32[1,4]{1,0:T(1,128)} %slots_ref.3, bf16[1,4,64,16,128]{4,3,2,1,0:T(8,128)(2,1)} %cached_ref.1), custom_call_target="tpu_custom_call" | custom-call | flops 1000 | bytes 1000 | tf_op jit(solution)/shard_map/pallas_call | solution.py:107
  13.3 1.3 collective-permute-start
  14.6 2.3 collective-permute-start.1
  17.0 1.0 collective-permute-start.2
  18.9 1.0 copy.15.end_ref
  19.9 6.2 %shard_map.110.own_ref = f32[2,4096,128]{2,1,0:T(8,128)} custom-call(bf16[256,4096]{1,0:T(8,128)(2,1)} %bitcast.88, bf16[256,512]{1,0:T(8,128)(2,1)} %bitcast.102, f32[4,256,16]{2,1,0:T(8,128)} %copy.15.end_ref), custom_call_target="tpu_custom_call" | custom-call | flops 268435456 | bytes 16777216 | tf_op jit(solution)/shard_map/pallas_call | solution.py:46
  26.2 0.6 fusion.2.gain_ref
  26.8 4.8 %shard_map.111 = (bf16[65,16,128]{2,1,0:T(8,128)(2,1)}, bf16[65,16,128]{2,1,0:T(8,128)(2,1)}, bf16[65,16,128]{2,1,0:T(8,128)(2,1)}, bf16[65,16,128]{2,1,0:T(8,128)(2,1)}) custom-call(s32[1]{0:T(128)} %bitcast.1.seq_ref, s32[1]{0:T(128)} %get-tuple-element.38.code_ref, f32[2,64]{1,0:T(2,128)} %copy-done.25, bf16[16,128]{1,0:T(8,128)(2,1)} %fusion.2.gain_ref, ...), custom_call_target="tpu_custom_call" | custom-call | flops 1000 | bytes 1000 | tf_op jit(solution)/shard_map/pallas_call | solution.py:146
  31.5 14.5 %collective-permute-done.1.refs_6_ = bf16[64,16,128]{2,1,0:T(8,128)(2,1)S(1)} collective-permute-done((bf16[64,16,128]{2,1,0:T(8,128)(2,1)}, bf16[64,16,128]{2,1,0:T(8,128)(2,1)S(1)}, u32[]{:S(2)}, u32[]{:S(2)}) %collective-permute-start.1) | collective-permute-done | bytes 262176 | tf_op jit(solution)/shard_map/ppermute | solution.py:487
  46.1 28.0 %collective-permute-start.3 = (bf16[65,16,128]{2,1,0:T(8,128)(2,1)}, bf16[65,16,128]{2,1,0:T(8,128)(2,1)S(1)}, u32[]{:S(2)}, u32[]{:S(2)}) collective-permute-start(bf16[65,16,128]{2,1,0:T(8,128)(2,1)} %get-tuple-element.46), channel_id=1, source_target_pairs={{0,4},{4,8},{8,12},{12,0},{1,5},{5,9},{9,13},{13,1},{2,6},{6,10},{... | collective-permute-start | bytes 798728 | tf_op jit(solution)/shard_map/ppermute | solution.py:487
  74.1 2.1 collective-permute-start.5
  76.2 8.9 %collective-permute-done.3.refs_1_ = bf16[65,16,128]{2,1,0:T(8,128)(2,1)S(1)} collective-permute-done((bf16[65,16,128]{2,1,0:T(8,128)(2,1)}, bf16[65,16,128]{2,1,0:T(8,128)(2,1)S(1)}, u32[]{:S(2)}, u32[]{:S(2)}) %collective-permute-start.3) | collective-permute-done | bytes 266272 | tf_op jit(solution)/shard_map/ppermute | solution.py:487
  85.1 15.2 %collective-permute-done.4.refs_2_ = bf16[65,16,128]{2,1,0:T(8,128)(2,1)S(1)} collective-permute-done((bf16[65,16,128]{2,1,0:T(8,128)(2,1)}, bf16[65,16,128]{2,1,0:T(8,128)(2,1)S(1)}, u32[]{:S(2)}, u32[]{:S(2)}) %collective-permute-start.4) | collective-permute-done | bytes 266272 | tf_op jit(solution)/shard_map/ppermute | solution.py:487
  100.3 2.4 collective-permute-done.5.refs_3_
  102.7 0.7 copy-done.22
  103.4 3.3 %shard_map.112 = (bf16[64,16,128]{2,1,0:T(8,128)(2,1)}, bf16[64,16,128]{2,1,0:T(8,128)(2,1)}, bf16[64,16,128]{2,1,0:T(8,128)(2,1)}, bf16[64,16,128]{2,1,0:T(8,128)(2,1)}) custom-call(s32[1]{0:T(128)} %bitcast.1.seq_ref, s32[1,4]{1,0:T(1,128)} %lengths_ref.3, s32[1,4]{1,0:T(1,128)} %slots_ref.3, bf16[1,4,64,16,128]{4,3,2,1,0:T(8,128)(2,1)} %cached_ref.1, ...), custom_call_target="tpu_custom_call" | custom-call | flops 1000 | bytes 1000 | tf_op jit(solution)/shard_map/pallas_call | solution.py:201
  106.7 19.3 %collective-permute-start.6 = (bf16[64,16,128]{2,1,0:T(8,128)(2,1)}, bf16[64,16,128]{2,1,0:T(8,128)(2,1)S(1)}, u32[]{:S(2)}, u32[]{:S(2)}) collective-permute-start(bf16[64,16,128]{2,1,0:T(8,128)(2,1)} %get-tuple-element.52), channel_id=1, source_target_pairs={{0,4},{4,8},{8,12},{12,0},{1,5},{5,9},{9,13},{13,1},{2,6},{6,10},{... | collective-permute-start | bytes 786440 | tf_op jit(solution)/shard_map/ppermute | solution.py:487
  126.0 3.1 %collective-permute-start.7 = (bf16[64,16,128]{2,1,0:T(8,128)(2,1)}, bf16[64,16,128]{2,1,0:T(8,128)(2,1)S(1)}, u32[]{:S(2)}, u32[]{:S(2)}) collective-permute-start(bf16[64,16,128]{2,1,0:T(8,128)(2,1)} %get-tuple-element.53), channel_id=1, source_target_pairs={{0,8},{4,12},{8,0},{12,4},{1,9},{5,13},{9,1},{13,5},{2,10},{6,14},... | collective-permute-start | bytes 786440 | tf_op jit(solution)/shard_map/ppermute | solution.py:487
  129.1 1.0 copy.16.run_ref
  130.1 5.5 %collective-permute-done.6.refs_1_ = bf16[64,16,128]{2,1,0:T(8,128)(2,1)S(1)} collective-permute-done((bf16[64,16,128]{2,1,0:T(8,128)(2,1)}, bf16[64,16,128]{2,1,0:T(8,128)(2,1)S(1)}, u32[]{:S(2)}, u32[]{:S(2)}) %collective-permute-start.6) | collective-permute-done | bytes 262176 | tf_op jit(solution)/shard_map/ppermute | solution.py:487
  135.6 12.2 %collective-permute-done.7.refs_2_ = bf16[64,16,128]{2,1,0:T(8,128)(2,1)S(1)} collective-permute-done((bf16[64,16,128]{2,1,0:T(8,128)(2,1)}, bf16[64,16,128]{2,1,0:T(8,128)(2,1)S(1)}, u32[]{:S(2)}, u32[]{:S(2)}) %collective-permute-start.7) | collective-permute-done | bytes 262176 | tf_op jit(solution)/shard_map/ppermute | solution.py:487
  147.8 0.7 copy-done.15
  148.6 4.9 %shard_map.113.refs_0_ = bf16[256,1024]{1,0:T(8,128)(2,1)} custom-call(s32[1]{0:T(128)} %bitcast.1.seq_ref, s32[1]{0:T(128)} %get-tuple-element.38.code_ref, f32[2,64]{1,0:T(2,128)} %copy-done.25, bf16[256,4096]{1,0:T(8,128)(2,1)} %bitcast.89, bf16[256,4096]{1,0:T(8,128)(2,1)} %bitcast.96, bf16[256,512]{1,0:T(8,128)(2,1)} %bitcast.103, ...), custom_call_target="tpu_custom_call" | custom-call | flops 1000 | bytes 1000 | tf_op jit(solution)/shard_map/pallas_call | solution.py:343
  153.5 1.3 collective-permute-start.11
  154.7 4.7 %shard_map.114.refs_2_.refs_4_ = bf16[256,1024]{1,0:T(8,128)(2,1)} custom-call(s32[1]{0:T(128)} %bitcast.1.seq_ref, s32[1]{0:T(128)} %get-tuple-element.38.code_ref, f32[2,64]{1,0:T(2,128)} %copy-done.25, bf16[256,4096]{1,0:T(8,128)(2,1)} %bitcast.90, bf16[256,4096]{1,0:T(8,128)(2,1)} %bitcast.97, bf16[256,512]{1,0:T(8,128)(2,1)} %bitcast.104, ...), custom_call_target="tpu_custom_call" | custom-call | flops 1000 | bytes 1000 | tf_op jit(solution)/shard_map/pallas_call | solution.py:343
  159.4 0.3 collective-permute-start.13
  159.8 1.0 collective-permute-start.9
  160.7 4.7 %shard_map.115.refs_4_.refs_8_ = bf16[256,1024]{1,0:T(8,128)(2,1)} custom-call(s32[1]{0:T(128)} %bitcast.1.seq_ref, s32[1]{0:T(128)} %get-tuple-element.38.code_ref, f32[2,64]{1,0:T(2,128)} %copy-done.25, bf16[256,4096]{1,0:T(8,128)(2,1)} %bitcast.91, bf16[256,4096]{1,0:T(8,128)(2,1)} %bitcast.98, bf16[256,512]{1,0:T(8,128)(2,1)} %bitcast.105, ...), custom_call_target="tpu_custom_call" | custom-call | flops 1000 | bytes 1000 | tf_op jit(solution)/shard_map/pallas_call | solution.py:343
  165.4 4.8 %shard_map.116.refs_6_.refs_12_ = bf16[256,1024]{1,0:T(8,128)(2,1)} custom-call(s32[1]{0:T(128)} %bitcast.1.seq_ref, s32[1]{0:T(128)} %get-tuple-element.38.code_ref, f32[2,64]{1,0:T(2,128)} %copy-done.25, bf16[256,4096]{1,0:T(8,128)(2,1)} %bitcast.92, bf16[256,4096]{1,0:T(8,128)(2,1)} %bitcast.99, bf16[256,512]{1,0:T(8,128)(2,1)} %bitcast.106, ...), custom_call_target="tpu_custom_call" | custom-call | flops 1000 | bytes 1000 | tf_op jit(solution)/shard_map/pallas_call | solution.py:343
  170.2 0.6 collective-permute-start.12
  170.8 7.4 %collective-permute-done.13.refs_2_.refs_6_ = bf16[256,1024]{1,0:T(8,128)(2,1)} collective-permute-done((bf16[256,1024]{1,0:T(8,128)(2,1)}, bf16[256,1024]{1,0:T(8,128)(2,1)}, u32[]{:S(2)}, u32[]{:S(2)}) %collective-permute-start.13) | collective-permute-done | bytes 524320 | tf_op jit(solution)/shard_map/ppermute | solution.py:585
  178.2 1.2 collective-permute-start.14
  179.4 1.2 collective-permute-start.18
  182.0 4.0 %shard_map.117 = bf16[512,256]{1,0:T(8,128)(2,1)} custom-call(s32[1]{0:T(128)} %bitcast.first_ref, bf16[256,1024]{1,0:T(8,128)(2,1)} %shard_map.113.refs_0_, bf16[256,1024]{1,0:T(8,128)(2,1)} %copy-done.2, bf16[256,1024]{1,0:T(8,128)(2,1)} %shard_map.114.refs_2_.refs_4_, bf16[256,1024]{1,0:T(8,128)(2,1)} %copy-done.3, ...), custom_call_target="tpu_custom_call" | custom-call | flops 1073741824 | bytes 6291456 | tf_op jit(solution)/shard_map/pallas_call | solution.py:419
  186.0 0.6 collective-permute-start.16
  186.7 6.4 %collective-permute-done.18.refs_4_.refs_10_ = bf16[256,1024]{1,0:T(8,128)(2,1)} collective-permute-done((bf16[256,1024]{1,0:T(8,128)(2,1)S(1)}, bf16[256,1024]{1,0:T(8,128)(2,1)}, u32[]{:S(2)}, u32[]{:S(2)}) %collective-permute-start.18) | collective-permute-done | bytes 524320 | tf_op jit(solution)/shard_map/ppermute | solution.py:585
  193.1 1.2 collective-permute-start.19
  194.2 10.1 %collective-permute-done.20.refs_6_.refs_14_ = bf16[256,1024]{1,0:T(8,128)(2,1)} collective-permute-done((bf16[256,1024]{1,0:T(8,128)(2,1)}, bf16[256,1024]{1,0:T(8,128)(2,1)}, u32[]{:S(2)}, u32[]{:S(2)}) %collective-permute-start.20) | collective-permute-done | bytes 524320 | tf_op jit(solution)/shard_map/ppermute | solution.py:585
  204.3 0.8 collective-permute-start.21
  205.1 4.0 %shard_map.118 = bf16[512,256]{1,0:T(8,128)(2,1)} custom-call(s32[1]{0:T(128)} %bitcast.16.first_ref, bf16[256,1024]{1,0:T(8,128)(2,1)} %shard_map.113.refs_0_, bf16[256,1024]{1,0:T(8,128)(2,1)} %copy-done.2, bf16[256,1024]{1,0:T(8,128)(2,1)} %shard_map.114.refs_2_.refs_4_, bf16[256,1024]{1,0:T(8,128)(2,1)} %copy-done.3, ...), custom_call_target="tpu_custom_call" | custom-call | flops 1073741824 | bytes 6291456 | tf_op jit(solution)/shard_map/pallas_call | solution.py:419
  209.1 0.3 collective-permute-start.15
  209.4 0.6 pad_add_fusion.first_ref
  210.1 0.8 copy-done.7
  211.2 0.8 copy-done.10
  211.9 5.6 %shard_map.119 = (bf16[512,256]{1,0:T(8,128)(2,1)}, bf16[512,256]{1,0:T(8,128)(2,1)}) custom-call(s32[2]{0:T(128)} %pad_add_fusion.first_ref, bf16[256,1024]{1,0:T(8,128)(2,1)} %copy-done.6, bf16[256,1024]{1,0:T(8,128)(2,1)} %copy-done.7, bf16[256,1024]{1,0:T(8,128)(2,1)} %collective-permute-done.13.refs_2_.refs_6_, bf16[256,1024]{1,0:T(8,128)(2,1)} %copy-done.8, ...), custom_call_target="tpu_custom_call" | custom-call | flops 2147483648 | bytes 8388608 | tf_op jit(solution)/shard_map/pallas_call | solution.py:419
  217.6 1.3 collective-permute-start.22
  218.9 4.6 %all-gather.7.cloned.1.call-done = bf16[16384,128]{1,0:T(8,128)(2,1)} async-done(((bf16[4096,128]{1,0:T(8,128)(2,1)}), bf16[16384,128]{1,0:T(8,128)(2,1)}) %all-gather.7.cloned.1.call-update) | async-done | bytes 4194320 | tf_op jit(solution)/shard_map/all_gather | solution.py:573
  223.5 5.5 %shard_map.120 = (bf16[512,256]{1,0:T(8,128)(2,1)}, bf16[512,256]{1,0:T(8,128)(2,1)}) custom-call(s32[1]{0:T(128)} %bitcast.16.first_ref, bf16[256,1024]{1,0:T(8,128)(2,1)} %shard_map.113.refs_0_, bf16[256,1024]{1,0:T(8,128)(2,1)} %copy-done.2, bf16[256,1024]{1,0:T(8,128)(2,1)} %copy-done.6, bf16[256,1024]{1,0:T(8,128)(2,1)} %copy-done.7, ...), custom_call_target="tpu_custom_call" | custom-call | flops 2147483648 | bytes 10485760 | tf_op jit(solution)/shard_map/pallas_call | solution.py:419
  229.0 0.3 collective-permute-start.25
  229.5 1.3 collective-permute-start.23
  230.7 5.4 %shard_map.121 = (bf16[512,256]{1,0:T(8,128)(2,1)}, bf16[512,256]{1,0:T(8,128)(2,1)}) custom-call(s32[1]{0:T(128)} %bitcast.first_ref, bf16[256,1024]{1,0:T(8,128)(2,1)} %shard_map.113.refs_0_, bf16[256,1024]{1,0:T(8,128)(2,1)} %copy-done.2, bf16[256,1024]{1,0:T(8,128)(2,1)} %copy-done.6, bf16[256,1024]{1,0:T(8,128)(2,1)} %copy-done.7, ...), custom_call_target="tpu_custom_call" | custom-call | flops 2147483648 | bytes 10485760 | tf_op jit(solution)/shard_map/pallas_call | solution.py:419
  236.1 0.3 collective-permute-done.25
  236.4 1.0 collective-permute-start.26
  237.4 1.0 add_convert_fusion
  238.4 0.5 collective-permute-start.27
  239.0 2.2 collective-permute-start.24
  241.2 1.4 collective-permute-done.26
  242.6 1.0 add_convert_fusion.1
  243.7 1.1 collective-permute-done.27
  244.8 2.5 collective-permute-start.28
  247.4 1.1 collective-permute-done.28
  249.0 1.0 copy-done.26
  (115 shorter events, 3.6 us)
Async XLA Ops:
  6.5 11.5 %copy-start.24 = (f32[1,256,64]{1,2,0:T(8,128)S(1)}, f32[1,256,64]{1,2,0:T(8,128)}, u32[]{:S(2)}) copy-start(f32[1,256,64]{1,2,0:T(8,128)} %param.16) | copy-start | bytes 196612
  6.5 174.6 %all-gather.5.cloned.1.call-start = ((), (), s32[]{:S(2)}) async-start(), calls=%async_computation | async-start | bytes 5242880 | tf_op jit(solution)/shard_map/all_gather | solution.py:573
  6.5 12.3 %copy-start.18 = (f32[1,256,64]{1,2,0:T(8,128)S(1)}, f32[1,256,64]{1,2,0:T(8,128)}, u32[]{:S(2)}) copy-start(f32[1,256,64]{1,2,0:T(8,128)} %param.15) | copy-start | bytes 196612
  9.6 213.9 %all-gather.7.cloned.1.call-start = ((), (), s32[]{:S(2)}) async-start(), calls=%async_computation.1 | async-start | bytes 5242880 | tf_op jit(solution)/shard_map/all_gather | solution.py:573
  13.3 18.3 %collective-permute-start = (bf16[64,16,128]{2,1,0:T(8,128)(2,1)}, bf16[64,16,128]{2,1,0:T(8,128)(2,1)S(1)}, u32[]{:S(2)}, u32[]{:S(2)}) collective-permute-start(bf16[64,16,128]{2,1,0:T(8,128)(2,1)} %get-tuple-element.41), channel_id=1, source_target_pairs={{0,4},{4,8},{8,12},{12,0},{1,5},{5,9},{9,13},{13,1},{2,6},{6,10},{... | collective-permute-start | bytes 786440 | tf_op jit(solution)/shard_map/ppermute | solution.py:487
  14.6 31.5 %collective-permute-start.1 = (bf16[64,16,128]{2,1,0:T(8,128)(2,1)}, bf16[64,16,128]{2,1,0:T(8,128)(2,1)S(1)}, u32[]{:S(2)}, u32[]{:S(2)}) collective-permute-start(bf16[64,16,128]{2,1,0:T(8,128)(2,1)} %get-tuple-element.42), channel_id=1, source_target_pairs={{0,8},{4,12},{8,0},{12,4},{1,9},{5,13},{9,1},{13,5},{2,10},{6,14},... | collective-permute-start | bytes 786440 | tf_op jit(solution)/shard_map/ppermute | solution.py:487
  17.0 29.1 %collective-permute-start.2 = (bf16[64,16,128]{2,1,0:T(8,128)(2,1)}, bf16[64,16,128]{2,1,0:T(8,128)(2,1)S(1)}, u32[]{:S(2)}, u32[]{:S(2)}) collective-permute-start(bf16[64,16,128]{2,1,0:T(8,128)(2,1)} %get-tuple-element.43), channel_id=1, source_target_pairs={{0,12},{4,0},{8,4},{12,8},{1,13},{5,1},{9,5},{13,9},{2,14},{6,2},{... | collective-permute-start | bytes 786440 | tf_op jit(solution)/shard_map/ppermute | solution.py:487
  18.4 8.4 %copy-start.25 = (f32[2,64]{1,0:T(2,128)}, f32[2,64]{1,0:T(2,128)S(1)}, u32[]{:S(2)}) copy-start(f32[2,64]{1,0:T(2,128)S(1)} %exp.8.total_ref) | copy-start | bytes 1540
  18.6 110.6 %copy-start.17 = (f32[256,4,16]{0,2,1:T(8,128)}, f32[256,4,16]{0,2,1:T(8,128)S(1)}, u32[]{:S(2)}) copy-start(f32[256,4,16]{0,2,1:T(8,128)S(1)} %reshape.105) | copy-start | bytes 196612
  31.5 116.3 %copy-start.11 = (bf16[64,16,128]{2,1,0:T(8,128)(2,1)}, bf16[64,16,128]{2,1,0:T(8,128)(2,1)S(1)}, u32[]{:S(2)}) copy-start(bf16[64,16,128]{2,1,0:T(8,128)(2,1)S(1)} %collective-permute-done.refs_5_) | copy-start | bytes 786436
  46.1 101.7 %copy-start.12 = (bf16[64,16,128]{2,1,0:T(8,128)(2,1)}, bf16[64,16,128]{2,1,0:T(8,128)(2,1)S(1)}, u32[]{:S(2)}) copy-start(bf16[64,16,128]{2,1,0:T(8,128)(2,1)S(1)} %collective-permute-done.1.refs_6_) | copy-start | bytes 786436
  46.1 101.7 %copy-start.13 = (bf16[64,16,128]{2,1,0:T(8,128)(2,1)}, bf16[64,16,128]{2,1,0:T(8,128)(2,1)S(1)}, u32[]{:S(2)}) copy-start(bf16[64,16,128]{2,1,0:T(8,128)(2,1)S(1)} %collective-permute-done.2.refs_7_) | copy-start | bytes 786436
  46.1 39.0 %collective-permute-start.3 = (bf16[65,16,128]{2,1,0:T(8,128)(2,1)}, bf16[65,16,128]{2,1,0:T(8,128)(2,1)S(1)}, u32[]{:S(2)}, u32[]{:S(2)}) collective-permute-start(bf16[65,16,128]{2,1,0:T(8,128)(2,1)} %get-tuple-element.46), channel_id=1, source_target_pairs={{0,4},{4,8},{8,12},{12,0},{1,5},{5,9},{9,13},{13,1},{2,6},{6,10},{... | collective-permute-start | bytes 798728 | tf_op jit(solution)/shard_map/ppermute | solution.py:487
  74.1 26.2 %collective-permute-start.4 = (bf16[65,16,128]{2,1,0:T(8,128)(2,1)}, bf16[65,16,128]{2,1,0:T(8,128)(2,1)S(1)}, u32[]{:S(2)}, u32[]{:S(2)}) collective-permute-start(bf16[65,16,128]{2,1,0:T(8,128)(2,1)} %get-tuple-element.48), channel_id=1, source_target_pairs={{0,8},{4,12},{8,0},{12,4},{1,9},{5,13},{9,1},{13,5},{2,10},{6,14},... | collective-permute-start | bytes 798728 | tf_op jit(solution)/shard_map/ppermute | solution.py:487
  74.1 28.6 %collective-permute-start.5 = (bf16[65,16,128]{2,1,0:T(8,128)(2,1)}, bf16[65,16,128]{2,1,0:T(8,128)(2,1)S(1)}, u32[]{:S(2)}, u32[]{:S(2)}) collective-permute-start(bf16[65,16,128]{2,1,0:T(8,128)(2,1)} %get-tuple-element.50), channel_id=1, source_target_pairs={{0,12},{4,0},{8,4},{12,8},{1,13},{5,1},{9,5},{13,9},{2,14},{6,2},{... | collective-permute-start | bytes 798728 | tf_op jit(solution)/shard_map/ppermute | solution.py:487
  85.1 17.6 %copy-start.20 = (bf16[65,16,128]{2,1,0:T(8,128)(2,1)}, bf16[65,16,128]{2,1,0:T(8,128)(2,1)S(1)}, u32[]{:S(2)}) copy-start(bf16[65,16,128]{2,1,0:T(8,128)(2,1)S(1)} %collective-permute-done.3.refs_1_) | copy-start | bytes 798724
  100.3 2.4 copy-start.21
  102.7 0.7 copy-start.22
  106.7 28.9 %collective-permute-start.6 = (bf16[64,16,128]{2,1,0:T(8,128)(2,1)}, bf16[64,16,128]{2,1,0:T(8,128)(2,1)S(1)}, u32[]{:S(2)}, u32[]{:S(2)}) collective-permute-start(bf16[64,16,128]{2,1,0:T(8,128)(2,1)} %get-tuple-element.52), channel_id=1, source_target_pairs={{0,4},{4,8},{8,12},{12,0},{1,5},{5,9},{9,13},{13,1},{2,6},{6,10},{... | collective-permute-start | bytes 786440 | tf_op jit(solution)/shard_map/ppermute | solution.py:487
  126.0 21.8 %collective-permute-start.7 = (bf16[64,16,128]{2,1,0:T(8,128)(2,1)}, bf16[64,16,128]{2,1,0:T(8,128)(2,1)S(1)}, u32[]{:S(2)}, u32[]{:S(2)}) collective-permute-start(bf16[64,16,128]{2,1,0:T(8,128)(2,1)} %get-tuple-element.53), channel_id=1, source_target_pairs={{0,8},{4,12},{8,0},{12,4},{1,9},{5,13},{9,1},{13,5},{2,10},{6,14},... | collective-permute-start | bytes 786440 | tf_op jit(solution)/shard_map/ppermute | solution.py:487
  129.1 18.7 %collective-permute-start.8 = (bf16[64,16,128]{2,1,0:T(8,128)(2,1)}, bf16[64,16,128]{2,1,0:T(8,128)(2,1)S(1)}, u32[]{:S(2)}, u32[]{:S(2)}) collective-permute-start(bf16[64,16,128]{2,1,0:T(8,128)(2,1)} %get-tuple-element.54), channel_id=1, source_target_pairs={{0,12},{4,0},{8,4},{12,8},{1,13},{5,1},{9,5},{13,9},{2,14},{6,2},{... | collective-permute-start | bytes 786440 | tf_op jit(solution)/shard_map/ppermute | solution.py:487
  135.6 12.2 %copy-start.14 = (bf16[64,16,128]{2,1,0:T(8,128)(2,1)}, bf16[64,16,128]{2,1,0:T(8,128)(2,1)S(1)}, u32[]{:S(2)}) copy-start(bf16[64,16,128]{2,1,0:T(8,128)(2,1)S(1)} %collective-permute-done.6.refs_1_) | copy-start | bytes 786436
  147.8 0.7 copy-start.15
  147.8 0.8 copy-start.16
  153.5 6.3 %copy-start = (bf16[256,1024]{1,0:T(8,128)(2,1)S(1)}, bf16[256,1024]{1,0:T(8,128)(2,1)}, u32[]{:S(2)}) copy-start(bf16[256,1024]{1,0:T(8,128)(2,1)} %shard_map.113.refs_0_) | copy-start | bytes 1572868
  153.5 16.8 %collective-permute-start.11 = (bf16[256,1024]{1,0:T(8,128)(2,1)}, bf16[256,1024]{1,0:T(8,128)(2,1)S(1)}, u32[]{:S(2)}, u32[]{:S(2)}) collective-permute-start(bf16[256,1024]{1,0:T(8,128)(2,1)} %shard_map.113.refs_0_), channel_id=1, source_target_pairs={{0,16},{16,0},{1,17},{17,1},{2,18},{18,2},{3,19},{19,3},{4,20},{20... | collective-permute-start | bytes 1572872 | tf_op jit(solution)/shard_map/ppermute | solution.py:585
  159.4 18.7 %collective-permute-start.13 = (bf16[256,1024]{1,0:T(8,128)(2,1)}, bf16[256,1024]{1,0:T(8,128)(2,1)}, u32[]{:S(2)}, u32[]{:S(2)}) collective-permute-start(bf16[256,1024]{1,0:T(8,128)(2,1)} %shard_map.114.refs_2_.refs_4_), channel_id=1, source_target_pairs={{0,16},{16,0},{1,17},{17,1},{2,18},{18,2},{3,19},{19,3},{4,20},{20... | collective-permute-start | bytes 1572872 | tf_op jit(solution)/shard_map/ppermute | solution.py:585
  159.8 20.9 %collective-permute-start.9 = (bf16[256,1024]{1,0:T(8,128)(2,1)S(1)}, bf16[256,1024]{1,0:T(8,128)(2,1)S(1)}, u32[]{:S(2)}, u32[]{:S(2)}) collective-permute-start(bf16[256,1024]{1,0:T(8,128)(2,1)S(1)} %copy-done), channel_id=1, source_target_pairs={{0,1},{1,0},{2,3},{3,2},{4,5},{5,4},{6,7},{7,6},{8,9},{9,8},{10,11... | collective-permute-start | bytes 1572872 | tf_op jit(solution)/shard_map/ppermute | solution.py:589
  160.7 20.2 %collective-permute-start.10 = (bf16[256,1024]{1,0:T(8,128)(2,1)}, bf16[256,1024]{1,0:T(8,128)(2,1)S(1)}, u32[]{:S(2)}, u32[]{:S(2)}) collective-permute-start(bf16[256,1024]{1,0:T(8,128)(2,1)} %shard_map.114.refs_2_.refs_4_), channel_id=1, source_target_pairs={{0,1},{1,0},{2,3},{3,2},{4,5},{5,4},{6,7},{7,6},{8,9},{9,8},{10,11... | collective-permute-start | bytes 1572872 | tf_op jit(solution)/shard_map/ppermute | solution.py:589
  165.4 4.8 %copy-start.1 = (bf16[256,1024]{1,0:T(8,128)(2,1)S(1)}, bf16[256,1024]{1,0:T(8,128)(2,1)}, u32[]{:S(2)}) copy-start(bf16[256,1024]{1,0:T(8,128)(2,1)} %shard_map.115.refs_4_.refs_8_) | copy-start | bytes 1572868
  170.2 39.8 %copy-start.6 = (bf16[256,1024]{1,0:T(8,128)(2,1)}, bf16[256,1024]{1,0:T(8,128)(2,1)S(1)}, u32[]{:S(2)}) copy-start(bf16[256,1024]{1,0:T(8,128)(2,1)S(1)} %collective-permute-done.11.refs_0_.refs_2_) | copy-start | bytes 1572868
  170.2 10.7 %collective-permute-start.12 = (bf16[256,1024]{1,0:T(8,128)(2,1)S(1)}, bf16[256,1024]{1,0:T(8,128)(2,1)S(1)}, u32[]{:S(2)}, u32[]{:S(2)}) collective-permute-start(bf16[256,1024]{1,0:T(8,128)(2,1)S(1)} %copy-done.1), channel_id=1, source_target_pairs={{0,1},{1,0},{2,3},{3,2},{4,5},{5,4},{6,7},{7,6},{8,9},{9,8},{10,11... | collective-permute-start | bytes 1572872 | tf_op jit(solution)/shard_map/ppermute | solution.py:589
  178.2 3.0 %collective-permute-start.14 = (bf16[256,1024]{1,0:T(8,128)(2,1)}, bf16[256,1024]{1,0:T(8,128)(2,1)S(1)}, u32[]{:S(2)}, u32[]{:S(2)}) collective-permute-start(bf16[256,1024]{1,0:T(8,128)(2,1)} %shard_map.116.refs_6_.refs_12_), channel_id=1, source_target_pairs={{0,1},{1,0},{2,3},{3,2},{4,5},{5,4},{6,7},{7,6},{8,9},{9,8},{10,11... | collective-permute-start | bytes 1572872 | tf_op jit(solution)/shard_map/ppermute | solution.py:589
  179.4 13.7 %collective-permute-start.18 = (bf16[256,1024]{1,0:T(8,128)(2,1)S(1)}, bf16[256,1024]{1,0:T(8,128)(2,1)}, u32[]{:S(2)}, u32[]{:S(2)}) collective-permute-start(bf16[256,1024]{1,0:T(8,128)(2,1)S(1)} %copy-done.1), channel_id=1, source_target_pairs={{0,16},{16,0},{1,17},{17,1},{2,18},{18,2},{3,19},{19,3},{4,20},{20... | collective-permute-start | bytes 1572872 | tf_op jit(solution)/shard_map/ppermute | solution.py:585
  180.6 0.8 copy-start.2
  180.6 23.7 %collective-permute-start.20 = (bf16[256,1024]{1,0:T(8,128)(2,1)}, bf16[256,1024]{1,0:T(8,128)(2,1)}, u32[]{:S(2)}, u32[]{:S(2)}) collective-permute-start(bf16[256,1024]{1,0:T(8,128)(2,1)} %shard_map.116.refs_6_.refs_12_), channel_id=1, source_target_pairs={{0,16},{16,0},{1,17},{17,1},{2,18},{18,2},{3,19},{19,3},{4,20},{20... | collective-permute-start | bytes 1572872 | tf_op jit(solution)/shard_map/ppermute | solution.py:585
  180.9 0.8 copy-start.3
  180.9 1.0 copy-start.4
  181.2 0.9 copy-start.5
  186.0 24.0 %collective-permute-start.16 = (bf16[256,1024]{1,0:T(8,128)(2,1)S(1)}, bf16[256,1024]{1,0:T(8,128)(2,1)S(1)}, u32[]{:S(2)}, u32[]{:S(2)}) collective-permute-start(bf16[256,1024]{1,0:T(8,128)(2,1)S(1)} %collective-permute-done.11.refs_0_.refs_2_), channel_id=1, source_target_pairs={{0,1},{1,0},{2,3},{3,2},{4,5},{5,4},{6,7},{7,6},{8,9},{9,8},{10,11... | collective-permute-start | bytes 1572872 | tf_op jit(solution)/shard_map/ppermute | solution.py:595
  186.6 23.4 %collective-permute-start.17 = (bf16[256,1024]{1,0:T(8,128)(2,1)}, bf16[256,1024]{1,0:T(8,128)(2,1)S(1)}, u32[]{:S(2)}, u32[]{:S(2)}) collective-permute-start(bf16[256,1024]{1,0:T(8,128)(2,1)} %collective-permute-done.13.refs_2_.refs_6_), channel_id=1, source_target_pairs={{0,1},{1,0},{2,3},{3,2},{4,5},{5,4},{6,7},{7,6},{8,9},{9,8},{10,11... | collective-permute-start | bytes 1572872 | tf_op jit(solution)/shard_map/ppermute | solution.py:595
  193.1 17.0 %collective-permute-start.19 = (bf16[256,1024]{1,0:T(8,128)(2,1)}, bf16[256,1024]{1,0:T(8,128)(2,1)S(1)}, u32[]{:S(2)}, u32[]{:S(2)}) collective-permute-start(bf16[256,1024]{1,0:T(8,128)(2,1)} %collective-permute-done.18.refs_4_.refs_10_), channel_id=1, source_target_pairs={{0,1},{1,0},{2,3},{3,2},{4,5},{5,4},{6,7},{7,6},{8,9},{9,8},{10,11... | collective-permute-start | bytes 1572872 | tf_op jit(solution)/shard_map/ppermute | solution.py:595
  204.3 5.7 %collective-permute-start.21 = (bf16[256,1024]{1,0:T(8,128)(2,1)}, bf16[256,1024]{1,0:T(8,128)(2,1)S(1)}, u32[]{:S(2)}, u32[]{:S(2)}) collective-permute-start(bf16[256,1024]{1,0:T(8,128)(2,1)} %collective-permute-done.20.refs_6_.refs_14_), channel_id=1, source_target_pairs={{0,1},{1,0},{2,3},{3,2},{4,5},{5,4},{6,7},{7,6},{8,9},{9,8},{10,11... | collective-permute-start | bytes 1572872 | tf_op jit(solution)/shard_map/ppermute | solution.py:595
  209.1 8.5 %collective-permute-start.15 = (bf16[512,256]{1,0:T(8,128)(2,1)}, bf16[512,256]{1,0:T(8,128)(2,1)S(1)}, u32[]{:S(2)}, u32[]{:S(2)}) collective-permute-start(bf16[512,256]{1,0:T(8,128)(2,1)} %shard_map.118), channel_id=1, source_target_pairs={{0,2},{2,0},{1,3},{3,1},{4,6},{6,4},{5,7},{7,5},{8,10},{10,8},{9,1... | collective-permute-start | bytes 786440 | tf_op jit(solution)/shard_map/ppermute | solution.py:448
  210.0 8.8 %copy-start.19 = (bf16[512,256]{1,0:T(8,128)(2,1)S(1)}, bf16[512,256]{1,0:T(8,128)(2,1)}, u32[]{:S(2)}) copy-start(bf16[512,256]{1,0:T(8,128)(2,1)} %shard_map.117) | copy-start | bytes 786436
  210.0 0.8 copy-start.7
  210.0 1.0 copy-start.8
  210.0 1.1 copy-start.9
  211.2 0.8 copy-start.10
  217.6 11.8 %collective-permute-start.22 = (bf16[512,256]{1,0:T(8,128)(2,1)}, bf16[512,256]{1,0:T(8,128)(2,1)S(1)}, u32[]{:S(2)}, u32[]{:S(2)}) collective-permute-start(bf16[512,256]{1,0:T(8,128)(2,1)} %get-tuple-element.63), channel_id=1, source_target_pairs={{0,2},{2,0},{1,3},{3,1},{4,6},{6,4},{5,7},{7,5},{8,10},{10,8},{9,1... | collective-permute-start | bytes 786440 | tf_op jit(solution)/shard_map/ppermute | solution.py:447
  223.5 5.9 %copy-start.23 = (bf16[512,256]{1,0:T(8,128)(2,1)S(1)}, bf16[512,256]{1,0:T(8,128)(2,1)}, u32[]{:S(2)}) copy-start(bf16[512,256]{1,0:T(8,128)(2,1)} %get-tuple-element.61) | copy-start | bytes 786436
  229.0 7.4 %collective-permute-start.25 = (bf16[512,256]{1,0:T(8,128)(2,1)}, bf16[512,256]{1,0:T(8,128)(2,1)S(1)}, u32[]{:S(2)}, u32[]{:S(2)}) collective-permute-start(bf16[512,256]{1,0:T(8,128)(2,1)} %get-tuple-element.66), channel_id=1, source_target_pairs={{0,2},{2,0},{1,3},{3,1},{4,6},{6,4},{5,7},{7,5},{8,10},{10,8},{9,1... | collective-permute-start | bytes 786440 | tf_op jit(solution)/shard_map/ppermute | solution.py:447
  229.4 7.0 %copy-start.27 = (bf16[512,256]{1,0:T(8,128)(2,1)S(1)}, bf16[512,256]{1,0:T(8,128)(2,1)}, u32[]{:S(2)}) copy-start(bf16[512,256]{1,0:T(8,128)(2,1)} %get-tuple-element.69) | copy-start | bytes 786436
  229.5 9.5 %collective-permute-start.23 = (bf16[512,256]{1,0:T(8,128)(2,1)S(1)}, bf16[512,256]{1,0:T(8,128)(2,1)S(1)}, u32[]{:S(2)}, u32[]{:S(2)}) collective-permute-start(bf16[512,256]{1,0:T(8,128)(2,1)S(1)} %add_convert_fusion.2), channel_id=1, source_target_pairs={{0,16},{16,0},{1,17},{17,1},{2,18},{18,2},{3,19},{19,3},{4,20},{20... | collective-permute-start | bytes 786440 | tf_op jit(solution)/shard_map/ppermute | solution.py:453
  236.4 6.2 %collective-permute-start.26 = (bf16[512,256]{1,0:T(8,128)(2,1)S(1)}, bf16[512,256]{1,0:T(8,128)(2,1)S(1)}, u32[]{:S(2)}, u32[]{:S(2)}) collective-permute-start(bf16[512,256]{1,0:T(8,128)(2,1)S(1)} %copy-done.27), channel_id=1, source_target_pairs={{0,2},{2,0},{1,3},{3,1},{4,6},{6,4},{5,7},{7,5},{8,10},{10,8},{9,1... | collective-permute-start | bytes 786440 | tf_op jit(solution)/shard_map/ppermute | solution.py:448
  238.4 6.3 %collective-permute-start.27 = (bf16[512,256]{1,0:T(8,128)(2,1)S(1)}, bf16[512,256]{1,0:T(8,128)(2,1)S(1)}, u32[]{:S(2)}, u32[]{:S(2)}) collective-permute-start(bf16[512,256]{1,0:T(8,128)(2,1)S(1)} %add_convert_fusion), channel_id=1, source_target_pairs={{0,16},{16,0},{1,17},{17,1},{2,18},{18,2},{3,19},{19,3},{4,20},{20... | collective-permute-start | bytes 786440 | tf_op jit(solution)/shard_map/ppermute | solution.py:453
  239.0 8.3 %collective-permute-start.24 = (bf16[2,256,256]{2,1,0:T(8,128)(2,1)S(1)}, bf16[2,256,256]{2,1,0:T(8,128)(2,1)S(1)}, u32[]{:S(2)}, u32[]{:S(2)}) collective-permute-start(bf16[2,256,256]{2,1,0:T(8,128)(2,1)S(1)} %pad_maximum_fusion), channel_id=1, source_target_pairs={{0,1},{1,0},{2,3},{3,2},{4,5},{5,4},{6,7},{7,6},{8,9},{9,8},{10,11... | collective-permute-start | bytes 786440 | tf_op jit(solution)/shard_map/ppermute | solution.py:455
  244.8 3.7 %collective-permute-start.28 = (bf16[2,256,256]{2,1,0:T(8,128)(2,1)S(1)}, bf16[2,256,256]{2,1,0:T(8,128)(2,1)S(1)}, u32[]{:S(2)}, u32[]{:S(2)}) collective-permute-start(bf16[2,256,256]{2,1,0:T(8,128)(2,1)S(1)} %pad_maximum_fusion.1), channel_id=1, source_target_pairs={{0,1},{1,0},{2,3},{3,2},{4,5},{5,4},{6,7},{7,6},{8,9},{9,8},{10,11... | collective-permute-start | bytes 786440 | tf_op jit(solution)/shard_map/ppermute | solution.py:455
  248.9 1.0 copy-start.26
Sparse Core Ops, SparseCore 0:
  9.7 133.1 all-gather.4
  144.5 78.9 all-gather.6
